TPU v7x, 32 devices: a whole 2x2x4 slice. The times are simulated.
32 devices in a mesh: grp: 2 (over x), cell: 16 (over z, y, core).
Axes of the slice: x: 2, y: 2, z: 4, core: 2. Of those that a mesh axis runs over, the one named last changes fastest.
Arguments:
- source_expr: bfloat16 [32768, 2048], P(('grp', 'cell')), parts along dimension 0, may hold values from 0 to 2
- target_expr: bfloat16 [32768, 2048], P(('grp', 'cell')), parts along dimension 0, may hold values from 0 to 2
- loadings: bfloat16 [2048, 256], P('cell'), may hold values from -0.125 to 0.125
- source_prev: float32 [32768, 256], P(('grp', 'cell')), parts along dimension 0, may hold values from 0.25 to 4, as said below
- target_prev: float32 [32768, 256], P(('grp', 'cell')), parts along dimension 0, may hold values from 0.25 to 4, as said below
- weights_prev: float32 [512], P('grp'), parts along dimension 0, may hold values from 0.25 to 4
- live_counts: int32 [2, 32], P(None, ('grp', 'cell')), parts along dimension 1, may hold values from 512 to 1024, as said below
Outputs:
- source_factor: float32 [32768, 256], P(('grp', 'cell')), parts along dimension 0
- target_factor: float32 [32768, 256], P(('grp', 'cell')), parts along dimension 0
- weights: float32 [512], P('grp'), parts along dimension 0
There are 2 independent parts, one for each index of `grp`. A program takes and returns all parts, laid end to end along the dimension named above; an argument that names none is the same for every part. Nothing has to cross between parts.
Inputs may be any that keep to these rules, and one draw needn't show every extreme that they name: `live_counts`: live cells of a time point on one device; the first that many rows of its block are live; in every draw some device holds 1024 live cells of each time point. `source_prev`: entries of the scaled source factor. `target_prev`: entries of the scaled target factor.
All inputs are finite; a program needn't handle non-finite values.
Results may differ from a plain program's by a relative error of at most 0.0003.
Values may be sent and summed in bfloat16 or wider, within the bound.
No kernel may reach another device: no remote copies, remote signals or barrier semaphores. Data moves between devices by JAX's collectives and lax.ppermute only.
A program may use at most 64 MiB of HBM per device.

v0:
```python
import jax
import jax.numpy as jnp
from jax import lax
from jax.sharding import PartitionSpec as P

D = 256
ITERS = 3


step_size = 1.0
precise = lax.Precision.HIGHEST


def column_tables(cross_src, cross_tgt, stats, col_mass):
    inverse = 1.0 / (D * col_mass)
    norm_q = stats[0]
    total_q = stats[1]
    norm_p = stats[2]
    total_p = stats[3]
    cost_cols = (
        norm_q * total_p + total_q * norm_p - 2.0 * jnp.sum(cross_src * cross_tgt, axis=0)
    ) / D
    kernel_mass = col_mass * jnp.exp(step_size * cost_cols / (col_mass * col_mass))
    mat_src = -2.0 * inverse * cross_tgt
    mat_tgt = -2.0 * inverse * cross_src
    coeffs = jnp.stack(
        [total_p * inverse, norm_p * inverse, total_q * inverse, norm_q * inverse, kernel_mass]
    )
    return (mat_src, mat_tgt, coeffs)


def kernel_of(embed, norms, factor, matrix, slope, offset):
    grad = (
        norms[:, None] * slope[None, :]
        + offset[None, :]
        + jnp.dot(embed, matrix, precision=precise)
    )
    return factor * jnp.exp(-step_size * grad)


def on_device(
    source_expr, target_expr, loadings, source_prev, target_prev, weights_prev, live_counts
):
    row_count = source_expr.shape[0]
    rank_size = source_prev.shape[1]
    cell_total = row_count * lax.axis_size("cell")
    gathered = lax.all_gather(loadings, "cell", axis=0, tiled=True)
    emb_src = jnp.dot(source_expr, gathered, preferred_element_type=jnp.float32)
    emb_tgt = jnp.dot(target_expr, gathered, preferred_element_type=jnp.float32)
    src_factor = source_prev / rank_size
    tgt_factor = target_prev / rank_size
    col_mass = weights_prev * (cell_total / rank_size)
    norm_src = jnp.sum(emb_src * emb_src, axis=1)
    norm_tgt = jnp.sum(emb_tgt * emb_tgt, axis=1)
    contract = (((0,), (0,)), ((), ()))
    cross_src = lax.dot_general(emb_src, src_factor, contract, precision=precise)
    cross_tgt = lax.dot_general(emb_tgt, tgt_factor, contract, precision=precise)
    stats = jnp.stack(
        [
            jnp.dot(norm_src, src_factor, precision=precise),
            jnp.sum(src_factor, axis=0),
            jnp.dot(norm_tgt, tgt_factor, precision=precise),
            jnp.sum(tgt_factor, axis=0),
        ]
    )
    full_src, full_tgt, full_stats = lax.psum((cross_src, cross_tgt, stats), "cell")
    mat_src, mat_tgt, coeffs = column_tables(full_src, full_tgt, full_stats, col_mass)
    kernel_src = kernel_of(emb_src, norm_src, src_factor, mat_src, coeffs[0], coeffs[1])
    kernel_tgt = kernel_of(emb_tgt, norm_tgt, tgt_factor, mat_tgt, coeffs[2], coeffs[3])
    kernel_mass = coeffs[4]
    local_row = jnp.arange(row_count, dtype=jnp.int32)
    live_src = local_row < live_counts[0, 0]
    live_tgt = local_row < live_counts[1, 0]
    ones_rank = jnp.ones((rank_size,), jnp.float32)
    start_src = jnp.dot(kernel_src, ones_rank, precision=precise)
    start_tgt = jnp.dot(kernel_tgt, ones_rank, precision=precise)
    totals = lax.psum(live_counts[:, 0].astype(jnp.float32), "cell")
    marg_src = jnp.where(live_src, cell_total / totals[0], jnp.float32(0.0))
    marg_tgt = jnp.where(live_tgt, cell_total / totals[1], jnp.float32(0.0))
    scale_src = marg_src / start_src
    scale_tgt = marg_tgt / start_tgt
    sum_src, sum_tgt = lax.psum(
        (
            jnp.dot(scale_src, kernel_src, precision=precise),
            jnp.dot(scale_tgt, kernel_tgt, precision=precise),
        ),
        "cell",
    )
    new_mass = jnp.cbrt(kernel_mass * sum_src * sum_tgt)
    dual_src = new_mass / sum_src
    dual_tgt = new_mass / sum_tgt

    def sweep(step_index, carry):
        dual_src, dual_tgt, scale_src, scale_tgt, new_mass = carry
        scale_src = marg_src / jnp.dot(kernel_src, dual_src, precision=precise)
        scale_tgt = marg_tgt / jnp.dot(kernel_tgt, dual_tgt, precision=precise)
        sum_src, sum_tgt = lax.psum(
            (
                jnp.dot(scale_src, kernel_src, precision=precise),
                jnp.dot(scale_tgt, kernel_tgt, precision=precise),
            ),
            "cell",
        )
        new_mass = jnp.cbrt(kernel_mass * sum_src * sum_tgt)
        return (new_mass / sum_src, new_mass / sum_tgt, scale_src, scale_tgt, new_mass)

    dual_src, dual_tgt, scale_src, scale_tgt, new_mass = lax.fori_loop(
        0, ITERS - 1, sweep, (dual_src, dual_tgt, scale_src, scale_tgt, new_mass)
    )
    source_factor = rank_size * (scale_src[:, None] * kernel_src * dual_src[None, :])
    target_factor = rank_size * (scale_tgt[:, None] * kernel_tgt * dual_tgt[None, :])
    weights = new_mass * (rank_size / cell_total)
    return (source_factor, target_factor, weights)


def solution(mesh):
    in_specs = (
        P(("grp", "cell"), None),
        P(("grp", "cell"), None),
        P("cell", None),
        P(("grp", "cell"), None),
        P(("grp", "cell"), None),
        P("grp"),
        P(None, ("grp", "cell")),
    )
    out_specs = (P(("grp", "cell"), None), P(("grp", "cell"), None), P("grp"))
    return jax.shard_map(
        on_device, mesh=mesh, in_specs=in_specs, out_specs=out_specs, check_vma=False
    )
```

profile of v0, /device:TPU:0, one launch (start us, length us, event | category | flops | bytes accessed | tf_op | source)
XLA Modules:
  0.0 305.8 jit_solution(16602146637463606097)
XLA Ops:
  7.2 0.0 all-gather.2.cloned.1.call-start
  7.2 0.7 all-gather.2.cloned.1.call-update
  7.9 0.0 all-reduce.8.cloned.1.call-start
  7.9 1.4 fusion.41
  9.3 1.4 multiply_reduce_fusion.3
  10.7 1.4 multiply_reduce_fusion.2
  12.1 0.7 convert_bitcast_fusion
  12.8 38.1 %all-gather.2.cloned.1.call-done = bf16[2048,256]{1,0:T(8,128)(2,1)} async-done(((bf16[128,256]{1,0:T(8,128)(2,1)}), bf16[2048,256]{1,0:T(8,128)(2,1)}) %all-gather.2.cloned.1.call-update) | async-done | bytes 1048592 | tf_op jit(solution)/shard_map/all_gather | solution.py:47
  50.8 4.9 %multiply_reduce_fusion = (f32[1024]{0:T(1024)S(1)}, f32[1024,256]{0,1:T(8,128)}) fusion(bf16[1024,2048]{1,0:T(8,128)(2,1)} %param.10, bf16[2048,256]{1,0:T(8,128)(2,1)} %all-gather.2.cloned.1.call-done), kind=kOutput, calls=%fused_computation.17 | convolution fusion | flops 1074265088 | bytes 6295552 | tf_op jit(solution)/shard_map/dot_general | solution.py:49
  55.7 0.5 fusion.12
  56.3 1.3 multiply_reduce_fusion.1
  57.6 0.0 copy-start.2
  57.6 0.5 fusion.16
  58.2 32.3 %all-reduce.2 = (f32[4,256]{1,0:T(4,128)S(1)}, f32[2]{0:T(128)S(1)}) all-reduce(f32[4,256]{1,0:T(4,128)S(1)} %pad_maximum_fusion, f32[2]{0:T(128)S(1)} %convert_bitcast_fusion), channel_id=1, replica_groups=mesh['grp'=2,'cell'=16] {'cell'}, use_global_device_ids=true, to_apply=%region_4.0 | all-reduce | flops 1026 | bytes 8208 | tf_op jit(solution)/shard_map/psum | solution.py:66
  90.5 3.0 fusion.10
  93.4 1.7 fusion.14
  95.2 0.0 all-reduce.8.cloned.1.call-update
  95.2 0.6 fusion.42
  97.2 85.5 %all-reduce.8.cloned.1.call-done = (f32[256,256]{1,0:T(8,128)}, f32[256,256]{1,0:T(8,128)}) async-done(((f32[256,256]{1,0:T(8,128)}, f32[256,256]{1,0:T(8,128)}), (f32[256,256]{1,0:T(8,128)}, f32[256,256]{1,0:T(8,128)})) %all-reduce.8.cloned.1.call-update) | async-done | bytes 524304 | tf_op jit(solution)/shard_map/psum | solution.py:66
  182.7 3.4 %fusion.6 = f32[1024,256]{1,0:T(8,128)S(1)} fusion(f32[1024,256]{0,1:T(8,128)} %get-tuple-element.152, f32[1024,256]{1,0:T(8,128)S(1)} %copy-done, f32[256]{0:T(256)S(1)} %get-tuple-element.143, f32[256]{0:T(256)S(1)} %get-tuple-element.135, f32[1024]{0:T(1024)S(1)} %get-tuple-element.151, f32[256,256]{1,0:T(8,128)} %get-tuple-element.129, ...), kind=kOutput, calls=%fused_computation.10 | convolution fusion | flops 806944768 | bytes 3415040 | tf_op jit(solution)/shard_map/dot_general | solution.py:36
  186.1 1.0 fusion.26
  187.1 0.0 copy-done.5
  187.1 0.1 multiply_reduce_fusion.4
  187.2 2.1 fusion.9
  189.3 1.0 fusion.28
  190.3 1.3 select_divide_fusion.2
  191.6 0.5 fusion.47
  192.1 0.5 fusion.48
  192.6 32.0 %all-reduce.1 = (f32[256]{0:T(256)S(1)}, f32[256]{0:T(256)S(1)}) all-reduce(f32[256]{0:T(256)S(1)} %bitcast.109, f32[256]{0:T(256)S(1)} %bitcast.108), channel_id=1, replica_groups=mesh['grp'=2,'cell'=16] {'cell'}, use_global_device_ids=true, to_apply=%region_10.11 | all-reduce | flops 512 | bytes 4096 | tf_op jit(solution)/shard_map/psum | solution.py:82
  224.7 0.5 copy-done.10
  225.2 68.8 %while.19 = (s32[]{:T(128)}, f32[256]{0:T(256)S(1)}, f32[256]{0:T(256)S(1)}, f32[1024]{0:T(1024)}, f32[1024]{0:T(1024)}, /*index=5*/f32[256]{0:T(256)}, f32[1024...) while((s32[]{:T(128)}, f32[256]{0:T(256)S(1)}, ...), condition=%wide.region_14.15_spmd.clone, body=%wide.region_11.14_spmd.clone.sunk | while | flops 12590594 | bytes 4280553 | solution.py:107
  225.2 1.0 fusion.94
  226.2 1.0 fusion.95
  227.2 1.3 select_divide_fusion.5
  228.5 0.5 fusion.96
  229.0 0.5 fusion.97
  229.5 29.5 %all-reduce.5 = (f32[256]{0:T(256)S(1)}, f32[256]{0:T(256)S(1)}) all-reduce(f32[256]{0:T(256)S(1)} %bitcast.92, f32[256]{0:T(256)S(1)} %bitcast.93), channel_id=1, replica_groups=mesh['grp'=2,'cell'=16] {'cell'}, use_global_device_ids=true, to_apply=%region_13.13 | all-reduce | flops 512 | bytes 4096 | tf_op jit(solution)/shard_map/while/body/eval_jaxpr/psum | solution.py:97
  259.1 0.5 copy-done.11
  259.6 1.0 fusion.94
  260.6 1.0 fusion.95
  261.6 1.3 select_divide_fusion.5
  262.9 0.5 fusion.96
  263.4 0.5 fusion.97
  263.9 29.5 %all-reduce.5 = (f32[256]{0:T(256)S(1)}, f32[256]{0:T(256)S(1)}) all-reduce(f32[256]{0:T(256)S(1)} %bitcast.92, f32[256]{0:T(256)S(1)} %bitcast.93), channel_id=1, replica_groups=mesh['grp'=2,'cell'=16] {'cell'}, use_global_device_ids=true, to_apply=%region_13.13 | all-reduce | flops 512 | bytes 4096 | tf_op jit(solution)/shard_map/while/body/eval_jaxpr/psum | solution.py:97
  293.5 0.5 copy-done.11
  294.0 1.2 broadcast_multiply_fusion
  295.2 1.9 multiply_multiply_fusion
  297.1 1.8 multiply_multiply_fusion.1
  (41 shorter events, 0.2 us)
Async XLA Ops:
  7.2 43.7 %all-gather.2.cloned.1.call-start = ((), (), s32[]{:S(2)}) async-start(), calls=%async_computation | async-start | bytes 1114112 | tf_op jit(solution)/shard_map/all_gather | solution.py:47
  7.9 174.8 %all-reduce.8.cloned.1.call-start = ((), (), s32[]{:S(2)}) async-start(), calls=%async_computation.1 | async-start | bytes 1048576 | tf_op jit(solution)/shard_map/psum | solution.py:66
  12.8 43.0 %copy-start = (f32[1024,256]{1,0:T(8,128)S(1)}, f32[1024,256]{1,0:T(8,128)}, u32[]{:S(2)}) copy-start(f32[1024,256]{1,0:T(8,128)} %param.13) | copy-start | bytes 3145732
  50.8 5.5 %copy-start.13 = (bf16[1024,2048]{1,0:T(8,128)(2,1)S(1)}, bf16[1024,2048]{1,0:T(8,128)(2,1)}, u32[]{:S(2)}) copy-start(bf16[1024,2048]{1,0:T(8,128)(2,1)} %param.9) | copy-start | bytes 12582916
  50.8 5.5 %copy-start.14 = (bf16[2048,256]{1,0:T(8,128)(2,1)S(1)}, bf16[2048,256]{1,0:T(8,128)(2,1)}, u32[]{:S(2)}) copy-start(bf16[2048,256]{1,0:T(8,128)(2,1)} %all-gather.2.cloned.1.call-done) | copy-start | bytes 3145732
  56.3 1.4 copy-start.1
  57.6 125.0 %copy-start.2 = (f32[1024,256]{0,1:T(8,128)}, f32[1024,256]{0,1:T(8,128)S(1)}, u32[]{:S(2)}) copy-start(f32[1024,256]{0,1:T(8,128)S(1)} %get-tuple-element.154) | copy-start | bytes 3145732
  57.6 37.6 %copy-start.12 = (f32[256]{0:T(256)S(1)}, f32[256]{0:T(256)}, u32[]{:S(2)}) copy-start(f32[256]{0:T(256)} %param.14) | copy-start | bytes 3076
  182.7 4.4 %copy-start.4 = (f32[256,256]{1,0:T(8,128)S(1)}, f32[256,256]{1,0:T(8,128)}, u32[]{:S(2)}) copy-start(f32[256,256]{1,0:T(8,128)} %get-tuple-element.128) | copy-start | bytes 786436
  182.7 4.4 %copy-start.5 = (f32[256,256]{1,0:T(8,128)S(1)}, f32[256,256]{1,0:T(8,128)}, u32[]{:S(2)}) copy-start(f32[256,256]{1,0:T(8,128)} %get-tuple-element.129) | copy-start | bytes 786436
  182.7 4.5 %copy-start.3 = (f32[1024,256]{0,1:T(8,128)S(1)}, f32[1024,256]{0,1:T(8,128)}, u32[]{:S(2)}) copy-start(f32[1024,256]{0,1:T(8,128)} %copy-done.2) | copy-start | bytes 3145732
  191.6 33.1 %copy-start.6 = (f32[1024]{0:T(1024)}, f32[1024]{0:T(1024)S(1)}, u32[]{:S(2)}) copy-start(f32[1024]{0:T(1024)S(1)} %get-tuple-element.246) | copy-start | bytes 12292
  191.6 33.1 %copy-start.8 = (f32[1024]{0:T(1024)}, f32[1024]{0:T(1024)S(1)}, u32[]{:S(2)}) copy-start(f32[1024]{0:T(1024)S(1)} %get-tuple-element.245) | copy-start | bytes 12292
  224.6 0.6 copy-start.10
  228.4 30.6 %copy-start.7 = (f32[1024]{0:T(1024)}, f32[1024]{0:T(1024)S(1)}, u32[]{:S(2)}) copy-start(f32[1024]{0:T(1024)S(1)} %get-tuple-element.274) | copy-start | bytes 12292 | tf_op jit(solution)/shard_map/while
  228.4 30.6 %copy-start.9 = (f32[1024]{0:T(1024)}, f32[1024]{0:T(1024)S(1)}, u32[]{:S(2)}) copy-start(f32[1024]{0:T(1024)S(1)} %get-tuple-element.273) | copy-start | bytes 12292 | tf_op jit(solution)/shard_map/while
  259.0 0.6 copy-start.11
  262.8 30.6 %copy-start.7 = (f32[1024]{0:T(1024)}, f32[1024]{0:T(1024)S(1)}, u32[]{:S(2)}) copy-start(f32[1024]{0:T(1024)S(1)} %get-tuple-element.274) | copy-start | bytes 12292 | tf_op jit(solution)/shard_map/while
  262.8 30.6 %copy-start.9 = (f32[1024]{0:T(1024)}, f32[1024]{0:T(1024)S(1)}, u32[]{:S(2)}) copy-start(f32[1024]{0:T(1024)S(1)} %get-tuple-element.273) | copy-start | bytes 12292 | tf_op jit(solution)/shard_map/while
  293.4 0.6 copy-start.11
Sparse Core Ops, SparseCore 0:
  10.2 40.6 all-gather.1
  95.3 87.2 all-reduce.7
where the time goes:
time: 306 us
  waiting for transfers between devices  124 us (41%)
  blocking collectives  123 us (40%)
  matrix products  26.5 us (9%)
  between operations  15.6 us (5%)
  other arithmetic  12.4 us (4%)
  local copies, waits for them, and re-layouts  3.65 us (1%)
    psum x1, waiting for transfers between devices, on_device(): lax.psum((cross_src, cross_tgt, stats), 'cell')  85.5 us
    psum x2, blocking collectives, sweep(): lax.psum((jnp.dot(scale_src, kernel_src, precision=precise), jnp.dot(scal...  59 us
    all_gather x1, waiting for transfers between devices, on_device(): gathered = lax.all_gather(loadings, 'cell', axis=0, tiled=True)  38.1 us
    psum x1, blocking collectives, on_device(): lax.psum((cross_src, cross_tgt, stats), 'cell')  32.3 us
    psum x1, blocking collectives, on_device(): lax.psum((jnp.dot(scale_src, kernel_src, precision=precise), jnp.dot(scal...  32 us
  transfers between devices with their start and end apart: 2, of which 2 were waited for; matrix products, arithmetic and copies ran while one was open for 2% of the time, Pallas kernels for 0%

commit v1 on v0

v1 whole, which is shorter than its diff:
```python
import jax
import jax.numpy as jnp
from jax import lax
from jax.sharding import PartitionSpec as P

D = 256
ITERS = 3


step_size = 1.0
precise = lax.Precision.HIGHEST


def partners(count, mask):
    return [(i, i ^ mask) for i in range(count)]


def swap(value, count, mask):
    return lax.ppermute(value, "cell", partners(count, mask))


def gather_loadings(loadings, count):
    top = count.bit_length() - 1
    stack = loadings[None]
    masks = [1 << b for b in range(top)]
    if top >= 3:
        high, low = masks[-1], masks[-2]
        pieces = [stack] + [swap(stack, count, m) for m in (low, high, low | high)]
        stack = jnp.concatenate(pieces)
        masks = masks[:-2]
    order = list(range(stack.shape[0]))
    order = [0, low, high, low | high] if top >= 3 else [0]
    for mask in reversed(masks):
        stack = jnp.concatenate([stack, swap(stack, count, mask)])
        order = order + [o | mask for o in order]
    return stack, order


def total_over_cells(value, count):
    copies = jnp.broadcast_to(value[None], (count,) + value.shape)
    return jnp.sum(lax.all_to_all(copies, "cell", 0, 0), axis=0)


def same_core(count):
    return [list(range(0, count, 2)), list(range(1, count, 2))]


def column_tables(cross_src, cross_tgt, stats, col_mass):
    inverse = 1.0 / (D * col_mass)
    norm_q = stats[0]
    total_q = stats[1]
    norm_p = stats[2]
    total_p = stats[3]
    cost_cols = (
        norm_q * total_p + total_q * norm_p - 2.0 * jnp.sum(cross_src * cross_tgt, axis=0)
    ) / D
    kernel_mass = col_mass * jnp.exp(step_size * cost_cols / (col_mass * col_mass))
    mat_src = -2.0 * inverse * cross_tgt
    mat_tgt = -2.0 * inverse * cross_src
    coeffs = jnp.stack(
        [total_p * inverse, norm_p * inverse, total_q * inverse, norm_q * inverse, kernel_mass]
    )
    return (mat_src, mat_tgt, coeffs)


def kernel_of(embed, norms, factor, matrix, slope, offset):
    grad = (
        norms[:, None] * slope[None, :]
        + offset[None, :]
        + jnp.dot(embed, matrix, precision=precise)
    )
    return factor * jnp.exp(-step_size * grad)


def on_device(
    source_expr, target_expr, loadings, source_prev, target_prev, weights_prev, live_counts
):
    count = lax.axis_size("cell")
    me = lax.axis_index("cell")
    core = me % 2
    half = count // 2
    row_count = source_expr.shape[0]
    rank_size = source_prev.shape[1]
    cell_total = row_count * count
    stack, order = gather_loadings(loadings, count)
    place = [0] * count
    for position, mask in enumerate(order):
        place[mask] = position
    chosen = jnp.asarray(place, jnp.int32)[jnp.arange(count, dtype=jnp.int32) ^ me]
    gathered = stack[chosen].reshape(-1, loadings.shape[1])
    emb_src = jnp.dot(source_expr, gathered, preferred_element_type=jnp.float32)
    emb_tgt = jnp.dot(target_expr, gathered, preferred_element_type=jnp.float32)
    src_factor = source_prev / rank_size
    tgt_factor = target_prev / rank_size
    col_mass = weights_prev * (cell_total / rank_size)
    norm_src = jnp.sum(emb_src * emb_src, axis=1)
    norm_tgt = jnp.sum(emb_tgt * emb_tgt, axis=1)
    contract = (((0,), (0,)), ((), ()))
    cross_src = lax.dot_general(emb_src, src_factor, contract, precision=precise)
    cross_tgt = lax.dot_general(emb_tgt, tgt_factor, contract, precision=precise)
    live = live_counts[:, 0].astype(jnp.float32)

    def extras(norms, factor, number):
        return jnp.concatenate(
            [
                jnp.dot(norms[None, :], factor, precision=precise),
                jnp.sum(factor, axis=0)[None, :],
                jnp.full((1, rank_size), number),
                jnp.zeros((5, rank_size), jnp.float32),
            ]
        )

    part_src = jnp.concatenate([cross_src, extras(norm_src, src_factor, live[0])])
    part_tgt = jnp.concatenate([cross_tgt, extras(norm_tgt, tgt_factor, live[1])])
    first = core == 0
    own = jnp.where(first, part_src, part_tgt)
    own = own + swap(jnp.where(first, part_tgt, part_src), count, 1)
    rows = D // half
    blocks = jnp.concatenate(
        [
            own[:D].reshape(half, rows, rank_size),
            jnp.broadcast_to(own[D:][None], (half, 8, rank_size)),
        ],
        axis=1,
    )
    groups = same_core(count)
    blocks = jnp.sum(lax.all_to_all(blocks, "cell", 0, 0, axis_index_groups=groups), axis=0)
    copies = jnp.broadcast_to(blocks[:rows][None], (half, rows, rank_size))
    full = lax.all_to_all(copies, "cell", 0, 0, axis_index_groups=groups).reshape(D, rank_size)
    full = jnp.concatenate([full, blocks[rows:]])
    other = swap(full, count, 1)
    sum_a = jnp.where(first, full, other)
    sum_b = jnp.where(first, other, full)
    full_stats = jnp.concatenate([sum_a[D : D + 2], sum_b[D : D + 2]])
    mat_src, mat_tgt, coeffs = column_tables(sum_a[:D], sum_b[:D], full_stats, col_mass)
    kernel_src = kernel_of(emb_src, norm_src, src_factor, mat_src, coeffs[0], coeffs[1])
    kernel_tgt = kernel_of(emb_tgt, norm_tgt, tgt_factor, mat_tgt, coeffs[2], coeffs[3])
    kernel_mass = coeffs[4]
    local_row = jnp.arange(row_count, dtype=jnp.int32)
    live_src = local_row < live_counts[0, 0]
    live_tgt = local_row < live_counts[1, 0]
    marg_src = jnp.where(live_src, cell_total / sum_a[D + 2, 0], jnp.float32(0.0))
    marg_tgt = jnp.where(live_tgt, cell_total / sum_b[D + 2, 0], jnp.float32(0.0))
    dual_src = jnp.ones((rank_size,), jnp.float32)
    dual_tgt = jnp.ones((rank_size,), jnp.float32)
    for _ in range(ITERS):
        scale_src = marg_src / jnp.dot(kernel_src, dual_src, precision=precise)
        scale_tgt = marg_tgt / jnp.dot(kernel_tgt, dual_tgt, precision=precise)
        sums = jnp.concatenate(
            [
                jnp.dot(scale_src[None, :], kernel_src, precision=precise),
                jnp.dot(scale_tgt[None, :], kernel_tgt, precision=precise),
            ],
            axis=1,
        )
        sums = total_over_cells(sums, count)
        sum_src, sum_tgt = sums[0, :rank_size], sums[0, rank_size:]
        new_mass = jnp.cbrt(kernel_mass * sum_src * sum_tgt)
        dual_src = new_mass / sum_src
        dual_tgt = new_mass / sum_tgt
    source_factor = rank_size * (scale_src[:, None] * kernel_src * dual_src[None, :])
    target_factor = rank_size * (scale_tgt[:, None] * kernel_tgt * dual_tgt[None, :])
    weights = new_mass * (rank_size / cell_total)
    return (source_factor, target_factor, weights)


def solution(mesh):
    in_specs = (
        P(("grp", "cell"), None),
        P(("grp", "cell"), None),
        P("cell", None),
        P(("grp", "cell"), None),
        P(("grp", "cell"), None),
        P("grp"),
        P(None, ("grp", "cell")),
    )
    out_specs = (P(("grp", "cell"), None), P(("grp", "cell"), None), P("grp"))
    return jax.shard_map(
        on_device, mesh=mesh, in_specs=in_specs, out_specs=out_specs, check_vma=False
    )
```

time: 306 us -> 125 us (0.41)
  waiting for transfers between devices: 124 us -> 21.7 us
  blocking collectives: 123 us -> 33.9 us
  starting transfers between devices: 0.08 us -> 15.2 us
  between operations: 15.6 us -> 2.49 us
  local copies, waits for them, and re-layouts: 3.65 us -> 13.4 us
    psum x4 -> x0, blocking collectives: 123 us -> none  [the longest x2 59 us: sweep(): lax.psum((jnp.dot(scale_src, kernel_src, precision=precise), jnp.dot(scal...]
    psum x1 -> x0, waiting for transfers between devices: 85.5 us -> none  [on_device(): lax.psum((cross_src, cross_tgt, stats), 'cell')]
    all_gather x1 -> x0, waiting for transfers between devices: 38.1 us -> none  [on_device(): gathered = lax.all_gather(loadings, 'cell', axis=0, tiled=True)]
    all_to_all x0 -> x3, blocking collectives: none -> 33.9 us  [the longest x2 18.4 us: total_over_cells(): return jnp.sum(lax.all_to_all(copies, 'cell', 0, 0), axis=0)]
    all_to_all x0 -> x2, waiting for transfers between devices: none -> 13.9 us  [the longest x1 8.26 us: on_device(): lax.all_to_all(copies, 'cell', 0, 0, axis_index_groups=groups)]
    ppermute x0 -> x7, starting transfers between devices: none -> 7.91 us  [swap(): return lax.ppermute(value, 'cell', partners(count, mask))]
    ppermute x0 -> x7, waiting for transfers between devices: none -> 7.81 us  [swap(): return lax.ppermute(value, 'cell', partners(count, mask))]
    all_to_all x0 -> x2, starting transfers between devices: none -> 7.25 us  [the longest x1 3.66 us: total_over_cells(): return jnp.sum(lax.all_to_all(copies, 'cell', 0, 0), axis=0)]
  transfers between devices with their start and end apart: 2 -> 9, of which waited for: 2 -> 7; matrix products, arithmetic and copies ran while one was open for 2% -> 7% of each run, Pallas kernels for 0% -> 0%
where the time goes in v1:
time: 125 us; the launch traced here: 124 us
  blocking collectives  33.9 us (27%)
  matrix products  26.5 us (21%)
  waiting for transfers between devices  21.7 us (17%)
  starting transfers between devices  15.2 us (12%)
  local copies, waits for them, and re-layouts  13.4 us (11%)
  other arithmetic  11.3 us (9%)
  between operations  2.49 us (2%)
    all_to_all x2, blocking collectives, total_over_cells(): return jnp.sum(lax.all_to_all(copies, 'cell', 0, 0), axis=0)  18.4 us
    all_to_all x1, blocking collectives, on_device(): lax.all_to_all(blocks, 'cell', 0, 0, axis_index_groups=groups)  15.5 us
    all_to_all x1, waiting for transfers between devices, on_device(): lax.all_to_all(copies, 'cell', 0, 0, axis_index_groups=groups)  8.26 us
    ppermute x7, starting transfers between devices, swap(): return lax.ppermute(value, 'cell', partners(count, mask))  7.91 us
    ppermute x7, waiting for transfers between devices, swap(): return lax.ppermute(value, 'cell', partners(count, mask))  7.81 us
    dot_general x2, matrix products, kernel_of(): jnp.dot(embed, matrix, precision=precise)  6.54 us
    all_to_all x1, waiting for transfers between devices, total_over_cells(): return jnp.sum(lax.all_to_all(copies, 'cell', 0, 0), axis=0)  5.63 us
    unnamed x22, local copies, waits for them, and re-layouts  4.45 us
  transfers between devices with their start and end apart: 9, of which 7 were waited for; matrix products, arithmetic and copies ran while one was open for 7% of the time, Pallas kernels for 0%

profile of v1, /device:TPU:0, one launch (start us, length us, event | category | flops | bytes accessed | tf_op | source)
XLA Modules:
  0.0 124.5 jit_solution(921715857156767884)
XLA Ops:
  0.6 3.1 %collective-permute-start = (bf16[1,128,256]{2,1,0:T(8,128)(2,1)}, bf16[1,128,256]{2,1,0:T(8,128)(2,1)S(1)}, u32[]{:S(2)}, u32[]{:S(2)}) collective-permute-start(bf16[1,128,256]{2,1,0:T(8,128)(2,1)} %bitcast.99), channel_id=1, source_target_pairs={{0,4},{1,5},{2,6},{3,7},{4,0},{5,1},{6,2},{7,3},{8,12},{9,13},{10,... | collective-permute-start | bytes 196616 | tf_op jit(solution)/shard_map/ppermute | solution.py:19
  3.7 2.6 %collective-permute-start.1 = (bf16[1,128,256]{2,1,0:T(8,128)(2,1)}, bf16[1,128,256]{2,1,0:T(8,128)(2,1)S(1)}, u32[]{:S(2)}, u32[]{:S(2)}) collective-permute-start(bf16[1,128,256]{2,1,0:T(8,128)(2,1)} %bitcast.100), channel_id=1, source_target_pairs={{0,8},{1,9},{2,10},{3,11},{4,12},{5,13},{6,14},{7,15},{8,0},{9,1},... | collective-permute-start | bytes 196616 | tf_op jit(solution)/shard_map/ppermute | solution.py:19
  6.3 1.5 %constant_dynamic-update-slice_fusion.4 = (bf16[8,128,256]{2,1,0:T(8,128)(2,1)}, bf16[16,128,256]{2,1,0:T(8,128)(2,1)S(1)}) fusion(bf16[128,256]{1,0:T(8,128)(2,1)} %param.10), kind=kLoop, calls=%fused_computation.46 | loop fusion | bytes 196608
  7.9 1.3 %gather_fusion = s32[16]{0:T(128)S(1)} fusion(s32[16]{0:T(128)} %constant.51.clone, s32[1024]{0:T(1024)S(1)} %pad_clamp_fusion.1), kind=kCustom, calls=%fused_computation | custom fusion | bytes 192 | tf_op jit(solution)/shard_map/gather | solution.py:89
  9.2 0.7 convert_element_type.4
  9.9 1.3 %collective-permute-done.1 = bf16[1,128,256]{2,1,0:T(8,128)(2,1)S(1)} collective-permute-done((bf16[1,128,256]{2,1,0:T(8,128)(2,1)}, bf16[1,128,256]{2,1,0:T(8,128)(2,1)S(1)}, u32[]{:S(2)}, u32[]{:S(2)}) %collective-permute-start.1) | collective-permute-done | bytes 65568 | tf_op jit(solution)/shard_map/ppermute | solution.py:19
  11.2 1.4 %collective-permute-done.2 = bf16[1,128,256]{2,1,0:T(8,128)(2,1)S(1)} collective-permute-done((bf16[1,128,256]{2,1,0:T(8,128)(2,1)}, bf16[1,128,256]{2,1,0:T(8,128)(2,1)S(1)}, u32[]{:S(2)}, u32[]{:S(2)}) %collective-permute-start.2) | collective-permute-done | bytes 65568 | tf_op jit(solution)/shard_map/ppermute | solution.py:19
  12.6 0.9 pad_maximum_fusion.2
  13.5 1.6 %collective-permute-start.3 = (bf16[4,128,256]{2,1,0:T(8,128)(2,1)S(1)}, bf16[4,128,256]{2,1,0:T(8,128)(2,1)S(1)}, u32[]{:S(2)}, u32[]{:S(2)}) collective-permute-start(bf16[4,128,256]{2,1,0:T(8,128)(2,1)S(1)} %pad_maximum_fusion.2), channel_id=1, source_target_pairs={{0,2},{1,3},{2,0},{3,1},{4,6},{5,7},{6,4},{7,5},{8,10},{9,11},{10,... | collective-permute-start | bytes 786440 | tf_op jit(solution)/shard_map/ppermute | solution.py:19
  15.1 0.6 constant_dynamic-update-slice_fusion.3
  15.7 0.6 constant_dynamic-update-slice_fusion.2
  16.4 0.6 constant_dynamic-update-slice_fusion.1
  17.0 3.0 %collective-permute-done.3 = bf16[4,128,256]{2,1,0:T(8,128)(2,1)S(1)} collective-permute-done((bf16[4,128,256]{2,1,0:T(8,128)(2,1)S(1)}, bf16[4,128,256]{2,1,0:T(8,128)(2,1)S(1)}, u32[]{:S(2)}, u32[]{:S(2)}) %collective-permute-start.3) | collective-permute-done | bytes 262176 | tf_op jit(solution)/shard_map/ppermute | solution.py:19
  20.0 0.7 constant_dynamic-update-slice_fusion
  20.7 0.7 fusion.50
  21.4 1.4 %multiply_reduce_fusion.2 = f32[256]{0:T(256)S(1)} fusion(f32[1024,256]{1,0:T(8,128)} %param.12), kind=kLoop, calls=%fused_computation.14 | loop fusion | flops 524032 | bytes 1049600 | tf_op jit(solution)/shard_map/reduce_sum | solution.py:107
  23.6 0.9 copy-done.5
  24.6 4.2 %multiply_reduce_fusion.1 = (f32[1024]{0:T(1024)S(1)}, f32[256,1024]{1,0:T(8,128)S(1)}) fusion(bf16[2048,256]{1,0:T(8,128)(2,1)S(1)} %bitcast.96, bf16[1024,2048]{1,0:T(8,128)(2,1)} %param.8), kind=kOutput, calls=%fused_computation.13 | convolution fusion | flops 1074265088 | bytes 6295552 | tf_op jit(solution)/shard_map/dot_general | solution.py:91
  28.8 3.0 %multiply_reduce_fusion = (f32[1024]{0:T(1024)S(1)}, f32[256,1024]{1,0:T(8,128)S(1)}) fusion(bf16[2048,256]{1,0:T(8,128)(2,1)} %bitcast.97, bf16[1024,2048]{1,0:T(8,128)(2,1)S(1)} %copy-done.8), kind=kOutput, calls=%fused_computation.12 | convolution fusion | flops 1074265088 | bytes 6295552 | tf_op jit(solution)/shard_map/dot_general | solution.py:92
  31.8 1.7 %fusion.8 = f32[256,256]{1,0:T(8,128)} fusion(f32[256,1024]{1,0:T(8,128)S(1)} %get-tuple-element.43, f32[1024,256]{1,0:T(8,128)S(1)} %copy-done), kind=kOutput, calls=%fused_computation.17 | convolution fusion | flops 805568512 | bytes 2359296 | tf_op jit(solution)/shard_map/dot_general | solution.py:100
  34.1 1.0 fusion.12
  35.7 0.7 broadcast_in_dim.42
  36.4 1.0 concatenate.36
  37.4 0.6 broadcast_in_dim.40
  38.7 1.2 collective-permute-done.5
  40.0 15.5 %all_to_all.25 = f32[8,40,256]{2,1,0:T(8,128)S(1)} all-to-all(f32[8,40,256]{2,1,0:T(8,128)S(1)} %pad_maximum_fusion), channel_id=1, replica_groups={{0,2,4,6,8,10,12,14},{1,3,5,7,9,11,13,15},{16,18,20,22,24,26,28,30},{17..., dimensions={0} | all-to-all | bytes 655360 | tf_op jit(solution)/shard_map/all_to_all | solution.py:127
  55.5 0.7 broadcast_in_dim.44
  56.2 3.6 %all-to-all-start.1 = ((f32[8,32,256]{2,1,0:T(8,128)}), f32[8,32,256]{2,1,0:T(8,128)S(1)}, u32[]{:S(2)}, u32[]{:S(2)}) async-start(f32[8,32,256]{2,1,0:T(8,128)} %broadcast_in_dim.44), calls=%async_computation.1 | async-start | bytes 524288 | tf_op jit(solution)/shard_map/all_to_all | solution.py:129
  59.8 8.3 %all-to-all-done.1 = f32[8,32,256]{2,1,0:T(8,128)S(1)} async-done(((f32[8,32,256]{2,1,0:T(8,128)}), f32[8,32,256]{2,1,0:T(8,128)S(1)}, u32[]{:S(2)}, u32[]{:S(2)}) %all-to-all-start.1) | async-done | bytes 262176 | tf_op jit(solution)/shard_map/all_to_all | solution.py:129
  68.8 0.9 collective-permute-done.6
  71.0 3.3 %fusion.2 = f32[1024,256]{1,0:T(8,128)S(1)} fusion(f32[256,1024]{1,0:T(8,128)} %copy-done.3, f32[1024,256]{1,0:T(8,128)S(1)} %copy-done, f32[256]{0:T(256)S(1)} %get-tuple-element.34, f32[256]{0:T(256)S(1)} %get-tuple-element.5, f32[1024]{0:T(1024)S(1)} %get-tuple-element.42, f32[264,256]{1,0:T(8,128)S(1)} %get-tuple-element.7, f32[256]{0:T(256)S(1)} %get-tuple-element.35), kind=kOutput, calls=%fused_computation.5 | convolution fusion | flops 806944768 | bytes 3415040 | tf_op jit(solution)/shard_map/dot_general | solution.py:70
  74.2 1.0 fusion.26
  77.1 3.3 %fusion.5 = f32[1024,256]{1,0:T(8,128)S(1)} fusion(f32[256,1024]{1,0:T(8,128)} %copy-done.2, f32[1024,256]{1,0:T(8,128)S(1)} %copy-done.1, f32[256]{0:T(256)S(1)} %get-tuple-element.36, f32[256]{0:T(256)S(1)} %get-tuple-element.37, f32[1024]{0:T(1024)S(1)} %get-tuple-element.44, f32[264,256]{1,0:T(8,128)S(1)} %get-tuple-element.8, f32[256]{0:T(256)S(1)} %get-tuple-element.35), kind=kOutput, calls=%fused_computation.9 | convolution fusion | flops 806944768 | bytes 3415040 | tf_op jit(solution)/shard_map/dot_general | solution.py:70
  80.3 1.0 fusion.28
  82.1 0.6 select_divide_fusion.5
  83.9 3.7 %all-to-all-start.2 = ((f32[16,1,512]{2,1,0:T(1,128)}), f32[16,1,512]{2,1,0:T(1,128)S(1)}, u32[]{:S(2)}, u32[]{:S(2)}) async-start(f32[16,1,512]{2,1,0:T(1,128)} %broadcast_in_dim.92), calls=%async_computation.2 | async-start | bytes 65536 | tf_op jit(solution)/shard_map/all_to_all | solution.py:41
  87.6 1.0 multiply_reduce_fusion.4
  88.6 5.6 %all-to-all-done.2 = f32[16,1,512]{2,1,0:T(1,128)S(1)} async-done(((f32[16,1,512]{2,1,0:T(1,128)}), f32[16,1,512]{2,1,0:T(1,128)S(1)}, u32[]{:S(2)}, u32[]{:S(2)}) %all-to-all-start.2) | async-done | bytes 32800 | tf_op jit(solution)/shard_map/all_to_all | solution.py:41
  94.3 1.0 fusion.55
  96.4 1.0 fusion.53
  97.4 0.7 select_divide_fusion.4
  98.6 9.2 %all_to_all.26 = f32[16,1,512]{2,1,0:T(1,128)S(1)} all-to-all(f32[16,1,512]{2,1,0:T(1,128)S(1)} %broadcast_in_dim.94), channel_id=1, replica_groups=mesh['grp'=2,'cell'=16] {'cell'}, dimensions={0} | all-to-all | bytes 65536 | tf_op jit(solution)/shard_map/all_to_all | solution.py:41
  107.9 1.0 fusion.59
  110.1 1.0 fusion.57
  111.0 0.7 select_divide_fusion.3
  112.3 9.2 %all_to_all.27 = f32[16,1,512]{2,1,0:T(1,128)S(1)} all-to-all(f32[16,1,512]{2,1,0:T(1,128)S(1)} %broadcast_in_dim.96), channel_id=1, replica_groups=mesh['grp'=2,'cell'=16] {'cell'}, dimensions={0} | all-to-all | bytes 65536 | tf_op jit(solution)/shard_map/all_to_all | solution.py:41
  122.1 1.2 multiply_multiply_fusion.1
  123.3 1.2 multiply_multiply_fusion
  (76 shorter events, 11.2 us)
Async XLA Ops:
  0.6 22.1 %copy-start.1 = (f32[1024,256]{1,0:T(8,128)S(1)}, f32[1024,256]{1,0:T(8,128)}, u32[]{:S(2)}) copy-start(f32[1024,256]{1,0:T(8,128)} %param.11) | copy-start | bytes 3145732
  0.6 9.2 %collective-permute-start = (bf16[1,128,256]{2,1,0:T(8,128)(2,1)}, bf16[1,128,256]{2,1,0:T(8,128)(2,1)S(1)}, u32[]{:S(2)}, u32[]{:S(2)}) collective-permute-start(bf16[1,128,256]{2,1,0:T(8,128)(2,1)} %bitcast.99), channel_id=1, source_target_pairs={{0,4},{1,5},{2,6},{3,7},{4,0},{5,1},{6,2},{7,3},{8,12},{9,13},{10,... | collective-permute-start | bytes 196616 | tf_op jit(solution)/shard_map/ppermute | solution.py:19
  3.7 7.5 %collective-permute-start.1 = (bf16[1,128,256]{2,1,0:T(8,128)(2,1)}, bf16[1,128,256]{2,1,0:T(8,128)(2,1)S(1)}, u32[]{:S(2)}, u32[]{:S(2)}) collective-permute-start(bf16[1,128,256]{2,1,0:T(8,128)(2,1)} %bitcast.100), channel_id=1, source_target_pairs={{0,8},{1,9},{2,10},{3,11},{4,12},{5,13},{6,14},{7,15},{8,0},{9,1},... | collective-permute-start | bytes 196616 | tf_op jit(solution)/shard_map/ppermute | solution.py:19
  6.3 6.3 %collective-permute-start.2 = (bf16[1,128,256]{2,1,0:T(8,128)(2,1)}, bf16[1,128,256]{2,1,0:T(8,128)(2,1)S(1)}, u32[]{:S(2)}, u32[]{:S(2)}) collective-permute-start(bf16[1,128,256]{2,1,0:T(8,128)(2,1)} %bitcast.101), channel_id=1, source_target_pairs={{0,12},{1,13},{2,14},{3,15},{4,8},{5,9},{6,10},{7,11},{8,4},{9,5},... | collective-permute-start | bytes 196616 | tf_op jit(solution)/shard_map/ppermute | solution.py:19
  13.5 6.5 %collective-permute-start.3 = (bf16[4,128,256]{2,1,0:T(8,128)(2,1)S(1)}, bf16[4,128,256]{2,1,0:T(8,128)(2,1)S(1)}, u32[]{:S(2)}, u32[]{:S(2)}) collective-permute-start(bf16[4,128,256]{2,1,0:T(8,128)(2,1)S(1)} %pad_maximum_fusion.2), channel_id=1, source_target_pairs={{0,2},{1,3},{2,0},{3,1},{4,6},{5,7},{6,4},{7,5},{8,10},{9,11},{10,... | collective-permute-start | bytes 786440 | tf_op jit(solution)/shard_map/ppermute | solution.py:19
  20.7 2.2 %collective-permute-start.4 = (bf16[8,128,256]{2,1,0:T(8,128)(2,1)}, bf16[8,128,256]{2,1,0:T(8,128)(2,1)S(1)}, u32[]{:S(2)}, u32[]{:S(2)}) collective-permute-start(bf16[8,128,256]{2,1,0:T(8,128)(2,1)} %get-tuple-element.13), channel_id=1, source_target_pairs={{0,1},{1,0},{2,3},{3,2},{4,5},{5,4},{6,7},{7,6},{8,9},{9,8},{10,11... | collective-permute-start | bytes 1572872 | tf_op jit(solution)/shard_map/ppermute | solution.py:19
  23.6 1.0 copy-start.5
  23.6 5.1 %copy-start.8 = (bf16[1024,2048]{1,0:T(8,128)(2,1)S(1)}, bf16[1024,2048]{1,0:T(8,128)(2,1)}, u32[]{:S(2)}) copy-start(bf16[1024,2048]{1,0:T(8,128)(2,1)} %param.9) | copy-start | bytes 12582916
  28.8 5.3 %copy-start.2 = (f32[256,1024]{1,0:T(8,128)}, f32[256,1024]{1,0:T(8,128)S(1)}, u32[]{:S(2)}) copy-start(f32[256,1024]{1,0:T(8,128)S(1)} %get-tuple-element.45) | copy-start | bytes 3145732
  28.8 3.0 %copy-start = (f32[1024,256]{1,0:T(8,128)S(1)}, f32[1024,256]{1,0:T(8,128)}, u32[]{:S(2)}) copy-start(f32[1024,256]{1,0:T(8,128)} %param.12) | copy-start | bytes 3145732
  31.7 3.3 %copy-start.3 = (f32[256,1024]{1,0:T(8,128)}, f32[256,1024]{1,0:T(8,128)S(1)}, u32[]{:S(2)}) copy-start(f32[256,1024]{1,0:T(8,128)S(1)} %get-tuple-element.43) | copy-start | bytes 3145732
  35.1 33.1 %copy-start.7 = (s32[2,1]{0,1:T(1,128)S(1)}, s32[2,1]{0,1:T(1,128)}, u32[]{:S(2)}) copy-start(s32[2,1]{0,1:T(1,128)} %param.14) | copy-start | bytes 28
  35.1 35.8 %copy-start.6 = (f32[256]{0:T(256)S(1)}, f32[256]{0:T(256)}, u32[]{:S(2)}) copy-start(f32[256]{0:T(256)} %param.13) | copy-start | bytes 3076
  38.1 1.7 %collective-permute-start.5 = (f32[264,256]{1,0:T(8,128)S(1)}, f32[264,256]{1,0:T(8,128)S(1)}, u32[]{:S(2)}, u32[]{:S(2)}) collective-permute-start(f32[264,256]{1,0:T(8,128)S(1)} %broadcast_select_fusion.2), channel_id=1, source_target_pairs={{0,1},{1,0},{2,3},{3,2},{4,5},{5,4},{6,7},{7,6},{8,9},{9,8},{10,11... | collective-permute-start | bytes 811016 | tf_op jit(solution)/shard_map/ppermute | solution.py:19
  56.2 11.9 %all-to-all-start.1 = ((f32[8,32,256]{2,1,0:T(8,128)}), f32[8,32,256]{2,1,0:T(8,128)S(1)}, u32[]{:S(2)}, u32[]{:S(2)}) async-start(f32[8,32,256]{2,1,0:T(8,128)} %broadcast_in_dim.44), calls=%async_computation.1 | async-start | bytes 524288 | tf_op jit(solution)/shard_map/all_to_all | solution.py:129
  68.1 1.6 %collective-permute-start.6 = (f32[264,256]{1,0:T(8,128)S(1)}, f32[264,256]{1,0:T(8,128)S(1)}, u32[]{:S(2)}, u32[]{:S(2)}) collective-permute-start(f32[264,256]{1,0:T(8,128)S(1)} %pad_maximum_fusion.1), channel_id=1, source_target_pairs={{0,1},{1,0},{2,3},{3,2},{4,5},{5,4},{6,7},{7,6},{8,9},{9,8},{10,11... | collective-permute-start | bytes 811016 | tf_op jit(solution)/shard_map/ppermute | solution.py:19
  69.8 10.6 %copy-start.4 = (f32[264,256]{1,0:T(8,128)}, f32[264,256]{1,0:T(8,128)S(1)}, u32[]{:S(2)}) copy-start(f32[264,256]{1,0:T(8,128)S(1)} %get-tuple-element.8) | copy-start | bytes 811012
  83.9 10.3 %all-to-all-start.2 = ((f32[16,1,512]{2,1,0:T(1,128)}), f32[16,1,512]{2,1,0:T(1,128)S(1)}, u32[]{:S(2)}, u32[]{:S(2)}) async-start(f32[16,1,512]{2,1,0:T(1,128)} %broadcast_in_dim.92), calls=%async_computation.2 | async-start | bytes 65536 | tf_op jit(solution)/shard_map/all_to_all | solution.py:41

commit v2 on v0

v2 whole, which is shorter than its diff:
```python
import functools

import jax
import jax.numpy as jnp
from jax import lax
from jax.experimental import pallas as pl
from jax.experimental.pallas import tpu as pltpu
from jax.sharding import PartitionSpec as P

D = 256
ITERS = 3
STEPS = 4
EXTRA = 8

step_size = 1.0
f32 = jnp.float32
bf16 = jnp.bfloat16
LIMIT = 24 * 1024 * 1024


def swap(value, count, mask):
    return lax.ppermute(value, "cell", [(i, i ^ mask) for i in range(count)])


def gather_loadings(loadings, count):
    bits = [1 << b for b in range(count.bit_length() - 1)]
    low, high = bits[-2], bits[-1]
    own = loadings[None]
    stack = jnp.concatenate([own] + [swap(own, count, m) for m in (low, high, low | high)])
    masks = [0, low, high, low | high]
    for bit in reversed(bits[2:-2]):
        stack = jnp.concatenate([stack, swap(stack, count, bit)])
        masks = masks + [m | bit for m in masks]
    across = swap(stack, count, 2)
    pair = swap(stack, count, 1)
    both = swap(across, count, 1)
    return [
        (stack, masks),
        (pair, [m | 1 for m in masks]),
        (across, [m | 2 for m in masks]),
        (both, [m | 3 for m in masks]),
    ]


def halves(value):
    upper = value.astype(bf16)
    return upper, (value - upper.astype(f32)).astype(bf16)


def dot3(a, b, left, right):
    dims = (((left,), (right,)), ((), ()))
    dot = functools.partial(lax.dot_general, dimension_numbers=dims, preferred_element_type=f32)
    return dot(a[0], b[0]) + (dot(a[0], b[1]) + dot(a[1], b[0]))


def embed_kernel(masks, place, live, xs, xt, *refs):
    pieces = refs[: len(masks)]
    qs, qt, emb_s, emb_t, own, send, table, cross, stats = refs[len(masks) :]
    step = pl.program_id(0)
    me = place[0]
    rank = qs.shape[1]

    @pl.when(step == 0)
    def _():
        rows = pieces[0].shape[1]
        for piece, mask_list in zip(pieces, masks):
            for j, mask in enumerate(mask_list):
                start = pl.multiple_of((me ^ mask) * rows, rows)
                table[pl.ds(start, rows), :] = piece[j]
        cross[...] = jnp.zeros_like(cross)
        stats[...] = jnp.zeros_like(stats)

    for t, (x, q, emb) in enumerate(((xs, qs, emb_s), (xt, qt, emb_t))):
        value = jnp.dot(x[...], table[...], preferred_element_type=f32)
        emb[...] = value
        factor = q[...] / rank
        norms = jnp.sum(value * value, axis=1, keepdims=True)
        stats[2 * t : 2 * t + 1, :] += jnp.sum(norms * factor, axis=0, keepdims=True)
        stats[2 * t + 1 : 2 * t + 2, :] += jnp.sum(factor, axis=0, keepdims=True)
        cross[t] += dot3(halves(value), halves(factor), 0, 0)

    @pl.when(step == pl.num_programs(0) - 1)
    def _():
        stats[4:5, :] = jnp.full((1, rank), live[0].astype(f32))
        stats[5:6, :] = jnp.full((1, rank), live[1].astype(f32))
        core = me % 2
        blocks, rows = own.shape[0], own.shape[1] - EXTRA
        for b in range(blocks):
            own[b, 0:rows, :] = cross[core, b * rows : (b + 1) * rows, :]
            send[b, 0:rows, :] = cross[1 - core, b * rows : (b + 1) * rows, :]
            own[b, rows:, :] = stats[...]
            send[b, rows:, :] = stats[...]


def embed(place, live, xs, xt, pieces, qs, qt, half):
    rows, genes = xs.shape
    rank = qs.shape[1]
    block = rows // STEPS
    dim = pieces[0][0].shape[2]
    block_rows = dim // half + EXTRA
    masks = [m for _, m in pieces]
    whole = lambda shape: pl.BlockSpec(shape, lambda i: (0,) * len(shape))
    part = lambda width: pl.BlockSpec((block, width), lambda i: (i, 0))
    smem = pl.BlockSpec(memory_space=pltpu.SMEM)
    return pl.pallas_call(
        functools.partial(embed_kernel, masks),
        grid=(STEPS,),
        in_specs=[smem, smem, part(genes), part(genes)]
        + [whole(p.shape) for p, _ in pieces]
        + [part(rank), part(rank)],
        out_specs=[part(dim), part(dim), whole((half, block_rows, rank)), whole((half, block_rows, rank))],
        out_shape=[jax.ShapeDtypeStruct((rows, dim), f32)] * 2
        + [jax.ShapeDtypeStruct((half, block_rows, rank), f32)] * 2,
        scratch_shapes=[
            pltpu.VMEM((genes, dim), bf16),
            pltpu.VMEM((2, dim, rank), f32),
            pltpu.VMEM((EXTRA, rank), f32),
        ],
        compiler_params=pltpu.CompilerParams(vmem_limit_bytes=LIMIT),
        name="embed",
    )(place, live, xs, xt, *[p for p, _ in pieces], qs, qt)


def marginal(step, block, live, total, cells):
    row = lax.broadcasted_iota(jnp.int32, (block, 1), 0) + step * block
    return jnp.where(row < live, cells / total, 0.0)


def store_sums(sums, copies):
    for i in range(copies.shape[0]):
        copies[i] = sums[...]


def kernels_kernel(
    cells, place, live, es, et, qs, qt, mine, other, stats, weights, ks, kt, copies, mass_out,
    mats, coeffs, sums,
):
    step = pl.program_id(0)
    core = place[0] % 2
    block, rank = qs.shape

    @pl.when(step == 0)
    def _():
        first = core == 0
        a, b = mine[...], other[...]
        cross_s, cross_t = jnp.where(first, a, b), jnp.where(first, b, a)
        col_mass = weights[...] * (cells / rank)
        inverse = 1.0 / (D * col_mass)
        norm_q, total_q, norm_p, total_p = (stats[i : i + 1, :] for i in range(4))
        cost = (
            norm_q * total_p + total_q * norm_p
            - 2.0 * jnp.sum(cross_s * cross_t, axis=0, keepdims=True)
        ) / D
        mass_out[...] = col_mass * jnp.exp(step_size * cost / (col_mass * col_mass))
        mats[0], mats[1] = halves((-2.0 * inverse) * cross_t)
        mats[2], mats[3] = halves((-2.0 * inverse) * cross_s)
        coeffs[0:1, :] = total_p * inverse
        coeffs[1:2, :] = norm_p * inverse
        coeffs[2:3, :] = total_q * inverse
        coeffs[3:4, :] = norm_q * inverse
        sums[...] = jnp.zeros_like(sums)

    for t, (e, q, k) in enumerate(((es, qs, ks), (et, qt, kt))):
        value = e[...]
        norms = jnp.sum(value * value, axis=1, keepdims=True)
        grad = (
            norms * coeffs[2 * t : 2 * t + 1, :] + coeffs[2 * t + 1 : 2 * t + 2, :]
            + dot3(halves(value), (mats[2 * t], mats[2 * t + 1]), 1, 0)
        )
        kernel = (q[...] / rank) * jnp.exp(-step_size * grad)
        k[...] = kernel
        total = stats[4 + t, 0]
        scale = marginal(step, block, live[t], total, cells) / jnp.sum(kernel, axis=1, keepdims=True)
        sums[t : t + 1, :] += jnp.sum(scale * kernel, axis=0, keepdims=True)

    @pl.when(step == pl.num_programs(0) - 1)
    def _():
        store_sums(sums, copies)


def cube_root(x):
    y = jnp.exp(jnp.log(x) * (1.0 / 3.0))
    refined = y - (y - x / (y * y)) * (1.0 / 3.0)
    return jnp.where((x > 0.0) & (x < jnp.inf), refined, y)


def duals_of(parts, kernel_mass):
    sums = jnp.sum(parts[...], axis=0)
    sum_s, sum_t = sums[0:1, :], sums[1:2, :]
    mass = cube_root(kernel_mass[...] * sum_s * sum_t)
    return mass, mass / sum_s, mass / sum_t


def sweep_kernel(cells, last, live, ks, kt, parts, kernel_mass, stats, *refs):
    if last:
        ss, st, copies, sums, duals = refs
    else:
        copies, sums, duals = refs
    step = pl.program_id(0)
    block = ks.shape[0]

    @pl.when(step == 0)
    def _():
        _, dual_s, dual_t = duals_of(parts, kernel_mass)
        duals[0:1, :] = dual_s
        duals[1:2, :] = dual_t
        sums[...] = jnp.zeros_like(sums)

    for t, k in enumerate((ks, kt)):
        kernel = k[...]
        weighted = jnp.sum(kernel * duals[t : t + 1, :], axis=1, keepdims=True)
        scale = marginal(step, block, live[t], stats[4 + t, 0], cells) / weighted
        scaled = scale * kernel
        sums[t : t + 1, :] += jnp.sum(scaled, axis=0, keepdims=True)
        if last:
            (ss, st)[t][...] = scaled

    @pl.when(step == pl.num_programs(0) - 1)
    def _():
        store_sums(sums, copies)


def finish_kernel(cells, ss, st, parts, kernel_mass, fs, ft, weights, duals):
    step = pl.program_id(0)
    rank = ss.shape[1]

    @pl.when(step == 0)
    def _():
        mass, dual_s, dual_t = duals_of(parts, kernel_mass)
        duals[0:1, :] = dual_s
        duals[1:2, :] = dual_t
        weights[...] = mass * (rank / cells)

    fs[...] = rank * (ss[...] * duals[0:1, :])
    ft[...] = rank * (st[...] * duals[1:2, :])


def specs(rows, rank):
    block = rows // STEPS
    whole = lambda shape: pl.BlockSpec(shape, lambda i: (0,) * len(shape))
    part = pl.BlockSpec((block, rank), lambda i: (i, 0))
    smem = pl.BlockSpec(memory_space=pltpu.SMEM)
    return whole, part, smem


def kernels(cells, count, place, live, es, et, qs, qt, mine, other, stats, weights):
    rows, rank = qs.shape
    dim = es.shape[1]
    whole, part, smem = specs(rows, rank)
    wide = pl.BlockSpec((rows // STEPS, dim), lambda i: (i, 0))
    return pl.pallas_call(
        functools.partial(kernels_kernel, cells),
        grid=(STEPS,),
        in_specs=[smem, smem, wide, wide, part, part, whole((dim, rank)), whole((dim, rank)),
                  whole((EXTRA, rank)), whole((1, rank))],
        out_specs=[part, part, whole((count, 2, rank)), whole((1, rank))],
        out_shape=[jax.ShapeDtypeStruct((rows, rank), f32)] * 2
        + [jax.ShapeDtypeStruct((count, 2, rank), f32), jax.ShapeDtypeStruct((1, rank), f32)],
        scratch_shapes=[
            pltpu.VMEM((4, dim, rank), bf16),
            pltpu.VMEM((8, rank), f32),
            pltpu.VMEM((2, rank), f32),
        ],
        compiler_params=pltpu.CompilerParams(vmem_limit_bytes=LIMIT),
        name="kernels",
    )(place, live, es, et, qs, qt, mine, other, stats, weights)


def sweep(cells, count, last, live, ks, kt, parts, kernel_mass, stats):
    rows, rank = ks.shape
    whole, part, smem = specs(rows, rank)
    scaled = [jax.ShapeDtypeStruct((rows, rank), f32)] * 2 if last else []
    return pl.pallas_call(
        functools.partial(sweep_kernel, cells, last),
        grid=(STEPS,),
        in_specs=[smem, part, part, whole(parts.shape), whole((1, rank)), whole((EXTRA, rank))],
        out_specs=[part] * len(scaled) + [whole((count, 2, rank))],
        out_shape=scaled + [jax.ShapeDtypeStruct((count, 2, rank), f32)],
        scratch_shapes=[pltpu.VMEM((2, rank), f32), pltpu.VMEM((2, rank), f32)],
        compiler_params=pltpu.CompilerParams(vmem_limit_bytes=LIMIT),
        name="sweep",
    )(live, ks, kt, parts, kernel_mass, stats)


def finish(cells, ss, st, parts, kernel_mass):
    rows, rank = ss.shape
    whole, part, _ = specs(rows, rank)
    return pl.pallas_call(
        functools.partial(finish_kernel, cells),
        grid=(STEPS,),
        in_specs=[part, part, whole(parts.shape), whole((1, rank))],
        out_specs=[part, part, whole((1, rank))],
        out_shape=[jax.ShapeDtypeStruct((rows, rank), f32)] * 2
        + [jax.ShapeDtypeStruct((1, rank), f32)],
        scratch_shapes=[pltpu.VMEM((2, rank), f32)],
        compiler_params=pltpu.CompilerParams(vmem_limit_bytes=LIMIT),
        name="finish",
    )(ss, st, parts, kernel_mass)


def on_device(
    source_expr, target_expr, loadings, source_prev, target_prev, weights_prev, live_counts
):
    count = lax.axis_size("cell")
    half = count // 2
    place = lax.axis_index("cell").astype(jnp.int32)[None]
    live = live_counts[:, 0]
    rows, rank = source_prev.shape
    dim = loadings.shape[1]
    cells = rows * count
    exchange = functools.partial(lax.all_to_all, axis_name="cell", split_axis=0, concat_axis=0)
    groups = [list(range(0, count, 2)), list(range(1, count, 2))]

    pieces = gather_loadings(loadings, count)
    emb_s, emb_t, own, send = embed(
        place, live, source_expr, target_expr, pieces, source_prev, target_prev, half
    )
    own = own + swap(send, count, 1)
    shard = jnp.sum(exchange(own, axis_index_groups=groups), axis=0)
    share = dim // half
    mine = exchange(
        jnp.broadcast_to(shard[:share][None], (half, share, rank)), axis_index_groups=groups
    ).reshape(dim, rank)
    stats = shard[share:]
    other = swap(mine, count, 1)
    ks, kt, copies, kernel_mass = kernels(
        cells, count, place, live, emb_s, emb_t, source_prev, target_prev, mine, other, stats,
        weights_prev[None],
    )
    scaled = []
    for step_index in range(1, ITERS):
        last = step_index == ITERS - 1
        *scaled, copies = sweep(
            cells, count, last, live, ks, kt, exchange(copies), kernel_mass, stats
        )
    out_s, out_t, weights = finish(cells, *scaled, exchange(copies), kernel_mass)
    return out_s, out_t, weights[0]


def solution(mesh):
    in_specs = (
        P(("grp", "cell"), None),
        P(("grp", "cell"), None),
        P("cell", None),
        P(("grp", "cell"), None),
        P(("grp", "cell"), None),
        P("grp"),
        P(None, ("grp", "cell")),
    )
    out_specs = (P(("grp", "cell"), None), P(("grp", "cell"), None), P("grp"))
    return jax.shard_map(
        on_device, mesh=mesh, in_specs=in_specs, out_specs=out_specs, check_vma=False
    )
```

time: 306 us -> 111 us (0.36)
  waiting for transfers between devices: 124 us -> 14.4 us
  blocking collectives: 123 us -> 55.3 us
  matrix products: 26.5 us -> 0 us
  Pallas kernels: 0 us -> 16.5 us
  between operations: 15.6 us -> 0.74 us
  other arithmetic: 12.4 us -> 0.94 us
  local copies, waits for them, and re-layouts: 3.65 us -> 14.7 us
  starting transfers between devices: 0.08 us -> 7.73 us
    psum x4 -> x0, blocking collectives: 123 us -> none  [the longest x2 59 us: sweep(): lax.psum((jnp.dot(scale_src, kernel_src, precision=precise), jnp.dot(scal...]
    psum x1 -> x0, waiting for transfers between devices: 85.5 us -> none  [on_device(): lax.psum((cross_src, cross_tgt, stats), 'cell')]
    all_to_all x0 -> x5, blocking collectives: none -> 55.3 us  [the longest x3 28.6 us: on_device(): exchange(copies)]
    all_gather x1 -> x0, waiting for transfers between devices: 38.1 us -> none  [on_device(): gathered = lax.all_gather(loadings, 'cell', axis=0, tiled=True)]
    dot_general x20 -> x0, matrix products: 26.5 us -> none  [the longest x2 5.54 us: kernel_of(): jnp.dot(embed, matrix, precision=precise)]
    pallas_call x0 -> x5, Pallas kernels: none -> 16.5 us  [the longest x1 8.61 us: embed(): pl.pallas_call(functools.partial(embed_kernel, masks), grid=(STEPS,), in_...]
    ppermute x0 -> x8, waiting for transfers between devices: none -> 14.4 us  [swap(): return lax.ppermute(value, 'cell', [(i, i ^ mask) for i in range(count)])]
    unnamed x24 -> x34, local copies, waits for them, and re-layouts: 0.59 us -> 14.6 us
  transfers between devices with their start and end apart: 2 -> 8, of which waited for: 2 -> 6; matrix products, arithmetic and copies ran while one was open for 2% -> 0% of each run, Pallas kernels for 0% -> 0%
where the time goes in v2:
time: 111 us; the launch traced here: 110 us
  blocking collectives  55.3 us (50%)
  Pallas kernels  16.5 us (15%)
  local copies, waits for them, and re-layouts  14.7 us (13%)
  waiting for transfers between devices  14.4 us (13%)
  starting transfers between devices  7.73 us (7%)
    all_to_all x3, blocking collectives, on_device(): exchange(copies)  28.6 us
    all_to_all x1, blocking collectives, on_device(): shard = jnp.sum(exchange(own, axis_index_groups=groups), axis=0)  15.1 us
    unnamed x34, local copies, waits for them, and re-layouts  14.6 us
    ppermute x8, waiting for transfers between devices, swap(): return lax.ppermute(value, 'cell', [(i, i ^ mask) for i in range(count)])  14.4 us
    all_to_all x1, blocking collectives, on_device(): exchange(jnp.broadcast_to(shard[:share][None], (half, share, rank)), axis...  11.6 us
    pallas_call x1, Pallas kernels, embed(): pl.pallas_call(functools.partial(embed_kernel, masks), grid=(STEPS,), in_...  8.61 us
    ppermute x8, starting transfers between devices, swap(): return lax.ppermute(value, 'cell', [(i, i ^ mask) for i in range(count)])  7.73 us
    pallas_call x1, Pallas kernels, kernels(): pl.pallas_call(functools.partial(kernels_kernel, cells), grid=(STEPS,), i...  3.12 us
  transfers between devices with their start and end apart: 8, of which 6 were waited for; matrix products, arithmetic and copies ran while one was open for 0% of the time, Pallas kernels for 0%

profile of v2, /device:TPU:0, one launch (start us, length us, event | category | flops | bytes accessed | tf_op | source)
XLA Modules:
  0.0 110.3 jit_solution(10460463251063019641)
XLA Ops:
  0.6 5.1 %collective-permute-start.2 = (bf16[1,128,256]{2,1,0:T(8,128)(2,1)}, bf16[1,128,256]{2,1,0:T(8,128)(2,1)S(1)}, u32[]{:S(2)}, u32[]{:S(2)}) collective-permute-start(bf16[1,128,256]{2,1,0:T(8,128)(2,1)} %bitcast.13), channel_id=1, source_target_pairs={{0,12},{1,13},{2,14},{3,15},{4,8},{5,9},{6,10},{7,11},{8,4},{9,5},... | collective-permute-start | bytes 196616 | tf_op jit(solution)/shard_map/ppermute | solution.py:22
  5.7 0.0 collective-permute-start.1
  5.7 0.6 collective-permute-start
  6.4 2.2 %collective-permute-done.2 = bf16[1,128,256]{2,1,0:T(8,128)(2,1)S(1)} collective-permute-done((bf16[1,128,256]{2,1,0:T(8,128)(2,1)}, bf16[1,128,256]{2,1,0:T(8,128)(2,1)S(1)}, u32[]{:S(2)}, u32[]{:S(2)}) %collective-permute-start.2) | collective-permute-done | bytes 65568 | tf_op jit(solution)/shard_map/ppermute | solution.py:22
  8.6 3.0 %collective-permute-done.1 = bf16[1,128,256]{2,1,0:T(8,128)(2,1)S(1)} collective-permute-done((bf16[1,128,256]{2,1,0:T(8,128)(2,1)}, bf16[1,128,256]{2,1,0:T(8,128)(2,1)S(1)}, u32[]{:S(2)}, u32[]{:S(2)}) %collective-permute-start.1) | collective-permute-done | bytes 65568 | tf_op jit(solution)/shard_map/ppermute | solution.py:22
  11.6 0.0 collective-permute-done
  11.6 0.9 pad_maximum_fusion.refs_0_
  12.4 1.6 %collective-permute-start.4 = (bf16[4,128,256]{2,1,0:T(8,128)(2,1)S(1)}, bf16[4,128,256]{2,1,0:T(8,128)(2,1)S(1)}, u32[]{:S(2)}, u32[]{:S(2)}) collective-permute-start(bf16[4,128,256]{2,1,0:T(8,128)(2,1)S(1)} %pad_maximum_fusion.refs_0_), channel_id=1, source_target_pairs={{0,2},{1,3},{2,0},{3,1},{4,6},{5,7},{6,4},{7,5},{8,10},{9,11},{10,... | collective-permute-start | bytes 786440 | tf_op jit(solution)/shard_map/ppermute | solution.py:22
  14.0 0.0 collective-permute-start.3
  14.0 6.4 %collective-permute-done.4.refs_2_ = bf16[4,128,256]{2,1,0:T(8,128)(2,1)S(1)} collective-permute-done((bf16[4,128,256]{2,1,0:T(8,128)(2,1)S(1)}, bf16[4,128,256]{2,1,0:T(8,128)(2,1)S(1)}, u32[]{:S(2)}, u32[]{:S(2)}) %collective-permute-start.4) | collective-permute-done | bytes 262176 | tf_op jit(solution)/shard_map/ppermute | solution.py:22
  20.4 0.0 collective-permute-start.5
  20.4 0.0 copy-start.8
  20.4 0.7 copy-done.8
  21.1 0.0 collective-permute-done.3.refs_1_
  21.1 0.0 copy-start.10
  21.1 0.7 copy-done.10
  21.8 0.1 collective-permute-done.5.refs_3_
  21.9 0.7 copy-done.12
  22.6 2.2 %copy-done = bf16[1024,2048]{1,0:T(8,128)(2,1)S(1)} copy-done((bf16[1024,2048]{1,0:T(8,128)(2,1)S(1)}, bf16[1024,2048]{1,0:T(8,128)(2,1)}, u32[]{:S(2)}) %copy-start) | copy-done | bytes 4194328
  24.8 2.2 %copy-done.1 = bf16[1024,2048]{1,0:T(8,128)(2,1)S(1)} copy-done((bf16[1024,2048]{1,0:T(8,128)(2,1)S(1)}, bf16[1024,2048]{1,0:T(8,128)(2,1)}, u32[]{:S(2)}) %copy-start.1) | copy-done | bytes 4194328
  27.0 1.2 %copy-done.2 = f32[1024,256]{1,0:T(8,128)S(1)} copy-done((f32[1024,256]{1,0:T(8,128)S(1)}, f32[1024,256]{1,0:T(8,128)}, u32[]{:S(2)}) %copy-start.2) | copy-done | bytes 1048600
  28.2 1.2 %copy-done.4 = f32[1024,256]{1,0:T(8,128)S(1)} copy-done((f32[1024,256]{1,0:T(8,128)S(1)}, f32[1024,256]{1,0:T(8,128)}, u32[]{:S(2)}) %copy-start.4) | copy-done | bytes 1048600
  29.5 0.9 copy-done.9
  30.4 0.9 copy-done.11
  31.4 0.9 copy-done.13
  32.3 0.7 copy-done.14
  33.0 8.6 %embed.1 = (f32[1024,256]{1,0:T(8,128)S(1)}, f32[1024,256]{1,0:T(8,128)S(1)}, f32[8,40,256]{2,1,0:T(8,128)S(1)}, f32[8,40,256]{2,1,0:T(8,128)S(1)}) custom-call(s32[1]{0:T(128)} %bitcast.1.place, s32[2]{0:T(128)S(1)} %bitcast.8, bf16[1024,2048]{1,0:T(8,128)(2,1)S(1)} %copy-done, bf16[1024,2048]{1,0:T(8,128)(2,1)S(1)} %copy-done.1, ...), custom_call_target="tpu_custom_call" | custom-call | tf_op jit(solution)/shard_map/embed/pallas_call | solution.py:105
  41.6 0.0 copy-start.6
  41.6 1.0 copy-done.6
  42.6 0.4 collective-permute-start.6
  42.9 1.3 %collective-permute-done.6 = f32[8,40,256]{2,1,0:T(8,128)S(1)} collective-permute-done((f32[8,40,256]{2,1,0:T(8,128)S(1)}, f32[8,40,256]{2,1,0:T(8,128)S(1)}, u32[]{:S(2)}, u32[]{:S(2)}) %collective-permute-start.6) | collective-permute-done | bytes 327712 | tf_op jit(solution)/shard_map/ppermute | solution.py:22
  44.3 15.1 %all_to_all.25 = f32[8,40,256]{2,1,0:T(8,128)S(1)} all-to-all(f32[8,40,256]{2,1,0:T(8,128)S(1)} %add.3), channel_id=1, replica_groups={{0,2,4,6,8,10,12,14},{1,3,5,7,9,11,13,15},{16,18,20,22,24,26,28,30},{17..., dimensions={0} | all-to-all | bytes 655360 | tf_op jit(solution)/shard_map/all_to_all | solution.py:319
  59.4 11.6 %all_to_all.26 = f32[8,32,256]{2,1,0:T(8,128)S(1)} all-to-all(f32[8,32,256]{2,1,0:T(8,128)S(1)} %broadcast_in_dim.17), channel_id=1, replica_groups={{0,2,4,6,8,10,12,14},{1,3,5,7,9,11,13,15},{16,18,20,22,24,26,28,30},{17..., dimensions={0} | all-to-all | bytes 524288 | tf_op jit(solution)/shard_map/all_to_all | solution.py:321
  71.0 0.0 collective-permute-start.7
  71.1 1.5 %collective-permute-done.7.other = f32[256,256]{1,0:T(8,128)S(1)} collective-permute-done((f32[256,256]{1,0:T(8,128)S(1)}, f32[256,256]{1,0:T(8,128)S(1)}, u32[]{:S(2)}, u32[]{:S(2)}) %collective-permute-start.7) | collective-permute-done | bytes 262176 | tf_op jit(solution)/shard_map/ppermute | solution.py:22
  72.6 0.0 copy-done.3
  72.6 0.0 copy-done.5
  72.6 0.0 copy-done.15
  72.6 0.0 copy-done.16
  72.6 0.0 copy-start.7
  72.6 1.2 %copy-done.7 = f32[1024,256]{1,0:T(8,128)S(1)} copy-done((f32[1024,256]{1,0:T(8,128)S(1)}, f32[1024,256]{1,0:T(8,128)}, u32[]{:S(2)}) %copy-start.7) | copy-done | bytes 1048600
  73.8 3.1 %kernels.1 = (f32[1024,256]{1,0:T(8,128)S(1)}, f32[1024,256]{1,0:T(8,128)S(1)}, f32[16,2,256]{2,1,0:T(2,128)S(1)}, f32[1,256]{1,0:T(1,128)S(1)}) custom-call(s32[1]{0:T(128)} %bitcast.1.place, s32[2]{0:T(128)S(1)} %bitcast.9, f32[1024,256]{1,0:T(8,128)S(1)} %get-tuple-element.17.es, f32[1024,256]{1,0:T(8,128)S(1)} %copy-done.7, f32[1024,256]{1,0:T(8,128)S(1)} %copy-done.3, ...), custom_call_target="tpu_custom_call" | custom-call | tf_op jit(solution)/shard_map/kernels/pallas_call | solution.py:251
  77.0 10.1 %all_to_all.27.parts = f32[16,2,256]{2,1,0:T(2,128)S(1)} all-to-all(f32[16,2,256]{2,1,0:T(2,128)S(1)} %get-tuple-element.23), channel_id=1, replica_groups=mesh['grp'=2,'cell'=16] {'cell'}, dimensions={0} | all-to-all | bytes 65536 | tf_op jit(solution)/shard_map/all_to_all | solution.py:334
  87.1 1.5 %sweep.2 = f32[16,2,256]{2,1,0:T(2,128)S(1)} custom-call(s32[2]{0:T(128)S(1)} %bitcast.10, f32[1024,256]{1,0:T(8,128)S(1)} %get-tuple-element.21.ks, f32[1024,256]{1,0:T(8,128)S(1)} %get-tuple-element.22.kt, f32[16,2,256]{2,1,0:T(2,128)S(1)} %all_to_all.27.parts, f32[1,256]{1,0:T(1,128)S(1)} %get-tuple-element.24.kernel_mass, f32[8,256]{1,0:T(8,128)S(1)} %slice.9.stats), custom_call_target="tpu_custom_call" | custom-call | tf_op jit(solution)/shard_map/sweep/pallas_call | solution.py:273
  88.6 9.2 %all_to_all.28.parts = f32[16,2,256]{2,1,0:T(2,128)S(1)} all-to-all(f32[16,2,256]{2,1,0:T(2,128)S(1)} %sweep.2), channel_id=1, replica_groups=mesh['grp'=2,'cell'=16] {'cell'}, dimensions={0} | all-to-all | bytes 65536 | tf_op jit(solution)/shard_map/all_to_all | solution.py:334
  97.8 1.4 %sweep.3 = (f32[1024,256]{1,0:T(8,128)S(1)}, f32[1024,256]{1,0:T(8,128)S(1)}, f32[16,2,256]{2,1,0:T(2,128)S(1)}) custom-call(s32[2]{0:T(128)S(1)} %bitcast.11, f32[1024,256]{1,0:T(8,128)S(1)} %get-tuple-element.21.ks, f32[1024,256]{1,0:T(8,128)S(1)} %get-tuple-element.22.kt, f32[16,2,256]{2,1,0:T(2,128)S(1)} %all_to_all.28.parts, ...), custom_call_target="tpu_custom_call" | custom-call | tf_op jit(solution)/shard_map/sweep/pallas_call | solution.py:273
  99.2 9.2 %all_to_all.29.parts = f32[16,2,256]{2,1,0:T(2,128)S(1)} all-to-all(f32[16,2,256]{2,1,0:T(2,128)S(1)} %get-tuple-element.27), channel_id=1, replica_groups=mesh['grp'=2,'cell'=16] {'cell'}, dimensions={0} | all-to-all | bytes 65536 | tf_op jit(solution)/shard_map/all_to_all | solution.py:336
  108.4 1.9 %finish.1 = (f32[1024,256]{1,0:T(8,128)}, f32[1024,256]{1,0:T(8,128)}, f32[1,256]{1,0:T(1,128)}) custom-call(f32[1024,256]{1,0:T(8,128)S(1)} %get-tuple-element.25.ss, f32[1024,256]{1,0:T(8,128)S(1)} %get-tuple-element.26.st, f32[16,2,256]{2,1,0:T(2,128)S(1)} %all_to_all.29.parts, f32[1,256]{1,0:T(1,128)S(1)} %get-tuple-element.24.kernel_mass), custom_call_target="tpu_custom_call" | custom-call | tf_op jit(solution)/shard_map/finish/pallas_call | solution.py:288
  (18 shorter events, 0.1 us)
Async XLA Ops:
  0.6 7.9 %collective-permute-start.2 = (bf16[1,128,256]{2,1,0:T(8,128)(2,1)}, bf16[1,128,256]{2,1,0:T(8,128)(2,1)S(1)}, u32[]{:S(2)}, u32[]{:S(2)}) collective-permute-start(bf16[1,128,256]{2,1,0:T(8,128)(2,1)} %bitcast.13), channel_id=1, source_target_pairs={{0,12},{1,13},{2,14},{3,15},{4,8},{5,9},{6,10},{7,11},{8,4},{9,5},... | collective-permute-start | bytes 196616 | tf_op jit(solution)/shard_map/ppermute | solution.py:22
  5.7 5.8 %collective-permute-start.1 = (bf16[1,128,256]{2,1,0:T(8,128)(2,1)}, bf16[1,128,256]{2,1,0:T(8,128)(2,1)S(1)}, u32[]{:S(2)}, u32[]{:S(2)}) collective-permute-start(bf16[1,128,256]{2,1,0:T(8,128)(2,1)} %bitcast.14), channel_id=1, source_target_pairs={{0,8},{1,9},{2,10},{3,11},{4,12},{5,13},{6,14},{7,15},{8,0},{9,1},... | collective-permute-start | bytes 196616 | tf_op jit(solution)/shard_map/ppermute | solution.py:22
  5.7 5.8 %collective-permute-start = (bf16[1,128,256]{2,1,0:T(8,128)(2,1)}, bf16[1,128,256]{2,1,0:T(8,128)(2,1)S(1)}, u32[]{:S(2)}, u32[]{:S(2)}) collective-permute-start(bf16[1,128,256]{2,1,0:T(8,128)(2,1)} %bitcast.15), channel_id=1, source_target_pairs={{0,4},{1,5},{2,6},{3,7},{4,0},{5,1},{6,2},{7,3},{8,12},{9,13},{10,... | collective-permute-start | bytes 196616 | tf_op jit(solution)/shard_map/ppermute | solution.py:22
  12.4 7.9 %collective-permute-start.4 = (bf16[4,128,256]{2,1,0:T(8,128)(2,1)S(1)}, bf16[4,128,256]{2,1,0:T(8,128)(2,1)S(1)}, u32[]{:S(2)}, u32[]{:S(2)}) collective-permute-start(bf16[4,128,256]{2,1,0:T(8,128)(2,1)S(1)} %pad_maximum_fusion.refs_0_), channel_id=1, source_target_pairs={{0,2},{1,3},{2,0},{3,1},{4,6},{5,7},{6,4},{7,5},{8,10},{9,11},{10,... | collective-permute-start | bytes 786440 | tf_op jit(solution)/shard_map/ppermute | solution.py:22
  14.0 7.1 %collective-permute-start.3 = (bf16[4,128,256]{2,1,0:T(8,128)(2,1)S(1)}, bf16[4,128,256]{2,1,0:T(8,128)(2,1)S(1)}, u32[]{:S(2)}, u32[]{:S(2)}) collective-permute-start(bf16[4,128,256]{2,1,0:T(8,128)(2,1)S(1)} %pad_maximum_fusion.refs_0_), channel_id=1, source_target_pairs={{0,1},{1,0},{2,3},{3,2},{4,5},{5,4},{6,7},{7,6},{8,9},{9,8},{10,11... | collective-permute-start | bytes 786440 | tf_op jit(solution)/shard_map/ppermute | solution.py:22
  20.4 1.5 %collective-permute-start.5 = (bf16[4,128,256]{2,1,0:T(8,128)(2,1)S(1)}, bf16[4,128,256]{2,1,0:T(8,128)(2,1)S(1)}, u32[]{:S(2)}, u32[]{:S(2)}) collective-permute-start(bf16[4,128,256]{2,1,0:T(8,128)(2,1)S(1)} %collective-permute-done.4.refs_2_), channel_id=1, source_target_pairs={{0,1},{1,0},{2,3},{3,2},{4,5},{5,4},{6,7},{7,6},{8,9},{9,8},{10,11... | collective-permute-start | bytes 786440 | tf_op jit(solution)/shard_map/ppermute | solution.py:22
  20.4 0.7 copy-start.8
  21.1 0.7 copy-start.10
  21.9 0.7 copy-start.12
  22.6 2.2 %copy-start = (bf16[1024,2048]{1,0:T(8,128)(2,1)S(1)}, bf16[1024,2048]{1,0:T(8,128)(2,1)}, u32[]{:S(2)}) copy-start(bf16[1024,2048]{1,0:T(8,128)(2,1)} %xs.1) | copy-start | bytes 12582916
  24.8 2.2 %copy-start.1 = (bf16[1024,2048]{1,0:T(8,128)(2,1)S(1)}, bf16[1024,2048]{1,0:T(8,128)(2,1)}, u32[]{:S(2)}) copy-start(bf16[1024,2048]{1,0:T(8,128)(2,1)} %xt.1) | copy-start | bytes 12582916
  27.0 1.2 %copy-start.2 = (f32[1024,256]{1,0:T(8,128)S(1)}, f32[1024,256]{1,0:T(8,128)}, u32[]{:S(2)}) copy-start(f32[1024,256]{1,0:T(8,128)} %qs.1) | copy-start | bytes 3145732
  28.2 1.2 %copy-start.4 = (f32[1024,256]{1,0:T(8,128)S(1)}, f32[1024,256]{1,0:T(8,128)}, u32[]{:S(2)}) copy-start(f32[1024,256]{1,0:T(8,128)} %qt.1) | copy-start | bytes 3145732
  29.4 0.9 copy-start.9
  30.4 0.9 copy-start.11
  31.3 0.9 copy-start.13
  32.3 0.7 copy-start.14
  33.0 39.6 %copy-start.3 = (f32[1024,256]{1,0:T(8,128)S(1)}, f32[1024,256]{1,0:T(8,128)}, u32[]{:S(2)}) copy-start(f32[1024,256]{1,0:T(8,128)} %qs.1) | copy-start | bytes 3145732
  33.0 39.6 %copy-start.5 = (f32[1024,256]{1,0:T(8,128)S(1)}, f32[1024,256]{1,0:T(8,128)}, u32[]{:S(2)}) copy-start(f32[1024,256]{1,0:T(8,128)} %qt.1) | copy-start | bytes 3145732
  33.0 39.6 %copy-start.15 = (s32[2,1]{0,1:T(1,128)S(1)}, s32[2,1]{0,1:T(1,128)}, u32[]{:S(2)}) copy-start(s32[2,1]{0,1:T(1,128)} %param.13) | copy-start | bytes 28
  33.0 39.6 %copy-start.16 = (f32[256]{0:T(256)S(1)}, f32[256]{0:T(256)}, u32[]{:S(2)}) copy-start(f32[256]{0:T(256)} %param.12) | copy-start | bytes 3076
  41.6 1.0 copy-start.6
  42.6 1.6 %collective-permute-start.6 = (f32[8,40,256]{2,1,0:T(8,128)S(1)}, f32[8,40,256]{2,1,0:T(8,128)S(1)}, u32[]{:S(2)}, u32[]{:S(2)}) collective-permute-start(f32[8,40,256]{2,1,0:T(8,128)S(1)} %get-tuple-element.20), channel_id=1, source_target_pairs={{0,1},{1,0},{2,3},{3,2},{4,5},{5,4},{6,7},{7,6},{8,9},{9,8},{10,11... | collective-permute-start | bytes 983048 | tf_op jit(solution)/shard_map/ppermute | solution.py:22
  71.0 1.5 %collective-permute-start.7 = (f32[256,256]{1,0:T(8,128)S(1)}, f32[256,256]{1,0:T(8,128)S(1)}, u32[]{:S(2)}, u32[]{:S(2)}) collective-permute-start(f32[256,256]{1,0:T(8,128)S(1)} %bitcast.6), channel_id=1, source_target_pairs={{0,1},{1,0},{2,3},{3,2},{4,5},{5,4},{6,7},{7,6},{8,9},{9,8},{10,11... | collective-permute-start | bytes 786440 | tf_op jit(solution)/shard_map/ppermute | solution.py:22
  72.6 1.2 %copy-start.7 = (f32[1024,256]{1,0:T(8,128)S(1)}, f32[1024,256]{1,0:T(8,128)}, u32[]{:S(2)}) copy-start(f32[1024,256]{1,0:T(8,128)} %copy-done.6) | copy-start | bytes 3145732

commit v3 on v0

v3 whole, which is shorter than its diff:
```python
import functools

import jax
import jax.numpy as jnp
from jax import lax
from jax.experimental import pallas as pl
from jax.experimental.pallas import tpu as pltpu
from jax.sharding import PartitionSpec as P

D = 256
ITERS = 3
STEPS = 4

step_size = 1.0
f32 = jnp.float32
bf16 = jnp.bfloat16
LIMIT = 16 * 1024 * 1024


def swap(value, count, mask):
    return lax.ppermute(value, "cell", [(i, i ^ mask) for i in range(count)])


def halves(value):
    upper = value.astype(bf16)
    return upper, (value - upper.astype(f32)).astype(bf16)


def dot3(a, b, left, right):
    dims = (((left,), (right,)), ((), ()))
    dot = functools.partial(lax.dot_general, dimension_numbers=dims, preferred_element_type=f32)
    return dot(a[0], b[0]) + (dot(a[0], b[1]) + dot(a[1], b[0]))


VMEM = pl.BlockSpec(memory_space=pltpu.VMEM)
SMEM = pl.BlockSpec(memory_space=pltpu.SMEM)
HBM = pl.BlockSpec(memory_space=pltpu.HBM)
ANY = pl.BlockSpec(memory_space=pl.ANY)


def far(*arrays):
    return [pltpu.with_memory_space_constraint(a, pltpu.HBM) for a in arrays]


def near(*arrays):
    return [pltpu.with_memory_space_constraint(a, pltpu.VMEM) for a in arrays]


def array(shape, dtype=f32):
    return jax.ShapeDtypeStruct(shape, dtype)


def call(body, name, in_specs, out_specs, out_shape, scratch=(), cost=None):
    return pl.pallas_call(
        body,
        in_specs=in_specs,
        out_specs=out_specs,
        out_shape=out_shape,
        scratch_shapes=list(scratch),
        compiler_params=pltpu.CompilerParams(vmem_limit_bytes=LIMIT),
        cost_estimate=cost,
        name=name,
    )


def rows_of(step, block):
    return pl.ds(pl.multiple_of(step * block, block), block)


def fetch_kernel(qs, qt, qs_out, qt_out, turned, totals, sems):
    pairs = ((qs, qs_out), (qt, qt_out))
    copies = [pltpu.make_async_copy(a, b, sems.at[i]) for i, (a, b) in enumerate(pairs)]
    for copy in copies:
        copy.start()
    rank = qs.shape[1]
    for t, q in enumerate((qs_out, qt_out)):
        copies[t].wait()
        factor = q[...] / rank
        totals[t : t + 1, :] = jnp.sum(factor, axis=0, keepdims=True)
        turned[t] = factor.T.astype(bf16)


def fetch(*arrays):
    rows, rank = arrays[0].shape
    size = sum(a.size * a.dtype.itemsize for a in arrays)
    return call(
        fetch_kernel, "fetch", [HBM] * 2, [VMEM] * 4,
        [pltpu.VMEM(a.shape, a.dtype) for a in arrays]
        + [pltpu.VMEM((2, rank, rows), bf16), array((2, rank))],
        [pltpu.SemaphoreType.DMA((2,))],
        pl.CostEstimate(flops=0, bytes_accessed=size, transcendentals=0),
    )(*far(*arrays))


def stack_kernel(*refs):
    pieces, out = refs[:4], refs[-1]
    for i, piece in enumerate(pieces):
        out[i] = piece[...]


def stack_pieces(pieces, after):
    return call(
        stack_kernel, "stack", [VMEM] * 4 + [ANY] * len(after), VMEM,
        array((4,) + pieces[0].shape, pieces[0].dtype),
    )(*pieces, *after)


def joined_table(me, j, even, odd):
    swapped = (me & 1) == 1
    a, b = even[j], odd[j]
    return jnp.concatenate([jnp.where(swapped, b, a), jnp.where(swapped, a, b)])


def first_kernel(masks, place, xs, xt, even, odd, part_s, part_t, later_s, later_t, held, sems):
    me = place[0]
    width = 2 * even.shape[1]

    def copy(x, mask, out, sem):
        start = pl.multiple_of(((me ^ mask) >> 1) * width, width)
        made = pltpu.make_async_copy(x.at[:, pl.ds(start, width)], out, sem)
        made.start()
        return made

    sets = ((xs, part_s, later_s), (xt, part_t, later_t))
    now = [
        [copy(x, m, held.at[t, j], sems.at[0, t, j]) for j, m in enumerate(masks)]
        for t, (x, _, _) in enumerate(sets)
    ]
    after = [
        copy(x, m | 2, later.at[j], sems.at[1, t, j])
        for t, (x, _, later) in enumerate(sets)
        for j, m in enumerate(masks)
    ]
    for t, (_, part, _) in enumerate(sets):
        value = None
        for j in range(len(masks)):
            now[t][j].wait()
            term = jnp.dot(held[t, j], joined_table(me, j, even, odd), preferred_element_type=f32)
            value = term if value is None else value + term
        part[...] = value
    for made in after:
        made.wait()


def first_half(place, xs, xt, masks, even, odd):
    rows, genes = xs.shape
    blocks, width, dim = even.shape
    held = (blocks, rows, 2 * width)
    return call(
        functools.partial(first_kernel, masks), "embed_first", [SMEM, HBM, HBM, VMEM, VMEM], [VMEM] * 4,
        [array((rows, dim))] * 2 + [pltpu.VMEM(held, bf16)] * 2,
        [pltpu.VMEM((2,) + held, bf16), pltpu.SemaphoreType.DMA((2, 2, blocks))],
        pl.CostEstimate(
            flops=2 * rows * genes * dim, bytes_accessed=4 * rows * genes, transcendentals=0
        ),
    )(place, *far(xs, xt), even, odd)


def gate_kernel(value, after, out):
    out[...] = value[...]


def gate(value, after):
    return call(
        gate_kernel, "gate", [VMEM, ANY], VMEM, array(value.shape, value.dtype)
    )(value, after)


def whole_kernel(masks, place, xs, xt, *refs):
    pieces, (part_s, part_t, table) = refs[:4], refs[4:]
    genes = pieces[0].shape[1]
    for piece, extra in zip(pieces, range(4)):
        for j, mask in enumerate(masks):
            start = pl.multiple_of((place[0] ^ (mask | extra)) * genes, genes)
            table[pl.ds(start, genes), :] = piece[j]
    for x, part in ((xs, part_s), (xt, part_t)):
        part[...] = jnp.dot(x[...], table[...], preferred_element_type=f32)


def whole_product(place, xs, xt, masks, *pieces):
    rows, genes = xs.shape
    dim = pieces[0].shape[2]
    return call(
        functools.partial(whole_kernel, masks), "embed_whole", [SMEM] + [VMEM] * 6, [VMEM] * 2,
        [array((rows, dim))] * 2, [pltpu.VMEM((genes, dim), bf16)],
    )(place, xs, xt, *pieces)


def second_kernel(
    place, live, xs, xt, part_s, part_t, even, odd, qs, qt, turned, totals,
    emb_s, emb_t, own, send,
):
    me = place[0]
    core = me & 1
    rows, rank = qs.shape
    dim = emb_s.shape[1]
    for t, (x, q, part, emb) in enumerate(
        ((xs, qs, part_s, emb_s), (xt, qt, part_t, emb_t))
    ):
        value = part[...]
        for j in range(x.shape[0]):
            table = joined_table(me, j, even, odd)
            value = value + jnp.dot(x[j], table, preferred_element_type=f32)
        emb[...] = value
        norms = jnp.sum(value * value, axis=1, keepdims=True)
        norm_sum = jnp.sum(norms * (q[...] / rank), axis=0, keepdims=True)
        mean = (jnp.sum(value, axis=0, keepdims=True) / rows).astype(bf16).astype(f32)
        rest = jnp.dot(turned[t], (value - mean).astype(bf16), preferred_element_type=f32)
        number = jnp.full((1, rank), live[t].astype(f32))
        tail = jnp.concatenate(
            [mean, totals[t : t + 1, :], norm_sum, number, jnp.zeros((4, rank), f32)]
        )

        def put(out):
            out[0:rank, :] = rest
            out[rank:, :] = tail

        pl.when(core == t)(lambda: put(own))
        pl.when(core != t)(lambda: put(send))


def second_half(place, live, xs, xt, parts, even, odd, qs, qt, turned, totals):
    rows, rank = qs.shape
    dim = even.shape[2]
    return call(
        second_kernel, "embed_second", [SMEM] * 2 + [VMEM] * 10, [VMEM] * 4,
        [array((rows, dim))] * 2 + [array((rank + 8, dim))] * 2,
    )(place, live, *near(xs, xt), *parts, even, odd, *near(qs, qt, turned), totals)


def split_row(row):
    high = row.astype(bf16).astype(f32)
    middle = (row - high).astype(bf16).astype(f32)
    return [high, middle, row - high - middle]


def tail_rows(cards):
    return -(-(8 + 4 * cards) // 16) * 16


def make_tail(norm, number, cards):
    width = norm.shape[1]
    rows = split_row(norm) + split_row(number) + [jnp.zeros((2, width), f32)] + cards
    used = sum(r.shape[0] for r in rows)
    filler = tail_rows((used - 8) // 4) - used
    if filler:
        rows.append(jnp.zeros((filler, width), f32))
    return jnp.concatenate(rows)


def three(tail, start):
    return (tail[start : start + 1] + tail[start + 1 : start + 2]) + tail[start + 2 : start + 3]


def pack_pair_kernel(own, recv, out):
    rank = own.shape[0] - 8
    out[0:rank, :] = (own[0:rank, :] + recv[0:rank, :]).astype(bf16)
    cards = []
    for ref in (own, recv):
        cards += [ref[rank : rank + 1, :]] + split_row(ref[rank + 1 : rank + 2, :])
    norm = own[rank + 2 : rank + 3, :] + recv[rank + 2 : rank + 3, :]
    number = own[rank + 3 : rank + 4, :] + recv[rank + 3 : rank + 4, :]
    out[rank:, :] = make_tail(norm, number, cards).astype(bf16)


def pack_pair(own, recv):
    rank, dim = own.shape[0] - 8, own.shape[1]
    return call(
        pack_pair_kernel, "pack_pair", [VMEM] * 2, VMEM, array((rank + tail_rows(2), dim), bf16)
    )(own, recv)


def pack_next_kernel(rank, cards, bit, place, own, recv, out):
    out[0:rank, :] = (own[0:rank, :].astype(f32) + recv[0:rank, :].astype(f32)).astype(bf16)
    a, b = own[rank:, :].astype(f32), recv[rank:, :].astype(f32)
    first = (place[0] & bit) == 0
    a_cards, b_cards = a[8 : 8 + 4 * cards], b[8 : 8 + 4 * cards]
    ordered = [jnp.where(first, a_cards, b_cards), jnp.where(first, b_cards, a_cards)]
    tail = make_tail(three(a, 0) + three(b, 0), three(a, 3) + three(b, 3), ordered)
    out[rank:, :] = tail.astype(bf16)


def pack_next(rank, cards, bit, place, own, recv):
    return call(
        functools.partial(pack_next_kernel, rank, cards, bit), "pack_next", [SMEM, VMEM, VMEM], VMEM,
        array((rank + tail_rows(2 * cards), own.shape[1]), bf16),
    )(place, own, recv)


def total_kernel(rank, cards, own, low, high, both, out):
    def unpack(ref):
        tail = ref[rank:, :].astype(f32)
        heights, means, sums = [], [], jnp.zeros((1, tail.shape[1]), f32)
        for c in range(cards):
            at = 8 + 4 * c
            heights.append(tail[at + 1 : at + 4])
            means += [tail[at : at + 1]] * 3
            sums = sums + three(tail, at + 1)
        left, right = jnp.concatenate(heights), jnp.concatenate(means)
        joined = lax.dot_general(
            left.T.astype(bf16), right.astype(bf16), (((1,), (0,)), ((), ())),
            preferred_element_type=f32,
        )
        return ref[0:rank, :].astype(f32) + joined, three(tail, 0), sums, three(tail, 3)

    parts = [unpack(ref) for ref in (own, low, high, both)]
    joined = [(a + b) + (c + d) for a, b, c, d in zip(*parts)]
    out[0:rank, :] = joined[0]
    out[rank:, :] = jnp.concatenate(joined[1:] + [jnp.zeros((5, out.shape[1]), f32)])


def total(rank, cards, *payloads):
    dim = payloads[0].shape[1]
    return call(
        functools.partial(total_kernel, rank, cards), "total", [VMEM] * 4, VMEM,
        array((rank + 8, dim)),
    )(*payloads)


def live_rows(step, block, live):
    return lax.broadcasted_iota(jnp.int32, (block, 1), 0) + step * block < live


def store_sums(sums, copies):
    for i in range(copies.shape[0]):
        copies[i] = sums[...]


def kernels_kernel(
    cells, place, live, es, et, qs, qt, mine, other, weights, ks, kt, copies, consts,
    mats, coeffs, sums,
):
    first = (place[0] & 1) == 0
    rows, rank = qs.shape
    block = rows // STEPS

    a, b = mine[...], other[...]
    source, target = jnp.where(first, a, b), jnp.where(first, b, a)
    cross_s, cross_t = source[0:rank].T, target[0:rank].T
    norm_q, total_q = source[rank : rank + 1], source[rank + 1 : rank + 2]
    norm_p, total_p = target[rank : rank + 1], target[rank + 1 : rank + 2]
    col_mass = weights[...] * (cells / rank)
    inverse = 1.0 / (D * col_mass)
    cost = (
        norm_q * total_p + total_q * norm_p
        - 2.0 * jnp.sum(cross_s * cross_t, axis=0, keepdims=True)
    ) / D
    consts[0:1, :] = col_mass * jnp.exp(step_size * cost / (col_mass * col_mass))
    consts[1:2, :] = cells / source[rank + 2 : rank + 3]
    consts[2:3, :] = cells / target[rank + 2 : rank + 3]
    mats[0], mats[1] = halves((-2.0 * inverse) * cross_t)
    mats[2], mats[3] = halves((-2.0 * inverse) * cross_s)
    coeffs[0:1, :] = total_p * inverse
    coeffs[1:2, :] = norm_p * inverse
    coeffs[2:3, :] = total_q * inverse
    coeffs[3:4, :] = norm_q * inverse
    sums[...] = jnp.zeros_like(sums)

    @pl.loop(0, STEPS)
    def _(step):
        at = rows_of(step, block)
        for t, (e, q, k) in enumerate(((es, qs, ks), (et, qt, kt))):
            value = e[at, :]
            norms = jnp.sum(value * value, axis=1, keepdims=True)
            grad = (
                norms * coeffs[2 * t : 2 * t + 1, :] + coeffs[2 * t + 1 : 2 * t + 2, :]
                + dot3(halves(value), (mats[2 * t], mats[2 * t + 1]), 1, 0)
            )
            kernel = (q[at, :] / rank) * jnp.exp(-step_size * grad)
            k[at, :] = kernel
            level = jnp.where(live_rows(step, block, live[t]), consts[1 + t : 2 + t, 0:1], 0.0)
            scale = level / jnp.sum(kernel, axis=1, keepdims=True)
            sums[t : t + 1, :] += jnp.sum(scale * kernel, axis=0, keepdims=True)

    store_sums(sums, copies)


def cube_root(x):
    y = jnp.exp(jnp.log(x) * (1.0 / 3.0))
    refined = y - (y - x / (y * y)) * (1.0 / 3.0)
    return jnp.where((x > 0.0) & (x < jnp.inf), refined, y)


def duals_of(parts, consts):
    sums = jnp.sum(parts[...], axis=0)
    sum_s, sum_t = sums[0:1, :], sums[1:2, :]
    mass = cube_root(consts[0:1, :] * sum_s * sum_t)
    return mass, mass / sum_s, mass / sum_t


def sweep_kernel(last, live, ks, kt, parts, consts, *refs):
    if last:
        ss, st, copies, sums, duals = refs
    else:
        copies, sums, duals = refs
    block = ks.shape[0] // STEPS

    _, duals[0:1, :], duals[1:2, :] = duals_of(parts, consts)
    sums[...] = jnp.zeros_like(sums)

    @pl.loop(0, STEPS)
    def _(step):
        at = rows_of(step, block)
        for t, k in enumerate((ks, kt)):
            kernel = k[at, :]
            weighted = jnp.sum(kernel * duals[t : t + 1, :], axis=1, keepdims=True)
            level = jnp.where(live_rows(step, block, live[t]), consts[1 + t : 2 + t, 0:1], 0.0)
            scaled = (level / weighted) * kernel
            sums[t : t + 1, :] += jnp.sum(scaled, axis=0, keepdims=True)
            if last:
                (ss, st)[t][at, :] = scaled

    store_sums(sums, copies)


def finish_kernel(cells, ss, st, parts, consts, fs, ft, weights, duals, held, sems):
    rows, rank = ss.shape
    block = rows // STEPS
    mass, duals[0:1, :], duals[1:2, :] = duals_of(parts, consts)
    weights[...] = mass * (rank / cells)
    copies = []
    for step in range(STEPS):
        at = slice(step * block, (step + 1) * block)
        for t, (s, out) in enumerate(((ss, fs), (st, ft))):
            held[t, at, :] = rank * (s[at, :] * duals[t : t + 1, :])
            copy = pltpu.make_async_copy(held.at[t, at], out.at[at], sems.at[t, step])
            copy.start()
            copies.append(copy)
    for copy in copies:
        copy.wait()


def kernels(cells, count, place, live, es, et, qs, qt, mine, other, weights):
    rows, rank = qs.shape
    dim = es.shape[1]
    return call(
        functools.partial(kernels_kernel, cells), "kernels", [SMEM, SMEM] + [VMEM] * 7, [VMEM] * 4,
        [array((rows, rank))] * 2 + [array((count, 2, rank)), array((8, rank))],
        [pltpu.VMEM((4, dim, rank), bf16), pltpu.VMEM((8, rank), f32), pltpu.VMEM((2, rank), f32)],
    )(place, live, es, et, *near(qs, qt), mine, other, weights)


def sweep(count, last, live, ks, kt, parts, consts):
    rows, rank = ks.shape
    scaled = [array((rows, rank))] * 2 if last else []
    return call(
        functools.partial(sweep_kernel, last), "sweep", [SMEM] + [VMEM] * 4,
        [VMEM] * (len(scaled) + 1), scaled + [array((count, 2, rank))],
        [pltpu.VMEM((2, rank), f32), pltpu.VMEM((2, rank), f32)],
    )(live, ks, kt, parts, consts)


def finish(cells, ss, st, parts, consts):
    rows, rank = ss.shape
    return call(
        functools.partial(finish_kernel, cells), "finish", [VMEM] * 4, [HBM, HBM, VMEM],
        [array((rows, rank))] * 2 + [array((1, rank))],
        [
            pltpu.VMEM((2, rank), f32),
            pltpu.VMEM((2, rows, rank), f32),
            pltpu.SemaphoreType.DMA((2, STEPS)),
        ],
    )(ss, st, parts, consts)


def on_device(
    source_expr, target_expr, loadings, source_prev, target_prev, weights_prev, live_counts
):
    count = lax.axis_size("cell")
    place = lax.axis_index("cell").astype(jnp.int32)[None]
    live = live_counts[:, 0]
    rows, rank = source_prev.shape
    cells = rows * count
    bits = [1 << b for b in range(count.bit_length() - 1)]
    low, high = bits[-2], bits[-1]
    between = bits[1:-2]
    exchange = functools.partial(lax.all_to_all, axis_name="cell", split_axis=0, concat_axis=0)

    masks = [0, low, high, low | high]
    pieces = [loadings] + [swap(loadings, count, m) for m in masks[1:]]
    qs, qt, turned, totals = fetch(source_prev, target_prev)
    stack = stack_pieces(pieces, [totals])
    for bit in reversed(between[1:]):
        stack = jnp.concatenate([stack, swap(stack, count, bit)])
        masks = masks + [m | bit for m in masks]
    across = swap(stack, count, 2)
    pair = swap(stack, count, 1)
    if loadings.shape[0] % 64 == 0:
        *parts, xs, xt = first_half(place, source_expr, target_expr, masks, stack, pair)
        both = swap(gate(across, parts[0]), count, 1)
    else:
        both = swap(across, count, 1)
        parts = whole_product(place, source_expr, target_expr, masks, stack, pair, across, both)
        xs = xt = jnp.zeros((1, rows, 2 * loadings.shape[0]), bf16)
    emb_s, emb_t, own, send = second_half(
        place, live, xs, xt, parts, across, both, qs, qt, turned, totals
    )

    payload = pack_pair(own, swap(send, count, 1))
    cards = 2
    for bit in between:
        payload = pack_next(rank, cards, bit, place, payload, swap(payload, count, bit))
        cards = 2 * cards
    others = [swap(payload, count, m) for m in (low, high, low | high)]
    mine = total(rank, cards, payload, *others)
    other = swap(mine, count, 1)

    ks, kt, copies, consts = kernels(
        cells, count, place, live, emb_s, emb_t, qs, qt, mine, other, weights_prev[None]
    )
    scaled = []
    for step_index in range(1, ITERS):
        last = step_index == ITERS - 1
        *scaled, copies = sweep(count, last, live, ks, kt, exchange(copies), consts)
    out_s, out_t, weights = finish(cells, *scaled, exchange(copies), consts)
    return out_s, out_t, weights[0]


def solution(mesh):
    in_specs = (
        P(("grp", "cell"), None),
        P(("grp", "cell"), None),
        P("cell", None),
        P(("grp", "cell"), None),
        P(("grp", "cell"), None),
        P("grp"),
        P(None, ("grp", "cell")),
    )
    out_specs = (P(("grp", "cell"), None), P(("grp", "cell"), None), P("grp"))
    return jax.shard_map(
        on_device, mesh=mesh, in_specs=in_specs, out_specs=out_specs, check_vma=False
    )
```

time: 306 us -> 91.9 us (0.30)
  waiting for transfers between devices: 124 us -> 25.1 us
  blocking collectives: 123 us -> 29.8 us
  matrix products: 26.5 us -> 0 us
  Pallas kernels: 0 us -> 21.3 us
  between operations: 15.6 us -> 0.72 us
  starting transfers between devices: 0.08 us -> 13.7 us
  other arithmetic: 12.4 us -> 0 us
    psum x4 -> x0, blocking collectives: 123 us -> none  [the longest x2 59 us: sweep(): lax.psum((jnp.dot(scale_src, kernel_src, precision=precise), jnp.dot(scal...]
    psum x1 -> x0, waiting for transfers between devices: 85.5 us -> none  [on_device(): lax.psum((cross_src, cross_tgt, stats), 'cell')]
    all_gather x1 -> x0, waiting for transfers between devices: 38.1 us -> none  [on_device(): gathered = lax.all_gather(loadings, 'cell', axis=0, tiled=True)]
    all_to_all x0 -> x3, blocking collectives: none -> 29.8 us  [the longest x2 20.6 us: on_device(): *scaled, copies = sweep(count, last, live, ks, kt, exchange(copies), consts)]
    dot_general x20 -> x0, matrix products: 26.5 us -> none  [the longest x2 5.54 us: kernel_of(): jnp.dot(embed, matrix, precision=precise)]
    ppermute x0 -> x12, waiting for transfers between devices: none -> 25.1 us  [swap(): return lax.ppermute(value, 'cell', [(i, i ^ mask) for i in range(count)])]
    pallas_call x0 -> x12, Pallas kernels: none -> 21.3 us  [the longest x1 4.98 us: first_half(): call(functools.partial(first_kernel, masks), 'embed_first', [SMEM, HBM, H...]
    ppermute x0 -> x12, starting transfers between devices: none -> 13.7 us  [swap(): return lax.ppermute(value, 'cell', [(i, i ^ mask) for i in range(count)])]
  transfers between devices with their start and end apart: 2 -> 12, of which waited for: 2 -> 10; matrix products, arithmetic and copies ran while one was open for 2% -> 0% of each run, Pallas kernels for 0% -> 7%
where the time goes in v3:
time: 91.9 us; the launch traced here: 91.6 us
  blocking collectives  29.8 us (32%)
  waiting for transfers between devices  25.1 us (27%)
  Pallas kernels  21.3 us (23%)
  starting transfers between devices  13.7 us (15%)
    ppermute x12, waiting for transfers between devices, swap(): return lax.ppermute(value, 'cell', [(i, i ^ mask) for i in range(count)])  25.1 us
    all_to_all x2, blocking collectives, on_device(): *scaled, copies = sweep(count, last, live, ks, kt, exchange(copies), consts)  20.6 us
    ppermute x12, starting transfers between devices, swap(): return lax.ppermute(value, 'cell', [(i, i ^ mask) for i in range(count)])  13.7 us
    all_to_all x1, blocking collectives, on_device(): out_s, out_t, weights = finish(cells, *scaled, exchange(copies), consts)  9.2 us
    pallas_call x1, Pallas kernels, first_half(): call(functools.partial(first_kernel, masks), 'embed_first', [SMEM, HBM, H...  4.98 us
    pallas_call x1, Pallas kernels, second_half(): call(second_kernel, 'embed_second', [SMEM] * 2 + [VMEM] * 10, [VMEM] * 4,...  4.38 us
    pallas_call x2, Pallas kernels, sweep(): call(functools.partial(sweep_kernel, last), 'sweep', [SMEM] + [VMEM] * 4,...  3.36 us
    pallas_call x1, Pallas kernels, kernels(): call(functools.partial(kernels_kernel, cells), 'kernels', [SMEM, SMEM] +...  3.36 us
  transfers between devices with their start and end apart: 12, of which 10 were waited for; matrix products, arithmetic and copies ran while one was open for 0% of the time, Pallas kernels for 7%

profile of v3, /device:TPU:0, one launch (start us, length us, event | category | flops | bytes accessed | tf_op | source)
XLA Modules:
  0.0 91.6 jit_solution(9042211356310248981)
XLA Ops:
  0.6 4.1 %collective-permute-start.1 = (bf16[128,256]{1,0:T(8,128)(2,1)}, bf16[128,256]{1,0:T(8,128)(2,1)S(1)}, u32[]{:S(2)}, u32[]{:S(2)}) collective-permute-start(bf16[128,256]{1,0:T(8,128)(2,1)} %refs_0_.1), channel_id=1, source_target_pairs={{0,8},{1,9},{2,10},{3,11},{4,12},{5,13},{6,14},{7,15},{8,0},{9,1},... | collective-permute-start | bytes 196616 | tf_op jit(solution)/shard_map/ppermute | solution.py:21
  4.7 1.6 %collective-permute-start = (bf16[128,256]{1,0:T(8,128)(2,1)}, bf16[128,256]{1,0:T(8,128)(2,1)S(1)}, u32[]{:S(2)}, u32[]{:S(2)}) collective-permute-start(bf16[128,256]{1,0:T(8,128)(2,1)} %refs_0_.1), channel_id=1, source_target_pairs={{0,4},{1,5},{2,6},{3,7},{4,0},{5,1},{6,2},{7,3},{8,12},{9,13},{10,... | collective-permute-start | bytes 196616 | tf_op jit(solution)/shard_map/ppermute | solution.py:21
  6.3 0.0 collective-permute-start.2
  6.3 1.8 %fetch.1 = (f32[1024,256]{1,0:T(8,128)S(1)}, f32[1024,256]{1,0:T(8,128)S(1)}, bf16[2,256,1024]{2,1,0:T(8,128)(2,1)S(1)}, f32[2,256]{1,0:T(2,128)S(1)}) custom-call(f32[1024,256]{1,0:T(8,128)} %qs.1, f32[1024,256]{1,0:T(8,128)} %qt.1), custom_call_target="tpu_custom_call" | custom-call | bytes 2097152 | tf_op jit(solution)/shard_map/fetch/pallas_call | solution.py:86
  8.1 0.0 collective-permute-done.1.refs_2_
  8.1 1.1 %collective-permute-done.refs_1_ = bf16[128,256]{1,0:T(8,128)(2,1)S(1)} collective-permute-done((bf16[128,256]{1,0:T(8,128)(2,1)}, bf16[128,256]{1,0:T(8,128)(2,1)S(1)}, u32[]{:S(2)}, u32[]{:S(2)}) %collective-permute-start) | collective-permute-done | bytes 65568 | tf_op jit(solution)/shard_map/ppermute | solution.py:21
  9.2 3.4 %collective-permute-done.2.refs_3_ = bf16[128,256]{1,0:T(8,128)(2,1)S(1)} collective-permute-done((bf16[128,256]{1,0:T(8,128)(2,1)}, bf16[128,256]{1,0:T(8,128)(2,1)S(1)}, u32[]{:S(2)}, u32[]{:S(2)}) %collective-permute-start.2) | collective-permute-done | bytes 65568 | tf_op jit(solution)/shard_map/ppermute | solution.py:21
  12.6 0.0 copy-start
  12.6 0.8 copy-done
  13.4 0.1 collective-permute-start.3
  13.5 1.6 %collective-permute-start.4 = (bf16[4,128,256]{2,1,0:T(8,128)(2,1)S(1)}, bf16[4,128,256]{2,1,0:T(8,128)(2,1)}, u32[]{:S(2)}, u32[]{:S(2)}) collective-permute-start(bf16[4,128,256]{2,1,0:T(8,128)(2,1)S(1)} %stack.1.even), channel_id=1, source_target_pairs={{0,2},{1,3},{2,0},{3,1},{4,6},{5,7},{6,4},{7,5},{8,10},{9,11},{10,... | collective-permute-start | bytes 786440 | tf_op jit(solution)/shard_map/ppermute | solution.py:21
  15.1 0.1 collective-permute-done.3.odd
  15.2 0.0 copy-start.1
  15.2 5.0 %embed_first.1 = (f32[1024,256]{1,0:T(8,128)S(1)}, f32[1024,256]{1,0:T(8,128)S(1)}, bf16[4,1024,256]{2,1,0:T(8,128)(2,1)S(1)}, bf16[4,1024,256]{2,1,0:T(8,128)(2,1)S(1)}) custom-call(s32[1]{0:T(128)} %bitcast.1.place, bf16[1024,2048]{1,0:T(8,128)(2,1)} %xs.1, bf16[1024,2048]{1,0:T(8,128)(2,1)} %xt.1, bf16[4,128,256]{2,1,0:T(8,128)(2,1)S(1)} %stack.1.even, ...), custom_call_target="tpu_custom_call" | custom-call | flops 1073741824 | bytes 8388608 | tf_op jit(solution)/shard_map/embed_first/pallas_call | solution.py:149
  20.2 2.2 %collective-permute-done.4.value.even = bf16[4,128,256]{2,1,0:T(8,128)(2,1)} collective-permute-done((bf16[4,128,256]{2,1,0:T(8,128)(2,1)S(1)}, bf16[4,128,256]{2,1,0:T(8,128)(2,1)}, u32[]{:S(2)}, u32[]{:S(2)}) %collective-permute-start.4) | collective-permute-done | bytes 262176 | tf_op jit(solution)/shard_map/ppermute | solution.py:21
  22.4 1.0 %gate.1 = bf16[4,128,256]{2,1,0:T(8,128)(2,1)S(1)} custom-call(bf16[4,128,256]{2,1,0:T(8,128)(2,1)} %collective-permute-done.4.value.even, f32[1024,256]{1,0:T(8,128)S(1)} %get-tuple-element.28.after.part_s), custom_call_target="tpu_custom_call" | custom-call | tf_op jit(solution)/shard_map/gate/pallas_call | solution.py:164
  23.3 0.1 collective-permute-start.5
  23.4 1.5 %collective-permute-done.5.odd = bf16[4,128,256]{2,1,0:T(8,128)(2,1)S(1)} collective-permute-done((bf16[4,128,256]{2,1,0:T(8,128)(2,1)S(1)}, bf16[4,128,256]{2,1,0:T(8,128)(2,1)S(1)}, u32[]{:S(2)}, u32[]{:S(2)}) %collective-permute-start.5) | collective-permute-done | bytes 262176 | tf_op jit(solution)/shard_map/ppermute | solution.py:21
  24.9 0.0 copy-done.1
  24.9 0.0 copy-start.2
  24.9 4.4 %embed_second.1 = (f32[1024,256]{1,0:T(8,128)S(1)}, f32[1024,256]{1,0:T(8,128)S(1)}, f32[264,256]{1,0:T(8,128)S(1)}, f32[264,256]{1,0:T(8,128)S(1)}) custom-call(s32[1]{0:T(128)} %bitcast.1.place, s32[2]{0:T(128)S(1)} %bitcast.4, bf16[4,1024,256]{2,1,0:T(8,128)(2,1)S(1)} %get-tuple-element.26.xs, bf16[4,1024,256]{2,1,0:T(8,128)(2,1)S(1)} %get-tuple-element.27.xt, ...), custom_call_target="tpu_custom_call" | custom-call | tf_op jit(solution)/shard_map/embed_second/pallas_call | solution.py:225
  29.3 0.2 collective-permute-start.6
  29.5 1.4 %collective-permute-done.6.recv = f32[264,256]{1,0:T(8,128)S(1)} collective-permute-done((f32[264,256]{1,0:T(8,128)S(1)}, f32[264,256]{1,0:T(8,128)S(1)}, u32[]{:S(2)}, u32[]{:S(2)}) %collective-permute-start.6) | collective-permute-done | bytes 270368 | tf_op jit(solution)/shard_map/ppermute | solution.py:21
  30.9 0.1 pack_pair.1.own
  31.0 1.6 %collective-permute-start.7 = (bf16[272,256]{1,0:T(8,128)(2,1)S(1)}, bf16[272,256]{1,0:T(8,128)(2,1)S(1)}, u32[]{:S(2)}, u32[]{:S(2)}) collective-permute-start(bf16[272,256]{1,0:T(8,128)(2,1)S(1)} %pack_pair.1.own), channel_id=1, source_target_pairs={{0,2},{1,3},{2,0},{3,1},{4,6},{5,7},{6,4},{7,5},{8,10},{9,11},{10,... | collective-permute-start | bytes 417800 | tf_op jit(solution)/shard_map/ppermute | solution.py:21
  32.6 4.2 %collective-permute-done.7.recv = bf16[272,256]{1,0:T(8,128)(2,1)S(1)} collective-permute-done((bf16[272,256]{1,0:T(8,128)(2,1)S(1)}, bf16[272,256]{1,0:T(8,128)(2,1)S(1)}, u32[]{:S(2)}, u32[]{:S(2)}) %collective-permute-start.7) | collective-permute-done | bytes 139296 | tf_op jit(solution)/shard_map/ppermute | solution.py:21
  36.8 0.1 pack_next.1.own
  36.8 1.3 %collective-permute-start.10 = (bf16[288,256]{1,0:T(8,128)(2,1)S(1)}, bf16[288,256]{1,0:T(8,128)(2,1)S(1)}, u32[]{:S(2)}, u32[]{:S(2)}) collective-permute-start(bf16[288,256]{1,0:T(8,128)(2,1)S(1)} %pack_next.1.own), channel_id=1, source_target_pairs={{0,12},{1,13},{2,14},{3,15},{4,8},{5,9},{6,10},{7,11},{8,4},{9,5},... | collective-permute-start | bytes 442376 | tf_op jit(solution)/shard_map/ppermute | solution.py:21
  38.2 0.1 collective-permute-start.9
  38.3 3.0 %collective-permute-start.8 = (bf16[288,256]{1,0:T(8,128)(2,1)S(1)}, bf16[288,256]{1,0:T(8,128)(2,1)S(1)}, u32[]{:S(2)}, u32[]{:S(2)}) collective-permute-start(bf16[288,256]{1,0:T(8,128)(2,1)S(1)} %pack_next.1.own), channel_id=1, source_target_pairs={{0,4},{1,5},{2,6},{3,7},{4,0},{5,1},{6,2},{7,3},{8,12},{9,13},{10,... | collective-permute-start | bytes 442376 | tf_op jit(solution)/shard_map/ppermute | solution.py:21
  41.3 4.2 %collective-permute-done.10.both = bf16[288,256]{1,0:T(8,128)(2,1)S(1)} collective-permute-done((bf16[288,256]{1,0:T(8,128)(2,1)S(1)}, bf16[288,256]{1,0:T(8,128)(2,1)S(1)}, u32[]{:S(2)}, u32[]{:S(2)}) %collective-permute-start.10) | collective-permute-done | bytes 147488 | tf_op jit(solution)/shard_map/ppermute | solution.py:21
  45.5 5.5 %collective-permute-done.9.high = bf16[288,256]{1,0:T(8,128)(2,1)S(1)} collective-permute-done((bf16[288,256]{1,0:T(8,128)(2,1)S(1)}, bf16[288,256]{1,0:T(8,128)(2,1)S(1)}, u32[]{:S(2)}, u32[]{:S(2)}) %collective-permute-start.9) | collective-permute-done | bytes 147488 | tf_op jit(solution)/shard_map/ppermute | solution.py:21
  51.0 0.0 collective-permute-done.8.low
  51.0 0.4 total.1.mine
  51.4 0.1 collective-permute-start.11
  51.5 1.5 %collective-permute-done.11.other = f32[264,256]{1,0:T(8,128)S(1)} collective-permute-done((f32[264,256]{1,0:T(8,128)S(1)}, f32[264,256]{1,0:T(8,128)S(1)}, u32[]{:S(2)}, u32[]{:S(2)}) %collective-permute-start.11) | collective-permute-done | bytes 270368 | tf_op jit(solution)/shard_map/ppermute | solution.py:21
  53.0 0.0 copy-done.2
  53.0 3.4 %kernels.1 = (f32[1024,256]{1,0:T(8,128)S(1)}, f32[1024,256]{1,0:T(8,128)S(1)}, f32[16,2,256]{2,1,0:T(2,128)S(1)}, f32[8,256]{1,0:T(8,128)S(1)}) custom-call(s32[1]{0:T(128)} %bitcast.1.place, s32[2]{0:T(128)S(1)} %bitcast.5, f32[1024,256]{1,0:T(8,128)S(1)} %get-tuple-element.33.es, f32[1024,256]{1,0:T(8,128)S(1)} %get-tuple-element.34.et, ...), custom_call_target="tpu_custom_call" | custom-call | tf_op jit(solution)/shard_map/kernels/pallas_call | solution.py:436
  56.4 11.4 %all_to_all.15.parts = f32[16,2,256]{2,1,0:T(2,128)S(1)} all-to-all(f32[16,2,256]{2,1,0:T(2,128)S(1)} %get-tuple-element.39), channel_id=1, replica_groups=mesh['grp'=2,'cell'=16] {'cell'}, dimensions={0} | all-to-all | bytes 65536 | tf_op jit(solution)/shard_map/all_to_all | solution.py:514
  67.8 1.7 %sweep.2 = f32[16,2,256]{2,1,0:T(2,128)S(1)} custom-call(s32[2]{0:T(128)S(1)} %bitcast.6, f32[1024,256]{1,0:T(8,128)S(1)} %get-tuple-element.37.ks, f32[1024,256]{1,0:T(8,128)S(1)} %get-tuple-element.38.kt, f32[16,2,256]{2,1,0:T(2,128)S(1)} %all_to_all.15.parts, f32[8,256]{1,0:T(8,128)S(1)} %get-tuple-element.40.consts), custom_call_target="tpu_custom_call" | custom-call | tf_op jit(solution)/shard_map/sweep/pallas_call | solution.py:446
  69.5 9.2 %all_to_all.16.parts = f32[16,2,256]{2,1,0:T(2,128)S(1)} all-to-all(f32[16,2,256]{2,1,0:T(2,128)S(1)} %sweep.2), channel_id=1, replica_groups=mesh['grp'=2,'cell'=16] {'cell'}, dimensions={0} | all-to-all | bytes 65536 | tf_op jit(solution)/shard_map/all_to_all | solution.py:514
  78.7 1.7 %sweep.3 = (f32[1024,256]{1,0:T(8,128)S(1)}, f32[1024,256]{1,0:T(8,128)S(1)}, f32[16,2,256]{2,1,0:T(2,128)S(1)}) custom-call(s32[2]{0:T(128)S(1)} %bitcast.7, f32[1024,256]{1,0:T(8,128)S(1)} %get-tuple-element.37.ks, f32[1024,256]{1,0:T(8,128)S(1)} %get-tuple-element.38.kt, f32[16,2,256]{2,1,0:T(2,128)S(1)} %all_to_all.16.parts, ...), custom_call_target="tpu_custom_call" | custom-call | tf_op jit(solution)/shard_map/sweep/pallas_call | solution.py:446
  80.3 9.2 %all_to_all.17.parts = f32[16,2,256]{2,1,0:T(2,128)S(1)} all-to-all(f32[16,2,256]{2,1,0:T(2,128)S(1)} %get-tuple-element.43), channel_id=1, replica_groups=mesh['grp'=2,'cell'=16] {'cell'}, dimensions={0} | all-to-all | bytes 65536 | tf_op jit(solution)/shard_map/all_to_all | solution.py:515
  89.5 2.0 %finish.1 = (f32[1024,256]{1,0:T(8,128)}, f32[1024,256]{1,0:T(8,128)}, f32[1,256]{1,0:T(1,128)}) custom-call(f32[1024,256]{1,0:T(8,128)S(1)} %get-tuple-element.41.ss, f32[1024,256]{1,0:T(8,128)S(1)} %get-tuple-element.42.st, f32[16,2,256]{2,1,0:T(2,128)S(1)} %all_to_all.17.parts, f32[8,256]{1,0:T(8,128)S(1)} %get-tuple-element.40.consts), custom_call_target="tpu_custom_call" | custom-call | tf_op jit(solution)/shard_map/finish/pallas_call | solution.py:455
  (1 shorter events, 0.0 us)
Async XLA Ops:
  0.6 7.5 %collective-permute-start.1 = (bf16[128,256]{1,0:T(8,128)(2,1)}, bf16[128,256]{1,0:T(8,128)(2,1)S(1)}, u32[]{:S(2)}, u32[]{:S(2)}) collective-permute-start(bf16[128,256]{1,0:T(8,128)(2,1)} %refs_0_.1), channel_id=1, source_target_pairs={{0,8},{1,9},{2,10},{3,11},{4,12},{5,13},{6,14},{7,15},{8,0},{9,1},... | collective-permute-start | bytes 196616 | tf_op jit(solution)/shard_map/ppermute | solution.py:21
  4.7 4.5 %collective-permute-start = (bf16[128,256]{1,0:T(8,128)(2,1)}, bf16[128,256]{1,0:T(8,128)(2,1)S(1)}, u32[]{:S(2)}, u32[]{:S(2)}) collective-permute-start(bf16[128,256]{1,0:T(8,128)(2,1)} %refs_0_.1), channel_id=1, source_target_pairs={{0,4},{1,5},{2,6},{3,7},{4,0},{5,1},{6,2},{7,3},{8,12},{9,13},{10,... | collective-permute-start | bytes 196616 | tf_op jit(solution)/shard_map/ppermute | solution.py:21
  6.3 6.3 %collective-permute-start.2 = (bf16[128,256]{1,0:T(8,128)(2,1)}, bf16[128,256]{1,0:T(8,128)(2,1)S(1)}, u32[]{:S(2)}, u32[]{:S(2)}) collective-permute-start(bf16[128,256]{1,0:T(8,128)(2,1)} %refs_0_.1), channel_id=1, source_target_pairs={{0,12},{1,13},{2,14},{3,15},{4,8},{5,9},{6,10},{7,11},{8,4},{9,5},... | collective-permute-start | bytes 196616 | tf_op jit(solution)/shard_map/ppermute | solution.py:21
  12.6 0.8 copy-start
  13.4 1.7 %collective-permute-start.3 = (bf16[4,128,256]{2,1,0:T(8,128)(2,1)S(1)}, bf16[4,128,256]{2,1,0:T(8,128)(2,1)}, u32[]{:S(2)}, u32[]{:S(2)}) collective-permute-start(bf16[4,128,256]{2,1,0:T(8,128)(2,1)S(1)} %stack.1.even), channel_id=1, source_target_pairs={{0,1},{1,0},{2,3},{3,2},{4,5},{5,4},{6,7},{7,6},{8,9},{9,8},{10,11... | collective-permute-start | bytes 786440 | tf_op jit(solution)/shard_map/ppermute | solution.py:21
  13.5 8.8 %collective-permute-start.4 = (bf16[4,128,256]{2,1,0:T(8,128)(2,1)S(1)}, bf16[4,128,256]{2,1,0:T(8,128)(2,1)}, u32[]{:S(2)}, u32[]{:S(2)}) collective-permute-start(bf16[4,128,256]{2,1,0:T(8,128)(2,1)S(1)} %stack.1.even), channel_id=1, source_target_pairs={{0,2},{1,3},{2,0},{3,1},{4,6},{5,7},{6,4},{7,5},{8,10},{9,11},{10,... | collective-permute-start | bytes 786440 | tf_op jit(solution)/shard_map/ppermute | solution.py:21
  15.2 9.7 %copy-start.1 = (s32[2,1]{0,1:T(1,128)S(1)}, s32[2,1]{0,1:T(1,128)}, u32[]{:S(2)}) copy-start(s32[2,1]{0,1:T(1,128)} %param.13) | copy-start | bytes 28
  23.3 1.6 %collective-permute-start.5 = (bf16[4,128,256]{2,1,0:T(8,128)(2,1)S(1)}, bf16[4,128,256]{2,1,0:T(8,128)(2,1)S(1)}, u32[]{:S(2)}, u32[]{:S(2)}) collective-permute-start(bf16[4,128,256]{2,1,0:T(8,128)(2,1)S(1)} %gate.1), channel_id=1, source_target_pairs={{0,1},{1,0},{2,3},{3,2},{4,5},{5,4},{6,7},{7,6},{8,9},{9,8},{10,11... | collective-permute-start | bytes 786440 | tf_op jit(solution)/shard_map/ppermute | solution.py:21
  24.9 28.1 %copy-start.2 = (f32[256]{0:T(256)S(1)}, f32[256]{0:T(256)}, u32[]{:S(2)}) copy-start(f32[256]{0:T(256)} %param.12) | copy-start | bytes 3076
  29.3 1.6 %collective-permute-start.6 = (f32[264,256]{1,0:T(8,128)S(1)}, f32[264,256]{1,0:T(8,128)S(1)}, u32[]{:S(2)}, u32[]{:S(2)}) collective-permute-start(f32[264,256]{1,0:T(8,128)S(1)} %get-tuple-element.36), channel_id=1, source_target_pairs={{0,1},{1,0},{2,3},{3,2},{4,5},{5,4},{6,7},{7,6},{8,9},{9,8},{10,11... | collective-permute-start | bytes 811016 | tf_op jit(solution)/shard_map/ppermute | solution.py:21
  31.0 5.8 %collective-permute-start.7 = (bf16[272,256]{1,0:T(8,128)(2,1)S(1)}, bf16[272,256]{1,0:T(8,128)(2,1)S(1)}, u32[]{:S(2)}, u32[]{:S(2)}) collective-permute-start(bf16[272,256]{1,0:T(8,128)(2,1)S(1)} %pack_pair.1.own), channel_id=1, source_target_pairs={{0,2},{1,3},{2,0},{3,1},{4,6},{5,7},{6,4},{7,5},{8,10},{9,11},{10,... | collective-permute-start | bytes 417800 | tf_op jit(solution)/shard_map/ppermute | solution.py:21
  36.8 8.6 %collective-permute-start.10 = (bf16[288,256]{1,0:T(8,128)(2,1)S(1)}, bf16[288,256]{1,0:T(8,128)(2,1)S(1)}, u32[]{:S(2)}, u32[]{:S(2)}) collective-permute-start(bf16[288,256]{1,0:T(8,128)(2,1)S(1)} %pack_next.1.own), channel_id=1, source_target_pairs={{0,12},{1,13},{2,14},{3,15},{4,8},{5,9},{6,10},{7,11},{8,4},{9,5},... | collective-permute-start | bytes 442376 | tf_op jit(solution)/shard_map/ppermute | solution.py:21
  38.2 12.9 %collective-permute-start.9 = (bf16[288,256]{1,0:T(8,128)(2,1)S(1)}, bf16[288,256]{1,0:T(8,128)(2,1)S(1)}, u32[]{:S(2)}, u32[]{:S(2)}) collective-permute-start(bf16[288,256]{1,0:T(8,128)(2,1)S(1)} %pack_next.1.own), channel_id=1, source_target_pairs={{0,8},{1,9},{2,10},{3,11},{4,12},{5,13},{6,14},{7,15},{8,0},{9,1},... | collective-permute-start | bytes 442376 | tf_op jit(solution)/shard_map/ppermute | solution.py:21
  38.3 12.7 %collective-permute-start.8 = (bf16[288,256]{1,0:T(8,128)(2,1)S(1)}, bf16[288,256]{1,0:T(8,128)(2,1)S(1)}, u32[]{:S(2)}, u32[]{:S(2)}) collective-permute-start(bf16[288,256]{1,0:T(8,128)(2,1)S(1)} %pack_next.1.own), channel_id=1, source_target_pairs={{0,4},{1,5},{2,6},{3,7},{4,0},{5,1},{6,2},{7,3},{8,12},{9,13},{10,... | collective-permute-start | bytes 442376 | tf_op jit(solution)/shard_map/ppermute | solution.py:21
  51.4 1.6 %collective-permute-start.11 = (f32[264,256]{1,0:T(8,128)S(1)}, f32[264,256]{1,0:T(8,128)S(1)}, u32[]{:S(2)}, u32[]{:S(2)}) collective-permute-start(f32[264,256]{1,0:T(8,128)S(1)} %total.1.mine), channel_id=1, source_target_pairs={{0,1},{1,0},{2,3},{3,2},{4,5},{5,4},{6,7},{7,6},{8,9},{9,8},{10,11... | collective-permute-start | bytes 811016 | tf_op jit(solution)/shard_map/ppermute | solution.py:21

commit v4 on v3

--- a/solution.py
+++ b/solution.py
@@ -93,15 +93,15 @@
 
 
 def stack_kernel(*refs):
-    pieces, out = refs[:4], refs[-1]
-    for i, piece in enumerate(pieces):
-        out[i] = piece[...]
+    out = refs[-1]
+    for i in range(out.shape[0]):
+        out[i] = refs[i][...]
 
 
 def stack_pieces(pieces, after):
     return call(
-        stack_kernel, "stack", [VMEM] * 4 + [ANY] * len(after), VMEM,
-        array((4,) + pieces[0].shape, pieces[0].dtype),
+        stack_kernel, "stack", [VMEM] * len(pieces) + [ANY] * len(after), VMEM,
+        array((len(pieces),) + pieces[0].shape, pieces[0].dtype),
     )(*pieces, *after)
 
 
@@ -111,7 +111,7 @@
     return jnp.concatenate([jnp.where(swapped, b, a), jnp.where(swapped, a, b)])
 
 
-def first_kernel(masks, place, xs, xt, even, odd, part_s, part_t, later_s, later_t, held, sems):
+def first_kernel(masks, later_masks, place, xs, xt, even, odd, part_s, part_t, later_s, later_t, held, sems):
     me = place[0]
     width = 2 * even.shape[1]
 
@@ -122,18 +122,19 @@
         return made
 
     sets = ((xs, part_s, later_s), (xt, part_t, later_t))
+    blocks = len(masks)
     now = [
-        [copy(x, m, held.at[t, j], sems.at[0, t, j]) for j, m in enumerate(masks)]
+        [copy(x, m, held.at[t, j], sems.at[t, j]) for j, m in enumerate(masks)]
         for t, (x, _, _) in enumerate(sets)
     ]
     after = [
-        copy(x, m | 2, later.at[j], sems.at[1, t, j])
+        copy(x, m, later.at[j], sems.at[t, blocks + j])
+        for j, m in enumerate(later_masks)
         for t, (x, _, later) in enumerate(sets)
-        for j, m in enumerate(masks)
     ]
     for t, (_, part, _) in enumerate(sets):
         value = None
-        for j in range(len(masks)):
+        for j in range(blocks):
             now[t][j].wait()
             term = jnp.dot(held[t, j], joined_table(me, j, even, odd), preferred_element_type=f32)
             value = term if value is None else value + term
@@ -142,14 +143,18 @@
         made.wait()
 
 
-def first_half(place, xs, xt, masks, even, odd):
+def first_share(place, xs, xt, masks, later_masks, even, odd):
     rows, genes = xs.shape
     blocks, width, dim = even.shape
-    held = (blocks, rows, 2 * width)
-    return call(
-        functools.partial(first_kernel, masks), "embed_first", [SMEM, HBM, HBM, VMEM, VMEM], [VMEM] * 4,
-        [array((rows, dim))] * 2 + [pltpu.VMEM(held, bf16)] * 2,
-        [pltpu.VMEM((2,) + held, bf16), pltpu.SemaphoreType.DMA((2, 2, blocks))],
+    later = (len(later_masks), rows, 2 * width)
+    return call(
+        functools.partial(first_kernel, masks, later_masks), "embed_first",
+        [SMEM, HBM, HBM, VMEM, VMEM], [VMEM] * 4,
+        [array((rows, dim))] * 2 + [pltpu.VMEM(later, bf16)] * 2,
+        [
+            pltpu.VMEM((2, blocks, rows, 2 * width), bf16),
+            pltpu.SemaphoreType.DMA((2, blocks + len(later_masks))),
+        ],
         pl.CostEstimate(
             flops=2 * rows * genes * dim, bytes_accessed=4 * rows * genes, transcendentals=0
         ),
@@ -166,42 +171,52 @@
     )(value, after)
 
 
+def next_kernel(at, place, xs, xt, part_s, part_t, even, odd, out_s, out_t):
+    me = place[0]
+    for x, part, out in ((xs, part_s, out_s), (xt, part_t, out_t)):
+        value = part[...]
+        for j in range(even.shape[0]):
+            table = joined_table(me, j, even, odd)
+            value = value + jnp.dot(x[at + j], table, preferred_element_type=f32)
+        out[...] = value
+
+
+def next_share(at, place, xs, xt, parts, even, odd):
+    shape = parts[0].shape
+    return call(
+        functools.partial(next_kernel, at), "embed_next", [SMEM] + [VMEM] * 6, [VMEM] * 2,
+        [array(shape)] * 2,
+        cost=pl.CostEstimate(
+            flops=4 * shape[0] * shape[1] * 4 * even.shape[1], bytes_accessed=0, transcendentals=0
+        ),
+    )(place, xs, xt, *parts, even, odd)
+
+
 def whole_kernel(masks, place, xs, xt, *refs):
-    pieces, (part_s, part_t, table) = refs[:4], refs[4:]
+    pieces, (part_s, part_t, table) = refs[:-3], refs[-3:]
     genes = pieces[0].shape[1]
-    for piece, extra in zip(pieces, range(4)):
-        for j, mask in enumerate(masks):
-            start = pl.multiple_of((place[0] ^ (mask | extra)) * genes, genes)
+    for piece, places in zip(pieces, masks):
+        for j, mask in enumerate(places):
+            start = pl.multiple_of((place[0] ^ mask) * genes, genes)
             table[pl.ds(start, genes), :] = piece[j]
     for x, part in ((xs, part_s), (xt, part_t)):
         part[...] = jnp.dot(x[...], table[...], preferred_element_type=f32)
 
 
-def whole_product(place, xs, xt, masks, *pieces):
+def whole_product(place, xs, xt, masks, pieces):
     rows, genes = xs.shape
     dim = pieces[0].shape[2]
     return call(
-        functools.partial(whole_kernel, masks), "embed_whole", [SMEM] + [VMEM] * 6, [VMEM] * 2,
-        [array((rows, dim))] * 2, [pltpu.VMEM((genes, dim), bf16)],
+        functools.partial(whole_kernel, masks), "embed_whole", [SMEM] + [VMEM] * (2 + len(pieces)),
+        [VMEM] * 2, [array((rows, dim))] * 2, [pltpu.VMEM((genes, dim), bf16)],
     )(place, xs, xt, *pieces)
 
 
-def second_kernel(
-    place, live, xs, xt, part_s, part_t, even, odd, qs, qt, turned, totals,
-    emb_s, emb_t, own, send,
-):
-    me = place[0]
-    core = me & 1
+def cross_kernel(place, live, es, et, qs, qt, turned, totals, own, send):
+    core = place[0] & 1
     rows, rank = qs.shape
-    dim = emb_s.shape[1]
-    for t, (x, q, part, emb) in enumerate(
-        ((xs, qs, part_s, emb_s), (xt, qt, part_t, emb_t))
-    ):
-        value = part[...]
-        for j in range(x.shape[0]):
-            table = joined_table(me, j, even, odd)
-            value = value + jnp.dot(x[j], table, preferred_element_type=f32)
-        emb[...] = value
+    for t, (emb, q) in enumerate(((es, qs), (et, qt))):
+        value = emb[...]
         norms = jnp.sum(value * value, axis=1, keepdims=True)
         norm_sum = jnp.sum(norms * (q[...] / rank), axis=0, keepdims=True)
         mean = (jnp.sum(value, axis=0, keepdims=True) / rows).astype(bf16).astype(f32)
@@ -219,13 +234,11 @@
         pl.when(core != t)(lambda: put(send))
 
 
-def second_half(place, live, xs, xt, parts, even, odd, qs, qt, turned, totals):
-    rows, rank = qs.shape
-    dim = even.shape[2]
-    return call(
-        second_kernel, "embed_second", [SMEM] * 2 + [VMEM] * 10, [VMEM] * 4,
-        [array((rows, dim))] * 2 + [array((rank + 8, dim))] * 2,
-    )(place, live, *near(xs, xt), *parts, even, odd, *near(qs, qt, turned), totals)
+def cross(place, live, es, et, qs, qt, turned, totals):
+    rank, dim = qs.shape[1], es.shape[1]
+    return call(
+        cross_kernel, "cross", [SMEM] * 2 + [VMEM] * 6, [VMEM] * 2, [array((rank + 8, dim))] * 2,
+    )(place, live, es, et, *near(qs, qt, turned), totals)
 
 
 def split_row(row):
@@ -270,24 +283,42 @@
     )(own, recv)
 
 
-def pack_next_kernel(rank, cards, bit, place, own, recv, out):
-    out[0:rank, :] = (own[0:rank, :].astype(f32) + recv[0:rank, :].astype(f32)).astype(bf16)
-    a, b = own[rank:, :].astype(f32), recv[rank:, :].astype(f32)
-    first = (place[0] & bit) == 0
-    a_cards, b_cards = a[8 : 8 + 4 * cards], b[8 : 8 + 4 * cards]
-    ordered = [jnp.where(first, a_cards, b_cards), jnp.where(first, b_cards, a_cards)]
-    tail = make_tail(three(a, 0) + three(b, 0), three(a, 3) + three(b, 3), ordered)
-    out[rank:, :] = tail.astype(bf16)
-
-
-def pack_next(rank, cards, bit, place, own, recv):
-    return call(
-        functools.partial(pack_next_kernel, rank, cards, bit), "pack_next", [SMEM, VMEM, VMEM], VMEM,
-        array((rank + tail_rows(2 * cards), own.shape[1]), bf16),
-    )(place, own, recv)
-
-
-def total_kernel(rank, cards, own, low, high, both, out):
+def ordered_cards(tails, cards, flags):
+    lists = [tail[8 : 8 + 4 * cards] for tail in tails]
+    for flag in flags:
+        lists = [
+            jnp.concatenate([jnp.where(flag, a, b), jnp.where(flag, b, a)])
+            for a, b in zip(lists[::2], lists[1::2])
+        ]
+    return lists[0]
+
+
+def tree(values):
+    while len(values) > 1:
+        values = [a + b for a, b in zip(values[::2], values[1::2])]
+    return values[0]
+
+
+def merge_kernel(rank, cards, bits, place, *refs):
+    payloads, out = refs[:-1], refs[-1]
+    out[0:rank, :] = tree([p[0:rank, :].astype(f32) for p in payloads]).astype(bf16)
+    tails = [p[rank:, :].astype(f32) for p in payloads]
+    listed = ordered_cards(tails, cards, [(place[0] & bit) == 0 for bit in bits])
+    norm, number = (tree([three(tail, i) for tail in tails]) for i in (0, 3))
+    out[rank:, :] = make_tail(norm, number, [listed]).astype(bf16)
+
+
+def merge(rank, cards, bits, place, *payloads):
+    return call(
+        functools.partial(merge_kernel, rank, cards, bits), "merge",
+        [SMEM] + [VMEM] * len(payloads), VMEM,
+        array((rank + tail_rows(len(payloads) * cards), payloads[0].shape[1]), bf16),
+    )(place, *payloads)
+
+
+def total_kernel(rank, cards, *refs):
+    payloads, out = refs[:-1], refs[-1]
+
     def unpack(ref):
         tail = ref[rank:, :].astype(f32)
         heights, means, sums = [], [], jnp.zeros((1, tail.shape[1]), f32)
@@ -303,8 +334,7 @@
         )
         return ref[0:rank, :].astype(f32) + joined, three(tail, 0), sums, three(tail, 3)
 
-    parts = [unpack(ref) for ref in (own, low, high, both)]
-    joined = [(a + b) + (c + d) for a, b, c, d in zip(*parts)]
+    joined = [tree(list(values)) for values in zip(*[unpack(ref) for ref in payloads])]
     out[0:rank, :] = joined[0]
     out[rank:, :] = jnp.concatenate(joined[1:] + [jnp.zeros((5, out.shape[1]), f32)])
 
@@ -312,7 +342,7 @@
 def total(rank, cards, *payloads):
     dim = payloads[0].shape[1]
     return call(
-        functools.partial(total_kernel, rank, cards), "total", [VMEM] * 4, VMEM,
+        functools.partial(total_kernel, rank, cards), "total", [VMEM] * len(payloads), VMEM,
         array((rank + 8, dim)),
     )(*payloads)
 
@@ -472,37 +502,40 @@
     rows, rank = source_prev.shape
     cells = rows * count
     bits = [1 << b for b in range(count.bit_length() - 1)]
-    low, high = bits[-2], bits[-1]
-    between = bits[1:-2]
+    opposite = bits[-1] | bits[-2]
     exchange = functools.partial(lax.all_to_all, axis_name="cell", split_axis=0, concat_axis=0)
 
-    masks = [0, low, high, low | high]
-    pieces = [loadings] + [swap(loadings, count, m) for m in masks[1:]]
     qs, qt, turned, totals = fetch(source_prev, target_prev)
-    stack = stack_pieces(pieces, [totals])
-    for bit in reversed(between[1:]):
-        stack = jnp.concatenate([stack, swap(stack, count, bit)])
-        masks = masks + [m | bit for m in masks]
-    across = swap(stack, count, 2)
-    pair = swap(stack, count, 1)
-    if loadings.shape[0] % 64 == 0:
-        *parts, xs, xt = first_half(place, source_expr, target_expr, masks, stack, pair)
-        both = swap(gate(across, parts[0]), count, 1)
+    stack = stack_pieces([loadings, swap(loadings, count, opposite)], [totals])
+    masks = [0, opposite]
+    if count == 16 and loadings.shape[0] % 64 == 0:
+        quad = [2, 4, 6]
+        arrived = [swap(stack, count, m) for m in quad]
+        later = [m ^ q for q in quad for m in masks]
+        *parts, xs, xt = first_share(
+            place, source_expr, target_expr, masks, later, stack, swap(stack, count, 1)
+        )
+        arrived = [gate(piece, parts[0]) for piece in arrived]
+        for i, piece in enumerate(arrived):
+            parts = next_share(2 * i, place, xs, xt, parts, piece, swap(piece, count, 1))
     else:
-        both = swap(across, count, 1)
-        parts = whole_product(place, source_expr, target_expr, masks, stack, pair, across, both)
-        xs = xt = jnp.zeros((1, rows, 2 * loadings.shape[0]), bf16)
-    emb_s, emb_t, own, send = second_half(
-        place, live, xs, xt, parts, across, both, qs, qt, turned, totals
-    )
+        for bit in reversed(bits[:-1]):
+            stack = jnp.concatenate([stack, swap(stack, count, bit)])
+            masks = masks + [m ^ bit for m in masks]
+        parts = whole_product(place, source_expr, target_expr, [masks], [stack])
+    emb_s, emb_t = parts
+    own, send = cross(place, live, emb_s, emb_t, qs, qt, turned, totals)
 
     payload = pack_pair(own, swap(send, count, 1))
     cards = 2
-    for bit in between:
-        payload = pack_next(rank, cards, bit, place, payload, swap(payload, count, bit))
-        cards = 2 * cards
-    others = [swap(payload, count, m) for m in (low, high, low | high)]
-    mine = total(rank, cards, payload, *others)
+    inner = bits[1:-1]
+    while inner:
+        used, inner = inner[:2], inner[2:]
+        steps = [used[0], used[1], used[0] | used[1]] if len(used) == 2 else used
+        others = [swap(payload, count, m) for m in steps]
+        payload = merge(rank, cards, used, place, payload, *others)
+        cards = cards * (1 + len(others))
+    mine = total(rank, cards, payload, swap(payload, count, opposite))
     other = swap(mine, count, 1)
 
     ks, kt, copies, consts = kernels(

time: 91.9 us -> 85.1 us (0.926)
  waiting for transfers between devices: 25.1 us -> 16.7 us
  starting transfers between devices: 13.7 us -> 16.9 us
  Pallas kernels: 21.3 us -> 18.5 us
  blocking collectives: 29.8 us -> 31 us
    ppermute x12 -> x14, waiting for transfers between devices: 25.1 us -> 16.7 us  [swap(): return lax.ppermute(value, 'cell', [(i, i ^ mask) for i in range(count)])]
    ppermute x12 -> x14, starting transfers between devices: 13.7 us -> 16.9 us  [swap(): return lax.ppermute(value, 'cell', [(i, i ^ mask) for i in range(count)])]
    pallas_call x5 -> x8, Pallas kernels: 9.8 us -> 7.92 us  [the longest x1 3.64 us: first_share(): call(functools.partial(first_kernel, masks, later_masks), 'embed_first',...]
    all_to_all x2, blocking collectives: 20.6 us -> 21.8 us  [on_device(): *scaled, copies = sweep(count, last, live, ks, kt, exchange(copies), consts)]
    pallas_call x1 -> x3, Pallas kernels: 0.97 us -> 0.03 us  [gate(): call(gate_kernel, 'gate', [VMEM, ANY], VMEM, array(value.shape, value.dty...]
  transfers between devices with their start and end apart: 12 -> 14, of which waited for: 10 -> 8; matrix products, arithmetic and copies ran while one was open for 0% -> 0% of each run, Pallas kernels for 7% -> 8%
where the time goes in v4:
time: 85.1 us; the launch traced here: 84.8 us
  blocking collectives  31 us (36%)
  Pallas kernels  18.5 us (22%)
  starting transfers between devices  16.9 us (20%)
  waiting for transfers between devices  16.7 us (20%)
    all_to_all x2, blocking collectives, on_device(): *scaled, copies = sweep(count, last, live, ks, kt, exchange(copies), consts)  21.8 us
    ppermute x14, starting transfers between devices, swap(): return lax.ppermute(value, 'cell', [(i, i ^ mask) for i in range(count)])  16.9 us
    ppermute x14, waiting for transfers between devices, swap(): return lax.ppermute(value, 'cell', [(i, i ^ mask) for i in range(count)])  16.7 us
    all_to_all x1, blocking collectives, on_device(): out_s, out_t, weights = finish(cells, *scaled, exchange(copies), consts)  9.2 us
    pallas_call x1, Pallas kernels, first_share(): call(functools.partial(first_kernel, masks, later_masks), 'embed_first',...  3.64 us
    pallas_call x1, Pallas kernels, kernels(): call(functools.partial(kernels_kernel, cells), 'kernels', [SMEM, SMEM] +...  3.4 us
    pallas_call x2, Pallas kernels, sweep(): call(functools.partial(sweep_kernel, last), 'sweep', [SMEM] + [VMEM] * 4,...  3.36 us
    pallas_call x3, Pallas kernels, next_share(): call(functools.partial(next_kernel, at), 'embed_next', [SMEM] + [VMEM] *...  2.12 us
  transfers between devices with their start and end apart: 14, of which 8 were waited for; matrix products, arithmetic and copies ran while one was open for 0% of the time, Pallas kernels for 8%

profile of v4, /device:TPU:0, one launch (start us, length us, event | category | flops | bytes accessed | tf_op | source)
XLA Modules:
  0.0 84.8 jit_solution(9552163050498334849)
XLA Ops:
  0.6 5.1 %collective-permute-start = (bf16[128,256]{1,0:T(8,128)(2,1)}, bf16[128,256]{1,0:T(8,128)(2,1)S(1)}, u32[]{:S(2)}, u32[]{:S(2)}) collective-permute-start(bf16[128,256]{1,0:T(8,128)(2,1)} %refs_0_.1), channel_id=1, source_target_pairs={{0,12},{1,13},{2,14},{3,15},{4,8},{5,9},{6,10},{7,11},{8,4},{9,5},... | collective-permute-start | bytes 196616 | tf_op jit(solution)/shard_map/ppermute | solution.py:21
  5.7 1.8 %fetch.1 = (f32[1024,256]{1,0:T(8,128)S(1)}, f32[1024,256]{1,0:T(8,128)S(1)}, bf16[2,256,1024]{2,1,0:T(8,128)(2,1)S(1)}, f32[2,256]{1,0:T(2,128)S(1)}) custom-call(f32[1024,256]{1,0:T(8,128)} %qs.1, f32[1024,256]{1,0:T(8,128)} %qt.1), custom_call_target="tpu_custom_call" | custom-call | bytes 2097152 | tf_op jit(solution)/shard_map/fetch/pallas_call | solution.py:86
  7.5 0.7 collective-permute-done.refs_1_
  8.3 0.8 copy-done
  9.1 0.1 collective-permute-start.1
  9.2 1.8 %collective-permute-start.2 = (bf16[2,128,256]{2,1,0:T(8,128)(2,1)S(1)}, bf16[2,128,256]{2,1,0:T(8,128)(2,1)S(1)}, u32[]{:S(2)}, u32[]{:S(2)}) collective-permute-start(bf16[2,128,256]{2,1,0:T(8,128)(2,1)S(1)} %stack.1.even), channel_id=1, source_target_pairs={{0,2},{1,3},{2,0},{3,1},{4,6},{5,7},{6,4},{7,5},{8,10},{9,11},{10,... | collective-permute-start | bytes 393224 | tf_op jit(solution)/shard_map/ppermute | solution.py:21
  11.0 0.8 collective-permute-start.6
  11.8 1.0 %collective-permute-start.4 = (bf16[2,128,256]{2,1,0:T(8,128)(2,1)S(1)}, bf16[2,128,256]{2,1,0:T(8,128)(2,1)S(1)}, u32[]{:S(2)}, u32[]{:S(2)}) collective-permute-start(bf16[2,128,256]{2,1,0:T(8,128)(2,1)S(1)} %stack.1.even), channel_id=1, source_target_pairs={{0,4},{1,5},{2,6},{3,7},{4,0},{5,1},{6,2},{7,3},{8,12},{9,13},{10,... | collective-permute-start | bytes 393224 | tf_op jit(solution)/shard_map/ppermute | solution.py:21
  12.7 0.0 collective-permute-done.1.odd
  12.7 3.6 %embed_first.1 = (f32[1024,256]{1,0:T(8,128)S(1)}, f32[1024,256]{1,0:T(8,128)S(1)}, bf16[6,1024,256]{2,1,0:T(8,128)(2,1)S(1)}, bf16[6,1024,256]{2,1,0:T(8,128)(2,1)S(1)}) custom-call(s32[1]{0:T(128)} %bitcast.1.place, bf16[1024,2048]{1,0:T(8,128)(2,1)} %xs.1, bf16[1024,2048]{1,0:T(8,128)(2,1)} %xt.1, bf16[2,128,256]{2,1,0:T(8,128)(2,1)S(1)} %stack.1.even, ...), custom_call_target="tpu_custom_call" | custom-call | flops 1073741824 | bytes 8388608 | tf_op jit(solution)/shard_map/embed_first/pallas_call | solution.py:150
  16.4 1.2 %collective-permute-done.2.value = bf16[2,128,256]{2,1,0:T(8,128)(2,1)S(1)} collective-permute-done((bf16[2,128,256]{2,1,0:T(8,128)(2,1)S(1)}, bf16[2,128,256]{2,1,0:T(8,128)(2,1)S(1)}, u32[]{:S(2)}, u32[]{:S(2)}) %collective-permute-start.2) | collective-permute-done | bytes 131104 | tf_op jit(solution)/shard_map/ppermute | solution.py:21
  17.6 0.1 collective-permute-start.3
  17.6 1.5 %collective-permute-done.4.value = bf16[2,128,256]{2,1,0:T(8,128)(2,1)S(1)} collective-permute-done((bf16[2,128,256]{2,1,0:T(8,128)(2,1)S(1)}, bf16[2,128,256]{2,1,0:T(8,128)(2,1)S(1)}, u32[]{:S(2)}, u32[]{:S(2)}) %collective-permute-start.4) | collective-permute-done | bytes 131104 | tf_op jit(solution)/shard_map/ppermute | solution.py:21
  19.2 0.1 collective-permute-start.5
  19.2 0.0 collective-permute-done.6.value
  19.3 0.5 collective-permute-start.7
  19.8 0.0 collective-permute-done.3.odd
  19.8 0.7 embed_next.3
  20.5 0.0 collective-permute-done.5.odd
  20.6 0.7 embed_next.4
  21.3 0.0 collective-permute-done.7.odd
  21.3 0.0 copy-start.1
  21.3 0.7 embed_next.5
  22.0 0.0 copy-start.2
  22.0 0.0 copy-done.1
  22.0 1.8 %cross.1 = (f32[264,256]{1,0:T(8,128)S(1)}, f32[264,256]{1,0:T(8,128)S(1)}) custom-call(s32[1]{0:T(128)} %bitcast.1.place, s32[2]{0:T(128)S(1)} %bitcast.4, f32[1024,256]{1,0:T(8,128)S(1)} %get-tuple-element.38.es, f32[1024,256]{1,0:T(8,128)S(1)} %get-tuple-element.39.et, f32[1024,256]{1,0:T(8,128)S(1)} %get-tuple-element.40.qs, ...), custom_call_target="tpu_custom_call" | custom-call | tf_op jit(solution)/shard_map/cross/pallas_call | solution.py:239
  23.8 0.2 collective-permute-start.8
  24.1 1.4 %collective-permute-done.8.recv = f32[264,256]{1,0:T(8,128)S(1)} collective-permute-done((f32[264,256]{1,0:T(8,128)S(1)}, f32[264,256]{1,0:T(8,128)S(1)}, u32[]{:S(2)}, u32[]{:S(2)}) %collective-permute-start.8) | collective-permute-done | bytes 270368 | tf_op jit(solution)/shard_map/ppermute | solution.py:21
  25.5 2.1 %collective-permute-start.11 = (bf16[272,256]{1,0:T(8,128)(2,1)S(1)}, bf16[272,256]{1,0:T(8,128)(2,1)S(1)}, u32[]{:S(2)}, u32[]{:S(2)}) collective-permute-start(bf16[272,256]{1,0:T(8,128)(2,1)S(1)} %pack_pair.1.refs_0_), channel_id=1, source_target_pairs={{0,6},{1,7},{2,4},{3,5},{4,2},{5,3},{6,0},{7,1},{8,14},{9,15},{10,... | collective-permute-start | bytes 417800 | tf_op jit(solution)/shard_map/ppermute | solution.py:21
  27.6 1.2 %collective-permute-start.10 = (bf16[272,256]{1,0:T(8,128)(2,1)S(1)}, bf16[272,256]{1,0:T(8,128)(2,1)S(1)}, u32[]{:S(2)}, u32[]{:S(2)}) collective-permute-start(bf16[272,256]{1,0:T(8,128)(2,1)S(1)} %pack_pair.1.refs_0_), channel_id=1, source_target_pairs={{0,4},{1,5},{2,6},{3,7},{4,0},{5,1},{6,2},{7,3},{8,12},{9,13},{10,... | collective-permute-start | bytes 417800 | tf_op jit(solution)/shard_map/ppermute | solution.py:21
  28.8 0.3 collective-permute-start.9
  29.1 3.9 %collective-permute-done.11.refs_3_ = bf16[272,256]{1,0:T(8,128)(2,1)S(1)} collective-permute-done((bf16[272,256]{1,0:T(8,128)(2,1)S(1)}, bf16[272,256]{1,0:T(8,128)(2,1)S(1)}, u32[]{:S(2)}, u32[]{:S(2)}) %collective-permute-start.11) | collective-permute-done | bytes 139296 | tf_op jit(solution)/shard_map/ppermute | solution.py:21
  33.0 2.5 %collective-permute-done.10.refs_2_ = bf16[272,256]{1,0:T(8,128)(2,1)S(1)} collective-permute-done((bf16[272,256]{1,0:T(8,128)(2,1)S(1)}, bf16[272,256]{1,0:T(8,128)(2,1)S(1)}, u32[]{:S(2)}, u32[]{:S(2)}) %collective-permute-start.10) | collective-permute-done | bytes 139296 | tf_op jit(solution)/shard_map/ppermute | solution.py:21
  35.5 0.0 collective-permute-done.9.refs_1_
  35.5 0.1 merge.1.refs_0_
  35.6 3.6 %collective-permute-start.12 = (bf16[304,256]{1,0:T(8,128)(2,1)S(1)}, bf16[304,256]{1,0:T(8,128)(2,1)S(1)}, u32[]{:S(2)}, u32[]{:S(2)}) collective-permute-start(bf16[304,256]{1,0:T(8,128)(2,1)S(1)} %merge.1.refs_0_), channel_id=1, source_target_pairs={{0,12},{1,13},{2,14},{3,15},{4,8},{5,9},{6,10},{7,11},{8,4},{9,5},... | collective-permute-start | bytes 466952 | tf_op jit(solution)/shard_map/ppermute | solution.py:21
  39.2 3.9 %collective-permute-done.12.refs_1_ = bf16[304,256]{1,0:T(8,128)(2,1)S(1)} collective-permute-done((bf16[304,256]{1,0:T(8,128)(2,1)S(1)}, bf16[304,256]{1,0:T(8,128)(2,1)S(1)}, u32[]{:S(2)}, u32[]{:S(2)}) %collective-permute-start.12) | collective-permute-done | bytes 155680 | tf_op jit(solution)/shard_map/ppermute | solution.py:21
  43.1 0.3 total.1.mine
  43.4 0.1 collective-permute-start.13
  43.5 1.5 %collective-permute-done.13.other = f32[264,256]{1,0:T(8,128)S(1)} collective-permute-done((f32[264,256]{1,0:T(8,128)S(1)}, f32[264,256]{1,0:T(8,128)S(1)}, u32[]{:S(2)}, u32[]{:S(2)}) %collective-permute-start.13) | collective-permute-done | bytes 270368 | tf_op jit(solution)/shard_map/ppermute | solution.py:21
  45.0 0.0 copy-done.2
  45.0 3.4 %kernels.1 = (f32[1024,256]{1,0:T(8,128)S(1)}, f32[1024,256]{1,0:T(8,128)S(1)}, f32[16,2,256]{2,1,0:T(2,128)S(1)}, f32[8,256]{1,0:T(8,128)S(1)}) custom-call(s32[1]{0:T(128)} %bitcast.1.place, s32[2]{0:T(128)S(1)} %bitcast.5, f32[1024,256]{1,0:T(8,128)S(1)} %get-tuple-element.38.es, f32[1024,256]{1,0:T(8,128)S(1)} %get-tuple-element.39.et, ...), custom_call_target="tpu_custom_call" | custom-call | tf_op jit(solution)/shard_map/kernels/pallas_call | solution.py:466
  48.4 12.6 %all_to_all.15.parts = f32[16,2,256]{2,1,0:T(2,128)S(1)} all-to-all(f32[16,2,256]{2,1,0:T(2,128)S(1)} %get-tuple-element.47), channel_id=1, replica_groups=mesh['grp'=2,'cell'=16] {'cell'}, dimensions={0} | all-to-all | bytes 65536 | tf_op jit(solution)/shard_map/all_to_all | solution.py:547
  61.0 1.7 %sweep.2 = f32[16,2,256]{2,1,0:T(2,128)S(1)} custom-call(s32[2]{0:T(128)S(1)} %bitcast.6, f32[1024,256]{1,0:T(8,128)S(1)} %get-tuple-element.45.ks, f32[1024,256]{1,0:T(8,128)S(1)} %get-tuple-element.46.kt, f32[16,2,256]{2,1,0:T(2,128)S(1)} %all_to_all.15.parts, f32[8,256]{1,0:T(8,128)S(1)} %get-tuple-element.48.consts), custom_call_target="tpu_custom_call" | custom-call | tf_op jit(solution)/shard_map/sweep/pallas_call | solution.py:476
  62.7 9.2 %all_to_all.16.parts = f32[16,2,256]{2,1,0:T(2,128)S(1)} all-to-all(f32[16,2,256]{2,1,0:T(2,128)S(1)} %sweep.2), channel_id=1, replica_groups=mesh['grp'=2,'cell'=16] {'cell'}, dimensions={0} | all-to-all | bytes 65536 | tf_op jit(solution)/shard_map/all_to_all | solution.py:547
  71.9 1.7 %sweep.3 = (f32[1024,256]{1,0:T(8,128)S(1)}, f32[1024,256]{1,0:T(8,128)S(1)}, f32[16,2,256]{2,1,0:T(2,128)S(1)}) custom-call(s32[2]{0:T(128)S(1)} %bitcast.7, f32[1024,256]{1,0:T(8,128)S(1)} %get-tuple-element.45.ks, f32[1024,256]{1,0:T(8,128)S(1)} %get-tuple-element.46.kt, f32[16,2,256]{2,1,0:T(2,128)S(1)} %all_to_all.16.parts, ...), custom_call_target="tpu_custom_call" | custom-call | tf_op jit(solution)/shard_map/sweep/pallas_call | solution.py:476
  73.6 9.2 %all_to_all.17.parts = f32[16,2,256]{2,1,0:T(2,128)S(1)} all-to-all(f32[16,2,256]{2,1,0:T(2,128)S(1)} %get-tuple-element.51), channel_id=1, replica_groups=mesh['grp'=2,'cell'=16] {'cell'}, dimensions={0} | all-to-all | bytes 65536 | tf_op jit(solution)/shard_map/all_to_all | solution.py:548
  82.8 2.0 %finish.1 = (f32[1024,256]{1,0:T(8,128)}, f32[1024,256]{1,0:T(8,128)}, f32[1,256]{1,0:T(1,128)}) custom-call(f32[1024,256]{1,0:T(8,128)S(1)} %get-tuple-element.49.ss, f32[1024,256]{1,0:T(8,128)S(1)} %get-tuple-element.50.st, f32[16,2,256]{2,1,0:T(2,128)S(1)} %all_to_all.17.parts, f32[8,256]{1,0:T(8,128)S(1)} %get-tuple-element.48.consts), custom_call_target="tpu_custom_call" | custom-call | tf_op jit(solution)/shard_map/finish/pallas_call | solution.py:485
  (6 shorter events, 0.1 us)
Async XLA Ops:
  0.6 7.6 %collective-permute-start = (bf16[128,256]{1,0:T(8,128)(2,1)}, bf16[128,256]{1,0:T(8,128)(2,1)S(1)}, u32[]{:S(2)}, u32[]{:S(2)}) collective-permute-start(bf16[128,256]{1,0:T(8,128)(2,1)} %refs_0_.1), channel_id=1, source_target_pairs={{0,12},{1,13},{2,14},{3,15},{4,8},{5,9},{6,10},{7,11},{8,4},{9,5},... | collective-permute-start | bytes 196616 | tf_op jit(solution)/shard_map/ppermute | solution.py:21
  8.3 0.8 copy-start
  9.1 3.6 %collective-permute-start.1 = (bf16[2,128,256]{2,1,0:T(8,128)(2,1)S(1)}, bf16[2,128,256]{2,1,0:T(8,128)(2,1)S(1)}, u32[]{:S(2)}, u32[]{:S(2)}) collective-permute-start(bf16[2,128,256]{2,1,0:T(8,128)(2,1)S(1)} %stack.1.even), channel_id=1, source_target_pairs={{0,1},{1,0},{2,3},{3,2},{4,5},{5,4},{6,7},{7,6},{8,9},{9,8},{10,11... | collective-permute-start | bytes 393224 | tf_op jit(solution)/shard_map/ppermute | solution.py:21
  9.2 8.4 %collective-permute-start.2 = (bf16[2,128,256]{2,1,0:T(8,128)(2,1)S(1)}, bf16[2,128,256]{2,1,0:T(8,128)(2,1)S(1)}, u32[]{:S(2)}, u32[]{:S(2)}) collective-permute-start(bf16[2,128,256]{2,1,0:T(8,128)(2,1)S(1)} %stack.1.even), channel_id=1, source_target_pairs={{0,2},{1,3},{2,0},{3,1},{4,6},{5,7},{6,4},{7,5},{8,10},{9,11},{10,... | collective-permute-start | bytes 393224 | tf_op jit(solution)/shard_map/ppermute | solution.py:21
  11.0 8.2 %collective-permute-start.6 = (bf16[2,128,256]{2,1,0:T(8,128)(2,1)S(1)}, bf16[2,128,256]{2,1,0:T(8,128)(2,1)S(1)}, u32[]{:S(2)}, u32[]{:S(2)}) collective-permute-start(bf16[2,128,256]{2,1,0:T(8,128)(2,1)S(1)} %stack.1.even), channel_id=1, source_target_pairs={{0,6},{1,7},{2,4},{3,5},{4,2},{5,3},{6,0},{7,1},{8,14},{9,15},{10,... | collective-permute-start | bytes 393224 | tf_op jit(solution)/shard_map/ppermute | solution.py:21
  11.8 7.4 %collective-permute-start.4 = (bf16[2,128,256]{2,1,0:T(8,128)(2,1)S(1)}, bf16[2,128,256]{2,1,0:T(8,128)(2,1)S(1)}, u32[]{:S(2)}, u32[]{:S(2)}) collective-permute-start(bf16[2,128,256]{2,1,0:T(8,128)(2,1)S(1)} %stack.1.even), channel_id=1, source_target_pairs={{0,4},{1,5},{2,6},{3,7},{4,0},{5,1},{6,2},{7,3},{8,12},{9,13},{10,... | collective-permute-start | bytes 393224 | tf_op jit(solution)/shard_map/ppermute | solution.py:21
  17.6 2.3 %collective-permute-start.3 = (bf16[2,128,256]{2,1,0:T(8,128)(2,1)S(1)}, bf16[2,128,256]{2,1,0:T(8,128)(2,1)S(1)}, u32[]{:S(2)}, u32[]{:S(2)}) collective-permute-start(bf16[2,128,256]{2,1,0:T(8,128)(2,1)S(1)} %gate.3.even), channel_id=1, source_target_pairs={{0,1},{1,0},{2,3},{3,2},{4,5},{5,4},{6,7},{7,6},{8,9},{9,8},{10,11... | collective-permute-start | bytes 393224 | tf_op jit(solution)/shard_map/ppermute | solution.py:21
  19.2 1.4 %collective-permute-start.5 = (bf16[2,128,256]{2,1,0:T(8,128)(2,1)S(1)}, bf16[2,128,256]{2,1,0:T(8,128)(2,1)S(1)}, u32[]{:S(2)}, u32[]{:S(2)}) collective-permute-start(bf16[2,128,256]{2,1,0:T(8,128)(2,1)S(1)} %gate.4.even), channel_id=1, source_target_pairs={{0,1},{1,0},{2,3},{3,2},{4,5},{5,4},{6,7},{7,6},{8,9},{9,8},{10,11... | collective-permute-start | bytes 393224 | tf_op jit(solution)/shard_map/ppermute | solution.py:21
  19.3 2.0 %collective-permute-start.7 = (bf16[2,128,256]{2,1,0:T(8,128)(2,1)S(1)}, bf16[2,128,256]{2,1,0:T(8,128)(2,1)S(1)}, u32[]{:S(2)}, u32[]{:S(2)}) collective-permute-start(bf16[2,128,256]{2,1,0:T(8,128)(2,1)S(1)} %gate.5.even), channel_id=1, source_target_pairs={{0,1},{1,0},{2,3},{3,2},{4,5},{5,4},{6,7},{7,6},{8,9},{9,8},{10,11... | collective-permute-start | bytes 393224 | tf_op jit(solution)/shard_map/ppermute | solution.py:21
  21.3 0.7 copy-start.1
  22.0 23.0 %copy-start.2 = (f32[256]{0:T(256)S(1)}, f32[256]{0:T(256)}, u32[]{:S(2)}) copy-start(f32[256]{0:T(256)} %param.12) | copy-start | bytes 3076
  23.8 1.6 %collective-permute-start.8 = (f32[264,256]{1,0:T(8,128)S(1)}, f32[264,256]{1,0:T(8,128)S(1)}, u32[]{:S(2)}, u32[]{:S(2)}) collective-permute-start(f32[264,256]{1,0:T(8,128)S(1)} %get-tuple-element.44), channel_id=1, source_target_pairs={{0,1},{1,0},{2,3},{3,2},{4,5},{5,4},{6,7},{7,6},{8,9},{9,8},{10,11... | collective-permute-start | bytes 811016 | tf_op jit(solution)/shard_map/ppermute | solution.py:21
  25.5 7.5 %collective-permute-start.11 = (bf16[272,256]{1,0:T(8,128)(2,1)S(1)}, bf16[272,256]{1,0:T(8,128)(2,1)S(1)}, u32[]{:S(2)}, u32[]{:S(2)}) collective-permute-start(bf16[272,256]{1,0:T(8,128)(2,1)S(1)} %pack_pair.1.refs_0_), channel_id=1, source_target_pairs={{0,6},{1,7},{2,4},{3,5},{4,2},{5,3},{6,0},{7,1},{8,14},{9,15},{10,... | collective-permute-start | bytes 417800 | tf_op jit(solution)/shard_map/ppermute | solution.py:21
  27.6 7.9 %collective-permute-start.10 = (bf16[272,256]{1,0:T(8,128)(2,1)S(1)}, bf16[272,256]{1,0:T(8,128)(2,1)S(1)}, u32[]{:S(2)}, u32[]{:S(2)}) collective-permute-start(bf16[272,256]{1,0:T(8,128)(2,1)S(1)} %pack_pair.1.refs_0_), channel_id=1, source_target_pairs={{0,4},{1,5},{2,6},{3,7},{4,0},{5,1},{6,2},{7,3},{8,12},{9,13},{10,... | collective-permute-start | bytes 417800 | tf_op jit(solution)/shard_map/ppermute | solution.py:21
  28.8 6.7 %collective-permute-start.9 = (bf16[272,256]{1,0:T(8,128)(2,1)S(1)}, bf16[272,256]{1,0:T(8,128)(2,1)S(1)}, u32[]{:S(2)}, u32[]{:S(2)}) collective-permute-start(bf16[272,256]{1,0:T(8,128)(2,1)S(1)} %pack_pair.1.refs_0_), channel_id=1, source_target_pairs={{0,2},{1,3},{2,0},{3,1},{4,6},{5,7},{6,4},{7,5},{8,10},{9,11},{10,... | collective-permute-start | bytes 417800 | tf_op jit(solution)/shard_map/ppermute | solution.py:21
  35.6 7.5 %collective-permute-start.12 = (bf16[304,256]{1,0:T(8,128)(2,1)S(1)}, bf16[304,256]{1,0:T(8,128)(2,1)S(1)}, u32[]{:S(2)}, u32[]{:S(2)}) collective-permute-start(bf16[304,256]{1,0:T(8,128)(2,1)S(1)} %merge.1.refs_0_), channel_id=1, source_target_pairs={{0,12},{1,13},{2,14},{3,15},{4,8},{5,9},{6,10},{7,11},{8,4},{9,5},... | collective-permute-start | bytes 466952 | tf_op jit(solution)/shard_map/ppermute | solution.py:21
  43.4 1.6 %collective-permute-start.13 = (f32[264,256]{1,0:T(8,128)S(1)}, f32[264,256]{1,0:T(8,128)S(1)}, u32[]{:S(2)}, u32[]{:S(2)}) collective-permute-start(f32[264,256]{1,0:T(8,128)S(1)} %total.1.mine), channel_id=1, source_target_pairs={{0,1},{1,0},{2,3},{3,2},{4,5},{5,4},{6,7},{7,6},{8,9},{9,8},{10,11... | collective-permute-start | bytes 811016 | tf_op jit(solution)/shard_map/ppermute | solution.py:21

commit v5 on v4

v5 whole, which is shorter than its diff:
```python
import functools

import jax
import jax.numpy as jnp
from jax import lax
from jax.experimental import pallas as pl
from jax.experimental.pallas import tpu as pltpu
from jax.sharding import PartitionSpec as P

D = 256
ITERS = 3
STEPS = 4

step_size = 1.0
f32 = jnp.float32
bf16 = jnp.bfloat16
LIMIT = 16 * 1024 * 1024


def swap(value, count, mask):
    return lax.ppermute(value, "cell", [(i, i ^ mask) for i in range(count)])


def halves(value):
    upper = value.astype(bf16)
    return upper, (value - upper.astype(f32)).astype(bf16)


def dot3(a, b, left, right):
    dims = (((left,), (right,)), ((), ()))
    dot = functools.partial(lax.dot_general, dimension_numbers=dims, preferred_element_type=f32)
    return dot(a[0], b[0]) + (dot(a[0], b[1]) + dot(a[1], b[0]))


VMEM = pl.BlockSpec(memory_space=pltpu.VMEM)
SMEM = pl.BlockSpec(memory_space=pltpu.SMEM)
HBM = pl.BlockSpec(memory_space=pltpu.HBM)
ANY = pl.BlockSpec(memory_space=pl.ANY)


def far(*arrays):
    return [pltpu.with_memory_space_constraint(a, pltpu.HBM) for a in arrays]


def near(*arrays):
    return [pltpu.with_memory_space_constraint(a, pltpu.VMEM) for a in arrays]


def array(shape, dtype=f32):
    return jax.ShapeDtypeStruct(shape, dtype)


def call(body, name, in_specs, out_specs, out_shape, scratch=(), cost=None):
    return pl.pallas_call(
        body,
        in_specs=in_specs,
        out_specs=out_specs,
        out_shape=out_shape,
        scratch_shapes=list(scratch),
        compiler_params=pltpu.CompilerParams(vmem_limit_bytes=LIMIT),
        cost_estimate=cost,
        name=name,
    )


def rows_of(step, block):
    return pl.ds(pl.multiple_of(step * block, block), block)


def fetch_kernel(qs, qt, table, q_out, table_out, turned, totals, sems):
    pairs = ((qs, q_out.at[0]), (qt, q_out.at[1]), (table, table_out))
    copies = [pltpu.make_async_copy(a, b, sems.at[i]) for i, (a, b) in enumerate(pairs)]
    for copy in copies:
        copy.start()
    rank = qs.shape[1]
    for t in range(2):
        copies[t].wait()
        factor = q_out[t] / rank
        totals[t] = jnp.sum(factor, axis=0, keepdims=True)
        turned[t] = factor.T.astype(bf16)
    copies[2].wait()


def fetch(qs, qt, table):
    rows, rank = qs.shape
    return call(
        fetch_kernel, "fetch", [HBM] * 3, [VMEM] * 4,
        [
            pltpu.VMEM((2, rows, rank), f32), pltpu.VMEM(table.shape, table.dtype),
            pltpu.VMEM((2, rank, rows), bf16), array((2, 1, rank)),
        ],
        [pltpu.SemaphoreType.DMA((3,))],
        pl.CostEstimate(flops=0, bytes_accessed=8 * rows * rank, transcendentals=0),
    )(*far(qs, qt, table))


def stack_kernel(*refs):
    out = refs[-1]
    for i in range(out.shape[0]):
        out[i] = refs[i][...]


def stack_pieces(pieces, after):
    return call(
        stack_kernel, "stack", [VMEM] * len(pieces) + [ANY] * len(after), VMEM,
        array((len(pieces),) + pieces[0].shape, pieces[0].dtype),
    )(*pieces, *after)


def joined_table(me, j, even, odd):
    swapped = (me & 1) == 1
    a, b = even[j], odd[j]
    return jnp.concatenate([jnp.where(swapped, b, a), jnp.where(swapped, a, b)])


def first_kernel(masks, later_masks, place, xs, xt, even, odd, part, later, held, sems):
    me = place[0]
    width = 2 * even.shape[1]

    def copy(x, mask, out, sem):
        start = pl.multiple_of(((me ^ mask) >> 1) * width, width)
        made = pltpu.make_async_copy(x.at[:, pl.ds(start, width)], out, sem)
        made.start()
        return made

    blocks = len(masks)
    now = [
        [copy(x, m, held.at[t, j], sems.at[t, j]) for j, m in enumerate(masks)]
        for t, x in enumerate((xs, xt))
    ]
    after = [
        copy(x, m, later.at[t, j], sems.at[t, blocks + j])
        for j, m in enumerate(later_masks)
        for t, x in enumerate((xs, xt))
    ]
    for t in range(2):
        value = None
        for j in range(blocks):
            now[t][j].wait()
            term = jnp.dot(held[t, j], joined_table(me, j, even, odd), preferred_element_type=f32)
            value = term if value is None else value + term
        part[t] = value
    for made in after:
        made.wait()


def first_share(place, xs, xt, masks, later_masks, even, odd):
    rows, genes = xs.shape
    blocks, width, dim = even.shape
    return call(
        functools.partial(first_kernel, masks, later_masks), "embed_first",
        [SMEM, HBM, HBM, VMEM, VMEM], [VMEM] * 2,
        [array((2, rows, dim)), pltpu.VMEM((2, len(later_masks), rows, 2 * width), bf16)],
        [
            pltpu.VMEM((2, blocks, rows, 2 * width), bf16),
            pltpu.SemaphoreType.DMA((2, blocks + len(later_masks))),
        ],
        pl.CostEstimate(
            flops=2 * rows * genes * dim, bytes_accessed=4 * rows * genes, transcendentals=0
        ),
    )(place, *far(xs, xt), even, odd)


def gate_kernel(value, after, out):
    out[...] = value[...]


def gate(value, after):
    return call(
        gate_kernel, "gate", [VMEM, ANY], VMEM, array(value.shape, value.dtype)
    )(value, after)


def next_kernel(at, place, x, part, even, odd, out):
    me = place[0]
    tables = [joined_table(me, j, even, odd) for j in range(even.shape[0])]
    for t in range(2):
        value = part[t]
        for j, table in enumerate(tables):
            value = value + jnp.dot(x[t, at + j], table, preferred_element_type=f32)
        out[t] = value


def next_share(at, place, x, part, even, odd):
    _, rows, dim = part.shape
    return call(
        functools.partial(next_kernel, at), "embed_next", [SMEM] + [VMEM] * 4, VMEM, array(part.shape),
        cost=pl.CostEstimate(
            flops=16 * rows * dim * even.shape[1], bytes_accessed=0, transcendentals=0
        ),
    )(place, x, part, even, odd)


def whole_kernel(masks, place, xs, xt, pieces, part, table):
    genes = pieces.shape[1]
    for j, mask in enumerate(masks):
        start = pl.multiple_of((place[0] ^ mask) * genes, genes)
        table[pl.ds(start, genes), :] = pieces[j]
    for t, x in enumerate((xs, xt)):
        part[t] = jnp.dot(x[...], table[...], preferred_element_type=f32)


def whole_product(place, xs, xt, masks, pieces):
    rows, genes = xs.shape
    dim = pieces.shape[2]
    return call(
        functools.partial(whole_kernel, masks), "embed_whole", [SMEM] + [VMEM] * 3, VMEM,
        array((2, rows, dim)), [pltpu.VMEM((genes, dim), bf16)],
    )(place, xs, xt, pieces)


def fold(value):
    return jnp.sum(value.reshape(value.shape[0] // 8, 8, value.shape[1]), axis=0)


def add_to(sums, value):
    return value if sums is None else sums + value


def cross_kernel(flip, place, live, emb, q, turned, totals, out):
    t = (place[0] & 1) ^ flip
    _, rows, rank = q.shape
    block = rows // STEPS
    means = norms = rest = None
    for step in range(STEPS):
        at = slice(step * block, (step + 1) * block)
        value = emb[t, at, :]
        means = add_to(means, fold(value))
        squares = jnp.sum(value * value, axis=1, keepdims=True)
        norms = add_to(norms, fold(squares * q[t, at, :]))
    mean = (jnp.sum(means, axis=0, keepdims=True) / rows).astype(bf16).astype(f32)
    for step in range(STEPS):
        at = slice(step * block, (step + 1) * block)
        centred = (emb[t, at, :] - mean).astype(bf16)
        rest = add_to(rest, jnp.dot(turned[t, :, at], centred, preferred_element_type=f32))
    norm_sum = jnp.sum(norms, axis=0, keepdims=True) / rank
    lane = lax.broadcasted_iota(jnp.int32, (1, rank), 1)
    number = jnp.where(lane < rank // 2, live[0], live[1]).astype(f32)
    out[0:rank, :] = rest
    out[rank:, :] = jnp.concatenate([mean, totals[t], norm_sum, number, jnp.zeros((4, rank), f32)])


def cross(flip, place, live, emb, q, turned, totals):
    rank, dim = q.shape[2], emb.shape[2]
    return call(
        functools.partial(cross_kernel, flip), "cross", [SMEM] * 2 + [VMEM] * 4, VMEM,
        array((rank + 8, dim)),
        cost=pl.CostEstimate(flops=2 * rank * dim * q.shape[1], bytes_accessed=0, transcendentals=0),
    )(place, live, emb, *near(q, turned), totals)


def split_row(row):
    high = row.astype(bf16).astype(f32)
    middle = (row - high).astype(bf16).astype(f32)
    return [high, middle, row - high - middle]


def tail_rows(cards):
    return -(-(8 + 4 * cards) // 16) * 16


def make_tail(norm, number, cards):
    width = norm.shape[1]
    rows = split_row(norm) + split_row(number) + [jnp.zeros((2, width), f32)] + cards
    used = sum(r.shape[0] for r in rows)
    filler = tail_rows((used - 8) // 4) - used
    if filler:
        rows.append(jnp.zeros((filler, width), f32))
    return jnp.concatenate(rows)


def three(tail, start):
    return (tail[start : start + 1] + tail[start + 1 : start + 2]) + tail[start + 2 : start + 3]


def pack_pair_kernel(own, recv, out):
    rank = own.shape[0] - 8
    out[0:rank, :] = (own[0:rank, :] + recv[0:rank, :]).astype(bf16)
    cards = []
    for ref in (own, recv):
        cards += [ref[rank : rank + 1, :]] + split_row(ref[rank + 1 : rank + 2, :])
    norm = own[rank + 2 : rank + 3, :] + recv[rank + 2 : rank + 3, :]
    number = own[rank + 3 : rank + 4, :] + recv[rank + 3 : rank + 4, :]
    out[rank:, :] = make_tail(norm, number, cards).astype(bf16)


def pack_pair(own, recv):
    rank, dim = own.shape[0] - 8, own.shape[1]
    return call(
        pack_pair_kernel, "pack_pair", [VMEM] * 2, VMEM, array((rank + tail_rows(2), dim), bf16)
    )(own, recv)


def ordered_cards(tails, cards, flags):
    lists = [tail[8 : 8 + 4 * cards] for tail in tails]
    for flag in flags:
        lists = [
            jnp.concatenate([jnp.where(flag, a, b), jnp.where(flag, b, a)])
            for a, b in zip(lists[::2], lists[1::2])
        ]
    return lists[0]


def tree(values):
    while len(values) > 1:
        values = [a + b for a, b in zip(values[::2], values[1::2])]
    return values[0]


def merge_kernel(rank, cards, bits, place, *refs):
    payloads, out = refs[:-1], refs[-1]
    out[0:rank, :] = tree([p[0:rank, :].astype(f32) for p in payloads]).astype(bf16)
    tails = [p[rank:, :].astype(f32) for p in payloads]
    listed = ordered_cards(tails, cards, [(place[0] & bit) == 0 for bit in bits])
    norm, number = (tree([three(tail, i) for tail in tails]) for i in (0, 3))
    out[rank:, :] = make_tail(norm, number, [listed]).astype(bf16)


def merge(rank, cards, bits, place, *payloads):
    return call(
        functools.partial(merge_kernel, rank, cards, bits), "merge",
        [SMEM] + [VMEM] * len(payloads), VMEM,
        array((rank + tail_rows(len(payloads) * cards), payloads[0].shape[1]), bf16),
    )(place, *payloads)


def total_kernel(rank, cards, *refs):
    payloads, out = refs[:-1], refs[-1]

    def unpack(ref):
        tail = ref[rank:, :].astype(f32)
        heights, means, sums = [], [], jnp.zeros((1, tail.shape[1]), f32)
        for c in range(cards):
            at = 8 + 4 * c
            heights.append(tail[at + 1 : at + 4])
            means += [tail[at : at + 1]] * 3
            sums = sums + three(tail, at + 1)
        left, right = jnp.concatenate(heights), jnp.concatenate(means)
        joined = lax.dot_general(
            left.T.astype(bf16), right.astype(bf16), (((1,), (0,)), ((), ())),
            preferred_element_type=f32,
        )
        return ref[0:rank, :].astype(f32) + joined, three(tail, 0), sums, three(tail, 3)

    joined = [tree(list(values)) for values in zip(*[unpack(ref) for ref in payloads])]
    out[0:rank, :] = joined[0]
    out[rank:, :] = jnp.concatenate(joined[1:] + [jnp.zeros((5, out.shape[1]), f32)])


def total(rank, cards, *payloads):
    dim = payloads[0].shape[1]
    return call(
        functools.partial(total_kernel, rank, cards), "total", [VMEM] * len(payloads), VMEM,
        array((rank + 8, dim)),
    )(*payloads)


def live_rows(step, block, live):
    return lax.broadcasted_iota(jnp.int32, (block, 1), 0) + step * block < live


def store_sums(sums, copies):
    both = jnp.concatenate([jnp.sum(part, axis=0, keepdims=True) for part in sums])
    for i in range(copies.shape[0]):
        copies[i] = both


def kernel_half(cells, t, live, emb, q, weights, summed, put):
    _, rows, rank = q.shape
    block = rows // STEPS
    inverse = 1.0 / (D * (weights[...] * (cells / rank)))
    matrix = halves((-2.0 * inverse) * summed[0:rank, :].T)
    slope, offset = summed[rank + 1 : rank + 2, :] * inverse, summed[rank : rank + 1, :] * inverse
    numbers = summed[rank + 2 : rank + 3, :]
    level = cells / jnp.where(t == 0, numbers[:, 0:1], numbers[:, rank // 2 : rank // 2 + 1])
    sums = None
    for step in range(STEPS):
        at = slice(step * block, (step + 1) * block)
        value = emb[t, at, :]
        norms = jnp.sum(value * value, axis=1, keepdims=True)
        grad = norms * slope + offset + dot3(halves(value), matrix, 1, 0)
        kernel = (q[t, at, :] / rank) * jnp.exp(-step_size * grad)
        put(at, kernel)
        scale = jnp.where(live_rows(step, block, live[t]), level, 0.0)
        scale = scale / jnp.sum(kernel, axis=1, keepdims=True)
        sums = add_to(sums, fold(scale * kernel))
    return sums


def other_kernel(cells, place, live, emb, q, weights, mine, k, sums):
    def put(at, kernel):
        k[at, :] = kernel

    t = 1 - (place[0] & 1)
    sums[...] = kernel_half(cells, t, live, emb, q, weights, mine, put)


def own_kernel(cells, place, live, emb, q, weights, mine, other, k_other, sums_other, k, copies, consts):
    core = place[0] & 1
    rank = q.shape[2]

    def put(at, kernel):
        k[core, at, :] = kernel
        k[1 - core, at, :] = k_other[at, :]

    sums_own = kernel_half(cells, core, live, emb, q, weights, other, put)
    sums_out = sums_other[...]
    first = core == 0
    store_sums([jnp.where(first, sums_own, sums_out), jnp.where(first, sums_out, sums_own)], copies)

    a, b = mine[...], other[...]
    col_mass = weights[...] * (cells / rank)
    norm_a, total_a = a[rank : rank + 1], a[rank + 1 : rank + 2]
    norm_b, total_b = b[rank : rank + 1], b[rank + 1 : rank + 2]
    products = jnp.sum((a[0:rank] * b[0:rank]).T, axis=0, keepdims=True)
    mixed_a, mixed_b = norm_a * total_b, total_a * norm_b
    mixed = jnp.where(first, mixed_a, mixed_b) + jnp.where(first, mixed_b, mixed_a)
    cost = (mixed - 2.0 * products) / D
    consts[0:1, :] = col_mass * jnp.exp(step_size * cost / (col_mass * col_mass))
    numbers = a[rank + 2 : rank + 3]
    for t in range(2):
        at = t * (rank // 2)
        consts[1 + t : 2 + t, :] = jnp.broadcast_to(cells / numbers[:, at : at + 1], (1, rank))


def cube_root(x):
    y = jnp.exp(jnp.log(x) * (1.0 / 3.0))
    refined = y - (y - x / (y * y)) * (1.0 / 3.0)
    return jnp.where((x > 0.0) & (x < jnp.inf), refined, y)


def duals_of(parts, consts):
    sums = jnp.sum(parts[...], axis=0)
    sum_s, sum_t = sums[0:1, :], sums[1:2, :]
    mass = cube_root(consts[0:1, :] * sum_s * sum_t)
    return mass, mass / sum_s, mass / sum_t


def sweep_kernel(last, live, k, parts, consts, *refs):
    copies = refs[-1]
    block = k.shape[1] // STEPS

    _, dual_s, dual_t = duals_of(parts, consts)
    sums = [None, None]
    for step in range(STEPS):
        at = slice(step * block, (step + 1) * block)
        for t, dual in enumerate((dual_s, dual_t)):
            kernel = k[t, at, :]
            weighted = jnp.sum(kernel * dual, axis=1, keepdims=True)
            level = jnp.where(live_rows(step, block, live[t]), consts[1 + t : 2 + t, 0:1], 0.0)
            scaled = (level / weighted) * kernel
            if last:
                refs[0][t, at, :] = scaled
            sums[t] = add_to(sums[t], fold(scaled))
    store_sums(sums, copies)


def finish_kernel(cells, scaled, parts, consts, fs, ft, weights, held, sems):
    _, rows, rank = scaled.shape
    block = rows // STEPS
    mass, dual_s, dual_t = duals_of(parts, consts)
    weights[...] = mass * (rank / cells)
    copies = []
    for step in range(STEPS):
        at = slice(step * block, (step + 1) * block)
        for t, (dual, out) in enumerate(((dual_s, fs), (dual_t, ft))):
            held[t, at, :] = rank * (scaled[t, at, :] * dual)
            copy = pltpu.make_async_copy(held.at[t, at], out.at[at], sems.at[t, step])
            copy.start()
            copies.append(copy)
    for copy in copies:
        copy.wait()


def kernels(cells, count, place, live, emb, q, weights, mine, other):
    _, rows, rank = q.shape
    dim = emb.shape[2]
    k_other, sums_other = call(
        functools.partial(other_kernel, cells), "kernel_other", [SMEM, SMEM] + [VMEM] * 4, [VMEM] * 2,
        [array((rows, rank)), array((8, rank))],
        cost=pl.CostEstimate(flops=6 * rows * rank * dim, bytes_accessed=0, transcendentals=rows * rank),
    )(place, live, emb, *near(q), weights, mine)
    return call(
        functools.partial(own_kernel, cells), "kernel_own", [SMEM, SMEM] + [VMEM] * 7, [VMEM] * 3,
        [array((2, rows, rank)), array((count, 2, rank)), array((8, rank))],
        cost=pl.CostEstimate(flops=6 * rows * rank * dim, bytes_accessed=0, transcendentals=rows * rank),
    )(place, live, emb, *near(q), weights, mine, other, k_other, sums_other)


def sweep(count, last, live, k, parts, consts):
    _, rows, rank = k.shape
    scaled = [array((2, rows, rank))] if last else []
    return call(
        functools.partial(sweep_kernel, last), "sweep", [SMEM] + [VMEM] * 3,
        [VMEM] * (len(scaled) + 1), scaled + [array((count, 2, rank))],
    )(live, k, parts, consts)


def finish(cells, scaled, parts, consts):
    _, rows, rank = scaled.shape
    return call(
        functools.partial(finish_kernel, cells), "finish", [VMEM] * 3, [HBM, HBM, VMEM],
        [array((rows, rank))] * 2 + [array((1, rank))],
        [pltpu.VMEM((2, rows, rank), f32), pltpu.SemaphoreType.DMA((2, STEPS))],
    )(scaled, parts, consts)


def on_device(
    source_expr, target_expr, loadings, source_prev, target_prev, weights_prev, live_counts
):
    count = lax.axis_size("cell")
    place = lax.axis_index("cell").astype(jnp.int32)[None]
    live = live_counts[:, 0]
    rows, rank = source_prev.shape
    cells = rows * count
    bits = [1 << b for b in range(count.bit_length() - 1)]
    opposite = bits[-1] | bits[-2]
    exchange = functools.partial(lax.all_to_all, axis_name="cell", split_axis=0, concat_axis=0)

    q, own_table, turned, totals = fetch(source_prev, target_prev, loadings)
    stack = stack_pieces([own_table, swap(loadings, count, opposite)], [totals])
    masks = [0, opposite]
    if count == 16 and loadings.shape[0] % 64 == 0:
        quad = [2, 4, 6]
        arrived = [swap(stack, count, m) for m in quad]
        later = [m ^ q for q in quad for m in masks]
        emb, x = first_share(
            place, source_expr, target_expr, masks, later, stack, swap(stack, count, 1)
        )
        arrived = [gate(piece, emb) for piece in arrived]
        for i, piece in enumerate(arrived):
            emb = next_share(2 * i, place, x, emb, piece, swap(piece, count, 1))
    else:
        for bit in reversed(bits[:-1]):
            stack = jnp.concatenate([stack, swap(stack, count, bit)])
            masks = masks + [m ^ bit for m in masks]
        emb = whole_product(place, source_expr, target_expr, masks, stack)
    send = cross(1, place, live, emb, q, turned, totals)
    own = cross(0, place, live, emb, q, turned, totals)

    payload = pack_pair(own, swap(send, count, 1))
    cards = 2
    inner = bits[1:-1]
    while inner:
        used, inner = inner[:2], inner[2:]
        steps = [used[0], used[1], used[0] | used[1]] if len(used) == 2 else used
        others = [swap(payload, count, m) for m in steps]
        payload = merge(rank, cards, used, place, payload, *others)
        cards = cards * (1 + len(others))
    mine = total(rank, cards, payload, swap(payload, count, opposite))
    other = swap(mine, count, 1)

    k, copies, consts = kernels(
        cells, count, place, live, emb, q, weights_prev[None], mine, other
    )
    scaled = []
    for step_index in range(1, ITERS):
        last = step_index == ITERS - 1
        *scaled, copies = sweep(count, last, live, k, exchange(copies), consts)
    out_s, out_t, weights = finish(cells, *scaled, exchange(copies), consts)
    return out_s, out_t, weights[0]


def solution(mesh):
    in_specs = (
        P(("grp", "cell"), None),
        P(("grp", "cell"), None),
        P("cell", None),
        P(("grp", "cell"), None),
        P(("grp", "cell"), None),
        P("grp"),
        P(None, ("grp", "cell")),
    )
    out_specs = (P(("grp", "cell"), None), P(("grp", "cell"), None), P("grp"))
    return jax.shard_map(
        on_device, mesh=mesh, in_specs=in_specs, out_specs=out_specs, check_vma=False
    )
```

time: 85.1 us -> 81.3 us (0.955)
  waiting for transfers between devices: 16.7 us -> 14.2 us
    ppermute x14, waiting for transfers between devices: 16.7 us -> 14.2 us  [swap(): return lax.ppermute(value, 'cell', [(i, i ^ mask) for i in range(count)])]
    pallas_call x6 -> x8, Pallas kernels: 12.3 us -> 11.8 us  [the longest x2 2.59 us: sweep(): call(functools.partial(sweep_kernel, last), 'sweep', [SMEM] + [VMEM] * 3,...]
  transfers between devices with their start and end apart: 14 -> 14, of which waited for: 8 -> 7; matrix products, arithmetic and copies ran while one was open for 0% -> 0% of each run, Pallas kernels for 8% -> 12%
where the time goes in v5:
time: 81.3 us; the launch traced here: 81 us
  blocking collectives  31.1 us (38%)
  Pallas kernels  18 us (22%)
  starting transfers between devices  16.9 us (21%)
  waiting for transfers between devices  14.2 us (17%)
  between operations  0.83 us (1%)
    all_to_all x2, blocking collectives, on_device(): *scaled, copies = sweep(count, last, live, k, exchange(copies), consts)  21.9 us
    ppermute x14, starting transfers between devices, swap(): return lax.ppermute(value, 'cell', [(i, i ^ mask) for i in range(count)])  16.9 us
    ppermute x14, waiting for transfers between devices, swap(): return lax.ppermute(value, 'cell', [(i, i ^ mask) for i in range(count)])  14.2 us
    all_to_all x1, blocking collectives, on_device(): out_s, out_t, weights = finish(cells, *scaled, exchange(copies), consts)  9.2 us
    pallas_call x1, Pallas kernels, first_share(): call(functools.partial(first_kernel, masks, later_masks), 'embed_first',...  3.64 us
    pallas_call x2, Pallas kernels, sweep(): call(functools.partial(sweep_kernel, last), 'sweep', [SMEM] + [VMEM] * 3,...  2.59 us
    pallas_call x3, Pallas kernels, next_share(): call(functools.partial(next_kernel, at), 'embed_next', [SMEM] + [VMEM] *...  2.13 us
    pallas_call x1, Pallas kernels, finish(): call(functools.partial(finish_kernel, cells), 'finish', [VMEM] * 3, [HBM,...  2.01 us
  transfers between devices with their start and end apart: 14, of which 7 were waited for; matrix products, arithmetic and copies ran while one was open for 0% of the time, Pallas kernels for 12%

profile of v5, /device:TPU:0, one launch (start us, length us, event | category | flops | bytes accessed | tf_op | source)
XLA Modules:
  0.0 81.0 jit_solution(9689791678585030726)
XLA Ops:
  0.6 5.1 %collective-permute-start = (bf16[128,256]{1,0:T(8,128)(2,1)}, bf16[128,256]{1,0:T(8,128)(2,1)S(1)}, u32[]{:S(2)}, u32[]{:S(2)}) collective-permute-start(bf16[128,256]{1,0:T(8,128)(2,1)} %table.1), channel_id=1, source_target_pairs={{0,12},{1,13},{2,14},{3,15},{4,8},{5,9},{6,10},{7,11},{8,4},{9,5},... | collective-permute-start | bytes 196616 | tf_op jit(solution)/shard_map/ppermute | solution.py:21
  5.7 1.8 %fetch.1 = (f32[2,1024,256]{2,1,0:T(8,128)S(1)}, bf16[128,256]{1,0:T(8,128)(2,1)S(1)}, bf16[2,256,1024]{2,1,0:T(8,128)(2,1)S(1)}, f32[2,1,256]{2,1,0:T(1,128)S(1)}) custom-call(f32[1024,256]{1,0:T(8,128)} %qs.1, f32[1024,256]{1,0:T(8,128)} %qt.1, bf16[128,256]{1,0:T(8,128)(2,1)} %table.1), custom_call_target="tpu_custom_call" | custom-call | bytes 2097152 | tf_op jit(solution)/shard_map/fetch/pallas_call | solution.py:86
  7.5 0.7 collective-permute-done.refs_1_
  8.3 0.1 collective-permute-start.1
  8.3 1.8 %collective-permute-start.2 = (bf16[2,128,256]{2,1,0:T(8,128)(2,1)S(1)}, bf16[2,128,256]{2,1,0:T(8,128)(2,1)S(1)}, u32[]{:S(2)}, u32[]{:S(2)}) collective-permute-start(bf16[2,128,256]{2,1,0:T(8,128)(2,1)S(1)} %stack.1.even), channel_id=1, source_target_pairs={{0,2},{1,3},{2,0},{3,1},{4,6},{5,7},{6,4},{7,5},{8,10},{9,11},{10,... | collective-permute-start | bytes 393224 | tf_op jit(solution)/shard_map/ppermute | solution.py:21
  10.2 0.8 collective-permute-start.6
  10.9 1.0 %collective-permute-start.4 = (bf16[2,128,256]{2,1,0:T(8,128)(2,1)S(1)}, bf16[2,128,256]{2,1,0:T(8,128)(2,1)S(1)}, u32[]{:S(2)}, u32[]{:S(2)}) collective-permute-start(bf16[2,128,256]{2,1,0:T(8,128)(2,1)S(1)} %stack.1.even), channel_id=1, source_target_pairs={{0,4},{1,5},{2,6},{3,7},{4,0},{5,1},{6,2},{7,3},{8,12},{9,13},{10,... | collective-permute-start | bytes 393224 | tf_op jit(solution)/shard_map/ppermute | solution.py:21
  11.9 0.0 collective-permute-done.1.odd
  11.9 3.6 %embed_first.1 = (f32[2,1024,256]{2,1,0:T(8,128)S(1)}, bf16[2,6,1024,256]{3,2,1,0:T(8,128)(2,1)S(1)}) custom-call(s32[1]{0:T(128)} %bitcast.1.place, bf16[1024,2048]{1,0:T(8,128)(2,1)} %xs.1, bf16[1024,2048]{1,0:T(8,128)(2,1)} %xt.1, bf16[2,128,256]{2,1,0:T(8,128)(2,1)S(1)} %stack.1.even, bf16[2,128,256]{2,1,0:T(8,128)(2,1)S(1)} %collective-permute-done.1.odd), custom_call_target="tpu_custom_call" | custom-call | flops 1073741824 | bytes 8388608 | tf_op jit(solution)/shard_map/embed_first/pallas_call | solution.py:150
  15.6 1.1 %collective-permute-done.2.value = bf16[2,128,256]{2,1,0:T(8,128)(2,1)S(1)} collective-permute-done((bf16[2,128,256]{2,1,0:T(8,128)(2,1)S(1)}, bf16[2,128,256]{2,1,0:T(8,128)(2,1)S(1)}, u32[]{:S(2)}, u32[]{:S(2)}) %collective-permute-start.2) | collective-permute-done | bytes 131104 | tf_op jit(solution)/shard_map/ppermute | solution.py:21
  16.7 0.1 collective-permute-start.3
  16.8 1.5 %collective-permute-done.4.value = bf16[2,128,256]{2,1,0:T(8,128)(2,1)S(1)} collective-permute-done((bf16[2,128,256]{2,1,0:T(8,128)(2,1)S(1)}, bf16[2,128,256]{2,1,0:T(8,128)(2,1)S(1)}, u32[]{:S(2)}, u32[]{:S(2)}) %collective-permute-start.4) | collective-permute-done | bytes 131104 | tf_op jit(solution)/shard_map/ppermute | solution.py:21
  18.3 0.1 collective-permute-start.5
  18.4 0.0 collective-permute-done.6.value
  18.4 0.5 collective-permute-start.7
  19.0 0.0 collective-permute-done.3.odd
  19.0 0.7 embed_next.3.part
  19.7 0.0 collective-permute-done.5.odd
  19.7 0.7 embed_next.4.part
  20.4 0.0 copy-start
  20.5 0.0 collective-permute-done.7.odd
  20.5 0.7 embed_next.5.emb
  21.2 1.0 %cross.3 = f32[264,256]{1,0:T(8,128)S(1)} custom-call(s32[1]{0:T(128)} %bitcast.1.place, s32[2]{0:T(128)S(1)} %bitcast.4, f32[2,1024,256]{2,1,0:T(8,128)S(1)} %embed_next.5.emb, f32[2,1024,256]{2,1,0:T(8,128)S(1)} %get-tuple-element.23.q, bf16[2,256,1024]{2,1,0:T(8,128)(2,1)S(1)} %get-tuple-element.24.turned, f32[2,1,256]{2,1,0:T(1,128)S(1)} %get-tuple-element.20.refs_2_.totals), custom_call_target="tpu_custom_call" | custom-call | flops 134217728 | tf_op jit(solution)/shard_map/cross/pallas_call | solution.py:245
  22.2 0.0 copy-start.1
  22.2 0.2 collective-permute-start.8
  22.4 1.0 %cross.2.own = f32[264,256]{1,0:T(8,128)S(1)} custom-call(s32[1]{0:T(128)} %bitcast.1.place, s32[2]{0:T(128)S(1)} %bitcast.5, f32[2,1024,256]{2,1,0:T(8,128)S(1)} %embed_next.5.emb, f32[2,1024,256]{2,1,0:T(8,128)S(1)} %get-tuple-element.23.q, bf16[2,256,1024]{2,1,0:T(8,128)(2,1)S(1)} %get-tuple-element.24.turned, ...), custom_call_target="tpu_custom_call" | custom-call | flops 134217728 | tf_op jit(solution)/shard_map/cross/pallas_call | solution.py:245
  23.4 0.4 collective-permute-done.8.recv
  23.9 2.1 %collective-permute-start.11 = (bf16[272,256]{1,0:T(8,128)(2,1)S(1)}, bf16[272,256]{1,0:T(8,128)(2,1)S(1)}, u32[]{:S(2)}, u32[]{:S(2)}) collective-permute-start(bf16[272,256]{1,0:T(8,128)(2,1)S(1)} %pack_pair.1.refs_0_), channel_id=1, source_target_pairs={{0,6},{1,7},{2,4},{3,5},{4,2},{5,3},{6,0},{7,1},{8,14},{9,15},{10,... | collective-permute-start | bytes 417800 | tf_op jit(solution)/shard_map/ppermute | solution.py:21
  25.9 1.2 %collective-permute-start.10 = (bf16[272,256]{1,0:T(8,128)(2,1)S(1)}, bf16[272,256]{1,0:T(8,128)(2,1)S(1)}, u32[]{:S(2)}, u32[]{:S(2)}) collective-permute-start(bf16[272,256]{1,0:T(8,128)(2,1)S(1)} %pack_pair.1.refs_0_), channel_id=1, source_target_pairs={{0,4},{1,5},{2,6},{3,7},{4,0},{5,1},{6,2},{7,3},{8,12},{9,13},{10,... | collective-permute-start | bytes 417800 | tf_op jit(solution)/shard_map/ppermute | solution.py:21
  27.1 0.3 collective-permute-start.9
  27.4 3.9 %collective-permute-done.11.refs_3_ = bf16[272,256]{1,0:T(8,128)(2,1)S(1)} collective-permute-done((bf16[272,256]{1,0:T(8,128)(2,1)S(1)}, bf16[272,256]{1,0:T(8,128)(2,1)S(1)}, u32[]{:S(2)}, u32[]{:S(2)}) %collective-permute-start.11) | collective-permute-done | bytes 139296 | tf_op jit(solution)/shard_map/ppermute | solution.py:21
  31.3 2.5 %collective-permute-done.10.refs_2_ = bf16[272,256]{1,0:T(8,128)(2,1)S(1)} collective-permute-done((bf16[272,256]{1,0:T(8,128)(2,1)S(1)}, bf16[272,256]{1,0:T(8,128)(2,1)S(1)}, u32[]{:S(2)}, u32[]{:S(2)}) %collective-permute-start.10) | collective-permute-done | bytes 139296 | tf_op jit(solution)/shard_map/ppermute | solution.py:21
  33.9 0.0 collective-permute-done.9.refs_1_
  33.9 0.1 merge.1.refs_0_
  33.9 3.6 %collective-permute-start.12 = (bf16[304,256]{1,0:T(8,128)(2,1)S(1)}, bf16[304,256]{1,0:T(8,128)(2,1)S(1)}, u32[]{:S(2)}, u32[]{:S(2)}) collective-permute-start(bf16[304,256]{1,0:T(8,128)(2,1)S(1)} %merge.1.refs_0_), channel_id=1, source_target_pairs={{0,12},{1,13},{2,14},{3,15},{4,8},{5,9},{6,10},{7,11},{8,4},{9,5},... | collective-permute-start | bytes 466952 | tf_op jit(solution)/shard_map/ppermute | solution.py:21
  37.5 3.9 %collective-permute-done.12.refs_1_ = bf16[304,256]{1,0:T(8,128)(2,1)S(1)} collective-permute-done((bf16[304,256]{1,0:T(8,128)(2,1)S(1)}, bf16[304,256]{1,0:T(8,128)(2,1)S(1)}, u32[]{:S(2)}, u32[]{:S(2)}) %collective-permute-start.12) | collective-permute-done | bytes 155680 | tf_op jit(solution)/shard_map/ppermute | solution.py:21
  41.5 0.3 total.1.mine
  41.7 0.1 collective-permute-start.13
  41.8 0.0 copy-done.1
  41.8 1.6 %kernel_other.1 = (f32[1024,256]{1,0:T(8,128)S(1)}, f32[8,256]{1,0:T(8,128)S(1)}) custom-call(s32[1]{0:T(128)} %bitcast.1.place, s32[2]{0:T(128)S(1)} %bitcast.6, f32[2,1024,256]{2,1,0:T(8,128)S(1)} %embed_next.5.emb, f32[2,1024,256]{2,1,0:T(8,128)S(1)} %get-tuple-element.23.q, f32[1,256]{1,0:T(1,128)S(1)} %bitcast.10, f32[264,256]{1,0:T(8,128)S(1)} %total.1.mine), custom_call_target="tpu_custom_call" | custom-call | flops 402653184 | tf_op jit(solution)/shard_map/kernel_other/pallas_call | solution.py:478
  43.5 0.0 collective-permute-done.13.other
  43.5 1.8 %kernel_own.1 = (f32[2,1024,256]{2,1,0:T(8,128)S(1)}, f32[16,2,256]{2,1,0:T(2,128)S(1)}, f32[8,256]{1,0:T(8,128)S(1)}) custom-call(s32[1]{0:T(128)} %bitcast.1.place, s32[2]{0:T(128)S(1)} %bitcast.7, f32[2,1024,256]{2,1,0:T(8,128)S(1)} %embed_next.5.emb, f32[2,1024,256]{2,1,0:T(8,128)S(1)} %get-tuple-element.23.q, f32[1,256]{1,0:T(1,128)S(1)} %bitcast.11, ...), custom_call_target="tpu_custom_call" | custom-call | flops 402653184 | tf_op jit(solution)/shard_map/kernel_own/pallas_call | solution.py:483
  45.3 12.7 %all_to_all.15.parts = f32[16,2,256]{2,1,0:T(2,128)S(1)} all-to-all(f32[16,2,256]{2,1,0:T(2,128)S(1)} %get-tuple-element.28), channel_id=1, replica_groups=mesh['grp'=2,'cell'=16] {'cell'}, dimensions={0} | all-to-all | bytes 65536 | tf_op jit(solution)/shard_map/all_to_all | solution.py:559
  58.0 1.3 %sweep.2 = f32[16,2,256]{2,1,0:T(2,128)S(1)} custom-call(s32[2]{0:T(128)S(1)} %bitcast.8, f32[2,1024,256]{2,1,0:T(8,128)S(1)} %get-tuple-element.27.k, f32[16,2,256]{2,1,0:T(2,128)S(1)} %all_to_all.15.parts, f32[8,256]{1,0:T(8,128)S(1)} %get-tuple-element.29.consts), custom_call_target="tpu_custom_call" | custom-call | tf_op jit(solution)/shard_map/sweep/pallas_call | solution.py:493
  59.3 9.2 %all_to_all.16.parts = f32[16,2,256]{2,1,0:T(2,128)S(1)} all-to-all(f32[16,2,256]{2,1,0:T(2,128)S(1)} %sweep.2), channel_id=1, replica_groups=mesh['grp'=2,'cell'=16] {'cell'}, dimensions={0} | all-to-all | bytes 65536 | tf_op jit(solution)/shard_map/all_to_all | solution.py:559
  68.5 1.3 %sweep.3 = (f32[2,1024,256]{2,1,0:T(8,128)S(1)}, f32[16,2,256]{2,1,0:T(2,128)S(1)}) custom-call(s32[2]{0:T(128)S(1)} %bitcast.9, f32[2,1024,256]{2,1,0:T(8,128)S(1)} %get-tuple-element.27.k, f32[16,2,256]{2,1,0:T(2,128)S(1)} %all_to_all.16.parts, f32[8,256]{1,0:T(8,128)S(1)} %get-tuple-element.29.consts), custom_call_target="tpu_custom_call" | custom-call | tf_op jit(solution)/shard_map/sweep/pallas_call | solution.py:493
  69.8 9.2 %all_to_all.17.parts = f32[16,2,256]{2,1,0:T(2,128)S(1)} all-to-all(f32[16,2,256]{2,1,0:T(2,128)S(1)} %get-tuple-element.31), channel_id=1, replica_groups=mesh['grp'=2,'cell'=16] {'cell'}, dimensions={0} | all-to-all | bytes 65536 | tf_op jit(solution)/shard_map/all_to_all | solution.py:560
  79.0 2.0 %finish.1 = (f32[1024,256]{1,0:T(8,128)}, f32[1024,256]{1,0:T(8,128)}, f32[1,256]{1,0:T(1,128)}) custom-call(f32[2,1024,256]{2,1,0:T(8,128)S(1)} %get-tuple-element.30.scaled, f32[16,2,256]{2,1,0:T(2,128)S(1)} %all_to_all.17.parts, f32[8,256]{1,0:T(8,128)S(1)} %get-tuple-element.29.consts), custom_call_target="tpu_custom_call" | custom-call | tf_op jit(solution)/shard_map/finish/pallas_call | solution.py:501
  (6 shorter events, 0.1 us)
Async XLA Ops:
  0.6 7.6 %collective-permute-start = (bf16[128,256]{1,0:T(8,128)(2,1)}, bf16[128,256]{1,0:T(8,128)(2,1)S(1)}, u32[]{:S(2)}, u32[]{:S(2)}) collective-permute-start(bf16[128,256]{1,0:T(8,128)(2,1)} %table.1), channel_id=1, source_target_pairs={{0,12},{1,13},{2,14},{3,15},{4,8},{5,9},{6,10},{7,11},{8,4},{9,5},... | collective-permute-start | bytes 196616 | tf_op jit(solution)/shard_map/ppermute | solution.py:21
  8.3 3.6 %collective-permute-start.1 = (bf16[2,128,256]{2,1,0:T(8,128)(2,1)S(1)}, bf16[2,128,256]{2,1,0:T(8,128)(2,1)S(1)}, u32[]{:S(2)}, u32[]{:S(2)}) collective-permute-start(bf16[2,128,256]{2,1,0:T(8,128)(2,1)S(1)} %stack.1.even), channel_id=1, source_target_pairs={{0,1},{1,0},{2,3},{3,2},{4,5},{5,4},{6,7},{7,6},{8,9},{9,8},{10,11... | collective-permute-start | bytes 393224 | tf_op jit(solution)/shard_map/ppermute | solution.py:21
  8.3 8.3 %collective-permute-start.2 = (bf16[2,128,256]{2,1,0:T(8,128)(2,1)S(1)}, bf16[2,128,256]{2,1,0:T(8,128)(2,1)S(1)}, u32[]{:S(2)}, u32[]{:S(2)}) collective-permute-start(bf16[2,128,256]{2,1,0:T(8,128)(2,1)S(1)} %stack.1.even), channel_id=1, source_target_pairs={{0,2},{1,3},{2,0},{3,1},{4,6},{5,7},{6,4},{7,5},{8,10},{9,11},{10,... | collective-permute-start | bytes 393224 | tf_op jit(solution)/shard_map/ppermute | solution.py:21
  10.2 8.2 %collective-permute-start.6 = (bf16[2,128,256]{2,1,0:T(8,128)(2,1)S(1)}, bf16[2,128,256]{2,1,0:T(8,128)(2,1)S(1)}, u32[]{:S(2)}, u32[]{:S(2)}) collective-permute-start(bf16[2,128,256]{2,1,0:T(8,128)(2,1)S(1)} %stack.1.even), channel_id=1, source_target_pairs={{0,6},{1,7},{2,4},{3,5},{4,2},{5,3},{6,0},{7,1},{8,14},{9,15},{10,... | collective-permute-start | bytes 393224 | tf_op jit(solution)/shard_map/ppermute | solution.py:21
  10.9 7.4 %collective-permute-start.4 = (bf16[2,128,256]{2,1,0:T(8,128)(2,1)S(1)}, bf16[2,128,256]{2,1,0:T(8,128)(2,1)S(1)}, u32[]{:S(2)}, u32[]{:S(2)}) collective-permute-start(bf16[2,128,256]{2,1,0:T(8,128)(2,1)S(1)} %stack.1.even), channel_id=1, source_target_pairs={{0,4},{1,5},{2,6},{3,7},{4,0},{5,1},{6,2},{7,3},{8,12},{9,13},{10,... | collective-permute-start | bytes 393224 | tf_op jit(solution)/shard_map/ppermute | solution.py:21
  16.7 2.3 %collective-permute-start.3 = (bf16[2,128,256]{2,1,0:T(8,128)(2,1)S(1)}, bf16[2,128,256]{2,1,0:T(8,128)(2,1)S(1)}, u32[]{:S(2)}, u32[]{:S(2)}) collective-permute-start(bf16[2,128,256]{2,1,0:T(8,128)(2,1)S(1)} %gate.3.even), channel_id=1, source_target_pairs={{0,1},{1,0},{2,3},{3,2},{4,5},{5,4},{6,7},{7,6},{8,9},{9,8},{10,11... | collective-permute-start | bytes 393224 | tf_op jit(solution)/shard_map/ppermute | solution.py:21
  18.3 1.4 %collective-permute-start.5 = (bf16[2,128,256]{2,1,0:T(8,128)(2,1)S(1)}, bf16[2,128,256]{2,1,0:T(8,128)(2,1)S(1)}, u32[]{:S(2)}, u32[]{:S(2)}) collective-permute-start(bf16[2,128,256]{2,1,0:T(8,128)(2,1)S(1)} %gate.4.even), channel_id=1, source_target_pairs={{0,1},{1,0},{2,3},{3,2},{4,5},{5,4},{6,7},{7,6},{8,9},{9,8},{10,11... | collective-permute-start | bytes 393224 | tf_op jit(solution)/shard_map/ppermute | solution.py:21
  18.4 2.0 %collective-permute-start.7 = (bf16[2,128,256]{2,1,0:T(8,128)(2,1)S(1)}, bf16[2,128,256]{2,1,0:T(8,128)(2,1)S(1)}, u32[]{:S(2)}, u32[]{:S(2)}) collective-permute-start(bf16[2,128,256]{2,1,0:T(8,128)(2,1)S(1)} %gate.5.even), channel_id=1, source_target_pairs={{0,1},{1,0},{2,3},{3,2},{4,5},{5,4},{6,7},{7,6},{8,9},{9,8},{10,11... | collective-permute-start | bytes 393224 | tf_op jit(solution)/shard_map/ppermute | solution.py:21
  20.4 0.7 copy-start
  22.2 19.6 %copy-start.1 = (f32[256]{0:T(256)S(1)}, f32[256]{0:T(256)}, u32[]{:S(2)}) copy-start(f32[256]{0:T(256)} %param.12) | copy-start | bytes 3076
  22.2 1.6 %collective-permute-start.8 = (f32[264,256]{1,0:T(8,128)S(1)}, f32[264,256]{1,0:T(8,128)S(1)}, u32[]{:S(2)}, u32[]{:S(2)}) collective-permute-start(f32[264,256]{1,0:T(8,128)S(1)} %cross.3), channel_id=1, source_target_pairs={{0,1},{1,0},{2,3},{3,2},{4,5},{5,4},{6,7},{7,6},{8,9},{9,8},{10,11... | collective-permute-start | bytes 811016 | tf_op jit(solution)/shard_map/ppermute | solution.py:21
  23.9 7.5 %collective-permute-start.11 = (bf16[272,256]{1,0:T(8,128)(2,1)S(1)}, bf16[272,256]{1,0:T(8,128)(2,1)S(1)}, u32[]{:S(2)}, u32[]{:S(2)}) collective-permute-start(bf16[272,256]{1,0:T(8,128)(2,1)S(1)} %pack_pair.1.refs_0_), channel_id=1, source_target_pairs={{0,6},{1,7},{2,4},{3,5},{4,2},{5,3},{6,0},{7,1},{8,14},{9,15},{10,... | collective-permute-start | bytes 417800 | tf_op jit(solution)/shard_map/ppermute | solution.py:21
  25.9 7.9 %collective-permute-start.10 = (bf16[272,256]{1,0:T(8,128)(2,1)S(1)}, bf16[272,256]{1,0:T(8,128)(2,1)S(1)}, u32[]{:S(2)}, u32[]{:S(2)}) collective-permute-start(bf16[272,256]{1,0:T(8,128)(2,1)S(1)} %pack_pair.1.refs_0_), channel_id=1, source_target_pairs={{0,4},{1,5},{2,6},{3,7},{4,0},{5,1},{6,2},{7,3},{8,12},{9,13},{10,... | collective-permute-start | bytes 417800 | tf_op jit(solution)/shard_map/ppermute | solution.py:21
  27.1 6.7 %collective-permute-start.9 = (bf16[272,256]{1,0:T(8,128)(2,1)S(1)}, bf16[272,256]{1,0:T(8,128)(2,1)S(1)}, u32[]{:S(2)}, u32[]{:S(2)}) collective-permute-start(bf16[272,256]{1,0:T(8,128)(2,1)S(1)} %pack_pair.1.refs_0_), channel_id=1, source_target_pairs={{0,2},{1,3},{2,0},{3,1},{4,6},{5,7},{6,4},{7,5},{8,10},{9,11},{10,... | collective-permute-start | bytes 417800 | tf_op jit(solution)/shard_map/ppermute | solution.py:21
  33.9 7.5 %collective-permute-start.12 = (bf16[304,256]{1,0:T(8,128)(2,1)S(1)}, bf16[304,256]{1,0:T(8,128)(2,1)S(1)}, u32[]{:S(2)}, u32[]{:S(2)}) collective-permute-start(bf16[304,256]{1,0:T(8,128)(2,1)S(1)} %merge.1.refs_0_), channel_id=1, source_target_pairs={{0,12},{1,13},{2,14},{3,15},{4,8},{5,9},{6,10},{7,11},{8,4},{9,5},... | collective-permute-start | bytes 466952 | tf_op jit(solution)/shard_map/ppermute | solution.py:21
  41.7 1.7 %collective-permute-start.13 = (f32[264,256]{1,0:T(8,128)S(1)}, f32[264,256]{1,0:T(8,128)S(1)}, u32[]{:S(2)}, u32[]{:S(2)}) collective-permute-start(f32[264,256]{1,0:T(8,128)S(1)} %total.1.mine), channel_id=1, source_target_pairs={{0,1},{1,0},{2,3},{3,2},{4,5},{5,4},{6,7},{7,6},{8,9},{9,8},{10,11... | collective-permute-start | bytes 811016 | tf_op jit(solution)/shard_map/ppermute | solution.py:21

commit v6 on v5

--- a/solution.py
+++ b/solution.py
@@ -217,7 +217,7 @@
     return value if sums is None else sums + value
 
 
-def cross_kernel(flip, place, live, emb, q, turned, totals, out):
+def cross_kernel(flip, place, live, emb, q, turned, totals, out, *masks):
     t = (place[0] & 1) ^ flip
     _, rows, rank = q.shape
     block = rows // STEPS
@@ -238,13 +238,18 @@
     number = jnp.where(lane < rank // 2, live[0], live[1]).astype(f32)
     out[0:rank, :] = rest
     out[rank:, :] = jnp.concatenate([mean, totals[t], norm_sum, number, jnp.zeros((4, rank), f32)])
+    for mask in masks:
+        for i in range(2):
+            mask[i] = (lax.broadcasted_iota(jnp.int32, (rows, 1), 0) < live[i]).astype(f32)
 
 
 def cross(flip, place, live, emb, q, turned, totals):
-    rank, dim = q.shape[2], emb.shape[2]
-    return call(
-        functools.partial(cross_kernel, flip), "cross", [SMEM] * 2 + [VMEM] * 4, VMEM,
-        array((rank + 8, dim)),
+    _, rows, rank = q.shape
+    dim = emb.shape[2]
+    masks = [] if flip else [array((2, rows, 1))]
+    return call(
+        functools.partial(cross_kernel, flip), "cross", [SMEM] * 2 + [VMEM] * 4,
+        [VMEM] * (1 + len(masks)), [array((rank + 8, dim))] + masks,
         cost=pl.CostEstimate(flops=2 * rank * dim * q.shape[1], bytes_accessed=0, transcendentals=0),
     )(place, live, emb, *near(q, turned), totals)
 
@@ -355,24 +360,20 @@
     )(*payloads)
 
 
-def live_rows(step, block, live):
-    return lax.broadcasted_iota(jnp.int32, (block, 1), 0) + step * block < live
-
-
-def store_sums(sums, copies):
-    both = jnp.concatenate([jnp.sum(part, axis=0, keepdims=True) for part in sums])
+def store_sums(sums, levels, copies):
+    both = jnp.concatenate(
+        [level * jnp.sum(part, axis=0, keepdims=True) for part, level in zip(sums, levels)]
+    )
     for i in range(copies.shape[0]):
         copies[i] = both
 
 
-def kernel_half(cells, t, live, emb, q, weights, summed, put):
+def kernel_half(cells, t, mask, emb, q, weights, summed, k, sums_out):
     _, rows, rank = q.shape
     block = rows // STEPS
     inverse = 1.0 / (D * (weights[...] * (cells / rank)))
     matrix = halves((-2.0 * inverse) * summed[0:rank, :].T)
     slope, offset = summed[rank + 1 : rank + 2, :] * inverse, summed[rank : rank + 1, :] * inverse
-    numbers = summed[rank + 2 : rank + 3, :]
-    level = cells / jnp.where(t == 0, numbers[:, 0:1], numbers[:, rank // 2 : rank // 2 + 1])
     sums = None
     for step in range(STEPS):
         at = slice(step * block, (step + 1) * block)
@@ -380,47 +381,45 @@
         norms = jnp.sum(value * value, axis=1, keepdims=True)
         grad = norms * slope + offset + dot3(halves(value), matrix, 1, 0)
         kernel = (q[t, at, :] / rank) * jnp.exp(-step_size * grad)
-        put(at, kernel)
-        scale = jnp.where(live_rows(step, block, live[t]), level, 0.0)
-        scale = scale / jnp.sum(kernel, axis=1, keepdims=True)
+        k[at, :] = kernel
+        scale = mask[t, at, :] / jnp.sum(kernel, axis=1, keepdims=True)
         sums = add_to(sums, fold(scale * kernel))
-    return sums
-
-
-def other_kernel(cells, place, live, emb, q, weights, mine, k, sums):
-    def put(at, kernel):
-        k[at, :] = kernel
-
-    t = 1 - (place[0] & 1)
-    sums[...] = kernel_half(cells, t, live, emb, q, weights, mine, put)
-
-
-def own_kernel(cells, place, live, emb, q, weights, mine, other, k_other, sums_other, k, copies, consts):
-    core = place[0] & 1
-    rank = q.shape[2]
-
-    def put(at, kernel):
-        k[core, at, :] = kernel
-        k[1 - core, at, :] = k_other[at, :]
-
-    sums_own = kernel_half(cells, core, live, emb, q, weights, other, put)
-    sums_out = sums_other[...]
-    first = core == 0
-    store_sums([jnp.where(first, sums_own, sums_out), jnp.where(first, sums_out, sums_own)], copies)
-
+    sums_out[...] = sums
+
+
+def other_kernel(cells, place, mask, emb, q, weights, mine, k, sums):
+    kernel_half(cells, 1 - (place[0] & 1), mask, emb, q, weights, mine, k, sums)
+
+
+def levels_of(cells, summed):
+    rank = summed.shape[1]
+    numbers = summed[rank + 2 : rank + 3, :]
+    return cells / numbers[:, 0:1], cells / numbers[:, rank // 2 : rank // 2 + 1]
+
+
+def in_order(first, own, out):
+    return jnp.where(first, own, out), jnp.where(first, out, own)
+
+
+def write_tables(cells, first, weights, mine, other, consts):
+    rank = weights.shape[1]
     a, b = mine[...], other[...]
     col_mass = weights[...] * (cells / rank)
     norm_a, total_a = a[rank : rank + 1], a[rank + 1 : rank + 2]
     norm_b, total_b = b[rank : rank + 1], b[rank + 1 : rank + 2]
     products = jnp.sum((a[0:rank] * b[0:rank]).T, axis=0, keepdims=True)
-    mixed_a, mixed_b = norm_a * total_b, total_a * norm_b
-    mixed = jnp.where(first, mixed_a, mixed_b) + jnp.where(first, mixed_b, mixed_a)
-    cost = (mixed - 2.0 * products) / D
+    mixed = in_order(first, norm_a * total_b, total_a * norm_b)
+    cost = (mixed[0] + mixed[1] - 2.0 * products) / D
     consts[0:1, :] = col_mass * jnp.exp(step_size * cost / (col_mass * col_mass))
-    numbers = a[rank + 2 : rank + 3]
-    for t in range(2):
-        at = t * (rank // 2)
-        consts[1 + t : 2 + t, :] = jnp.broadcast_to(cells / numbers[:, at : at + 1], (1, rank))
+    for t, level in enumerate(levels_of(cells, mine)):
+        consts[1 + t : 2 + t, :] = jnp.broadcast_to(level, (1, rank))
+
+
+def own_kernel(cells, place, mask, emb, q, weights, mine, other, sums_other, k, copies, consts, sums):
+    core = place[0] & 1
+    write_tables(cells, core == 0, weights, mine, other, consts)
+    kernel_half(cells, core, mask, emb, q, weights, other, k, sums)
+    store_sums(in_order(core == 0, sums[...], sums_other[...]), levels_of(cells, mine), copies)
 
 
 def cube_root(x):
@@ -436,23 +435,26 @@
     return mass, mass / sum_s, mass / sum_t
 
 
-def sweep_kernel(last, live, k, parts, consts, *refs):
+def sweep_kernel(last, place, mask, k_own, k_other, parts, consts, *refs):
     copies = refs[-1]
-    block = k.shape[1] // STEPS
-
-    _, dual_s, dual_t = duals_of(parts, consts)
+    core = place[0] & 1
+    first = core == 0
+    block = k_own.shape[0] // STEPS
+
+    _, *duals = duals_of(parts, consts)
     sums = [None, None]
     for step in range(STEPS):
         at = slice(step * block, (step + 1) * block)
-        for t, dual in enumerate((dual_s, dual_t)):
-            kernel = k[t, at, :]
+        for i, (k, t, dual) in enumerate(
+            zip((k_own, k_other), (core, 1 - core), in_order(first, *duals))
+        ):
+            kernel = k[at, :]
             weighted = jnp.sum(kernel * dual, axis=1, keepdims=True)
-            level = jnp.where(live_rows(step, block, live[t]), consts[1 + t : 2 + t, 0:1], 0.0)
-            scaled = (level / weighted) * kernel
+            scaled = (mask[t, at, :] / weighted) * kernel
             if last:
                 refs[0][t, at, :] = scaled
-            sums[t] = add_to(sums[t], fold(scaled))
-    store_sums(sums, copies)
+            sums[i] = add_to(sums[i], fold(scaled))
+    store_sums(in_order(first, *sums), (consts[1:2, :], consts[2:3, :]), copies)
 
 
 def finish_kernel(cells, scaled, parts, consts, fs, ft, weights, held, sems):
@@ -460,11 +462,12 @@
     block = rows // STEPS
     mass, dual_s, dual_t = duals_of(parts, consts)
     weights[...] = mass * (rank / cells)
+    dual_s, dual_t = dual_s * (rank * consts[1:2, :]), dual_t * (rank * consts[2:3, :])
     copies = []
     for step in range(STEPS):
         at = slice(step * block, (step + 1) * block)
         for t, (dual, out) in enumerate(((dual_s, fs), (dual_t, ft))):
-            held[t, at, :] = rank * (scaled[t, at, :] * dual)
+            held[t, at, :] = scaled[t, at, :] * dual
             copy = pltpu.make_async_copy(held.at[t, at], out.at[at], sems.at[t, step])
             copy.start()
             copies.append(copy)
@@ -472,28 +475,28 @@
         copy.wait()
 
 
-def kernels(cells, count, place, live, emb, q, weights, mine, other):
+def kernels(cells, count, place, mask, emb, q, weights, mine, other):
     _, rows, rank = q.shape
     dim = emb.shape[2]
+    cost = pl.CostEstimate(flops=6 * rows * rank * dim, bytes_accessed=0, transcendentals=rows * rank)
     k_other, sums_other = call(
-        functools.partial(other_kernel, cells), "kernel_other", [SMEM, SMEM] + [VMEM] * 4, [VMEM] * 2,
-        [array((rows, rank)), array((8, rank))],
-        cost=pl.CostEstimate(flops=6 * rows * rank * dim, bytes_accessed=0, transcendentals=rows * rank),
-    )(place, live, emb, *near(q), weights, mine)
-    return call(
-        functools.partial(own_kernel, cells), "kernel_own", [SMEM, SMEM] + [VMEM] * 7, [VMEM] * 3,
-        [array((2, rows, rank)), array((count, 2, rank)), array((8, rank))],
-        cost=pl.CostEstimate(flops=6 * rows * rank * dim, bytes_accessed=0, transcendentals=rows * rank),
-    )(place, live, emb, *near(q), weights, mine, other, k_other, sums_other)
-
-
-def sweep(count, last, live, k, parts, consts):
-    _, rows, rank = k.shape
+        functools.partial(other_kernel, cells), "kernel_other", [SMEM] + [VMEM] * 5, [VMEM] * 2,
+        [array((rows, rank)), array((8, rank))], cost=cost,
+    )(place, mask, emb, *near(q), weights, mine)
+    k_own, copies, consts = call(
+        functools.partial(own_kernel, cells), "kernel_own", [SMEM] + [VMEM] * 7, [VMEM] * 3,
+        [array((rows, rank)), array((count, 2, rank)), array((8, rank))], [pltpu.VMEM((8, rank), f32)], cost,
+    )(place, mask, emb, *near(q), weights, mine, other, sums_other)
+    return k_own, k_other, copies, consts
+
+
+def sweep(count, last, place, mask, k_own, k_other, parts, consts):
+    rows, rank = k_own.shape
     scaled = [array((2, rows, rank))] if last else []
     return call(
-        functools.partial(sweep_kernel, last), "sweep", [SMEM] + [VMEM] * 3,
+        functools.partial(sweep_kernel, last), "sweep", [SMEM] + [VMEM] * 5,
         [VMEM] * (len(scaled) + 1), scaled + [array((count, 2, rank))],
-    )(live, k, parts, consts)
+    )(place, mask, k_own, k_other, parts, consts)
 
 
 def finish(cells, scaled, parts, consts):
@@ -535,8 +538,8 @@
             stack = jnp.concatenate([stack, swap(stack, count, bit)])
             masks = masks + [m ^ bit for m in masks]
         emb = whole_product(place, source_expr, target_expr, masks, stack)
-    send = cross(1, place, live, emb, q, turned, totals)
-    own = cross(0, place, live, emb, q, turned, totals)
+    (send,) = cross(1, place, live, emb, q, turned, totals)
+    own, mask = cross(0, place, live, emb, q, turned, totals)
 
     payload = pack_pair(own, swap(send, count, 1))
     cards = 2
@@ -550,13 +553,13 @@
     mine = total(rank, cards, payload, swap(payload, count, opposite))
     other = swap(mine, count, 1)
 
-    k, copies, consts = kernels(
-        cells, count, place, live, emb, q, weights_prev[None], mine, other
+    k_own, k_other, copies, consts = kernels(
+        cells, count, place, mask, emb, q, weights_prev[None], mine, other
     )
     scaled = []
     for step_index in range(1, ITERS):
         last = step_index == ITERS - 1
-        *scaled, copies = sweep(count, last, live, k, exchange(copies), consts)
+        *scaled, copies = sweep(count, last, place, mask, k_own, k_other, exchange(copies), consts)
     out_s, out_t, weights = finish(cells, *scaled, exchange(copies), consts)
     return out_s, out_t, weights[0]
 

time: 81.3 us -> 79.3 us (0.975)
  Pallas kernels: 18 us -> 15.9 us
    pallas_call x4, Pallas kernels: 6 us -> 3.72 us  [the longest x2 1.54 us: sweep(): call(functools.partial(sweep_kernel, last), 'sweep', [SMEM] + [VMEM] * 5,...]
  transfers between devices with their start and end apart: 14 -> 14, of which waited for: 7 -> 8; matrix products, arithmetic and copies ran while one was open for 0% -> 0% of each run, Pallas kernels for 12% -> 12%
where the time goes in v6:
time: 79.3 us; the launch traced here: 79.1 us
  blocking collectives  31 us (39%)
  starting transfers between devices  16.9 us (21%)
  Pallas kernels  15.9 us (20%)
  waiting for transfers between devices  14.4 us (18%)
  between operations  0.83 us (1%)
    all_to_all x2, blocking collectives, on_device(): exchange(copies)  21.8 us
    ppermute x14, starting transfers between devices, swap(): return lax.ppermute(value, 'cell', [(i, i ^ mask) for i in range(count)])  16.9 us
    ppermute x14, waiting for transfers between devices, swap(): return lax.ppermute(value, 'cell', [(i, i ^ mask) for i in range(count)])  14.4 us
    all_to_all x1, blocking collectives, on_device(): out_s, out_t, weights = finish(cells, *scaled, exchange(copies), consts)  9.2 us
    pallas_call x1, Pallas kernels, first_share(): call(functools.partial(first_kernel, masks, later_masks), 'embed_first',...  3.64 us
    pallas_call x2, Pallas kernels, cross(): call(functools.partial(cross_kernel, flip), 'cross', [SMEM] * 2 + [VMEM]...  2.15 us
    pallas_call x3, Pallas kernels, next_share(): call(functools.partial(next_kernel, at), 'embed_next', [SMEM] + [VMEM] *...  2.13 us
    pallas_call x1, Pallas kernels, finish(): call(functools.partial(finish_kernel, cells), 'finish', [VMEM] * 3, [HBM,...  2.01 us
  transfers between devices with their start and end apart: 14, of which 8 were waited for; matrix products, arithmetic and copies ran while one was open for 0% of the time, Pallas kernels for 12%

profile of v6, /device:TPU:0, one launch (start us, length us, event | category | flops | bytes accessed | tf_op | source)
XLA Modules:
  0.0 79.1 jit_solution(4621185291722960022)
XLA Ops:
  0.6 5.1 %collective-permute-start = (bf16[128,256]{1,0:T(8,128)(2,1)}, bf16[128,256]{1,0:T(8,128)(2,1)S(1)}, u32[]{:S(2)}, u32[]{:S(2)}) collective-permute-start(bf16[128,256]{1,0:T(8,128)(2,1)} %table.1), channel_id=1, source_target_pairs={{0,12},{1,13},{2,14},{3,15},{4,8},{5,9},{6,10},{7,11},{8,4},{9,5},... | collective-permute-start | bytes 196616 | tf_op jit(solution)/shard_map/ppermute | solution.py:21
  5.7 1.8 %fetch.1 = (f32[2,1024,256]{2,1,0:T(8,128)S(1)}, bf16[128,256]{1,0:T(8,128)(2,1)S(1)}, bf16[2,256,1024]{2,1,0:T(8,128)(2,1)S(1)}, f32[2,1,256]{2,1,0:T(1,128)S(1)}) custom-call(f32[1024,256]{1,0:T(8,128)} %qs.1, f32[1024,256]{1,0:T(8,128)} %qt.1, bf16[128,256]{1,0:T(8,128)(2,1)} %table.1), custom_call_target="tpu_custom_call" | custom-call | bytes 2097152 | tf_op jit(solution)/shard_map/fetch/pallas_call | solution.py:86
  7.5 0.7 collective-permute-done.refs_1_
  8.3 0.1 collective-permute-start.1
  8.3 1.8 %collective-permute-start.2 = (bf16[2,128,256]{2,1,0:T(8,128)(2,1)S(1)}, bf16[2,128,256]{2,1,0:T(8,128)(2,1)S(1)}, u32[]{:S(2)}, u32[]{:S(2)}) collective-permute-start(bf16[2,128,256]{2,1,0:T(8,128)(2,1)S(1)} %stack.1.even), channel_id=1, source_target_pairs={{0,2},{1,3},{2,0},{3,1},{4,6},{5,7},{6,4},{7,5},{8,10},{9,11},{10,... | collective-permute-start | bytes 393224 | tf_op jit(solution)/shard_map/ppermute | solution.py:21
  10.2 0.8 collective-permute-start.6
  10.9 1.0 %collective-permute-start.4 = (bf16[2,128,256]{2,1,0:T(8,128)(2,1)S(1)}, bf16[2,128,256]{2,1,0:T(8,128)(2,1)S(1)}, u32[]{:S(2)}, u32[]{:S(2)}) collective-permute-start(bf16[2,128,256]{2,1,0:T(8,128)(2,1)S(1)} %stack.1.even), channel_id=1, source_target_pairs={{0,4},{1,5},{2,6},{3,7},{4,0},{5,1},{6,2},{7,3},{8,12},{9,13},{10,... | collective-permute-start | bytes 393224 | tf_op jit(solution)/shard_map/ppermute | solution.py:21
  11.9 0.0 collective-permute-done.1.odd
  11.9 3.6 %embed_first.1 = (f32[2,1024,256]{2,1,0:T(8,128)S(1)}, bf16[2,6,1024,256]{3,2,1,0:T(8,128)(2,1)S(1)}) custom-call(s32[1]{0:T(128)} %bitcast.place, bf16[1024,2048]{1,0:T(8,128)(2,1)} %xs.1, bf16[1024,2048]{1,0:T(8,128)(2,1)} %xt.1, bf16[2,128,256]{2,1,0:T(8,128)(2,1)S(1)} %stack.1.even, bf16[2,128,256]{2,1,0:T(8,128)(2,1)S(1)} %collective-permute-done.1.odd), custom_call_target="tpu_custom_call" | custom-call | flops 1073741824 | bytes 8388608 | tf_op jit(solution)/shard_map/embed_first/pallas_call | solution.py:150
  15.6 1.1 %collective-permute-done.2.value = bf16[2,128,256]{2,1,0:T(8,128)(2,1)S(1)} collective-permute-done((bf16[2,128,256]{2,1,0:T(8,128)(2,1)S(1)}, bf16[2,128,256]{2,1,0:T(8,128)(2,1)S(1)}, u32[]{:S(2)}, u32[]{:S(2)}) %collective-permute-start.2) | collective-permute-done | bytes 131104 | tf_op jit(solution)/shard_map/ppermute | solution.py:21
  16.7 0.1 collective-permute-start.3
  16.8 1.5 %collective-permute-done.4.value = bf16[2,128,256]{2,1,0:T(8,128)(2,1)S(1)} collective-permute-done((bf16[2,128,256]{2,1,0:T(8,128)(2,1)S(1)}, bf16[2,128,256]{2,1,0:T(8,128)(2,1)S(1)}, u32[]{:S(2)}, u32[]{:S(2)}) %collective-permute-start.4) | collective-permute-done | bytes 131104 | tf_op jit(solution)/shard_map/ppermute | solution.py:21
  18.3 0.1 collective-permute-start.5
  18.4 0.0 collective-permute-done.6.value
  18.4 0.5 collective-permute-start.7
  19.0 0.0 collective-permute-done.3.odd
  19.0 0.7 embed_next.3.part
  19.7 0.0 collective-permute-done.5.odd
  19.7 0.7 embed_next.4.part
  20.4 0.0 copy-start.1
  20.5 0.0 collective-permute-done.7.odd
  20.5 0.7 embed_next.5.emb
  21.2 1.0 %cross.3 = f32[264,256]{1,0:T(8,128)S(1)} custom-call(s32[1]{0:T(128)} %bitcast.place, s32[2]{0:T(128)S(1)} %bitcast.6, f32[2,1024,256]{2,1,0:T(8,128)S(1)} %embed_next.5.emb, f32[2,1024,256]{2,1,0:T(8,128)S(1)} %get-tuple-element.25.q, bf16[2,256,1024]{2,1,0:T(8,128)(2,1)S(1)} %get-tuple-element.26.turned, f32[2,1,256]{2,1,0:T(1,128)S(1)} %get-tuple-element.22.refs_2_.totals), custom_call_target="tpu_custom_call" | custom-call | flops 134217728 | tf_op jit(solution)/shard_map/cross/pallas_call | solution.py:250
  22.2 0.0 copy-start
  22.2 0.2 collective-permute-start.8
  22.4 1.2 %cross.2 = (f32[264,256]{1,0:T(8,128)S(1)}, f32[2,1024,1]{2,1,0:T(8,128)S(1)}) custom-call(s32[1]{0:T(128)} %bitcast.place, s32[2]{0:T(128)S(1)} %bitcast.7, f32[2,1024,256]{2,1,0:T(8,128)S(1)} %embed_next.5.emb, f32[2,1024,256]{2,1,0:T(8,128)S(1)} %get-tuple-element.25.q, bf16[2,256,1024]{2,1,0:T(8,128)(2,1)S(1)} %get-tuple-element.26.turned, ...), custom_call_target="tpu_custom_call" | custom-call | flops 134217728 | tf_op jit(solution)/shard_map/cross/pallas_call | solution.py:250
  23.6 0.2 collective-permute-done.8.recv
  23.8 0.1 pack_pair.1.refs_0_
  23.9 2.1 %collective-permute-start.11 = (bf16[272,256]{1,0:T(8,128)(2,1)S(1)}, bf16[272,256]{1,0:T(8,128)(2,1)S(1)}, u32[]{:S(2)}, u32[]{:S(2)}) collective-permute-start(bf16[272,256]{1,0:T(8,128)(2,1)S(1)} %pack_pair.1.refs_0_), channel_id=1, source_target_pairs={{0,6},{1,7},{2,4},{3,5},{4,2},{5,3},{6,0},{7,1},{8,14},{9,15},{10,... | collective-permute-start | bytes 417800 | tf_op jit(solution)/shard_map/ppermute | solution.py:21
  26.0 1.2 %collective-permute-start.10 = (bf16[272,256]{1,0:T(8,128)(2,1)S(1)}, bf16[272,256]{1,0:T(8,128)(2,1)S(1)}, u32[]{:S(2)}, u32[]{:S(2)}) collective-permute-start(bf16[272,256]{1,0:T(8,128)(2,1)S(1)} %pack_pair.1.refs_0_), channel_id=1, source_target_pairs={{0,4},{1,5},{2,6},{3,7},{4,0},{5,1},{6,2},{7,3},{8,12},{9,13},{10,... | collective-permute-start | bytes 417800 | tf_op jit(solution)/shard_map/ppermute | solution.py:21
  27.2 0.3 collective-permute-start.9
  27.4 3.9 %collective-permute-done.11.refs_3_ = bf16[272,256]{1,0:T(8,128)(2,1)S(1)} collective-permute-done((bf16[272,256]{1,0:T(8,128)(2,1)S(1)}, bf16[272,256]{1,0:T(8,128)(2,1)S(1)}, u32[]{:S(2)}, u32[]{:S(2)}) %collective-permute-start.11) | collective-permute-done | bytes 139296 | tf_op jit(solution)/shard_map/ppermute | solution.py:21
  31.4 2.5 %collective-permute-done.10.refs_2_ = bf16[272,256]{1,0:T(8,128)(2,1)S(1)} collective-permute-done((bf16[272,256]{1,0:T(8,128)(2,1)S(1)}, bf16[272,256]{1,0:T(8,128)(2,1)S(1)}, u32[]{:S(2)}, u32[]{:S(2)}) %collective-permute-start.10) | collective-permute-done | bytes 139296 | tf_op jit(solution)/shard_map/ppermute | solution.py:21
  33.9 0.0 collective-permute-done.9.refs_1_
  33.9 0.1 merge.1.refs_0_
  34.0 3.6 %collective-permute-start.12 = (bf16[304,256]{1,0:T(8,128)(2,1)S(1)}, bf16[304,256]{1,0:T(8,128)(2,1)S(1)}, u32[]{:S(2)}, u32[]{:S(2)}) collective-permute-start(bf16[304,256]{1,0:T(8,128)(2,1)S(1)} %merge.1.refs_0_), channel_id=1, source_target_pairs={{0,12},{1,13},{2,14},{3,15},{4,8},{5,9},{6,10},{7,11},{8,4},{9,5},... | collective-permute-start | bytes 466952 | tf_op jit(solution)/shard_map/ppermute | solution.py:21
  37.6 3.9 %collective-permute-done.12.refs_1_ = bf16[304,256]{1,0:T(8,128)(2,1)S(1)} collective-permute-done((bf16[304,256]{1,0:T(8,128)(2,1)S(1)}, bf16[304,256]{1,0:T(8,128)(2,1)S(1)}, u32[]{:S(2)}, u32[]{:S(2)}) %collective-permute-start.12) | collective-permute-done | bytes 155680 | tf_op jit(solution)/shard_map/ppermute | solution.py:21
  41.5 0.3 total.1.mine
  41.8 0.1 collective-permute-start.13
  41.9 1.1 %kernel_other.1 = (f32[1024,256]{1,0:T(8,128)S(1)}, f32[8,256]{1,0:T(8,128)S(1)}) custom-call(s32[1]{0:T(128)} %bitcast.place, f32[2,1024,1]{2,1,0:T(8,128)S(1)} %get-tuple-element.27.mask, f32[2,1024,256]{2,1,0:T(8,128)S(1)} %embed_next.5.emb, f32[2,1024,256]{2,1,0:T(8,128)S(1)} %get-tuple-element.25.q, f32[1,256]{1,0:T(1,128)S(1)} %bitcast.4, ...), custom_call_target="tpu_custom_call" | custom-call | flops 402653184 | tf_op jit(solution)/shard_map/kernel_other/pallas_call | solution.py:482
  42.9 0.4 collective-permute-done.13.other
  43.4 1.1 %kernel_own.1 = (f32[1024,256]{1,0:T(8,128)S(1)}, f32[16,2,256]{2,1,0:T(2,128)S(1)}, f32[8,256]{1,0:T(8,128)S(1)}) custom-call(s32[1]{0:T(128)} %bitcast.place, f32[2,1024,1]{2,1,0:T(8,128)S(1)} %get-tuple-element.27.mask, f32[2,1024,256]{2,1,0:T(8,128)S(1)} %embed_next.5.emb, f32[2,1024,256]{2,1,0:T(8,128)S(1)} %get-tuple-element.25.q, ...), custom_call_target="tpu_custom_call" | custom-call | flops 402653184 | tf_op jit(solution)/shard_map/kernel_own/pallas_call | solution.py:486
  44.5 12.6 %all_to_all.15.parts = f32[16,2,256]{2,1,0:T(2,128)S(1)} all-to-all(f32[16,2,256]{2,1,0:T(2,128)S(1)} %get-tuple-element.32), channel_id=1, replica_groups=mesh['grp'=2,'cell'=16] {'cell'}, dimensions={0} | all-to-all | bytes 65536 | tf_op jit(solution)/shard_map/all_to_all | solution.py:562
  57.1 0.8 sweep.2
  57.9 9.2 %all_to_all.16.parts = f32[16,2,256]{2,1,0:T(2,128)S(1)} all-to-all(f32[16,2,256]{2,1,0:T(2,128)S(1)} %sweep.2), channel_id=1, replica_groups=mesh['grp'=2,'cell'=16] {'cell'}, dimensions={0} | all-to-all | bytes 65536 | tf_op jit(solution)/shard_map/all_to_all | solution.py:562
  67.1 0.8 sweep.3
  67.9 9.2 %all_to_all.17.parts = f32[16,2,256]{2,1,0:T(2,128)S(1)} all-to-all(f32[16,2,256]{2,1,0:T(2,128)S(1)} %get-tuple-element.35), channel_id=1, replica_groups=mesh['grp'=2,'cell'=16] {'cell'}, dimensions={0} | all-to-all | bytes 65536 | tf_op jit(solution)/shard_map/all_to_all | solution.py:563
  77.1 2.0 %finish.1 = (f32[1024,256]{1,0:T(8,128)}, f32[1024,256]{1,0:T(8,128)}, f32[1,256]{1,0:T(1,128)}) custom-call(f32[2,1024,256]{2,1,0:T(8,128)S(1)} %get-tuple-element.34.scaled, f32[16,2,256]{2,1,0:T(2,128)S(1)} %all_to_all.17.parts, f32[8,256]{1,0:T(8,128)S(1)} %get-tuple-element.33.consts), custom_call_target="tpu_custom_call" | custom-call | tf_op jit(solution)/shard_map/finish/pallas_call | solution.py:504
  (6 shorter events, 0.0 us)
Async XLA Ops:
  0.6 7.6 %collective-permute-start = (bf16[128,256]{1,0:T(8,128)(2,1)}, bf16[128,256]{1,0:T(8,128)(2,1)S(1)}, u32[]{:S(2)}, u32[]{:S(2)}) collective-permute-start(bf16[128,256]{1,0:T(8,128)(2,1)} %table.1), channel_id=1, source_target_pairs={{0,12},{1,13},{2,14},{3,15},{4,8},{5,9},{6,10},{7,11},{8,4},{9,5},... | collective-permute-start | bytes 196616 | tf_op jit(solution)/shard_map/ppermute | solution.py:21
  8.3 3.6 %collective-permute-start.1 = (bf16[2,128,256]{2,1,0:T(8,128)(2,1)S(1)}, bf16[2,128,256]{2,1,0:T(8,128)(2,1)S(1)}, u32[]{:S(2)}, u32[]{:S(2)}) collective-permute-start(bf16[2,128,256]{2,1,0:T(8,128)(2,1)S(1)} %stack.1.even), channel_id=1, source_target_pairs={{0,1},{1,0},{2,3},{3,2},{4,5},{5,4},{6,7},{7,6},{8,9},{9,8},{10,11... | collective-permute-start | bytes 393224 | tf_op jit(solution)/shard_map/ppermute | solution.py:21
  8.3 8.3 %collective-permute-start.2 = (bf16[2,128,256]{2,1,0:T(8,128)(2,1)S(1)}, bf16[2,128,256]{2,1,0:T(8,128)(2,1)S(1)}, u32[]{:S(2)}, u32[]{:S(2)}) collective-permute-start(bf16[2,128,256]{2,1,0:T(8,128)(2,1)S(1)} %stack.1.even), channel_id=1, source_target_pairs={{0,2},{1,3},{2,0},{3,1},{4,6},{5,7},{6,4},{7,5},{8,10},{9,11},{10,... | collective-permute-start | bytes 393224 | tf_op jit(solution)/shard_map/ppermute | solution.py:21
  10.2 8.2 %collective-permute-start.6 = (bf16[2,128,256]{2,1,0:T(8,128)(2,1)S(1)}, bf16[2,128,256]{2,1,0:T(8,128)(2,1)S(1)}, u32[]{:S(2)}, u32[]{:S(2)}) collective-permute-start(bf16[2,128,256]{2,1,0:T(8,128)(2,1)S(1)} %stack.1.even), channel_id=1, source_target_pairs={{0,6},{1,7},{2,4},{3,5},{4,2},{5,3},{6,0},{7,1},{8,14},{9,15},{10,... | collective-permute-start | bytes 393224 | tf_op jit(solution)/shard_map/ppermute | solution.py:21
  10.9 7.4 %collective-permute-start.4 = (bf16[2,128,256]{2,1,0:T(8,128)(2,1)S(1)}, bf16[2,128,256]{2,1,0:T(8,128)(2,1)S(1)}, u32[]{:S(2)}, u32[]{:S(2)}) collective-permute-start(bf16[2,128,256]{2,1,0:T(8,128)(2,1)S(1)} %stack.1.even), channel_id=1, source_target_pairs={{0,4},{1,5},{2,6},{3,7},{4,0},{5,1},{6,2},{7,3},{8,12},{9,13},{10,... | collective-permute-start | bytes 393224 | tf_op jit(solution)/shard_map/ppermute | solution.py:21
  16.7 2.3 %collective-permute-start.3 = (bf16[2,128,256]{2,1,0:T(8,128)(2,1)S(1)}, bf16[2,128,256]{2,1,0:T(8,128)(2,1)S(1)}, u32[]{:S(2)}, u32[]{:S(2)}) collective-permute-start(bf16[2,128,256]{2,1,0:T(8,128)(2,1)S(1)} %gate.3.even), channel_id=1, source_target_pairs={{0,1},{1,0},{2,3},{3,2},{4,5},{5,4},{6,7},{7,6},{8,9},{9,8},{10,11... | collective-permute-start | bytes 393224 | tf_op jit(solution)/shard_map/ppermute | solution.py:21
  18.3 1.4 %collective-permute-start.5 = (bf16[2,128,256]{2,1,0:T(8,128)(2,1)S(1)}, bf16[2,128,256]{2,1,0:T(8,128)(2,1)S(1)}, u32[]{:S(2)}, u32[]{:S(2)}) collective-permute-start(bf16[2,128,256]{2,1,0:T(8,128)(2,1)S(1)} %gate.4.even), channel_id=1, source_target_pairs={{0,1},{1,0},{2,3},{3,2},{4,5},{5,4},{6,7},{7,6},{8,9},{9,8},{10,11... | collective-permute-start | bytes 393224 | tf_op jit(solution)/shard_map/ppermute | solution.py:21
  18.4 2.0 %collective-permute-start.7 = (bf16[2,128,256]{2,1,0:T(8,128)(2,1)S(1)}, bf16[2,128,256]{2,1,0:T(8,128)(2,1)S(1)}, u32[]{:S(2)}, u32[]{:S(2)}) collective-permute-start(bf16[2,128,256]{2,1,0:T(8,128)(2,1)S(1)} %gate.5.even), channel_id=1, source_target_pairs={{0,1},{1,0},{2,3},{3,2},{4,5},{5,4},{6,7},{7,6},{8,9},{9,8},{10,11... | collective-permute-start | bytes 393224 | tf_op jit(solution)/shard_map/ppermute | solution.py:21
  20.4 0.7 copy-start.1
  22.2 19.7 %copy-start = (f32[256]{0:T(256)S(1)}, f32[256]{0:T(256)}, u32[]{:S(2)}) copy-start(f32[256]{0:T(256)} %param.12) | copy-start | bytes 3076
  22.2 1.6 %collective-permute-start.8 = (f32[264,256]{1,0:T(8,128)S(1)}, f32[264,256]{1,0:T(8,128)S(1)}, u32[]{:S(2)}, u32[]{:S(2)}) collective-permute-start(f32[264,256]{1,0:T(8,128)S(1)} %cross.3), channel_id=1, source_target_pairs={{0,1},{1,0},{2,3},{3,2},{4,5},{5,4},{6,7},{7,6},{8,9},{9,8},{10,11... | collective-permute-start | bytes 811016 | tf_op jit(solution)/shard_map/ppermute | solution.py:21
  23.9 7.5 %collective-permute-start.11 = (bf16[272,256]{1,0:T(8,128)(2,1)S(1)}, bf16[272,256]{1,0:T(8,128)(2,1)S(1)}, u32[]{:S(2)}, u32[]{:S(2)}) collective-permute-start(bf16[272,256]{1,0:T(8,128)(2,1)S(1)} %pack_pair.1.refs_0_), channel_id=1, source_target_pairs={{0,6},{1,7},{2,4},{3,5},{4,2},{5,3},{6,0},{7,1},{8,14},{9,15},{10,... | collective-permute-start | bytes 417800 | tf_op jit(solution)/shard_map/ppermute | solution.py:21
  26.0 7.9 %collective-permute-start.10 = (bf16[272,256]{1,0:T(8,128)(2,1)S(1)}, bf16[272,256]{1,0:T(8,128)(2,1)S(1)}, u32[]{:S(2)}, u32[]{:S(2)}) collective-permute-start(bf16[272,256]{1,0:T(8,128)(2,1)S(1)} %pack_pair.1.refs_0_), channel_id=1, source_target_pairs={{0,4},{1,5},{2,6},{3,7},{4,0},{5,1},{6,2},{7,3},{8,12},{9,13},{10,... | collective-permute-start | bytes 417800 | tf_op jit(solution)/shard_map/ppermute | solution.py:21
  27.2 6.7 %collective-permute-start.9 = (bf16[272,256]{1,0:T(8,128)(2,1)S(1)}, bf16[272,256]{1,0:T(8,128)(2,1)S(1)}, u32[]{:S(2)}, u32[]{:S(2)}) collective-permute-start(bf16[272,256]{1,0:T(8,128)(2,1)S(1)} %pack_pair.1.refs_0_), channel_id=1, source_target_pairs={{0,2},{1,3},{2,0},{3,1},{4,6},{5,7},{6,4},{7,5},{8,10},{9,11},{10,... | collective-permute-start | bytes 417800 | tf_op jit(solution)/shard_map/ppermute | solution.py:21
  34.0 7.5 %collective-permute-start.12 = (bf16[304,256]{1,0:T(8,128)(2,1)S(1)}, bf16[304,256]{1,0:T(8,128)(2,1)S(1)}, u32[]{:S(2)}, u32[]{:S(2)}) collective-permute-start(bf16[304,256]{1,0:T(8,128)(2,1)S(1)} %merge.1.refs_0_), channel_id=1, source_target_pairs={{0,12},{1,13},{2,14},{3,15},{4,8},{5,9},{6,10},{7,11},{8,4},{9,5},... | collective-permute-start | bytes 466952 | tf_op jit(solution)/shard_map/ppermute | solution.py:21
  41.8 1.6 %collective-permute-start.13 = (f32[264,256]{1,0:T(8,128)S(1)}, f32[264,256]{1,0:T(8,128)S(1)}, u32[]{:S(2)}, u32[]{:S(2)}) collective-permute-start(f32[264,256]{1,0:T(8,128)S(1)} %total.1.mine), channel_id=1, source_target_pairs={{0,1},{1,0},{2,3},{3,2},{4,5},{5,4},{6,7},{7,6},{8,9},{9,8},{10,11... | collective-permute-start | bytes 811016 | tf_op jit(solution)/shard_map/ppermute | solution.py:21

commit v7 on v6

--- a/solution.py
+++ b/solution.py
@@ -65,6 +65,14 @@
 
 def rows_of(step, block):
     return pl.ds(pl.multiple_of(step * block, block), block)
+
+
+def fold(value):
+    return jnp.sum(value.reshape(value.shape[0] // 8, 8, value.shape[1]), axis=0)
+
+
+def add_to(sums, value):
+    return value if sums is None else sums + value
 
 
 def fetch_kernel(qs, qt, table, q_out, table_out, turned, totals, sems):
@@ -171,7 +179,7 @@
     )(value, after)
 
 
-def next_kernel(at, place, x, part, even, odd, out):
+def next_kernel(at, place, x, part, even, odd, out, *sums):
     me = place[0]
     tables = [joined_table(me, j, even, odd) for j in range(even.shape[0])]
     for t in range(2):
@@ -179,61 +187,57 @@
         for j, table in enumerate(tables):
             value = value + jnp.dot(x[t, at + j], table, preferred_element_type=f32)
         out[t] = value
-
-
-def next_share(at, place, x, part, even, odd):
+        for ref in sums:
+            ref[t] = fold(value)
+
+
+def next_share(at, last, place, x, part, even, odd):
     _, rows, dim = part.shape
-    return call(
-        functools.partial(next_kernel, at), "embed_next", [SMEM] + [VMEM] * 4, VMEM, array(part.shape),
+    sums = [array((2, 8, dim))] if last else []
+    return call(
+        functools.partial(next_kernel, at), "embed_next", [SMEM] + [VMEM] * 4, [VMEM] * (1 + len(sums)),
+        [array(part.shape)] + sums,
         cost=pl.CostEstimate(
             flops=16 * rows * dim * even.shape[1], bytes_accessed=0, transcendentals=0
         ),
     )(place, x, part, even, odd)
 
 
-def whole_kernel(masks, place, xs, xt, pieces, part, table):
+def whole_kernel(masks, place, xs, xt, pieces, part, sums, table):
     genes = pieces.shape[1]
     for j, mask in enumerate(masks):
         start = pl.multiple_of((place[0] ^ mask) * genes, genes)
         table[pl.ds(start, genes), :] = pieces[j]
     for t, x in enumerate((xs, xt)):
-        part[t] = jnp.dot(x[...], table[...], preferred_element_type=f32)
+        value = jnp.dot(x[...], table[...], preferred_element_type=f32)
+        part[t] = value
+        sums[t] = fold(value)
 
 
 def whole_product(place, xs, xt, masks, pieces):
     rows, genes = xs.shape
     dim = pieces.shape[2]
     return call(
-        functools.partial(whole_kernel, masks), "embed_whole", [SMEM] + [VMEM] * 3, VMEM,
-        array((2, rows, dim)), [pltpu.VMEM((genes, dim), bf16)],
+        functools.partial(whole_kernel, masks), "embed_whole", [SMEM] + [VMEM] * 3, [VMEM] * 2,
+        [array((2, rows, dim)), array((2, 8, dim))], [pltpu.VMEM((genes, dim), bf16)],
     )(place, xs, xt, pieces)
 
 
-def fold(value):
-    return jnp.sum(value.reshape(value.shape[0] // 8, 8, value.shape[1]), axis=0)
-
-
-def add_to(sums, value):
-    return value if sums is None else sums + value
-
-
-def cross_kernel(flip, place, live, emb, q, turned, totals, out, *masks):
+def cross_kernel(flip, place, live, emb, sums, q, turned, totals, out, norms, *masks):
     t = (place[0] & 1) ^ flip
     _, rows, rank = q.shape
     block = rows // STEPS
-    means = norms = rest = None
+    mean = (jnp.sum(sums[t], axis=0, keepdims=True) / rows).astype(bf16).astype(f32)
+    norm_sum = rest = None
     for step in range(STEPS):
         at = slice(step * block, (step + 1) * block)
         value = emb[t, at, :]
-        means = add_to(means, fold(value))
+        centred = (value - mean).astype(bf16)
+        rest = add_to(rest, jnp.dot(turned[t, :, at], centred, preferred_element_type=f32))
         squares = jnp.sum(value * value, axis=1, keepdims=True)
-        norms = add_to(norms, fold(squares * q[t, at, :]))
-    mean = (jnp.sum(means, axis=0, keepdims=True) / rows).astype(bf16).astype(f32)
-    for step in range(STEPS):
-        at = slice(step * block, (step + 1) * block)
-        centred = (emb[t, at, :] - mean).astype(bf16)
-        rest = add_to(rest, jnp.dot(turned[t, :, at], centred, preferred_element_type=f32))
-    norm_sum = jnp.sum(norms, axis=0, keepdims=True) / rank
+        norms[at, :] = squares
+        norm_sum = add_to(norm_sum, fold(squares * q[t, at, :]))
+    norm_sum = jnp.sum(norm_sum, axis=0, keepdims=True) / rank
     lane = lax.broadcasted_iota(jnp.int32, (1, rank), 1)
     number = jnp.where(lane < rank // 2, live[0], live[1]).astype(f32)
     out[0:rank, :] = rest
@@ -243,15 +247,15 @@
             mask[i] = (lax.broadcasted_iota(jnp.int32, (rows, 1), 0) < live[i]).astype(f32)
 
 
-def cross(flip, place, live, emb, q, turned, totals):
+def cross(flip, place, live, emb, sums, q, turned, totals):
     _, rows, rank = q.shape
     dim = emb.shape[2]
     masks = [] if flip else [array((2, rows, 1))]
     return call(
-        functools.partial(cross_kernel, flip), "cross", [SMEM] * 2 + [VMEM] * 4,
-        [VMEM] * (1 + len(masks)), [array((rank + 8, dim))] + masks,
+        functools.partial(cross_kernel, flip), "cross", [SMEM] * 2 + [VMEM] * 5,
+        [VMEM] * (2 + len(masks)), [array((rank + 8, dim)), array((rows, 1))] + masks,
         cost=pl.CostEstimate(flops=2 * rank * dim * q.shape[1], bytes_accessed=0, transcendentals=0),
-    )(place, live, emb, *near(q, turned), totals)
+    )(place, live, emb, sums, *near(q, turned), totals)
 
 
 def split_row(row):
@@ -368,7 +372,7 @@
         copies[i] = both
 
 
-def kernel_half(cells, t, mask, emb, q, weights, summed, k, sums_out):
+def kernel_half(cells, t, mask, norms, emb, q, weights, summed, k, sums_out):
     _, rows, rank = q.shape
     block = rows // STEPS
     inverse = 1.0 / (D * (weights[...] * (cells / rank)))
@@ -378,8 +382,7 @@
     for step in range(STEPS):
         at = slice(step * block, (step + 1) * block)
         value = emb[t, at, :]
-        norms = jnp.sum(value * value, axis=1, keepdims=True)
-        grad = norms * slope + offset + dot3(halves(value), matrix, 1, 0)
+        grad = norms[at, :] * slope + offset + dot3(halves(value), matrix, 1, 0)
         kernel = (q[t, at, :] / rank) * jnp.exp(-step_size * grad)
         k[at, :] = kernel
         scale = mask[t, at, :] / jnp.sum(kernel, axis=1, keepdims=True)
@@ -387,8 +390,8 @@
     sums_out[...] = sums
 
 
-def other_kernel(cells, place, mask, emb, q, weights, mine, k, sums):
-    kernel_half(cells, 1 - (place[0] & 1), mask, emb, q, weights, mine, k, sums)
+def other_kernel(cells, place, mask, norms, emb, q, weights, mine, k, sums):
+    kernel_half(cells, 1 - (place[0] & 1), mask, norms, emb, q, weights, mine, k, sums)
 
 
 def levels_of(cells, summed):
@@ -415,10 +418,12 @@
         consts[1 + t : 2 + t, :] = jnp.broadcast_to(level, (1, rank))
 
 
-def own_kernel(cells, place, mask, emb, q, weights, mine, other, sums_other, k, copies, consts, sums):
+def own_kernel(
+    cells, place, mask, norms, emb, q, weights, mine, other, sums_other, k, copies, consts, sums
+):
     core = place[0] & 1
     write_tables(cells, core == 0, weights, mine, other, consts)
-    kernel_half(cells, core, mask, emb, q, weights, other, k, sums)
+    kernel_half(cells, core, mask, norms, emb, q, weights, other, k, sums)
     store_sums(in_order(core == 0, sums[...], sums_other[...]), levels_of(cells, mine), copies)
 
 
@@ -457,13 +462,14 @@
     store_sums(in_order(first, *sums), (consts[1:2, :], consts[2:3, :]), copies)
 
 
-def finish_kernel(cells, scaled, parts, consts, fs, ft, weights, held, sems):
+def finish_kernel(cells, scaled, parts, consts, fs, ft, weights, held, mass_held, sems, mass_sem):
     _, rows, rank = scaled.shape
     block = rows // STEPS
     mass, dual_s, dual_t = duals_of(parts, consts)
-    weights[...] = mass * (rank / cells)
+    mass_held[...] = mass * (rank / cells)
+    copies = [pltpu.make_async_copy(mass_held, weights, mass_sem)]
+    copies[0].start()
     dual_s, dual_t = dual_s * (rank * consts[1:2, :]), dual_t * (rank * consts[2:3, :])
-    copies = []
     for step in range(STEPS):
         at = slice(step * block, (step + 1) * block)
         for t, (dual, out) in enumerate(((dual_s, fs), (dual_t, ft))):
@@ -475,18 +481,18 @@
         copy.wait()
 
 
-def kernels(cells, count, place, mask, emb, q, weights, mine, other):
+def kernels(cells, count, place, mask, norms, emb, q, weights, mine, other):
     _, rows, rank = q.shape
     dim = emb.shape[2]
     cost = pl.CostEstimate(flops=6 * rows * rank * dim, bytes_accessed=0, transcendentals=rows * rank)
     k_other, sums_other = call(
-        functools.partial(other_kernel, cells), "kernel_other", [SMEM] + [VMEM] * 5, [VMEM] * 2,
+        functools.partial(other_kernel, cells), "kernel_other", [SMEM] + [VMEM] * 6, [VMEM] * 2,
         [array((rows, rank)), array((8, rank))], cost=cost,
-    )(place, mask, emb, *near(q), weights, mine)
+    )(place, mask, norms[1], emb, *near(q), weights, mine)
     k_own, copies, consts = call(
-        functools.partial(own_kernel, cells), "kernel_own", [SMEM] + [VMEM] * 7, [VMEM] * 3,
+        functools.partial(own_kernel, cells), "kernel_own", [SMEM] + [VMEM] * 8, [VMEM] * 3,
         [array((rows, rank)), array((count, 2, rank)), array((8, rank))], [pltpu.VMEM((8, rank), f32)], cost,
-    )(place, mask, emb, *near(q), weights, mine, other, sums_other)
+    )(place, mask, norms[0], emb, *near(q), weights, mine, other, sums_other)
     return k_own, k_other, copies, consts
 
 
@@ -502,9 +508,12 @@
 def finish(cells, scaled, parts, consts):
     _, rows, rank = scaled.shape
     return call(
-        functools.partial(finish_kernel, cells), "finish", [VMEM] * 3, [HBM, HBM, VMEM],
+        functools.partial(finish_kernel, cells), "finish", [VMEM] * 3, [HBM] * 3,
         [array((rows, rank))] * 2 + [array((1, rank))],
-        [pltpu.VMEM((2, rows, rank), f32), pltpu.SemaphoreType.DMA((2, STEPS))],
+        [
+            pltpu.VMEM((2, rows, rank), f32), pltpu.VMEM((1, rank), f32),
+            pltpu.SemaphoreType.DMA((2, STEPS)), pltpu.SemaphoreType.DMA,
+        ],
     )(scaled, parts, consts)
 
 
@@ -532,14 +541,15 @@
         )
         arrived = [gate(piece, emb) for piece in arrived]
         for i, piece in enumerate(arrived):
-            emb = next_share(2 * i, place, x, emb, piece, swap(piece, count, 1))
+            last = i == len(arrived) - 1
+            emb, *sums = next_share(2 * i, last, place, x, emb, piece, swap(piece, count, 1))
     else:
         for bit in reversed(bits[:-1]):
             stack = jnp.concatenate([stack, swap(stack, count, bit)])
             masks = masks + [m ^ bit for m in masks]
-        emb = whole_product(place, source_expr, target_expr, masks, stack)
-    (send,) = cross(1, place, live, emb, q, turned, totals)
-    own, mask = cross(0, place, live, emb, q, turned, totals)
+        emb, *sums = whole_product(place, source_expr, target_expr, masks, stack)
+    send, norms_other = cross(1, place, live, emb, *sums, q, turned, totals)
+    own, norms_own, mask = cross(0, place, live, emb, *sums, q, turned, totals)
 
     payload = pack_pair(own, swap(send, count, 1))
     cards = 2
@@ -554,7 +564,7 @@
     other = swap(mine, count, 1)
 
     k_own, k_other, copies, consts = kernels(
-        cells, count, place, mask, emb, q, weights_prev[None], mine, other
+        cells, count, place, mask, (norms_own, norms_other), emb, q, weights_prev[None], mine, other
     )
     scaled = []
     for step_index in range(1, ITERS):

time: 79.3 us -> 78.7 us (level)
  Pallas kernels: 15.9 us -> 15.1 us
  transfers between devices with their start and end apart: 14 -> 14, of which waited for: 8 -> 8; matrix products, arithmetic and copies ran while one was open for 0% -> 0% of each run, Pallas kernels for 12% -> 11%
where the time goes in v7:
time: 78.7 us; the launch traced here: 78.4 us
  blocking collectives  31 us (39%)
  starting transfers between devices  16.9 us (21%)
  Pallas kernels  15.1 us (19%)
  waiting for transfers between devices  14.6 us (19%)
  between operations  0.84 us (1%)
    all_to_all x2, blocking collectives, on_device(): exchange(copies)  21.8 us
    ppermute x14, starting transfers between devices, swap(): return lax.ppermute(value, 'cell', [(i, i ^ mask) for i in range(count)])  16.9 us
    ppermute x14, waiting for transfers between devices, swap(): return lax.ppermute(value, 'cell', [(i, i ^ mask) for i in range(count)])  14.6 us
    all_to_all x1, blocking collectives, on_device(): out_s, out_t, weights = finish(cells, *scaled, exchange(copies), consts)  9.2 us
    pallas_call x1, Pallas kernels, first_share(): call(functools.partial(first_kernel, masks, later_masks), 'embed_first',...  3.64 us
    pallas_call x3, Pallas kernels, next_share(): call(functools.partial(next_kernel, at), 'embed_next', [SMEM] + [VMEM] *...  2.13 us
    pallas_call x2, Pallas kernels, cross(): call(functools.partial(cross_kernel, flip), 'cross', [SMEM] * 2 + [VMEM]...  1.96 us
    pallas_call x1, Pallas kernels, fetch(): call(fetch_kernel, 'fetch', [HBM] * 3, [VMEM] * 4, [pltpu.VMEM((2, rows,...  1.79 us
  transfers between devices with their start and end apart: 14, of which 8 were waited for; matrix products, arithmetic and copies ran while one was open for 0% of the time, Pallas kernels for 11%

profile of v7, /device:TPU:0, one launch (start us, length us, event | category | flops | bytes accessed | tf_op | source)
XLA Modules:
  0.0 78.4 jit_solution(3237899927759971745)
XLA Ops:
  0.6 5.1 %collective-permute-start = (bf16[128,256]{1,0:T(8,128)(2,1)}, bf16[128,256]{1,0:T(8,128)(2,1)S(1)}, u32[]{:S(2)}, u32[]{:S(2)}) collective-permute-start(bf16[128,256]{1,0:T(8,128)(2,1)} %table.1), channel_id=1, source_target_pairs={{0,12},{1,13},{2,14},{3,15},{4,8},{5,9},{6,10},{7,11},{8,4},{9,5},... | collective-permute-start | bytes 196616 | tf_op jit(solution)/shard_map/ppermute | solution.py:21
  5.7 1.8 %fetch.1 = (f32[2,1024,256]{2,1,0:T(8,128)S(1)}, bf16[128,256]{1,0:T(8,128)(2,1)S(1)}, bf16[2,256,1024]{2,1,0:T(8,128)(2,1)S(1)}, f32[2,1,256]{2,1,0:T(1,128)S(1)}) custom-call(f32[1024,256]{1,0:T(8,128)} %qs.1, f32[1024,256]{1,0:T(8,128)} %qt.1, bf16[128,256]{1,0:T(8,128)(2,1)} %table.1), custom_call_target="tpu_custom_call" | custom-call | bytes 2097152 | tf_op jit(solution)/shard_map/fetch/pallas_call | solution.py:94
  7.5 0.7 collective-permute-done.refs_1_
  8.3 0.1 collective-permute-start.1
  8.3 1.8 %collective-permute-start.2 = (bf16[2,128,256]{2,1,0:T(8,128)(2,1)S(1)}, bf16[2,128,256]{2,1,0:T(8,128)(2,1)S(1)}, u32[]{:S(2)}, u32[]{:S(2)}) collective-permute-start(bf16[2,128,256]{2,1,0:T(8,128)(2,1)S(1)} %stack.1.even), channel_id=1, source_target_pairs={{0,2},{1,3},{2,0},{3,1},{4,6},{5,7},{6,4},{7,5},{8,10},{9,11},{10,... | collective-permute-start | bytes 393224 | tf_op jit(solution)/shard_map/ppermute | solution.py:21
  10.2 0.8 collective-permute-start.6
  10.9 1.0 %collective-permute-start.4 = (bf16[2,128,256]{2,1,0:T(8,128)(2,1)S(1)}, bf16[2,128,256]{2,1,0:T(8,128)(2,1)S(1)}, u32[]{:S(2)}, u32[]{:S(2)}) collective-permute-start(bf16[2,128,256]{2,1,0:T(8,128)(2,1)S(1)} %stack.1.even), channel_id=1, source_target_pairs={{0,4},{1,5},{2,6},{3,7},{4,0},{5,1},{6,2},{7,3},{8,12},{9,13},{10,... | collective-permute-start | bytes 393224 | tf_op jit(solution)/shard_map/ppermute | solution.py:21
  11.9 0.0 collective-permute-done.1.odd
  11.9 3.6 %embed_first.1 = (f32[2,1024,256]{2,1,0:T(8,128)S(1)}, bf16[2,6,1024,256]{3,2,1,0:T(8,128)(2,1)S(1)}) custom-call(s32[1]{0:T(128)} %bitcast.place, bf16[1024,2048]{1,0:T(8,128)(2,1)} %xs.1, bf16[1024,2048]{1,0:T(8,128)(2,1)} %xt.1, bf16[2,128,256]{2,1,0:T(8,128)(2,1)S(1)} %stack.1.even, bf16[2,128,256]{2,1,0:T(8,128)(2,1)S(1)} %collective-permute-done.1.odd), custom_call_target="tpu_custom_call" | custom-call | flops 1073741824 | bytes 8388608 | tf_op jit(solution)/shard_map/embed_first/pallas_call | solution.py:158
  15.6 1.1 %collective-permute-done.2.value = bf16[2,128,256]{2,1,0:T(8,128)(2,1)S(1)} collective-permute-done((bf16[2,128,256]{2,1,0:T(8,128)(2,1)S(1)}, bf16[2,128,256]{2,1,0:T(8,128)(2,1)S(1)}, u32[]{:S(2)}, u32[]{:S(2)}) %collective-permute-start.2) | collective-permute-done | bytes 131104 | tf_op jit(solution)/shard_map/ppermute | solution.py:21
  16.7 0.1 collective-permute-start.3
  16.8 1.5 %collective-permute-done.4.value = bf16[2,128,256]{2,1,0:T(8,128)(2,1)S(1)} collective-permute-done((bf16[2,128,256]{2,1,0:T(8,128)(2,1)S(1)}, bf16[2,128,256]{2,1,0:T(8,128)(2,1)S(1)}, u32[]{:S(2)}, u32[]{:S(2)}) %collective-permute-start.4) | collective-permute-done | bytes 131104 | tf_op jit(solution)/shard_map/ppermute | solution.py:21
  18.3 0.1 collective-permute-start.5
  18.4 0.0 collective-permute-done.6.value
  18.4 0.5 collective-permute-start.7
  19.0 0.0 collective-permute-done.3.odd
  19.0 0.7 embed_next.3.part
  19.7 0.0 collective-permute-done.5.odd
  19.7 0.7 embed_next.4.part
  20.4 0.0 copy-start.1
  20.5 0.0 collective-permute-done.7.odd
  20.5 0.7 embed_next.5
  21.2 0.9 %cross.3 = (f32[264,256]{1,0:T(8,128)S(1)}, f32[1024,1]{1,0:T(8,128)S(1)}) custom-call(s32[1]{0:T(128)} %bitcast.place, s32[2]{0:T(128)S(1)} %bitcast.6, f32[2,1024,256]{2,1,0:T(8,128)S(1)} %get-tuple-element.30.emb, f32[2,8,256]{2,1,0:T(8,128)S(1)} %get-tuple-element.31.sums, f32[2,1024,256]{2,1,0:T(8,128)S(1)} %get-tuple-element.32.q, ...), custom_call_target="tpu_custom_call" | custom-call | flops 134217728 | tf_op jit(solution)/shard_map/cross/pallas_call | solution.py:254
  22.1 0.0 copy-start
  22.1 0.2 collective-permute-start.8
  22.3 1.1 %cross.2 = (f32[264,256]{1,0:T(8,128)S(1)}, f32[1024,1]{1,0:T(8,128)S(1)}, f32[2,1024,1]{2,1,0:T(8,128)S(1)}) custom-call(s32[1]{0:T(128)} %bitcast.place, s32[2]{0:T(128)S(1)} %bitcast.7, f32[2,1024,256]{2,1,0:T(8,128)S(1)} %get-tuple-element.30.emb, f32[2,8,256]{2,1,0:T(8,128)S(1)} %get-tuple-element.31.sums, f32[2,1024,256]{2,1,0:T(8,128)S(1)} %get-tuple-element.32.q, ...), custom_call_target="tpu_custom_call" | custom-call | flops 134217728 | tf_op jit(solution)/shard_map/cross/pallas_call | solution.py:254
  23.4 0.3 collective-permute-done.8.recv
  23.7 0.1 pack_pair.1.refs_0_
  23.8 2.1 %collective-permute-start.11 = (bf16[272,256]{1,0:T(8,128)(2,1)S(1)}, bf16[272,256]{1,0:T(8,128)(2,1)S(1)}, u32[]{:S(2)}, u32[]{:S(2)}) collective-permute-start(bf16[272,256]{1,0:T(8,128)(2,1)S(1)} %pack_pair.1.refs_0_), channel_id=1, source_target_pairs={{0,6},{1,7},{2,4},{3,5},{4,2},{5,3},{6,0},{7,1},{8,14},{9,15},{10,... | collective-permute-start | bytes 417800 | tf_op jit(solution)/shard_map/ppermute | solution.py:21
  25.9 1.2 %collective-permute-start.10 = (bf16[272,256]{1,0:T(8,128)(2,1)S(1)}, bf16[272,256]{1,0:T(8,128)(2,1)S(1)}, u32[]{:S(2)}, u32[]{:S(2)}) collective-permute-start(bf16[272,256]{1,0:T(8,128)(2,1)S(1)} %pack_pair.1.refs_0_), channel_id=1, source_target_pairs={{0,4},{1,5},{2,6},{3,7},{4,0},{5,1},{6,2},{7,3},{8,12},{9,13},{10,... | collective-permute-start | bytes 417800 | tf_op jit(solution)/shard_map/ppermute | solution.py:21
  27.1 0.3 collective-permute-start.9
  27.4 3.9 %collective-permute-done.11.refs_3_ = bf16[272,256]{1,0:T(8,128)(2,1)S(1)} collective-permute-done((bf16[272,256]{1,0:T(8,128)(2,1)S(1)}, bf16[272,256]{1,0:T(8,128)(2,1)S(1)}, u32[]{:S(2)}, u32[]{:S(2)}) %collective-permute-start.11) | collective-permute-done | bytes 139296 | tf_op jit(solution)/shard_map/ppermute | solution.py:21
  31.3 2.5 %collective-permute-done.10.refs_2_ = bf16[272,256]{1,0:T(8,128)(2,1)S(1)} collective-permute-done((bf16[272,256]{1,0:T(8,128)(2,1)S(1)}, bf16[272,256]{1,0:T(8,128)(2,1)S(1)}, u32[]{:S(2)}, u32[]{:S(2)}) %collective-permute-start.10) | collective-permute-done | bytes 139296 | tf_op jit(solution)/shard_map/ppermute | solution.py:21
  33.8 0.0 collective-permute-done.9.refs_1_
  33.8 0.1 merge.1.refs_0_
  33.9 3.6 %collective-permute-start.12 = (bf16[304,256]{1,0:T(8,128)(2,1)S(1)}, bf16[304,256]{1,0:T(8,128)(2,1)S(1)}, u32[]{:S(2)}, u32[]{:S(2)}) collective-permute-start(bf16[304,256]{1,0:T(8,128)(2,1)S(1)} %merge.1.refs_0_), channel_id=1, source_target_pairs={{0,12},{1,13},{2,14},{3,15},{4,8},{5,9},{6,10},{7,11},{8,4},{9,5},... | collective-permute-start | bytes 466952 | tf_op jit(solution)/shard_map/ppermute | solution.py:21
  37.5 3.9 %collective-permute-done.12.refs_1_ = bf16[304,256]{1,0:T(8,128)(2,1)S(1)} collective-permute-done((bf16[304,256]{1,0:T(8,128)(2,1)S(1)}, bf16[304,256]{1,0:T(8,128)(2,1)S(1)}, u32[]{:S(2)}, u32[]{:S(2)}) %collective-permute-start.12) | collective-permute-done | bytes 155680 | tf_op jit(solution)/shard_map/ppermute | solution.py:21
  41.4 0.3 total.1.mine
  41.7 0.1 collective-permute-start.13
  41.8 1.1 %kernel_other.1 = (f32[1024,256]{1,0:T(8,128)S(1)}, f32[8,256]{1,0:T(8,128)S(1)}) custom-call(s32[1]{0:T(128)} %bitcast.place, f32[2,1024,1]{2,1,0:T(8,128)S(1)} %get-tuple-element.34.mask, f32[1024,1]{1,0:T(8,128)S(1)} %get-tuple-element.38.norms, f32[2,1024,256]{2,1,0:T(8,128)S(1)} %get-tuple-element.30.emb, f32[2,1024,256]{2,1,0:T(8,128)S(1)} %get-tuple-element.32.q, ...), custom_call_target="tpu_custom_call" | custom-call | flops 402653184 | tf_op jit(solution)/shard_map/kernel_other/pallas_call | solution.py:488
  42.8 0.5 collective-permute-done.13.other
  43.3 1.1 %kernel_own.1 = (f32[1024,256]{1,0:T(8,128)S(1)}, f32[16,2,256]{2,1,0:T(2,128)S(1)}, f32[8,256]{1,0:T(8,128)S(1)}) custom-call(s32[1]{0:T(128)} %bitcast.place, f32[2,1024,1]{2,1,0:T(8,128)S(1)} %get-tuple-element.34.mask, f32[1024,1]{1,0:T(8,128)S(1)} %get-tuple-element.35.norms, f32[2,1024,256]{2,1,0:T(8,128)S(1)} %get-tuple-element.30.emb, ...), custom_call_target="tpu_custom_call" | custom-call | flops 402653184 | tf_op jit(solution)/shard_map/kernel_own/pallas_call | solution.py:492
  44.4 12.6 %all_to_all.15.parts = f32[16,2,256]{2,1,0:T(2,128)S(1)} all-to-all(f32[16,2,256]{2,1,0:T(2,128)S(1)} %get-tuple-element.42), channel_id=1, replica_groups=mesh['grp'=2,'cell'=16] {'cell'}, dimensions={0} | all-to-all | bytes 65536 | tf_op jit(solution)/shard_map/all_to_all | solution.py:572
  57.0 0.8 sweep.2
  57.8 9.2 %all_to_all.16.parts = f32[16,2,256]{2,1,0:T(2,128)S(1)} all-to-all(f32[16,2,256]{2,1,0:T(2,128)S(1)} %sweep.2), channel_id=1, replica_groups=mesh['grp'=2,'cell'=16] {'cell'}, dimensions={0} | all-to-all | bytes 65536 | tf_op jit(solution)/shard_map/all_to_all | solution.py:572
  67.0 0.8 sweep.3
  67.8 9.2 %all_to_all.17.parts = f32[16,2,256]{2,1,0:T(2,128)S(1)} all-to-all(f32[16,2,256]{2,1,0:T(2,128)S(1)} %get-tuple-element.45), channel_id=1, replica_groups=mesh['grp'=2,'cell'=16] {'cell'}, dimensions={0} | all-to-all | bytes 65536 | tf_op jit(solution)/shard_map/all_to_all | solution.py:573
  77.0 1.5 %finish.1 = (f32[1024,256]{1,0:T(8,128)}, f32[1024,256]{1,0:T(8,128)}, f32[1,256]{1,0:T(1,128)}) custom-call(f32[2,1024,256]{2,1,0:T(8,128)S(1)} %get-tuple-element.44.scaled, f32[16,2,256]{2,1,0:T(2,128)S(1)} %all_to_all.17.parts, f32[8,256]{1,0:T(8,128)S(1)} %get-tuple-element.43.consts), custom_call_target="tpu_custom_call" | custom-call | tf_op jit(solution)/shard_map/finish/pallas_call | solution.py:510
  (6 shorter events, 0.0 us)
Async XLA Ops:
  0.6 7.6 %collective-permute-start = (bf16[128,256]{1,0:T(8,128)(2,1)}, bf16[128,256]{1,0:T(8,128)(2,1)S(1)}, u32[]{:S(2)}, u32[]{:S(2)}) collective-permute-start(bf16[128,256]{1,0:T(8,128)(2,1)} %table.1), channel_id=1, source_target_pairs={{0,12},{1,13},{2,14},{3,15},{4,8},{5,9},{6,10},{7,11},{8,4},{9,5},... | collective-permute-start | bytes 196616 | tf_op jit(solution)/shard_map/ppermute | solution.py:21
  8.3 3.6 %collective-permute-start.1 = (bf16[2,128,256]{2,1,0:T(8,128)(2,1)S(1)}, bf16[2,128,256]{2,1,0:T(8,128)(2,1)S(1)}, u32[]{:S(2)}, u32[]{:S(2)}) collective-permute-start(bf16[2,128,256]{2,1,0:T(8,128)(2,1)S(1)} %stack.1.even), channel_id=1, source_target_pairs={{0,1},{1,0},{2,3},{3,2},{4,5},{5,4},{6,7},{7,6},{8,9},{9,8},{10,11... | collective-permute-start | bytes 393224 | tf_op jit(solution)/shard_map/ppermute | solution.py:21
  8.3 8.3 %collective-permute-start.2 = (bf16[2,128,256]{2,1,0:T(8,128)(2,1)S(1)}, bf16[2,128,256]{2,1,0:T(8,128)(2,1)S(1)}, u32[]{:S(2)}, u32[]{:S(2)}) collective-permute-start(bf16[2,128,256]{2,1,0:T(8,128)(2,1)S(1)} %stack.1.even), channel_id=1, source_target_pairs={{0,2},{1,3},{2,0},{3,1},{4,6},{5,7},{6,4},{7,5},{8,10},{9,11},{10,... | collective-permute-start | bytes 393224 | tf_op jit(solution)/shard_map/ppermute | solution.py:21
  10.2 8.2 %collective-permute-start.6 = (bf16[2,128,256]{2,1,0:T(8,128)(2,1)S(1)}, bf16[2,128,256]{2,1,0:T(8,128)(2,1)S(1)}, u32[]{:S(2)}, u32[]{:S(2)}) collective-permute-start(bf16[2,128,256]{2,1,0:T(8,128)(2,1)S(1)} %stack.1.even), channel_id=1, source_target_pairs={{0,6},{1,7},{2,4},{3,5},{4,2},{5,3},{6,0},{7,1},{8,14},{9,15},{10,... | collective-permute-start | bytes 393224 | tf_op jit(solution)/shard_map/ppermute | solution.py:21
  10.9 7.4 %collective-permute-start.4 = (bf16[2,128,256]{2,1,0:T(8,128)(2,1)S(1)}, bf16[2,128,256]{2,1,0:T(8,128)(2,1)S(1)}, u32[]{:S(2)}, u32[]{:S(2)}) collective-permute-start(bf16[2,128,256]{2,1,0:T(8,128)(2,1)S(1)} %stack.1.even), channel_id=1, source_target_pairs={{0,4},{1,5},{2,6},{3,7},{4,0},{5,1},{6,2},{7,3},{8,12},{9,13},{10,... | collective-permute-start | bytes 393224 | tf_op jit(solution)/shard_map/ppermute | solution.py:21
  16.7 2.3 %collective-permute-start.3 = (bf16[2,128,256]{2,1,0:T(8,128)(2,1)S(1)}, bf16[2,128,256]{2,1,0:T(8,128)(2,1)S(1)}, u32[]{:S(2)}, u32[]{:S(2)}) collective-permute-start(bf16[2,128,256]{2,1,0:T(8,128)(2,1)S(1)} %gate.3.even), channel_id=1, source_target_pairs={{0,1},{1,0},{2,3},{3,2},{4,5},{5,4},{6,7},{7,6},{8,9},{9,8},{10,11... | collective-permute-start | bytes 393224 | tf_op jit(solution)/shard_map/ppermute | solution.py:21
  18.3 1.4 %collective-permute-start.5 = (bf16[2,128,256]{2,1,0:T(8,128)(2,1)S(1)}, bf16[2,128,256]{2,1,0:T(8,128)(2,1)S(1)}, u32[]{:S(2)}, u32[]{:S(2)}) collective-permute-start(bf16[2,128,256]{2,1,0:T(8,128)(2,1)S(1)} %gate.4.even), channel_id=1, source_target_pairs={{0,1},{1,0},{2,3},{3,2},{4,5},{5,4},{6,7},{7,6},{8,9},{9,8},{10,11... | collective-permute-start | bytes 393224 | tf_op jit(solution)/shard_map/ppermute | solution.py:21
  18.4 2.0 %collective-permute-start.7 = (bf16[2,128,256]{2,1,0:T(8,128)(2,1)S(1)}, bf16[2,128,256]{2,1,0:T(8,128)(2,1)S(1)}, u32[]{:S(2)}, u32[]{:S(2)}) collective-permute-start(bf16[2,128,256]{2,1,0:T(8,128)(2,1)S(1)} %gate.5.even), channel_id=1, source_target_pairs={{0,1},{1,0},{2,3},{3,2},{4,5},{5,4},{6,7},{7,6},{8,9},{9,8},{10,11... | collective-permute-start | bytes 393224 | tf_op jit(solution)/shard_map/ppermute | solution.py:21
  20.4 0.7 copy-start.1
  22.1 19.7 %copy-start = (f32[256]{0:T(256)S(1)}, f32[256]{0:T(256)}, u32[]{:S(2)}) copy-start(f32[256]{0:T(256)} %param.12) | copy-start | bytes 3076
  22.1 1.6 %collective-permute-start.8 = (f32[264,256]{1,0:T(8,128)S(1)}, f32[264,256]{1,0:T(8,128)S(1)}, u32[]{:S(2)}, u32[]{:S(2)}) collective-permute-start(f32[264,256]{1,0:T(8,128)S(1)} %get-tuple-element.37), channel_id=1, source_target_pairs={{0,1},{1,0},{2,3},{3,2},{4,5},{5,4},{6,7},{7,6},{8,9},{9,8},{10,11... | collective-permute-start | bytes 811016 | tf_op jit(solution)/shard_map/ppermute | solution.py:21
  23.8 7.5 %collective-permute-start.11 = (bf16[272,256]{1,0:T(8,128)(2,1)S(1)}, bf16[272,256]{1,0:T(8,128)(2,1)S(1)}, u32[]{:S(2)}, u32[]{:S(2)}) collective-permute-start(bf16[272,256]{1,0:T(8,128)(2,1)S(1)} %pack_pair.1.refs_0_), channel_id=1, source_target_pairs={{0,6},{1,7},{2,4},{3,5},{4,2},{5,3},{6,0},{7,1},{8,14},{9,15},{10,... | collective-permute-start | bytes 417800 | tf_op jit(solution)/shard_map/ppermute | solution.py:21
  25.9 7.9 %collective-permute-start.10 = (bf16[272,256]{1,0:T(8,128)(2,1)S(1)}, bf16[272,256]{1,0:T(8,128)(2,1)S(1)}, u32[]{:S(2)}, u32[]{:S(2)}) collective-permute-start(bf16[272,256]{1,0:T(8,128)(2,1)S(1)} %pack_pair.1.refs_0_), channel_id=1, source_target_pairs={{0,4},{1,5},{2,6},{3,7},{4,0},{5,1},{6,2},{7,3},{8,12},{9,13},{10,... | collective-permute-start | bytes 417800 | tf_op jit(solution)/shard_map/ppermute | solution.py:21
  27.1 6.7 %collective-permute-start.9 = (bf16[272,256]{1,0:T(8,128)(2,1)S(1)}, bf16[272,256]{1,0:T(8,128)(2,1)S(1)}, u32[]{:S(2)}, u32[]{:S(2)}) collective-permute-start(bf16[272,256]{1,0:T(8,128)(2,1)S(1)} %pack_pair.1.refs_0_), channel_id=1, source_target_pairs={{0,2},{1,3},{2,0},{3,1},{4,6},{5,7},{6,4},{7,5},{8,10},{9,11},{10,... | collective-permute-start | bytes 417800 | tf_op jit(solution)/shard_map/ppermute | solution.py:21
  33.9 7.5 %collective-permute-start.12 = (bf16[304,256]{1,0:T(8,128)(2,1)S(1)}, bf16[304,256]{1,0:T(8,128)(2,1)S(1)}, u32[]{:S(2)}, u32[]{:S(2)}) collective-permute-start(bf16[304,256]{1,0:T(8,128)(2,1)S(1)} %merge.1.refs_0_), channel_id=1, source_target_pairs={{0,12},{1,13},{2,14},{3,15},{4,8},{5,9},{6,10},{7,11},{8,4},{9,5},... | collective-permute-start | bytes 466952 | tf_op jit(solution)/shard_map/ppermute | solution.py:21
  41.7 1.6 %collective-permute-start.13 = (f32[264,256]{1,0:T(8,128)S(1)}, f32[264,256]{1,0:T(8,128)S(1)}, u32[]{:S(2)}, u32[]{:S(2)}) collective-permute-start(f32[264,256]{1,0:T(8,128)S(1)} %total.1.mine), channel_id=1, source_target_pairs={{0,1},{1,0},{2,3},{3,2},{4,5},{5,4},{6,7},{7,6},{8,9},{9,8},{10,11... | collective-permute-start | bytes 811016 | tf_op jit(solution)/shard_map/ppermute | solution.py:21

commit v8 on v7

--- a/solution.py
+++ b/solution.py
@@ -12,6 +12,7 @@
 STEPS = 4
 
 step_size = 1.0
+LOG2_E = 1.4426950408889634
 f32 = jnp.float32
 bf16 = jnp.bfloat16
 LIMIT = 16 * 1024 * 1024
@@ -26,10 +27,14 @@
     return upper, (value - upper.astype(f32)).astype(bf16)
 
 
-def dot3(a, b, left, right):
-    dims = (((left,), (right,)), ((), ()))
-    dot = functools.partial(lax.dot_general, dimension_numbers=dims, preferred_element_type=f32)
-    return dot(a[0], b[0]) + (dot(a[0], b[1]) + dot(a[1], b[0]))
+def stacked_left(value):
+    upper, lower = halves(value)
+    return jnp.concatenate([upper, upper, lower], axis=1)
+
+
+def stacked_right(value):
+    upper, lower = halves(value)
+    return jnp.concatenate([upper, lower, upper])
 
 
 VMEM = pl.BlockSpec(memory_space=pltpu.VMEM)
@@ -83,7 +88,7 @@
     rank = qs.shape[1]
     for t in range(2):
         copies[t].wait()
-        factor = q_out[t] / rank
+        factor = q_out[t] * (1.0 / rank)
         totals[t] = jnp.sum(factor, axis=0, keepdims=True)
         turned[t] = factor.T.astype(bf16)
     copies[2].wait()
@@ -179,65 +184,67 @@
     )(value, after)
 
 
-def next_kernel(at, place, x, part, even, odd, out, *sums):
-    me = place[0]
-    tables = [joined_table(me, j, even, odd) for j in range(even.shape[0])]
+def added_products(me, x, t, at, even, odd, value):
+    for j in range(even.shape[0]):
+        table = joined_table(me, j, even, odd)
+        value = value + jnp.dot(x[t, at + j], table, preferred_element_type=f32)
+    return value
+
+
+def next_kernel(at, place, x, part, even, odd, out):
     for t in range(2):
-        value = part[t]
-        for j, table in enumerate(tables):
-            value = value + jnp.dot(x[t, at + j], table, preferred_element_type=f32)
-        out[t] = value
-        for ref in sums:
-            ref[t] = fold(value)
-
-
-def next_share(at, last, place, x, part, even, odd):
-    _, rows, dim = part.shape
-    sums = [array((2, 8, dim))] if last else []
-    return call(
-        functools.partial(next_kernel, at), "embed_next", [SMEM] + [VMEM] * 4, [VMEM] * (1 + len(sums)),
-        [array(part.shape)] + sums,
+        out[t] = added_products(place[0], x, t, at, even, odd, part[t])
+
+
+def next_share(at, place, x, part, even, odd):
+    return call(
+        functools.partial(next_kernel, at), "embed_next", [SMEM] + [VMEM] * 4, VMEM, array(part.shape),
         cost=pl.CostEstimate(
-            flops=16 * rows * dim * even.shape[1], bytes_accessed=0, transcendentals=0
+            flops=16 * part.shape[1] * part.shape[2] * even.shape[1], bytes_accessed=0, transcendentals=0
         ),
     )(place, x, part, even, odd)
 
 
-def whole_kernel(masks, place, xs, xt, pieces, part, sums, table):
+def whole_kernel(masks, place, xs, xt, pieces, part, table):
     genes = pieces.shape[1]
     for j, mask in enumerate(masks):
         start = pl.multiple_of((place[0] ^ mask) * genes, genes)
         table[pl.ds(start, genes), :] = pieces[j]
     for t, x in enumerate((xs, xt)):
-        value = jnp.dot(x[...], table[...], preferred_element_type=f32)
-        part[t] = value
-        sums[t] = fold(value)
+        part[t] = jnp.dot(x[...], table[...], preferred_element_type=f32)
 
 
 def whole_product(place, xs, xt, masks, pieces):
     rows, genes = xs.shape
     dim = pieces.shape[2]
     return call(
-        functools.partial(whole_kernel, masks), "embed_whole", [SMEM] + [VMEM] * 3, [VMEM] * 2,
-        [array((2, rows, dim)), array((2, 8, dim))], [pltpu.VMEM((genes, dim), bf16)],
+        functools.partial(whole_kernel, masks), "embed_whole", [SMEM] + [VMEM] * 3, VMEM,
+        array((2, rows, dim)), [pltpu.VMEM((genes, dim), bf16)],
     )(place, xs, xt, pieces)
 
 
-def cross_kernel(flip, place, live, emb, sums, q, turned, totals, out, norms, *masks):
+def cross_kernel(flip, at, place, live, part, q, turned, totals, *refs):
+    if at is not None:
+        (x, even, odd), refs = refs[:3], refs[3:]
+    emb, out, norms, *masks = refs
     t = (place[0] & 1) ^ flip
     _, rows, rank = q.shape
     block = rows // STEPS
-    mean = (jnp.sum(sums[t], axis=0, keepdims=True) / rows).astype(bf16).astype(f32)
+    value = part[t]
+    if at is not None:
+        value = added_products(place[0], x, t, at, even, odd, value)
+    emb[...] = value
+    mean = (jnp.sum(fold(value), axis=0, keepdims=True) / rows).astype(bf16).astype(f32)
     norm_sum = rest = None
     for step in range(STEPS):
-        at = slice(step * block, (step + 1) * block)
-        value = emb[t, at, :]
+        span = slice(step * block, (step + 1) * block)
+        value = emb[span, :]
         centred = (value - mean).astype(bf16)
-        rest = add_to(rest, jnp.dot(turned[t, :, at], centred, preferred_element_type=f32))
+        rest = add_to(rest, jnp.dot(turned[t, :, span], centred, preferred_element_type=f32))
         squares = jnp.sum(value * value, axis=1, keepdims=True)
-        norms[at, :] = squares
-        norm_sum = add_to(norm_sum, fold(squares * q[t, at, :]))
-    norm_sum = jnp.sum(norm_sum, axis=0, keepdims=True) / rank
+        norms[span, :] = squares
+        norm_sum = add_to(norm_sum, fold(squares * q[t, span, :]))
+    norm_sum = jnp.sum(norm_sum, axis=0, keepdims=True) * (1.0 / rank)
     lane = lax.broadcasted_iota(jnp.int32, (1, rank), 1)
     number = jnp.where(lane < rank // 2, live[0], live[1]).astype(f32)
     out[0:rank, :] = rest
@@ -247,15 +254,16 @@
             mask[i] = (lax.broadcasted_iota(jnp.int32, (rows, 1), 0) < live[i]).astype(f32)
 
 
-def cross(flip, place, live, emb, sums, q, turned, totals):
+def cross(flip, at, place, live, part, q, turned, totals, *rest):
     _, rows, rank = q.shape
-    dim = emb.shape[2]
+    dim = part.shape[2]
     masks = [] if flip else [array((2, rows, 1))]
     return call(
-        functools.partial(cross_kernel, flip), "cross", [SMEM] * 2 + [VMEM] * 5,
-        [VMEM] * (2 + len(masks)), [array((rank + 8, dim)), array((rows, 1))] + masks,
+        functools.partial(cross_kernel, flip, at), "cross", [SMEM] * 2 + [VMEM] * (4 + len(rest)),
+        [VMEM] * (3 + len(masks)),
+        [array((rows, dim)), array((rank + 8, dim)), array((rows, 1))] + masks,
         cost=pl.CostEstimate(flops=2 * rank * dim * q.shape[1], bytes_accessed=0, transcendentals=0),
-    )(place, live, emb, sums, *near(q, turned), totals)
+    )(place, live, part, *near(q, turned), totals, *rest)
 
 
 def split_row(row):
@@ -375,15 +383,17 @@
 def kernel_half(cells, t, mask, norms, emb, q, weights, summed, k, sums_out):
     _, rows, rank = q.shape
     block = rows // STEPS
-    inverse = 1.0 / (D * (weights[...] * (cells / rank)))
-    matrix = halves((-2.0 * inverse) * summed[0:rank, :].T)
+    inverse = (-step_size * LOG2_E) / (D * (weights[...] * (cells / rank)))
+    matrix = stacked_right((-2.0 * inverse) * summed[0:rank, :].T)
     slope, offset = summed[rank + 1 : rank + 2, :] * inverse, summed[rank : rank + 1, :] * inverse
     sums = None
     for step in range(STEPS):
         at = slice(step * block, (step + 1) * block)
-        value = emb[t, at, :]
-        grad = norms[at, :] * slope + offset + dot3(halves(value), matrix, 1, 0)
-        kernel = (q[t, at, :] / rank) * jnp.exp(-step_size * grad)
+        value = emb[at, :]
+        grad = norms[at, :] * slope + offset + jnp.dot(
+            stacked_left(value), matrix, preferred_element_type=f32
+        )
+        kernel = (q[t, at, :] * (1.0 / rank)) * jnp.exp2(grad)
         k[at, :] = kernel
         scale = mask[t, at, :] / jnp.sum(kernel, axis=1, keepdims=True)
         sums = add_to(sums, fold(scale * kernel))
@@ -440,6 +450,20 @@
     return mass, mass / sum_s, mass / sum_t
 
 
+def row_sums(value):
+    folded = value[:, 0:128]
+    for start in range(128, value.shape[1], 128):
+        folded = folded + value[:, start : start + 128]
+    parts = jnp.concatenate(halves(folded), axis=1)
+    return jnp.dot(parts, jnp.ones((256, 128), bf16), preferred_element_type=f32)
+
+
+def scale_rows(value, scale):
+    return jnp.concatenate(
+        [scale * value[:, i : i + 128] for i in range(0, value.shape[1], 128)], axis=1
+    )
+
+
 def sweep_kernel(last, place, mask, k_own, k_other, parts, consts, *refs):
     copies = refs[-1]
     core = place[0] & 1
@@ -454,8 +478,7 @@
             zip((k_own, k_other), (core, 1 - core), in_order(first, *duals))
         ):
             kernel = k[at, :]
-            weighted = jnp.sum(kernel * dual, axis=1, keepdims=True)
-            scaled = (mask[t, at, :] / weighted) * kernel
+            scaled = scale_rows(kernel, mask[t, at, :] / row_sums(kernel * dual))
             if last:
                 refs[0][t, at, :] = scaled
             sums[i] = add_to(sums[i], fold(scaled))
@@ -483,16 +506,16 @@
 
 def kernels(cells, count, place, mask, norms, emb, q, weights, mine, other):
     _, rows, rank = q.shape
-    dim = emb.shape[2]
+    dim = emb[0].shape[1]
     cost = pl.CostEstimate(flops=6 * rows * rank * dim, bytes_accessed=0, transcendentals=rows * rank)
     k_other, sums_other = call(
         functools.partial(other_kernel, cells), "kernel_other", [SMEM] + [VMEM] * 6, [VMEM] * 2,
         [array((rows, rank)), array((8, rank))], cost=cost,
-    )(place, mask, norms[1], emb, *near(q), weights, mine)
+    )(place, mask, norms[1], emb[1], *near(q), weights, mine)
     k_own, copies, consts = call(
         functools.partial(own_kernel, cells), "kernel_own", [SMEM] + [VMEM] * 8, [VMEM] * 3,
         [array((rows, rank)), array((count, 2, rank)), array((8, rank))], [pltpu.VMEM((8, rank), f32)], cost,
-    )(place, mask, norms[0], emb, *near(q), weights, mine, other, sums_other)
+    )(place, mask, norms[0], emb[0], *near(q), weights, mine, other, sums_other)
     return k_own, k_other, copies, consts
 
 
@@ -540,16 +563,17 @@
             place, source_expr, target_expr, masks, later, stack, swap(stack, count, 1)
         )
         arrived = [gate(piece, emb) for piece in arrived]
-        for i, piece in enumerate(arrived):
-            last = i == len(arrived) - 1
-            emb, *sums = next_share(2 * i, last, place, x, emb, piece, swap(piece, count, 1))
+        for i, piece in enumerate(arrived[:-1]):
+            emb = next_share(2 * i, place, x, emb, piece, swap(piece, count, 1))
+        at, rest = 2 * len(arrived) - 2, (x, arrived[-1], swap(arrived[-1], count, 1))
     else:
         for bit in reversed(bits[:-1]):
             stack = jnp.concatenate([stack, swap(stack, count, bit)])
             masks = masks + [m ^ bit for m in masks]
-        emb, *sums = whole_product(place, source_expr, target_expr, masks, stack)
-    send, norms_other = cross(1, place, live, emb, *sums, q, turned, totals)
-    own, norms_own, mask = cross(0, place, live, emb, *sums, q, turned, totals)
+        emb = whole_product(place, source_expr, target_expr, masks, stack)
+        at, rest = None, ()
+    emb_other, send, norms_other = cross(1, at, place, live, emb, q, turned, totals, *rest)
+    emb_own, own, norms_own, mask = cross(0, at, place, live, emb, q, turned, totals, *rest)
 
     payload = pack_pair(own, swap(send, count, 1))
     cards = 2
@@ -564,7 +588,8 @@
     other = swap(mine, count, 1)
 
     k_own, k_other, copies, consts = kernels(
-        cells, count, place, mask, (norms_own, norms_other), emb, q, weights_prev[None], mine, other
+        cells, count, place, mask, (norms_own, norms_other), (emb_own, emb_other), q,
+        weights_prev[None], mine, other,
     )
     scaled = []
     for step_index in range(1, ITERS):

time: 78.7 us -> 78.1 us (level)
  waiting for transfers between devices: 14.6 us -> 13.5 us
    pallas_call x2, Pallas kernels: 1.96 us -> 3.32 us  [cross(): call(functools.partial(cross_kernel, flip, at), 'cross', [SMEM] * 2 + [VM...]
    ppermute x14, waiting for transfers between devices: 14.6 us -> 13.5 us  [swap(): return lax.ppermute(value, 'cell', [(i, i ^ mask) for i in range(count)])]
    pallas_call x3 -> x2, Pallas kernels: 2.13 us -> 1.42 us  [next_share(): call(functools.partial(next_kernel, at), 'embed_next', [SMEM] + [VMEM] *...]
  transfers between devices with their start and end apart: 14 -> 14, of which waited for: 8 -> 8; matrix products, arithmetic and copies ran while one was open for 0% -> 0% of each run, Pallas kernels for 11% -> 12%
where the time goes in v8:
time: 78.1 us; the launch traced here: 77.9 us
  blocking collectives  31.1 us (40%)
  starting transfers between devices  16.9 us (22%)
  Pallas kernels  15.5 us (20%)
  waiting for transfers between devices  13.5 us (17%)
  between operations  0.85 us (1%)
    all_to_all x2, blocking collectives, on_device(): exchange(copies)  21.9 us
    ppermute x14, starting transfers between devices, swap(): return lax.ppermute(value, 'cell', [(i, i ^ mask) for i in range(count)])  16.9 us
    ppermute x14, waiting for transfers between devices, swap(): return lax.ppermute(value, 'cell', [(i, i ^ mask) for i in range(count)])  13.5 us
    all_to_all x1, blocking collectives, on_device(): out_s, out_t, weights = finish(cells, *scaled, exchange(copies), consts)  9.2 us
    pallas_call x1, Pallas kernels, first_share(): call(functools.partial(first_kernel, masks, later_masks), 'embed_first',...  3.64 us
    pallas_call x2, Pallas kernels, cross(): call(functools.partial(cross_kernel, flip, at), 'cross', [SMEM] * 2 + [VM...  3.32 us
    pallas_call x1, Pallas kernels, fetch(): call(fetch_kernel, 'fetch', [HBM] * 3, [VMEM] * 4, [pltpu.VMEM((2, rows,...  1.79 us
  transfers between devices with their start and end apart: 14, of which 8 were waited for; matrix products, arithmetic and copies ran while one was open for 0% of the time, Pallas kernels for 12%

profile of v8, /device:TPU:0, one launch (start us, length us, event | category | flops | bytes accessed | tf_op | source)
XLA Modules:
  0.0 77.9 jit_solution(8279278198604292570)
XLA Ops:
  0.6 5.1 %collective-permute-start = (bf16[128,256]{1,0:T(8,128)(2,1)}, bf16[128,256]{1,0:T(8,128)(2,1)S(1)}, u32[]{:S(2)}, u32[]{:S(2)}) collective-permute-start(bf16[128,256]{1,0:T(8,128)(2,1)} %table.1), channel_id=1, source_target_pairs={{0,12},{1,13},{2,14},{3,15},{4,8},{5,9},{6,10},{7,11},{8,4},{9,5},... | collective-permute-start | bytes 196616 | tf_op jit(solution)/shard_map/ppermute | solution.py:22
  5.7 1.8 %fetch.1 = (f32[2,1024,256]{2,1,0:T(8,128)S(1)}, bf16[128,256]{1,0:T(8,128)(2,1)S(1)}, bf16[2,256,1024]{2,1,0:T(8,128)(2,1)S(1)}, f32[2,1,256]{2,1,0:T(1,128)S(1)}) custom-call(f32[1024,256]{1,0:T(8,128)} %qs.1, f32[1024,256]{1,0:T(8,128)} %qt.1, bf16[128,256]{1,0:T(8,128)(2,1)} %table.1), custom_call_target="tpu_custom_call" | custom-call | bytes 2097152 | tf_op jit(solution)/shard_map/fetch/pallas_call | solution.py:99
  7.5 0.7 collective-permute-done.refs_1_
  8.3 0.1 collective-permute-start.1
  8.3 1.8 %collective-permute-start.2 = (bf16[2,128,256]{2,1,0:T(8,128)(2,1)S(1)}, bf16[2,128,256]{2,1,0:T(8,128)(2,1)S(1)}, u32[]{:S(2)}, u32[]{:S(2)}) collective-permute-start(bf16[2,128,256]{2,1,0:T(8,128)(2,1)S(1)} %stack.1.even), channel_id=1, source_target_pairs={{0,2},{1,3},{2,0},{3,1},{4,6},{5,7},{6,4},{7,5},{8,10},{9,11},{10,... | collective-permute-start | bytes 393224 | tf_op jit(solution)/shard_map/ppermute | solution.py:22
  10.2 0.8 %collective-permute-start.4 = (bf16[2,128,256]{2,1,0:T(8,128)(2,1)S(1)}, bf16[2,128,256]{2,1,0:T(8,128)(2,1)S(1)}, u32[]{:S(2)}, u32[]{:S(2)}) collective-permute-start(bf16[2,128,256]{2,1,0:T(8,128)(2,1)S(1)} %stack.1.even), channel_id=1, source_target_pairs={{0,4},{1,5},{2,6},{3,7},{4,0},{5,1},{6,2},{7,3},{8,12},{9,13},{10,... | collective-permute-start | bytes 393224 | tf_op jit(solution)/shard_map/ppermute | solution.py:22
  11.0 0.9 %collective-permute-start.6 = (bf16[2,128,256]{2,1,0:T(8,128)(2,1)S(1)}, bf16[2,128,256]{2,1,0:T(8,128)(2,1)S(1)}, u32[]{:S(2)}, u32[]{:S(2)}) collective-permute-start(bf16[2,128,256]{2,1,0:T(8,128)(2,1)S(1)} %stack.1.even), channel_id=1, source_target_pairs={{0,6},{1,7},{2,4},{3,5},{4,2},{5,3},{6,0},{7,1},{8,14},{9,15},{10,... | collective-permute-start | bytes 393224 | tf_op jit(solution)/shard_map/ppermute | solution.py:22
  11.9 0.0 collective-permute-done.1.odd
  11.9 3.6 %embed_first.1 = (f32[2,1024,256]{2,1,0:T(8,128)S(1)}, bf16[2,6,1024,256]{3,2,1,0:T(8,128)(2,1)S(1)}) custom-call(s32[1]{0:T(128)} %bitcast.place, bf16[1024,2048]{1,0:T(8,128)(2,1)} %xs.1, bf16[1024,2048]{1,0:T(8,128)(2,1)} %xt.1, bf16[2,128,256]{2,1,0:T(8,128)(2,1)S(1)} %stack.1.even, bf16[2,128,256]{2,1,0:T(8,128)(2,1)S(1)} %collective-permute-done.1.odd), custom_call_target="tpu_custom_call" | custom-call | flops 1073741824 | bytes 8388608 | tf_op jit(solution)/shard_map/embed_first/pallas_call | solution.py:163
  15.6 0.0 collective-permute-done.2.value
  15.6 0.1 collective-permute-start.3
  15.7 0.8 %collective-permute-done.4.value = bf16[2,128,256]{2,1,0:T(8,128)(2,1)S(1)} collective-permute-done((bf16[2,128,256]{2,1,0:T(8,128)(2,1)S(1)}, bf16[2,128,256]{2,1,0:T(8,128)(2,1)S(1)}, u32[]{:S(2)}, u32[]{:S(2)}) %collective-permute-start.4) | collective-permute-done | bytes 131104 | tf_op jit(solution)/shard_map/ppermute | solution.py:22
  16.5 0.1 collective-permute-start.5
  16.6 1.7 %collective-permute-done.6.value = bf16[2,128,256]{2,1,0:T(8,128)(2,1)S(1)} collective-permute-done((bf16[2,128,256]{2,1,0:T(8,128)(2,1)S(1)}, bf16[2,128,256]{2,1,0:T(8,128)(2,1)S(1)}, u32[]{:S(2)}, u32[]{:S(2)}) %collective-permute-start.6) | collective-permute-done | bytes 131104 | tf_op jit(solution)/shard_map/ppermute | solution.py:22
  18.3 0.1 collective-permute-start.7
  18.3 0.0 collective-permute-done.3.odd
  18.4 0.7 embed_next.2.part
  19.1 0.0 copy-start.1
  19.1 0.0 collective-permute-done.5.odd
  19.1 0.7 embed_next.3.part
  19.8 0.0 collective-permute-done.7.refs_2_
  19.8 0.0 copy-done.1
  19.8 1.6 %cross.3 = (f32[1024,256]{1,0:T(8,128)S(1)}, f32[264,256]{1,0:T(8,128)S(1)}, f32[1024,1]{1,0:T(8,128)S(1)}) custom-call(s32[1]{0:T(128)} %bitcast.place, s32[2]{0:T(128)S(1)} %bitcast.6, f32[2,1024,256]{2,1,0:T(8,128)S(1)} %embed_next.3.part, f32[2,1024,256]{2,1,0:T(8,128)S(1)} %get-tuple-element.30.q, bf16[2,256,1024]{2,1,0:T(8,128)(2,1)S(1)} %get-tuple-element.31.turned, ...), custom_call_target="tpu_custom_call" | custom-call | flops 134217728 | tf_op jit(solution)/shard_map/cross/pallas_call | solution.py:261
  21.4 0.0 copy-start
  21.4 0.6 collective-permute-start.8
  22.0 1.8 %cross.2 = (f32[1024,256]{1,0:T(8,128)S(1)}, f32[264,256]{1,0:T(8,128)S(1)}, f32[1024,1]{1,0:T(8,128)S(1)}, f32[2,1024,1]{2,1,0:T(8,128)S(1)}) custom-call(s32[1]{0:T(128)} %bitcast.place, s32[2]{0:T(128)S(1)} %bitcast.7, f32[2,1024,256]{2,1,0:T(8,128)S(1)} %embed_next.3.part, f32[2,1024,256]{2,1,0:T(8,128)S(1)} %get-tuple-element.30.q, ...), custom_call_target="tpu_custom_call" | custom-call | flops 134217728 | tf_op jit(solution)/shard_map/cross/pallas_call | solution.py:261
  23.7 0.0 collective-permute-done.8.recv
  23.7 0.1 pack_pair.1.refs_0_
  23.8 1.8 %collective-permute-start.9 = (bf16[272,256]{1,0:T(8,128)(2,1)S(1)}, bf16[272,256]{1,0:T(8,128)(2,1)S(1)}, u32[]{:S(2)}, u32[]{:S(2)}) collective-permute-start(bf16[272,256]{1,0:T(8,128)(2,1)S(1)} %pack_pair.1.refs_0_), channel_id=1, source_target_pairs={{0,2},{1,3},{2,0},{3,1},{4,6},{5,7},{6,4},{7,5},{8,10},{9,11},{10,... | collective-permute-start | bytes 417800 | tf_op jit(solution)/shard_map/ppermute | solution.py:22
  25.6 0.8 %collective-permute-start.10 = (bf16[272,256]{1,0:T(8,128)(2,1)S(1)}, bf16[272,256]{1,0:T(8,128)(2,1)S(1)}, u32[]{:S(2)}, u32[]{:S(2)}) collective-permute-start(bf16[272,256]{1,0:T(8,128)(2,1)S(1)} %pack_pair.1.refs_0_), channel_id=1, source_target_pairs={{0,4},{1,5},{2,6},{3,7},{4,0},{5,1},{6,2},{7,3},{8,12},{9,13},{10,... | collective-permute-start | bytes 417800 | tf_op jit(solution)/shard_map/ppermute | solution.py:22
  26.5 0.9 %collective-permute-start.11 = (bf16[272,256]{1,0:T(8,128)(2,1)S(1)}, bf16[272,256]{1,0:T(8,128)(2,1)S(1)}, u32[]{:S(2)}, u32[]{:S(2)}) collective-permute-start(bf16[272,256]{1,0:T(8,128)(2,1)S(1)} %pack_pair.1.refs_0_), channel_id=1, source_target_pairs={{0,6},{1,7},{2,4},{3,5},{4,2},{5,3},{6,0},{7,1},{8,14},{9,15},{10,... | collective-permute-start | bytes 417800 | tf_op jit(solution)/shard_map/ppermute | solution.py:22
  27.4 2.1 %collective-permute-done.9.refs_1_ = bf16[272,256]{1,0:T(8,128)(2,1)S(1)} collective-permute-done((bf16[272,256]{1,0:T(8,128)(2,1)S(1)}, bf16[272,256]{1,0:T(8,128)(2,1)S(1)}, u32[]{:S(2)}, u32[]{:S(2)}) %collective-permute-start.9) | collective-permute-done | bytes 139296 | tf_op jit(solution)/shard_map/ppermute | solution.py:22
  29.5 2.7 %collective-permute-done.10.refs_2_ = bf16[272,256]{1,0:T(8,128)(2,1)S(1)} collective-permute-done((bf16[272,256]{1,0:T(8,128)(2,1)S(1)}, bf16[272,256]{1,0:T(8,128)(2,1)S(1)}, u32[]{:S(2)}, u32[]{:S(2)}) %collective-permute-start.10) | collective-permute-done | bytes 139296 | tf_op jit(solution)/shard_map/ppermute | solution.py:22
  32.2 1.5 %collective-permute-done.11.refs_3_ = bf16[272,256]{1,0:T(8,128)(2,1)S(1)} collective-permute-done((bf16[272,256]{1,0:T(8,128)(2,1)S(1)}, bf16[272,256]{1,0:T(8,128)(2,1)S(1)}, u32[]{:S(2)}, u32[]{:S(2)}) %collective-permute-start.11) | collective-permute-done | bytes 139296 | tf_op jit(solution)/shard_map/ppermute | solution.py:22
  33.7 0.1 merge.1.refs_0_
  33.8 3.8 %collective-permute-start.12 = (bf16[304,256]{1,0:T(8,128)(2,1)S(1)}, bf16[304,256]{1,0:T(8,128)(2,1)S(1)}, u32[]{:S(2)}, u32[]{:S(2)}) collective-permute-start(bf16[304,256]{1,0:T(8,128)(2,1)S(1)} %merge.1.refs_0_), channel_id=1, source_target_pairs={{0,12},{1,13},{2,14},{3,15},{4,8},{5,9},{6,10},{7,11},{8,4},{9,5},... | collective-permute-start | bytes 466952 | tf_op jit(solution)/shard_map/ppermute | solution.py:22
  37.6 3.4 %collective-permute-done.12.refs_1_ = bf16[304,256]{1,0:T(8,128)(2,1)S(1)} collective-permute-done((bf16[304,256]{1,0:T(8,128)(2,1)S(1)}, bf16[304,256]{1,0:T(8,128)(2,1)S(1)}, u32[]{:S(2)}, u32[]{:S(2)}) %collective-permute-start.12) | collective-permute-done | bytes 155680 | tf_op jit(solution)/shard_map/ppermute | solution.py:22
  41.0 0.3 total.1.mine
  41.2 0.1 collective-permute-start.13
  41.3 1.0 %kernel_other.1 = (f32[1024,256]{1,0:T(8,128)S(1)}, f32[8,256]{1,0:T(8,128)S(1)}) custom-call(s32[1]{0:T(128)} %bitcast.place, f32[2,1024,1]{2,1,0:T(8,128)S(1)} %get-tuple-element.32.mask, f32[1024,1]{1,0:T(8,128)S(1)} %get-tuple-element.37.norms, f32[1024,256]{1,0:T(8,128)S(1)} %get-tuple-element.38.emb, f32[2,1024,256]{2,1,0:T(8,128)S(1)} %get-tuple-element.30.q, ...), custom_call_target="tpu_custom_call" | custom-call | flops 402653184 | tf_op jit(solution)/shard_map/kernel_other/pallas_call | solution.py:511
  42.3 0.5 collective-permute-done.13.other
  42.9 1.1 %kernel_own.1 = (f32[1024,256]{1,0:T(8,128)S(1)}, f32[16,2,256]{2,1,0:T(2,128)S(1)}, f32[8,256]{1,0:T(8,128)S(1)}) custom-call(s32[1]{0:T(128)} %bitcast.place, f32[2,1024,1]{2,1,0:T(8,128)S(1)} %get-tuple-element.32.mask, f32[1024,1]{1,0:T(8,128)S(1)} %get-tuple-element.33.norms, f32[1024,256]{1,0:T(8,128)S(1)} %get-tuple-element.34.emb, ...), custom_call_target="tpu_custom_call" | custom-call | flops 402653184 | tf_op jit(solution)/shard_map/kernel_own/pallas_call | solution.py:515
  44.0 12.7 %all_to_all.15.parts = f32[16,2,256]{2,1,0:T(2,128)S(1)} all-to-all(f32[16,2,256]{2,1,0:T(2,128)S(1)} %get-tuple-element.42), channel_id=1, replica_groups=mesh['grp'=2,'cell'=16] {'cell'}, dimensions={0} | all-to-all | bytes 65536 | tf_op jit(solution)/shard_map/all_to_all | solution.py:597
  56.7 0.7 sweep.2
  57.4 9.2 %all_to_all.16.parts = f32[16,2,256]{2,1,0:T(2,128)S(1)} all-to-all(f32[16,2,256]{2,1,0:T(2,128)S(1)} %sweep.2), channel_id=1, replica_groups=mesh['grp'=2,'cell'=16] {'cell'}, dimensions={0} | all-to-all | bytes 65536 | tf_op jit(solution)/shard_map/all_to_all | solution.py:597
  66.6 0.7 sweep.3
  67.2 9.2 %all_to_all.17.parts = f32[16,2,256]{2,1,0:T(2,128)S(1)} all-to-all(f32[16,2,256]{2,1,0:T(2,128)S(1)} %get-tuple-element.45), channel_id=1, replica_groups=mesh['grp'=2,'cell'=16] {'cell'}, dimensions={0} | all-to-all | bytes 65536 | tf_op jit(solution)/shard_map/all_to_all | solution.py:598
  76.4 1.5 %finish.1 = (f32[1024,256]{1,0:T(8,128)}, f32[1024,256]{1,0:T(8,128)}, f32[1,256]{1,0:T(1,128)}) custom-call(f32[2,1024,256]{2,1,0:T(8,128)S(1)} %get-tuple-element.44.scaled, f32[16,2,256]{2,1,0:T(2,128)S(1)} %all_to_all.17.parts, f32[8,256]{1,0:T(8,128)S(1)} %get-tuple-element.43.consts), custom_call_target="tpu_custom_call" | custom-call | tf_op jit(solution)/shard_map/finish/pallas_call | solution.py:533
  (5 shorter events, 0.0 us)
Async XLA Ops:
  0.6 7.6 %collective-permute-start = (bf16[128,256]{1,0:T(8,128)(2,1)}, bf16[128,256]{1,0:T(8,128)(2,1)S(1)}, u32[]{:S(2)}, u32[]{:S(2)}) collective-permute-start(bf16[128,256]{1,0:T(8,128)(2,1)} %table.1), channel_id=1, source_target_pairs={{0,12},{1,13},{2,14},{3,15},{4,8},{5,9},{6,10},{7,11},{8,4},{9,5},... | collective-permute-start | bytes 196616 | tf_op jit(solution)/shard_map/ppermute | solution.py:22
  8.3 3.6 %collective-permute-start.1 = (bf16[2,128,256]{2,1,0:T(8,128)(2,1)S(1)}, bf16[2,128,256]{2,1,0:T(8,128)(2,1)S(1)}, u32[]{:S(2)}, u32[]{:S(2)}) collective-permute-start(bf16[2,128,256]{2,1,0:T(8,128)(2,1)S(1)} %stack.1.even), channel_id=1, source_target_pairs={{0,1},{1,0},{2,3},{3,2},{4,5},{5,4},{6,7},{7,6},{8,9},{9,8},{10,11... | collective-permute-start | bytes 393224 | tf_op jit(solution)/shard_map/ppermute | solution.py:22
  8.3 7.2 %collective-permute-start.2 = (bf16[2,128,256]{2,1,0:T(8,128)(2,1)S(1)}, bf16[2,128,256]{2,1,0:T(8,128)(2,1)S(1)}, u32[]{:S(2)}, u32[]{:S(2)}) collective-permute-start(bf16[2,128,256]{2,1,0:T(8,128)(2,1)S(1)} %stack.1.even), channel_id=1, source_target_pairs={{0,2},{1,3},{2,0},{3,1},{4,6},{5,7},{6,4},{7,5},{8,10},{9,11},{10,... | collective-permute-start | bytes 393224 | tf_op jit(solution)/shard_map/ppermute | solution.py:22
  10.2 6.3 %collective-permute-start.4 = (bf16[2,128,256]{2,1,0:T(8,128)(2,1)S(1)}, bf16[2,128,256]{2,1,0:T(8,128)(2,1)S(1)}, u32[]{:S(2)}, u32[]{:S(2)}) collective-permute-start(bf16[2,128,256]{2,1,0:T(8,128)(2,1)S(1)} %stack.1.even), channel_id=1, source_target_pairs={{0,4},{1,5},{2,6},{3,7},{4,0},{5,1},{6,2},{7,3},{8,12},{9,13},{10,... | collective-permute-start | bytes 393224 | tf_op jit(solution)/shard_map/ppermute | solution.py:22
  11.0 7.3 %collective-permute-start.6 = (bf16[2,128,256]{2,1,0:T(8,128)(2,1)S(1)}, bf16[2,128,256]{2,1,0:T(8,128)(2,1)S(1)}, u32[]{:S(2)}, u32[]{:S(2)}) collective-permute-start(bf16[2,128,256]{2,1,0:T(8,128)(2,1)S(1)} %stack.1.even), channel_id=1, source_target_pairs={{0,6},{1,7},{2,4},{3,5},{4,2},{5,3},{6,0},{7,1},{8,14},{9,15},{10,... | collective-permute-start | bytes 393224 | tf_op jit(solution)/shard_map/ppermute | solution.py:22
  15.6 2.8 %collective-permute-start.3 = (bf16[2,128,256]{2,1,0:T(8,128)(2,1)S(1)}, bf16[2,128,256]{2,1,0:T(8,128)(2,1)S(1)}, u32[]{:S(2)}, u32[]{:S(2)}) collective-permute-start(bf16[2,128,256]{2,1,0:T(8,128)(2,1)S(1)} %gate.3.even), channel_id=1, source_target_pairs={{0,1},{1,0},{2,3},{3,2},{4,5},{5,4},{6,7},{7,6},{8,9},{9,8},{10,11... | collective-permute-start | bytes 393224 | tf_op jit(solution)/shard_map/ppermute | solution.py:22
  16.5 2.6 %collective-permute-start.5 = (bf16[2,128,256]{2,1,0:T(8,128)(2,1)S(1)}, bf16[2,128,256]{2,1,0:T(8,128)(2,1)S(1)}, u32[]{:S(2)}, u32[]{:S(2)}) collective-permute-start(bf16[2,128,256]{2,1,0:T(8,128)(2,1)S(1)} %gate.4.even), channel_id=1, source_target_pairs={{0,1},{1,0},{2,3},{3,2},{4,5},{5,4},{6,7},{7,6},{8,9},{9,8},{10,11... | collective-permute-start | bytes 393224 | tf_op jit(solution)/shard_map/ppermute | solution.py:22
  18.3 1.5 %collective-permute-start.7 = (bf16[2,128,256]{2,1,0:T(8,128)(2,1)S(1)}, bf16[2,128,256]{2,1,0:T(8,128)(2,1)S(1)}, u32[]{:S(2)}, u32[]{:S(2)}) collective-permute-start(bf16[2,128,256]{2,1,0:T(8,128)(2,1)S(1)} %gate.5.refs_1_), channel_id=1, source_target_pairs={{0,1},{1,0},{2,3},{3,2},{4,5},{5,4},{6,7},{7,6},{8,9},{9,8},{10,11... | collective-permute-start | bytes 393224 | tf_op jit(solution)/shard_map/ppermute | solution.py:22
  19.1 0.8 copy-start.1
  21.4 19.9 %copy-start = (f32[256]{0:T(256)S(1)}, f32[256]{0:T(256)}, u32[]{:S(2)}) copy-start(f32[256]{0:T(256)} %param.12) | copy-start | bytes 3076
  21.4 2.3 %collective-permute-start.8 = (f32[264,256]{1,0:T(8,128)S(1)}, f32[264,256]{1,0:T(8,128)S(1)}, u32[]{:S(2)}, u32[]{:S(2)}) collective-permute-start(f32[264,256]{1,0:T(8,128)S(1)} %get-tuple-element.36), channel_id=1, source_target_pairs={{0,1},{1,0},{2,3},{3,2},{4,5},{5,4},{6,7},{7,6},{8,9},{9,8},{10,11... | collective-permute-start | bytes 811016 | tf_op jit(solution)/shard_map/ppermute | solution.py:22
  23.8 5.7 %collective-permute-start.9 = (bf16[272,256]{1,0:T(8,128)(2,1)S(1)}, bf16[272,256]{1,0:T(8,128)(2,1)S(1)}, u32[]{:S(2)}, u32[]{:S(2)}) collective-permute-start(bf16[272,256]{1,0:T(8,128)(2,1)S(1)} %pack_pair.1.refs_0_), channel_id=1, source_target_pairs={{0,2},{1,3},{2,0},{3,1},{4,6},{5,7},{6,4},{7,5},{8,10},{9,11},{10,... | collective-permute-start | bytes 417800 | tf_op jit(solution)/shard_map/ppermute | solution.py:22
  25.6 6.6 %collective-permute-start.10 = (bf16[272,256]{1,0:T(8,128)(2,1)S(1)}, bf16[272,256]{1,0:T(8,128)(2,1)S(1)}, u32[]{:S(2)}, u32[]{:S(2)}) collective-permute-start(bf16[272,256]{1,0:T(8,128)(2,1)S(1)} %pack_pair.1.refs_0_), channel_id=1, source_target_pairs={{0,4},{1,5},{2,6},{3,7},{4,0},{5,1},{6,2},{7,3},{8,12},{9,13},{10,... | collective-permute-start | bytes 417800 | tf_op jit(solution)/shard_map/ppermute | solution.py:22
  26.5 7.3 %collective-permute-start.11 = (bf16[272,256]{1,0:T(8,128)(2,1)S(1)}, bf16[272,256]{1,0:T(8,128)(2,1)S(1)}, u32[]{:S(2)}, u32[]{:S(2)}) collective-permute-start(bf16[272,256]{1,0:T(8,128)(2,1)S(1)} %pack_pair.1.refs_0_), channel_id=1, source_target_pairs={{0,6},{1,7},{2,4},{3,5},{4,2},{5,3},{6,0},{7,1},{8,14},{9,15},{10,... | collective-permute-start | bytes 417800 | tf_op jit(solution)/shard_map/ppermute | solution.py:22
  33.8 7.2 %collective-permute-start.12 = (bf16[304,256]{1,0:T(8,128)(2,1)S(1)}, bf16[304,256]{1,0:T(8,128)(2,1)S(1)}, u32[]{:S(2)}, u32[]{:S(2)}) collective-permute-start(bf16[304,256]{1,0:T(8,128)(2,1)S(1)} %merge.1.refs_0_), channel_id=1, source_target_pairs={{0,12},{1,13},{2,14},{3,15},{4,8},{5,9},{6,10},{7,11},{8,4},{9,5},... | collective-permute-start | bytes 466952 | tf_op jit(solution)/shard_map/ppermute | solution.py:22
  41.2 1.6 %collective-permute-start.13 = (f32[264,256]{1,0:T(8,128)S(1)}, f32[264,256]{1,0:T(8,128)S(1)}, u32[]{:S(2)}, u32[]{:S(2)}) collective-permute-start(f32[264,256]{1,0:T(8,128)S(1)} %total.1.mine), channel_id=1, source_target_pairs={{0,1},{1,0},{2,3},{3,2},{4,5},{5,4},{6,7},{7,6},{8,9},{9,8},{10,11... | collective-permute-start | bytes 811016 | tf_op jit(solution)/shard_map/ppermute | solution.py:22

commit v9 on v8

--- a/solution.py
+++ b/solution.py
@@ -556,7 +556,7 @@
     stack = stack_pieces([own_table, swap(loadings, count, opposite)], [totals])
     masks = [0, opposite]
     if count == 16 and loadings.shape[0] % 64 == 0:
-        quad = [2, 4, 6]
+        quad = [6, 4, 2]
         arrived = [swap(stack, count, m) for m in quad]
         later = [m ^ q for q in quad for m in masks]
         emb, x = first_share(
@@ -581,7 +581,8 @@
     while inner:
         used, inner = inner[:2], inner[2:]
         steps = [used[0], used[1], used[0] | used[1]] if len(used) == 2 else used
-        others = [swap(payload, count, m) for m in steps]
+        moved = {m: swap(payload, count, m) for m in steps[1:2] + steps[:1] + steps[2:]}
+        others = [moved[m] for m in steps]
         payload = merge(rank, cards, used, place, payload, *others)
         cards = cards * (1 + len(others))
     mine = total(rank, cards, payload, swap(payload, count, opposite))

time: 78.1 us -> 77.9 us (level)
  blocking collectives: 31.1 us -> 30.3 us
    all_to_all x2, blocking collectives: 21.9 us -> 21.1 us  [on_device(): exchange(copies)]
where the time goes in v9:
time: 77.9 us; the launch traced here: 77.6 us
  blocking collectives  30.3 us (39%)
  starting transfers between devices  16.9 us (22%)
  Pallas kernels  15.5 us (20%)
  waiting for transfers between devices  14.1 us (18%)
  between operations  0.83 us (1%)
    all_to_all x2, blocking collectives, on_device(): exchange(copies)  21.1 us
    ppermute x14, starting transfers between devices, swap(): return lax.ppermute(value, 'cell', [(i, i ^ mask) for i in range(count)])  16.9 us
    ppermute x14, waiting for transfers between devices, swap(): return lax.ppermute(value, 'cell', [(i, i ^ mask) for i in range(count)])  14.1 us
    all_to_all x1, blocking collectives, on_device(): out_s, out_t, weights = finish(cells, *scaled, exchange(copies), consts)  9.2 us
    pallas_call x1, Pallas kernels, first_share(): call(functools.partial(first_kernel, masks, later_masks), 'embed_first',...  3.64 us
    pallas_call x2, Pallas kernels, cross(): call(functools.partial(cross_kernel, flip, at), 'cross', [SMEM] * 2 + [VM...  3.32 us
    pallas_call x1, Pallas kernels, fetch(): call(fetch_kernel, 'fetch', [HBM] * 3, [VMEM] * 4, [pltpu.VMEM((2, rows,...  1.79 us
  transfers between devices with their start and end apart: 14, of which 8 were waited for; matrix products, arithmetic and copies ran while one was open for 0% of the time, Pallas kernels for 12%

profile of v9, /device:TPU:0, one launch (start us, length us, event | category | flops | bytes accessed | tf_op | source)
XLA Modules:
  0.0 77.6 jit_solution(13848082036972481823)
XLA Ops:
  0.6 5.1 %collective-permute-start = (bf16[128,256]{1,0:T(8,128)(2,1)}, bf16[128,256]{1,0:T(8,128)(2,1)S(1)}, u32[]{:S(2)}, u32[]{:S(2)}) collective-permute-start(bf16[128,256]{1,0:T(8,128)(2,1)} %table.1), channel_id=1, source_target_pairs={{0,12},{1,13},{2,14},{3,15},{4,8},{5,9},{6,10},{7,11},{8,4},{9,5},... | collective-permute-start | bytes 196616 | tf_op jit(solution)/shard_map/ppermute | solution.py:22
  5.7 1.8 %fetch.1 = (f32[2,1024,256]{2,1,0:T(8,128)S(1)}, bf16[128,256]{1,0:T(8,128)(2,1)S(1)}, bf16[2,256,1024]{2,1,0:T(8,128)(2,1)S(1)}, f32[2,1,256]{2,1,0:T(1,128)S(1)}) custom-call(f32[1024,256]{1,0:T(8,128)} %qs.1, f32[1024,256]{1,0:T(8,128)} %qt.1, bf16[128,256]{1,0:T(8,128)(2,1)} %table.1), custom_call_target="tpu_custom_call" | custom-call | bytes 2097152 | tf_op jit(solution)/shard_map/fetch/pallas_call | solution.py:99
  7.5 0.7 collective-permute-done.refs_1_
  8.3 0.1 collective-permute-start.1
  8.3 2.1 %collective-permute-start.2 = (bf16[2,128,256]{2,1,0:T(8,128)(2,1)S(1)}, bf16[2,128,256]{2,1,0:T(8,128)(2,1)S(1)}, u32[]{:S(2)}, u32[]{:S(2)}) collective-permute-start(bf16[2,128,256]{2,1,0:T(8,128)(2,1)S(1)} %stack.1.even), channel_id=1, source_target_pairs={{0,6},{1,7},{2,4},{3,5},{4,2},{5,3},{6,0},{7,1},{8,14},{9,15},{10,... | collective-permute-start | bytes 393224 | tf_op jit(solution)/shard_map/ppermute | solution.py:22
  10.4 1.2 %collective-permute-start.4 = (bf16[2,128,256]{2,1,0:T(8,128)(2,1)S(1)}, bf16[2,128,256]{2,1,0:T(8,128)(2,1)S(1)}, u32[]{:S(2)}, u32[]{:S(2)}) collective-permute-start(bf16[2,128,256]{2,1,0:T(8,128)(2,1)S(1)} %stack.1.even), channel_id=1, source_target_pairs={{0,4},{1,5},{2,6},{3,7},{4,0},{5,1},{6,2},{7,3},{8,12},{9,13},{10,... | collective-permute-start | bytes 393224 | tf_op jit(solution)/shard_map/ppermute | solution.py:22
  11.6 0.3 collective-permute-start.6
  11.9 0.0 collective-permute-done.1.odd
  11.9 3.6 %embed_first.1 = (f32[2,1024,256]{2,1,0:T(8,128)S(1)}, bf16[2,6,1024,256]{3,2,1,0:T(8,128)(2,1)S(1)}) custom-call(s32[1]{0:T(128)} %bitcast.place, bf16[1024,2048]{1,0:T(8,128)(2,1)} %xs.1, bf16[1024,2048]{1,0:T(8,128)(2,1)} %xt.1, bf16[2,128,256]{2,1,0:T(8,128)(2,1)S(1)} %stack.1.even, bf16[2,128,256]{2,1,0:T(8,128)(2,1)S(1)} %collective-permute-done.1.odd), custom_call_target="tpu_custom_call" | custom-call | flops 1073741824 | bytes 8388608 | tf_op jit(solution)/shard_map/embed_first/pallas_call | solution.py:163
  15.6 0.1 collective-permute-done.2.value
  15.6 0.1 collective-permute-start.3
  15.7 2.6 %collective-permute-done.4.value = bf16[2,128,256]{2,1,0:T(8,128)(2,1)S(1)} collective-permute-done((bf16[2,128,256]{2,1,0:T(8,128)(2,1)S(1)}, bf16[2,128,256]{2,1,0:T(8,128)(2,1)S(1)}, u32[]{:S(2)}, u32[]{:S(2)}) %collective-permute-start.4) | collective-permute-done | bytes 131104 | tf_op jit(solution)/shard_map/ppermute | solution.py:22
  18.3 0.1 collective-permute-start.5
  18.4 0.0 collective-permute-done.6.value
  18.4 0.5 collective-permute-start.7
  19.0 0.0 collective-permute-done.3.odd
  19.0 0.7 embed_next.2.part
  19.7 0.0 copy-start.1
  19.7 0.0 collective-permute-done.5.odd
  19.7 0.7 embed_next.3.part
  20.4 0.0 collective-permute-done.7.refs_2_
  20.4 0.0 copy-done.1
  20.5 1.6 %cross.3 = (f32[1024,256]{1,0:T(8,128)S(1)}, f32[264,256]{1,0:T(8,128)S(1)}, f32[1024,1]{1,0:T(8,128)S(1)}) custom-call(s32[1]{0:T(128)} %bitcast.place, s32[2]{0:T(128)S(1)} %bitcast.6, f32[2,1024,256]{2,1,0:T(8,128)S(1)} %embed_next.3.part, f32[2,1024,256]{2,1,0:T(8,128)S(1)} %get-tuple-element.30.q, bf16[2,256,1024]{2,1,0:T(8,128)(2,1)S(1)} %get-tuple-element.31.turned, ...), custom_call_target="tpu_custom_call" | custom-call | flops 134217728 | tf_op jit(solution)/shard_map/cross/pallas_call | solution.py:261
  22.0 0.0 copy-start
  22.0 0.2 collective-permute-start.8
  22.3 1.8 %cross.2 = (f32[1024,256]{1,0:T(8,128)S(1)}, f32[264,256]{1,0:T(8,128)S(1)}, f32[1024,1]{1,0:T(8,128)S(1)}, f32[2,1024,1]{2,1,0:T(8,128)S(1)}) custom-call(s32[1]{0:T(128)} %bitcast.place, s32[2]{0:T(128)S(1)} %bitcast.7, f32[2,1024,256]{2,1,0:T(8,128)S(1)} %embed_next.3.part, f32[2,1024,256]{2,1,0:T(8,128)S(1)} %get-tuple-element.30.q, ...), custom_call_target="tpu_custom_call" | custom-call | flops 134217728 | tf_op jit(solution)/shard_map/cross/pallas_call | solution.py:261
  24.0 0.0 collective-permute-done.8.recv
  24.0 0.1 pack_pair.1.refs_0_
  24.1 1.2 %collective-permute-start.9 = (bf16[272,256]{1,0:T(8,128)(2,1)S(1)}, bf16[272,256]{1,0:T(8,128)(2,1)S(1)}, u32[]{:S(2)}, u32[]{:S(2)}) collective-permute-start(bf16[272,256]{1,0:T(8,128)(2,1)S(1)} %pack_pair.1.refs_0_), channel_id=1, source_target_pairs={{0,2},{1,3},{2,0},{3,1},{4,6},{5,7},{6,4},{7,5},{8,10},{9,11},{10,... | collective-permute-start | bytes 417800 | tf_op jit(solution)/shard_map/ppermute | solution.py:22
  25.3 0.8 %collective-permute-start.10 = (bf16[272,256]{1,0:T(8,128)(2,1)S(1)}, bf16[272,256]{1,0:T(8,128)(2,1)S(1)}, u32[]{:S(2)}, u32[]{:S(2)}) collective-permute-start(bf16[272,256]{1,0:T(8,128)(2,1)S(1)} %pack_pair.1.refs_0_), channel_id=1, source_target_pairs={{0,4},{1,5},{2,6},{3,7},{4,0},{5,1},{6,2},{7,3},{8,12},{9,13},{10,... | collective-permute-start | bytes 417800 | tf_op jit(solution)/shard_map/ppermute | solution.py:22
  26.2 1.5 %collective-permute-start.11 = (bf16[272,256]{1,0:T(8,128)(2,1)S(1)}, bf16[272,256]{1,0:T(8,128)(2,1)S(1)}, u32[]{:S(2)}, u32[]{:S(2)}) collective-permute-start(bf16[272,256]{1,0:T(8,128)(2,1)S(1)} %pack_pair.1.refs_0_), channel_id=1, source_target_pairs={{0,6},{1,7},{2,4},{3,5},{4,2},{5,3},{6,0},{7,1},{8,14},{9,15},{10,... | collective-permute-start | bytes 417800 | tf_op jit(solution)/shard_map/ppermute | solution.py:22
  27.7 2.4 %collective-permute-done.9.refs_1_ = bf16[272,256]{1,0:T(8,128)(2,1)S(1)} collective-permute-done((bf16[272,256]{1,0:T(8,128)(2,1)S(1)}, bf16[272,256]{1,0:T(8,128)(2,1)S(1)}, u32[]{:S(2)}, u32[]{:S(2)}) %collective-permute-start.9) | collective-permute-done | bytes 139296 | tf_op jit(solution)/shard_map/ppermute | solution.py:22
  30.1 1.8 %collective-permute-done.10.refs_2_ = bf16[272,256]{1,0:T(8,128)(2,1)S(1)} collective-permute-done((bf16[272,256]{1,0:T(8,128)(2,1)S(1)}, bf16[272,256]{1,0:T(8,128)(2,1)S(1)}, u32[]{:S(2)}, u32[]{:S(2)}) %collective-permute-start.10) | collective-permute-done | bytes 139296 | tf_op jit(solution)/shard_map/ppermute | solution.py:22
  31.9 2.4 %collective-permute-done.11.refs_3_ = bf16[272,256]{1,0:T(8,128)(2,1)S(1)} collective-permute-done((bf16[272,256]{1,0:T(8,128)(2,1)S(1)}, bf16[272,256]{1,0:T(8,128)(2,1)S(1)}, u32[]{:S(2)}, u32[]{:S(2)}) %collective-permute-start.11) | collective-permute-done | bytes 139296 | tf_op jit(solution)/shard_map/ppermute | solution.py:22
  34.3 0.1 merge.1.refs_0_
  34.4 3.6 %collective-permute-start.12 = (bf16[304,256]{1,0:T(8,128)(2,1)S(1)}, bf16[304,256]{1,0:T(8,128)(2,1)S(1)}, u32[]{:S(2)}, u32[]{:S(2)}) collective-permute-start(bf16[304,256]{1,0:T(8,128)(2,1)S(1)} %merge.1.refs_0_), channel_id=1, source_target_pairs={{0,12},{1,13},{2,14},{3,15},{4,8},{5,9},{6,10},{7,11},{8,4},{9,5},... | collective-permute-start | bytes 466952 | tf_op jit(solution)/shard_map/ppermute | solution.py:22
  38.0 3.5 %collective-permute-done.12.refs_1_ = bf16[304,256]{1,0:T(8,128)(2,1)S(1)} collective-permute-done((bf16[304,256]{1,0:T(8,128)(2,1)S(1)}, bf16[304,256]{1,0:T(8,128)(2,1)S(1)}, u32[]{:S(2)}, u32[]{:S(2)}) %collective-permute-start.12) | collective-permute-done | bytes 155680 | tf_op jit(solution)/shard_map/ppermute | solution.py:22
  41.5 0.3 total.1.mine
  41.8 0.1 collective-permute-start.13
  41.9 1.0 %kernel_other.1 = (f32[1024,256]{1,0:T(8,128)S(1)}, f32[8,256]{1,0:T(8,128)S(1)}) custom-call(s32[1]{0:T(128)} %bitcast.place, f32[2,1024,1]{2,1,0:T(8,128)S(1)} %get-tuple-element.32.mask, f32[1024,1]{1,0:T(8,128)S(1)} %get-tuple-element.37.norms, f32[1024,256]{1,0:T(8,128)S(1)} %get-tuple-element.38.emb, f32[2,1024,256]{2,1,0:T(8,128)S(1)} %get-tuple-element.30.q, ...), custom_call_target="tpu_custom_call" | custom-call | flops 402653184 | tf_op jit(solution)/shard_map/kernel_other/pallas_call | solution.py:511
  42.9 0.5 collective-permute-done.13.other
  43.4 1.1 %kernel_own.1 = (f32[1024,256]{1,0:T(8,128)S(1)}, f32[16,2,256]{2,1,0:T(2,128)S(1)}, f32[8,256]{1,0:T(8,128)S(1)}) custom-call(s32[1]{0:T(128)} %bitcast.place, f32[2,1024,1]{2,1,0:T(8,128)S(1)} %get-tuple-element.32.mask, f32[1024,1]{1,0:T(8,128)S(1)} %get-tuple-element.33.norms, f32[1024,256]{1,0:T(8,128)S(1)} %get-tuple-element.34.emb, ...), custom_call_target="tpu_custom_call" | custom-call | flops 402653184 | tf_op jit(solution)/shard_map/kernel_own/pallas_call | solution.py:515
  44.5 11.9 %all_to_all.15.parts = f32[16,2,256]{2,1,0:T(2,128)S(1)} all-to-all(f32[16,2,256]{2,1,0:T(2,128)S(1)} %get-tuple-element.42), channel_id=1, replica_groups=mesh['grp'=2,'cell'=16] {'cell'}, dimensions={0} | all-to-all | bytes 65536 | tf_op jit(solution)/shard_map/all_to_all | solution.py:598
  56.4 0.7 sweep.2
  57.1 9.2 %all_to_all.16.parts = f32[16,2,256]{2,1,0:T(2,128)S(1)} all-to-all(f32[16,2,256]{2,1,0:T(2,128)S(1)} %sweep.2), channel_id=1, replica_groups=mesh['grp'=2,'cell'=16] {'cell'}, dimensions={0} | all-to-all | bytes 65536 | tf_op jit(solution)/shard_map/all_to_all | solution.py:598
  66.3 0.7 sweep.3
  67.0 9.2 %all_to_all.17.parts = f32[16,2,256]{2,1,0:T(2,128)S(1)} all-to-all(f32[16,2,256]{2,1,0:T(2,128)S(1)} %get-tuple-element.45), channel_id=1, replica_groups=mesh['grp'=2,'cell'=16] {'cell'}, dimensions={0} | all-to-all | bytes 65536 | tf_op jit(solution)/shard_map/all_to_all | solution.py:599
  76.2 1.5 %finish.1 = (f32[1024,256]{1,0:T(8,128)}, f32[1024,256]{1,0:T(8,128)}, f32[1,256]{1,0:T(1,128)}) custom-call(f32[2,1024,256]{2,1,0:T(8,128)S(1)} %get-tuple-element.44.scaled, f32[16,2,256]{2,1,0:T(2,128)S(1)} %all_to_all.17.parts, f32[8,256]{1,0:T(8,128)S(1)} %get-tuple-element.43.consts), custom_call_target="tpu_custom_call" | custom-call | tf_op jit(solution)/shard_map/finish/pallas_call | solution.py:533
  (5 shorter events, 0.0 us)
Async XLA Ops:
  0.6 7.6 %collective-permute-start = (bf16[128,256]{1,0:T(8,128)(2,1)}, bf16[128,256]{1,0:T(8,128)(2,1)S(1)}, u32[]{:S(2)}, u32[]{:S(2)}) collective-permute-start(bf16[128,256]{1,0:T(8,128)(2,1)} %table.1), channel_id=1, source_target_pairs={{0,12},{1,13},{2,14},{3,15},{4,8},{5,9},{6,10},{7,11},{8,4},{9,5},... | collective-permute-start | bytes 196616 | tf_op jit(solution)/shard_map/ppermute | solution.py:22
  8.3 3.6 %collective-permute-start.1 = (bf16[2,128,256]{2,1,0:T(8,128)(2,1)S(1)}, bf16[2,128,256]{2,1,0:T(8,128)(2,1)S(1)}, u32[]{:S(2)}, u32[]{:S(2)}) collective-permute-start(bf16[2,128,256]{2,1,0:T(8,128)(2,1)S(1)} %stack.1.even), channel_id=1, source_target_pairs={{0,1},{1,0},{2,3},{3,2},{4,5},{5,4},{6,7},{7,6},{8,9},{9,8},{10,11... | collective-permute-start | bytes 393224 | tf_op jit(solution)/shard_map/ppermute | solution.py:22
  8.3 7.3 %collective-permute-start.2 = (bf16[2,128,256]{2,1,0:T(8,128)(2,1)S(1)}, bf16[2,128,256]{2,1,0:T(8,128)(2,1)S(1)}, u32[]{:S(2)}, u32[]{:S(2)}) collective-permute-start(bf16[2,128,256]{2,1,0:T(8,128)(2,1)S(1)} %stack.1.even), channel_id=1, source_target_pairs={{0,6},{1,7},{2,4},{3,5},{4,2},{5,3},{6,0},{7,1},{8,14},{9,15},{10,... | collective-permute-start | bytes 393224 | tf_op jit(solution)/shard_map/ppermute | solution.py:22
  10.4 7.9 %collective-permute-start.4 = (bf16[2,128,256]{2,1,0:T(8,128)(2,1)S(1)}, bf16[2,128,256]{2,1,0:T(8,128)(2,1)S(1)}, u32[]{:S(2)}, u32[]{:S(2)}) collective-permute-start(bf16[2,128,256]{2,1,0:T(8,128)(2,1)S(1)} %stack.1.even), channel_id=1, source_target_pairs={{0,4},{1,5},{2,6},{3,7},{4,0},{5,1},{6,2},{7,3},{8,12},{9,13},{10,... | collective-permute-start | bytes 393224 | tf_op jit(solution)/shard_map/ppermute | solution.py:22
  11.6 6.8 %collective-permute-start.6 = (bf16[2,128,256]{2,1,0:T(8,128)(2,1)S(1)}, bf16[2,128,256]{2,1,0:T(8,128)(2,1)S(1)}, u32[]{:S(2)}, u32[]{:S(2)}) collective-permute-start(bf16[2,128,256]{2,1,0:T(8,128)(2,1)S(1)} %stack.1.even), channel_id=1, source_target_pairs={{0,2},{1,3},{2,0},{3,1},{4,6},{5,7},{6,4},{7,5},{8,10},{9,11},{10,... | collective-permute-start | bytes 393224 | tf_op jit(solution)/shard_map/ppermute | solution.py:22
  15.6 3.3 %collective-permute-start.3 = (bf16[2,128,256]{2,1,0:T(8,128)(2,1)S(1)}, bf16[2,128,256]{2,1,0:T(8,128)(2,1)S(1)}, u32[]{:S(2)}, u32[]{:S(2)}) collective-permute-start(bf16[2,128,256]{2,1,0:T(8,128)(2,1)S(1)} %gate.3.even), channel_id=1, source_target_pairs={{0,1},{1,0},{2,3},{3,2},{4,5},{5,4},{6,7},{7,6},{8,9},{9,8},{10,11... | collective-permute-start | bytes 393224 | tf_op jit(solution)/shard_map/ppermute | solution.py:22
  18.3 1.4 %collective-permute-start.5 = (bf16[2,128,256]{2,1,0:T(8,128)(2,1)S(1)}, bf16[2,128,256]{2,1,0:T(8,128)(2,1)S(1)}, u32[]{:S(2)}, u32[]{:S(2)}) collective-permute-start(bf16[2,128,256]{2,1,0:T(8,128)(2,1)S(1)} %gate.4.even), channel_id=1, source_target_pairs={{0,1},{1,0},{2,3},{3,2},{4,5},{5,4},{6,7},{7,6},{8,9},{9,8},{10,11... | collective-permute-start | bytes 393224 | tf_op jit(solution)/shard_map/ppermute | solution.py:22
  18.4 2.0 %collective-permute-start.7 = (bf16[2,128,256]{2,1,0:T(8,128)(2,1)S(1)}, bf16[2,128,256]{2,1,0:T(8,128)(2,1)S(1)}, u32[]{:S(2)}, u32[]{:S(2)}) collective-permute-start(bf16[2,128,256]{2,1,0:T(8,128)(2,1)S(1)} %gate.5.refs_1_), channel_id=1, source_target_pairs={{0,1},{1,0},{2,3},{3,2},{4,5},{5,4},{6,7},{7,6},{8,9},{9,8},{10,11... | collective-permute-start | bytes 393224 | tf_op jit(solution)/shard_map/ppermute | solution.py:22
  19.7 0.8 copy-start.1
  22.0 19.8 %copy-start = (f32[256]{0:T(256)S(1)}, f32[256]{0:T(256)}, u32[]{:S(2)}) copy-start(f32[256]{0:T(256)} %param.12) | copy-start | bytes 3076
  22.0 2.0 %collective-permute-start.8 = (f32[264,256]{1,0:T(8,128)S(1)}, f32[264,256]{1,0:T(8,128)S(1)}, u32[]{:S(2)}, u32[]{:S(2)}) collective-permute-start(f32[264,256]{1,0:T(8,128)S(1)} %get-tuple-element.36), channel_id=1, source_target_pairs={{0,1},{1,0},{2,3},{3,2},{4,5},{5,4},{6,7},{7,6},{8,9},{9,8},{10,11... | collective-permute-start | bytes 811016 | tf_op jit(solution)/shard_map/ppermute | solution.py:22
  24.1 6.0 %collective-permute-start.9 = (bf16[272,256]{1,0:T(8,128)(2,1)S(1)}, bf16[272,256]{1,0:T(8,128)(2,1)S(1)}, u32[]{:S(2)}, u32[]{:S(2)}) collective-permute-start(bf16[272,256]{1,0:T(8,128)(2,1)S(1)} %pack_pair.1.refs_0_), channel_id=1, source_target_pairs={{0,2},{1,3},{2,0},{3,1},{4,6},{5,7},{6,4},{7,5},{8,10},{9,11},{10,... | collective-permute-start | bytes 417800 | tf_op jit(solution)/shard_map/ppermute | solution.py:22
  25.3 6.6 %collective-permute-start.10 = (bf16[272,256]{1,0:T(8,128)(2,1)S(1)}, bf16[272,256]{1,0:T(8,128)(2,1)S(1)}, u32[]{:S(2)}, u32[]{:S(2)}) collective-permute-start(bf16[272,256]{1,0:T(8,128)(2,1)S(1)} %pack_pair.1.refs_0_), channel_id=1, source_target_pairs={{0,4},{1,5},{2,6},{3,7},{4,0},{5,1},{6,2},{7,3},{8,12},{9,13},{10,... | collective-permute-start | bytes 417800 | tf_op jit(solution)/shard_map/ppermute | solution.py:22
  26.2 8.1 %collective-permute-start.11 = (bf16[272,256]{1,0:T(8,128)(2,1)S(1)}, bf16[272,256]{1,0:T(8,128)(2,1)S(1)}, u32[]{:S(2)}, u32[]{:S(2)}) collective-permute-start(bf16[272,256]{1,0:T(8,128)(2,1)S(1)} %pack_pair.1.refs_0_), channel_id=1, source_target_pairs={{0,6},{1,7},{2,4},{3,5},{4,2},{5,3},{6,0},{7,1},{8,14},{9,15},{10,... | collective-permute-start | bytes 417800 | tf_op jit(solution)/shard_map/ppermute | solution.py:22
  34.4 7.2 %collective-permute-start.12 = (bf16[304,256]{1,0:T(8,128)(2,1)S(1)}, bf16[304,256]{1,0:T(8,128)(2,1)S(1)}, u32[]{:S(2)}, u32[]{:S(2)}) collective-permute-start(bf16[304,256]{1,0:T(8,128)(2,1)S(1)} %merge.1.refs_0_), channel_id=1, source_target_pairs={{0,12},{1,13},{2,14},{3,15},{4,8},{5,9},{6,10},{7,11},{8,4},{9,5},... | collective-permute-start | bytes 466952 | tf_op jit(solution)/shard_map/ppermute | solution.py:22
  41.8 1.6 %collective-permute-start.13 = (f32[264,256]{1,0:T(8,128)S(1)}, f32[264,256]{1,0:T(8,128)S(1)}, u32[]{:S(2)}, u32[]{:S(2)}) collective-permute-start(f32[264,256]{1,0:T(8,128)S(1)} %total.1.mine), channel_id=1, source_target_pairs={{0,1},{1,0},{2,3},{3,2},{4,5},{5,4},{6,7},{7,6},{8,9},{9,8},{10,11... | collective-permute-start | bytes 811016 | tf_op jit(solution)/shard_map/ppermute | solution.py:22

commit v10 on v9

--- a/solution.py
+++ b/solution.py
@@ -341,9 +341,7 @@
     )(place, *payloads)
 
 
-def total_kernel(rank, cards, *refs):
-    payloads, out = refs[:-1], refs[-1]
-
+def total_of(rank, cards, *payloads):
     def unpack(ref):
         tail = ref[rank:, :].astype(f32)
         heights, means, sums = [], [], jnp.zeros((1, tail.shape[1]), f32)
@@ -359,17 +357,13 @@
         )
         return ref[0:rank, :].astype(f32) + joined, three(tail, 0), sums, three(tail, 3)
 
-    joined = [tree(list(values)) for values in zip(*[unpack(ref) for ref in payloads])]
-    out[0:rank, :] = joined[0]
-    out[rank:, :] = jnp.concatenate(joined[1:] + [jnp.zeros((5, out.shape[1]), f32)])
-
-
-def total(rank, cards, *payloads):
-    dim = payloads[0].shape[1]
-    return call(
-        functools.partial(total_kernel, rank, cards), "total", [VMEM] * len(payloads), VMEM,
-        array((rank + 8, dim)),
-    )(*payloads)
+    return [tree(list(values)) for values in zip(*[unpack(ref) for ref in payloads])]
+
+
+def store_total(parts, out):
+    rank = parts[0].shape[0]
+    out[0:rank, :] = parts[0]
+    out[rank:, :] = jnp.concatenate(parts[1:] + [jnp.zeros((5, out.shape[1]), f32)])
 
 
 def store_sums(sums, levels, copies):
@@ -380,12 +374,13 @@
         copies[i] = both
 
 
-def kernel_half(cells, t, mask, norms, emb, q, weights, summed, k, sums_out):
+def kernel_half(cells, t, mask, norms, emb, q, weights, parts, k, sums_out):
     _, rows, rank = q.shape
     block = rows // STEPS
     inverse = (-step_size * LOG2_E) / (D * (weights[...] * (cells / rank)))
-    matrix = stacked_right((-2.0 * inverse) * summed[0:rank, :].T)
-    slope, offset = summed[rank + 1 : rank + 2, :] * inverse, summed[rank : rank + 1, :] * inverse
+    product, norm, total, _ = parts
+    matrix = stacked_right((-2.0 * inverse) * product.T)
+    slope, offset = total * inverse, norm * inverse
     sums = None
     for step in range(STEPS):
         at = slice(step * block, (step + 1) * block)
@@ -400,8 +395,10 @@
     sums_out[...] = sums
 
 
-def other_kernel(cells, place, mask, norms, emb, q, weights, mine, k, sums):
-    kernel_half(cells, 1 - (place[0] & 1), mask, norms, emb, q, weights, mine, k, sums)
+def other_kernel(cells, cards, place, mask, norms, emb, q, weights, near_part, far_part, k, sums, mine):
+    parts = total_of(q.shape[2], cards, near_part, far_part)
+    store_total(parts, mine)
+    kernel_half(cells, 1 - (place[0] & 1), mask, norms, emb, q, weights, parts, k, sums)
 
 
 def levels_of(cells, summed):
@@ -416,11 +413,11 @@
 
 def write_tables(cells, first, weights, mine, other, consts):
     rank = weights.shape[1]
-    a, b = mine[...], other[...]
+    a = mine[...]
+    product_b, norm_b, total_b, _ = other
     col_mass = weights[...] * (cells / rank)
     norm_a, total_a = a[rank : rank + 1], a[rank + 1 : rank + 2]
-    norm_b, total_b = b[rank : rank + 1], b[rank + 1 : rank + 2]
-    products = jnp.sum((a[0:rank] * b[0:rank]).T, axis=0, keepdims=True)
+    products = jnp.sum((a[0:rank] * product_b).T, axis=0, keepdims=True)
     mixed = in_order(first, norm_a * total_b, total_a * norm_b)
     cost = (mixed[0] + mixed[1] - 2.0 * products) / D
     consts[0:1, :] = col_mass * jnp.exp(step_size * cost / (col_mass * col_mass))
@@ -429,11 +426,13 @@
 
 
 def own_kernel(
-    cells, place, mask, norms, emb, q, weights, mine, other, sums_other, k, copies, consts, sums
+    cells, cards, place, mask, norms, emb, q, weights, mine, near_part, far_part, sums_other,
+    k, copies, consts, sums,
 ):
     core = place[0] & 1
-    write_tables(cells, core == 0, weights, mine, other, consts)
-    kernel_half(cells, core, mask, norms, emb, q, weights, other, k, sums)
+    parts = total_of(q.shape[2], cards, near_part, far_part)
+    write_tables(cells, core == 0, weights, mine, parts, consts)
+    kernel_half(cells, core, mask, norms, emb, q, weights, parts, k, sums)
     store_sums(in_order(core == 0, sums[...], sums_other[...]), levels_of(cells, mine), copies)
 
 
@@ -504,18 +503,18 @@
         copy.wait()
 
 
-def kernels(cells, count, place, mask, norms, emb, q, weights, mine, other):
+def kernels(cells, cards, count, place, mask, norms, emb, q, weights, mine, other):
     _, rows, rank = q.shape
     dim = emb[0].shape[1]
     cost = pl.CostEstimate(flops=6 * rows * rank * dim, bytes_accessed=0, transcendentals=rows * rank)
-    k_other, sums_other = call(
-        functools.partial(other_kernel, cells), "kernel_other", [SMEM] + [VMEM] * 6, [VMEM] * 2,
-        [array((rows, rank)), array((8, rank))], cost=cost,
-    )(place, mask, norms[1], emb[1], *near(q), weights, mine)
+    k_other, sums_other, total = call(
+        functools.partial(other_kernel, cells, cards), "kernel_other", [SMEM] + [VMEM] * 7, [VMEM] * 3,
+        [array((rows, rank)), array((8, rank)), array((rank + 8, dim))], cost=cost,
+    )(place, mask, norms[1], emb[1], *near(q), weights, *mine)
     k_own, copies, consts = call(
-        functools.partial(own_kernel, cells), "kernel_own", [SMEM] + [VMEM] * 8, [VMEM] * 3,
+        functools.partial(own_kernel, cells, cards), "kernel_own", [SMEM] + [VMEM] * 9, [VMEM] * 3,
         [array((rows, rank)), array((count, 2, rank)), array((8, rank))], [pltpu.VMEM((8, rank), f32)], cost,
-    )(place, mask, norms[0], emb[0], *near(q), weights, mine, other, sums_other)
+    )(place, mask, norms[0], emb[0], *near(q), weights, total, *other, sums_other)
     return k_own, k_other, copies, consts
 
 
@@ -585,11 +584,11 @@
         others = [moved[m] for m in steps]
         payload = merge(rank, cards, used, place, payload, *others)
         cards = cards * (1 + len(others))
-    mine = total(rank, cards, payload, swap(payload, count, opposite))
-    other = swap(mine, count, 1)
+    mine = [payload, swap(payload, count, opposite)]
+    other = [swap(part, count, 1) for part in mine]
 
     k_own, k_other, copies, consts = kernels(
-        cells, count, place, mask, (norms_own, norms_other), (emb_own, emb_other), q,
+        cells, cards, count, place, mask, (norms_own, norms_other), (emb_own, emb_other), q,
         weights_prev[None], mine, other,
     )
     scaled = []

time: 77.9 us -> 77.7 us (level)
    pallas_call x3 -> x2, Pallas kernels: 2.35 us -> 2.46 us  [the longest x1 1.23 us: kernels(): call(functools.partial(own_kernel, cells, cards), 'kernel_own', [SMEM] +...]
    ppermute x14 -> x15, waiting for transfers between devices: 14.1 us -> 14.2 us  [swap(): return lax.ppermute(value, 'cell', [(i, i ^ mask) for i in range(count)])]
    ppermute x14 -> x15, starting transfers between devices: 16.9 us -> 16.8 us  [swap(): return lax.ppermute(value, 'cell', [(i, i ^ mask) for i in range(count)])]
  transfers between devices with their start and end apart: 14 -> 15, of which waited for: 8 -> 8; matrix products, arithmetic and copies ran while one was open for 0% -> 0% of each run, Pallas kernels for 12% -> 13%
where the time goes in v10:
time: 77.7 us; the launch traced here: 77.5 us
  blocking collectives  30.1 us (39%)
  starting transfers between devices  16.8 us (22%)
  Pallas kernels  15.6 us (20%)
  waiting for transfers between devices  14.2 us (18%)
  between operations  0.82 us (1%)
    all_to_all x2, blocking collectives, on_device(): exchange(copies)  20.8 us
    ppermute x15, starting transfers between devices, swap(): return lax.ppermute(value, 'cell', [(i, i ^ mask) for i in range(count)])  16.8 us
    ppermute x15, waiting for transfers between devices, swap(): return lax.ppermute(value, 'cell', [(i, i ^ mask) for i in range(count)])  14.2 us
    all_to_all x1, blocking collectives, on_device(): out_s, out_t, weights = finish(cells, *scaled, exchange(copies), consts)  9.2 us
    pallas_call x1, Pallas kernels, first_share(): call(functools.partial(first_kernel, masks, later_masks), 'embed_first',...  3.64 us
    pallas_call x2, Pallas kernels, cross(): call(functools.partial(cross_kernel, flip, at), 'cross', [SMEM] * 2 + [VM...  3.34 us
    pallas_call x1, Pallas kernels, fetch(): call(fetch_kernel, 'fetch', [HBM] * 3, [VMEM] * 4, [pltpu.VMEM((2, rows,...  1.79 us
  transfers between devices with their start and end apart: 15, of which 8 were waited for; matrix products, arithmetic and copies ran while one was open for 0% of the time, Pallas kernels for 13%

profile of v10, /device:TPU:0, one launch (start us, length us, event | category | flops | bytes accessed | tf_op | source)
XLA Modules:
  0.0 77.5 jit_solution(3708947807299649814)
XLA Ops:
  0.6 5.1 %collective-permute-start = (bf16[128,256]{1,0:T(8,128)(2,1)}, bf16[128,256]{1,0:T(8,128)(2,1)S(1)}, u32[]{:S(2)}, u32[]{:S(2)}) collective-permute-start(bf16[128,256]{1,0:T(8,128)(2,1)} %table.1), channel_id=1, source_target_pairs={{0,12},{1,13},{2,14},{3,15},{4,8},{5,9},{6,10},{7,11},{8,4},{9,5},... | collective-permute-start | bytes 196616 | tf_op jit(solution)/shard_map/ppermute | solution.py:22
  5.7 1.8 %fetch.1 = (f32[2,1024,256]{2,1,0:T(8,128)S(1)}, bf16[128,256]{1,0:T(8,128)(2,1)S(1)}, bf16[2,256,1024]{2,1,0:T(8,128)(2,1)S(1)}, f32[2,1,256]{2,1,0:T(1,128)S(1)}) custom-call(f32[1024,256]{1,0:T(8,128)} %qs.1, f32[1024,256]{1,0:T(8,128)} %qt.1, bf16[128,256]{1,0:T(8,128)(2,1)} %table.1), custom_call_target="tpu_custom_call" | custom-call | bytes 2097152 | tf_op jit(solution)/shard_map/fetch/pallas_call | solution.py:99
  7.5 0.7 collective-permute-done.refs_1_
  8.3 0.1 collective-permute-start.1
  8.3 2.1 %collective-permute-start.2 = (bf16[2,128,256]{2,1,0:T(8,128)(2,1)S(1)}, bf16[2,128,256]{2,1,0:T(8,128)(2,1)S(1)}, u32[]{:S(2)}, u32[]{:S(2)}) collective-permute-start(bf16[2,128,256]{2,1,0:T(8,128)(2,1)S(1)} %stack.1.even), channel_id=1, source_target_pairs={{0,6},{1,7},{2,4},{3,5},{4,2},{5,3},{6,0},{7,1},{8,14},{9,15},{10,... | collective-permute-start | bytes 393224 | tf_op jit(solution)/shard_map/ppermute | solution.py:22
  10.4 0.5 collective-permute-start.6
  10.9 1.0 %collective-permute-start.4 = (bf16[2,128,256]{2,1,0:T(8,128)(2,1)S(1)}, bf16[2,128,256]{2,1,0:T(8,128)(2,1)S(1)}, u32[]{:S(2)}, u32[]{:S(2)}) collective-permute-start(bf16[2,128,256]{2,1,0:T(8,128)(2,1)S(1)} %stack.1.even), channel_id=1, source_target_pairs={{0,4},{1,5},{2,6},{3,7},{4,0},{5,1},{6,2},{7,3},{8,12},{9,13},{10,... | collective-permute-start | bytes 393224 | tf_op jit(solution)/shard_map/ppermute | solution.py:22
  11.9 0.0 collective-permute-done.1.odd
  11.9 3.6 %embed_first.1 = (f32[2,1024,256]{2,1,0:T(8,128)S(1)}, bf16[2,6,1024,256]{3,2,1,0:T(8,128)(2,1)S(1)}) custom-call(s32[1]{0:T(128)} %bitcast.place, bf16[1024,2048]{1,0:T(8,128)(2,1)} %xs.1, bf16[1024,2048]{1,0:T(8,128)(2,1)} %xt.1, bf16[2,128,256]{2,1,0:T(8,128)(2,1)S(1)} %stack.1.even, bf16[2,128,256]{2,1,0:T(8,128)(2,1)S(1)} %collective-permute-done.1.odd), custom_call_target="tpu_custom_call" | custom-call | flops 1073741824 | bytes 8388608 | tf_op jit(solution)/shard_map/embed_first/pallas_call | solution.py:163
  15.6 0.1 collective-permute-done.2.value
  15.6 0.1 collective-permute-start.3
  15.7 2.6 %collective-permute-done.4.value = bf16[2,128,256]{2,1,0:T(8,128)(2,1)S(1)} collective-permute-done((bf16[2,128,256]{2,1,0:T(8,128)(2,1)S(1)}, bf16[2,128,256]{2,1,0:T(8,128)(2,1)S(1)}, u32[]{:S(2)}, u32[]{:S(2)}) %collective-permute-start.4) | collective-permute-done | bytes 131104 | tf_op jit(solution)/shard_map/ppermute | solution.py:22
  18.3 0.1 collective-permute-start.5
  18.4 0.0 collective-permute-done.6.value
  18.4 0.5 collective-permute-start.7
  19.0 0.0 collective-permute-done.3.odd
  19.0 0.7 embed_next.2.part
  19.7 0.0 copy-start.1
  19.7 0.0 collective-permute-done.5.odd
  19.7 0.7 embed_next.3.part
  20.4 0.0 collective-permute-done.7.refs_2_
  20.5 1.6 %cross.3 = (f32[1024,256]{1,0:T(8,128)S(1)}, f32[264,256]{1,0:T(8,128)S(1)}, f32[1024,1]{1,0:T(8,128)S(1)}) custom-call(s32[1]{0:T(128)} %bitcast.place, s32[2]{0:T(128)S(1)} %bitcast.6, f32[2,1024,256]{2,1,0:T(8,128)S(1)} %embed_next.3.part, f32[2,1024,256]{2,1,0:T(8,128)S(1)} %get-tuple-element.31.q, bf16[2,256,1024]{2,1,0:T(8,128)(2,1)S(1)} %get-tuple-element.32.turned, ...), custom_call_target="tpu_custom_call" | custom-call | flops 134217728 | tf_op jit(solution)/shard_map/cross/pallas_call | solution.py:261
  22.0 0.0 copy-start
  22.1 0.2 collective-permute-start.8
  22.3 1.8 %cross.2 = (f32[1024,256]{1,0:T(8,128)S(1)}, f32[264,256]{1,0:T(8,128)S(1)}, f32[1024,1]{1,0:T(8,128)S(1)}, f32[2,1024,1]{2,1,0:T(8,128)S(1)}) custom-call(s32[1]{0:T(128)} %bitcast.place, s32[2]{0:T(128)S(1)} %bitcast.7, f32[2,1024,256]{2,1,0:T(8,128)S(1)} %embed_next.3.part, f32[2,1024,256]{2,1,0:T(8,128)S(1)} %get-tuple-element.31.q, ...), custom_call_target="tpu_custom_call" | custom-call | flops 134217728 | tf_op jit(solution)/shard_map/cross/pallas_call | solution.py:261
  24.0 0.0 collective-permute-done.8.recv
  24.0 0.1 pack_pair.1.refs_0_
  24.1 1.2 %collective-permute-start.11 = (bf16[272,256]{1,0:T(8,128)(2,1)S(1)}, bf16[272,256]{1,0:T(8,128)(2,1)S(1)}, u32[]{:S(2)}, u32[]{:S(2)}) collective-permute-start(bf16[272,256]{1,0:T(8,128)(2,1)S(1)} %pack_pair.1.refs_0_), channel_id=1, source_target_pairs={{0,6},{1,7},{2,4},{3,5},{4,2},{5,3},{6,0},{7,1},{8,14},{9,15},{10,... | collective-permute-start | bytes 417800 | tf_op jit(solution)/shard_map/ppermute | solution.py:22
  25.4 1.1 %collective-permute-start.10 = (bf16[272,256]{1,0:T(8,128)(2,1)S(1)}, bf16[272,256]{1,0:T(8,128)(2,1)S(1)}, u32[]{:S(2)}, u32[]{:S(2)}) collective-permute-start(bf16[272,256]{1,0:T(8,128)(2,1)S(1)} %pack_pair.1.refs_0_), channel_id=1, source_target_pairs={{0,4},{1,5},{2,6},{3,7},{4,0},{5,1},{6,2},{7,3},{8,12},{9,13},{10,... | collective-permute-start | bytes 417800 | tf_op jit(solution)/shard_map/ppermute | solution.py:22
  26.4 1.3 %collective-permute-start.9 = (bf16[272,256]{1,0:T(8,128)(2,1)S(1)}, bf16[272,256]{1,0:T(8,128)(2,1)S(1)}, u32[]{:S(2)}, u32[]{:S(2)}) collective-permute-start(bf16[272,256]{1,0:T(8,128)(2,1)S(1)} %pack_pair.1.refs_0_), channel_id=1, source_target_pairs={{0,2},{1,3},{2,0},{3,1},{4,6},{5,7},{6,4},{7,5},{8,10},{9,11},{10,... | collective-permute-start | bytes 417800 | tf_op jit(solution)/shard_map/ppermute | solution.py:22
  27.7 3.9 %collective-permute-done.11.refs_3_ = bf16[272,256]{1,0:T(8,128)(2,1)S(1)} collective-permute-done((bf16[272,256]{1,0:T(8,128)(2,1)S(1)}, bf16[272,256]{1,0:T(8,128)(2,1)S(1)}, u32[]{:S(2)}, u32[]{:S(2)}) %collective-permute-start.11) | collective-permute-done | bytes 139296 | tf_op jit(solution)/shard_map/ppermute | solution.py:22
  31.6 1.4 %collective-permute-done.10.refs_2_ = bf16[272,256]{1,0:T(8,128)(2,1)S(1)} collective-permute-done((bf16[272,256]{1,0:T(8,128)(2,1)S(1)}, bf16[272,256]{1,0:T(8,128)(2,1)S(1)}, u32[]{:S(2)}, u32[]{:S(2)}) %collective-permute-start.10) | collective-permute-done | bytes 139296 | tf_op jit(solution)/shard_map/ppermute | solution.py:22
  33.0 1.0 %collective-permute-done.9.refs_1_ = bf16[272,256]{1,0:T(8,128)(2,1)S(1)} collective-permute-done((bf16[272,256]{1,0:T(8,128)(2,1)S(1)}, bf16[272,256]{1,0:T(8,128)(2,1)S(1)}, u32[]{:S(2)}, u32[]{:S(2)}) %collective-permute-start.9) | collective-permute-done | bytes 139296 | tf_op jit(solution)/shard_map/ppermute | solution.py:22
  34.0 0.1 merge.1.near_part
  34.1 3.6 %collective-permute-start.12 = (bf16[304,256]{1,0:T(8,128)(2,1)S(1)}, bf16[304,256]{1,0:T(8,128)(2,1)S(1)}, u32[]{:S(2)}, u32[]{:S(2)}) collective-permute-start(bf16[304,256]{1,0:T(8,128)(2,1)S(1)} %merge.1.near_part), channel_id=1, source_target_pairs={{0,12},{1,13},{2,14},{3,15},{4,8},{5,9},{6,10},{7,11},{8,4},{9,5},... | collective-permute-start | bytes 466952 | tf_op jit(solution)/shard_map/ppermute | solution.py:22
  37.7 0.0 collective-permute-start.13
  37.7 4.3 %collective-permute-done.12.far_part = bf16[304,256]{1,0:T(8,128)(2,1)S(1)} collective-permute-done((bf16[304,256]{1,0:T(8,128)(2,1)S(1)}, bf16[304,256]{1,0:T(8,128)(2,1)S(1)}, u32[]{:S(2)}, u32[]{:S(2)}) %collective-permute-start.12) | collective-permute-done | bytes 155680 | tf_op jit(solution)/shard_map/ppermute | solution.py:22
  42.0 0.0 collective-permute-start.14
  42.0 1.2 %kernel_other.1 = (f32[1024,256]{1,0:T(8,128)S(1)}, f32[8,256]{1,0:T(8,128)S(1)}, f32[264,256]{1,0:T(8,128)S(1)}) custom-call(s32[1]{0:T(128)} %bitcast.place, f32[2,1024,1]{2,1,0:T(8,128)S(1)} %get-tuple-element.33.mask, f32[1024,1]{1,0:T(8,128)S(1)} %get-tuple-element.36.norms, f32[1024,256]{1,0:T(8,128)S(1)} %get-tuple-element.37.emb, ...), custom_call_target="tpu_custom_call" | custom-call | flops 402653184 | tf_op jit(solution)/shard_map/kernel_other/pallas_call | solution.py:510
  43.3 0.0 collective-permute-done.13.near_part
  43.3 0.1 collective-permute-done.14.far_part
  43.4 1.2 %kernel_own.1 = (f32[1024,256]{1,0:T(8,128)S(1)}, f32[16,2,256]{2,1,0:T(2,128)S(1)}, f32[8,256]{1,0:T(8,128)S(1)}) custom-call(s32[1]{0:T(128)} %bitcast.place, f32[2,1024,1]{2,1,0:T(8,128)S(1)} %get-tuple-element.33.mask, f32[1024,1]{1,0:T(8,128)S(1)} %get-tuple-element.34.norms, f32[1024,256]{1,0:T(8,128)S(1)} %get-tuple-element.35.emb, ...), custom_call_target="tpu_custom_call" | custom-call | flops 402653184 | tf_op jit(solution)/shard_map/kernel_own/pallas_call | solution.py:514
  44.6 11.6 %all_to_all.15.parts = f32[16,2,256]{2,1,0:T(2,128)S(1)} all-to-all(f32[16,2,256]{2,1,0:T(2,128)S(1)} %get-tuple-element.44), channel_id=1, replica_groups=mesh['grp'=2,'cell'=16] {'cell'}, dimensions={0} | all-to-all | bytes 65536 | tf_op jit(solution)/shard_map/all_to_all | solution.py:597
  56.3 0.7 sweep.2
  56.9 9.2 %all_to_all.16.parts = f32[16,2,256]{2,1,0:T(2,128)S(1)} all-to-all(f32[16,2,256]{2,1,0:T(2,128)S(1)} %sweep.2), channel_id=1, replica_groups=mesh['grp'=2,'cell'=16] {'cell'}, dimensions={0} | all-to-all | bytes 65536 | tf_op jit(solution)/shard_map/all_to_all | solution.py:597
  66.2 0.7 sweep.3
  66.8 9.2 %all_to_all.17.parts = f32[16,2,256]{2,1,0:T(2,128)S(1)} all-to-all(f32[16,2,256]{2,1,0:T(2,128)S(1)} %get-tuple-element.47), channel_id=1, replica_groups=mesh['grp'=2,'cell'=16] {'cell'}, dimensions={0} | all-to-all | bytes 65536 | tf_op jit(solution)/shard_map/all_to_all | solution.py:598
  76.0 1.5 %finish.1 = (f32[1024,256]{1,0:T(8,128)}, f32[1024,256]{1,0:T(8,128)}, f32[1,256]{1,0:T(1,128)}) custom-call(f32[2,1024,256]{2,1,0:T(8,128)S(1)} %get-tuple-element.46.scaled, f32[16,2,256]{2,1,0:T(2,128)S(1)} %all_to_all.17.parts, f32[8,256]{1,0:T(8,128)S(1)} %get-tuple-element.45.consts), custom_call_target="tpu_custom_call" | custom-call | tf_op jit(solution)/shard_map/finish/pallas_call | solution.py:532
  (6 shorter events, 0.0 us)
Async XLA Ops:
  0.6 7.6 %collective-permute-start = (bf16[128,256]{1,0:T(8,128)(2,1)}, bf16[128,256]{1,0:T(8,128)(2,1)S(1)}, u32[]{:S(2)}, u32[]{:S(2)}) collective-permute-start(bf16[128,256]{1,0:T(8,128)(2,1)} %table.1), channel_id=1, source_target_pairs={{0,12},{1,13},{2,14},{3,15},{4,8},{5,9},{6,10},{7,11},{8,4},{9,5},... | collective-permute-start | bytes 196616 | tf_op jit(solution)/shard_map/ppermute | solution.py:22
  8.3 3.6 %collective-permute-start.1 = (bf16[2,128,256]{2,1,0:T(8,128)(2,1)S(1)}, bf16[2,128,256]{2,1,0:T(8,128)(2,1)S(1)}, u32[]{:S(2)}, u32[]{:S(2)}) collective-permute-start(bf16[2,128,256]{2,1,0:T(8,128)(2,1)S(1)} %stack.1.even), channel_id=1, source_target_pairs={{0,1},{1,0},{2,3},{3,2},{4,5},{5,4},{6,7},{7,6},{8,9},{9,8},{10,11... | collective-permute-start | bytes 393224 | tf_op jit(solution)/shard_map/ppermute | solution.py:22
  8.3 7.3 %collective-permute-start.2 = (bf16[2,128,256]{2,1,0:T(8,128)(2,1)S(1)}, bf16[2,128,256]{2,1,0:T(8,128)(2,1)S(1)}, u32[]{:S(2)}, u32[]{:S(2)}) collective-permute-start(bf16[2,128,256]{2,1,0:T(8,128)(2,1)S(1)} %stack.1.even), channel_id=1, source_target_pairs={{0,6},{1,7},{2,4},{3,5},{4,2},{5,3},{6,0},{7,1},{8,14},{9,15},{10,... | collective-permute-start | bytes 393224 | tf_op jit(solution)/shard_map/ppermute | solution.py:22
  10.4 8.0 %collective-permute-start.6 = (bf16[2,128,256]{2,1,0:T(8,128)(2,1)S(1)}, bf16[2,128,256]{2,1,0:T(8,128)(2,1)S(1)}, u32[]{:S(2)}, u32[]{:S(2)}) collective-permute-start(bf16[2,128,256]{2,1,0:T(8,128)(2,1)S(1)} %stack.1.even), channel_id=1, source_target_pairs={{0,2},{1,3},{2,0},{3,1},{4,6},{5,7},{6,4},{7,5},{8,10},{9,11},{10,... | collective-permute-start | bytes 393224 | tf_op jit(solution)/shard_map/ppermute | solution.py:22
  10.9 7.4 %collective-permute-start.4 = (bf16[2,128,256]{2,1,0:T(8,128)(2,1)S(1)}, bf16[2,128,256]{2,1,0:T(8,128)(2,1)S(1)}, u32[]{:S(2)}, u32[]{:S(2)}) collective-permute-start(bf16[2,128,256]{2,1,0:T(8,128)(2,1)S(1)} %stack.1.even), channel_id=1, source_target_pairs={{0,4},{1,5},{2,6},{3,7},{4,0},{5,1},{6,2},{7,3},{8,12},{9,13},{10,... | collective-permute-start | bytes 393224 | tf_op jit(solution)/shard_map/ppermute | solution.py:22
  15.6 3.3 %collective-permute-start.3 = (bf16[2,128,256]{2,1,0:T(8,128)(2,1)S(1)}, bf16[2,128,256]{2,1,0:T(8,128)(2,1)S(1)}, u32[]{:S(2)}, u32[]{:S(2)}) collective-permute-start(bf16[2,128,256]{2,1,0:T(8,128)(2,1)S(1)} %gate.3.even), channel_id=1, source_target_pairs={{0,1},{1,0},{2,3},{3,2},{4,5},{5,4},{6,7},{7,6},{8,9},{9,8},{10,11... | collective-permute-start | bytes 393224 | tf_op jit(solution)/shard_map/ppermute | solution.py:22
  18.3 1.4 %collective-permute-start.5 = (bf16[2,128,256]{2,1,0:T(8,128)(2,1)S(1)}, bf16[2,128,256]{2,1,0:T(8,128)(2,1)S(1)}, u32[]{:S(2)}, u32[]{:S(2)}) collective-permute-start(bf16[2,128,256]{2,1,0:T(8,128)(2,1)S(1)} %gate.4.even), channel_id=1, source_target_pairs={{0,1},{1,0},{2,3},{3,2},{4,5},{5,4},{6,7},{7,6},{8,9},{9,8},{10,11... | collective-permute-start | bytes 393224 | tf_op jit(solution)/shard_map/ppermute | solution.py:22
  18.4 2.0 %collective-permute-start.7 = (bf16[2,128,256]{2,1,0:T(8,128)(2,1)S(1)}, bf16[2,128,256]{2,1,0:T(8,128)(2,1)S(1)}, u32[]{:S(2)}, u32[]{:S(2)}) collective-permute-start(bf16[2,128,256]{2,1,0:T(8,128)(2,1)S(1)} %gate.5.refs_1_), channel_id=1, source_target_pairs={{0,1},{1,0},{2,3},{3,2},{4,5},{5,4},{6,7},{7,6},{8,9},{9,8},{10,11... | collective-permute-start | bytes 393224 | tf_op jit(solution)/shard_map/ppermute | solution.py:22
  19.7 0.8 copy-start.1
  22.0 20.0 %copy-start = (f32[256]{0:T(256)S(1)}, f32[256]{0:T(256)}, u32[]{:S(2)}) copy-start(f32[256]{0:T(256)} %param.12) | copy-start | bytes 3076
  22.1 2.0 %collective-permute-start.8 = (f32[264,256]{1,0:T(8,128)S(1)}, f32[264,256]{1,0:T(8,128)S(1)}, u32[]{:S(2)}, u32[]{:S(2)}) collective-permute-start(f32[264,256]{1,0:T(8,128)S(1)} %get-tuple-element.39), channel_id=1, source_target_pairs={{0,1},{1,0},{2,3},{3,2},{4,5},{5,4},{6,7},{7,6},{8,9},{9,8},{10,11... | collective-permute-start | bytes 811016 | tf_op jit(solution)/shard_map/ppermute | solution.py:22
  24.1 7.5 %collective-permute-start.11 = (bf16[272,256]{1,0:T(8,128)(2,1)S(1)}, bf16[272,256]{1,0:T(8,128)(2,1)S(1)}, u32[]{:S(2)}, u32[]{:S(2)}) collective-permute-start(bf16[272,256]{1,0:T(8,128)(2,1)S(1)} %pack_pair.1.refs_0_), channel_id=1, source_target_pairs={{0,6},{1,7},{2,4},{3,5},{4,2},{5,3},{6,0},{7,1},{8,14},{9,15},{10,... | collective-permute-start | bytes 417800 | tf_op jit(solution)/shard_map/ppermute | solution.py:22
  25.4 7.6 %collective-permute-start.10 = (bf16[272,256]{1,0:T(8,128)(2,1)S(1)}, bf16[272,256]{1,0:T(8,128)(2,1)S(1)}, u32[]{:S(2)}, u32[]{:S(2)}) collective-permute-start(bf16[272,256]{1,0:T(8,128)(2,1)S(1)} %pack_pair.1.refs_0_), channel_id=1, source_target_pairs={{0,4},{1,5},{2,6},{3,7},{4,0},{5,1},{6,2},{7,3},{8,12},{9,13},{10,... | collective-permute-start | bytes 417800 | tf_op jit(solution)/shard_map/ppermute | solution.py:22
  26.4 7.6 %collective-permute-start.9 = (bf16[272,256]{1,0:T(8,128)(2,1)S(1)}, bf16[272,256]{1,0:T(8,128)(2,1)S(1)}, u32[]{:S(2)}, u32[]{:S(2)}) collective-permute-start(bf16[272,256]{1,0:T(8,128)(2,1)S(1)} %pack_pair.1.refs_0_), channel_id=1, source_target_pairs={{0,2},{1,3},{2,0},{3,1},{4,6},{5,7},{6,4},{7,5},{8,10},{9,11},{10,... | collective-permute-start | bytes 417800 | tf_op jit(solution)/shard_map/ppermute | solution.py:22
  34.1 7.9 %collective-permute-start.12 = (bf16[304,256]{1,0:T(8,128)(2,1)S(1)}, bf16[304,256]{1,0:T(8,128)(2,1)S(1)}, u32[]{:S(2)}, u32[]{:S(2)}) collective-permute-start(bf16[304,256]{1,0:T(8,128)(2,1)S(1)} %merge.1.near_part), channel_id=1, source_target_pairs={{0,12},{1,13},{2,14},{3,15},{4,8},{5,9},{6,10},{7,11},{8,4},{9,5},... | collective-permute-start | bytes 466952 | tf_op jit(solution)/shard_map/ppermute | solution.py:22
  37.7 5.6 %collective-permute-start.13 = (bf16[304,256]{1,0:T(8,128)(2,1)S(1)}, bf16[304,256]{1,0:T(8,128)(2,1)S(1)}, u32[]{:S(2)}, u32[]{:S(2)}) collective-permute-start(bf16[304,256]{1,0:T(8,128)(2,1)S(1)} %merge.1.near_part), channel_id=1, source_target_pairs={{0,1},{1,0},{2,3},{3,2},{4,5},{5,4},{6,7},{7,6},{8,9},{9,8},{10,11... | collective-permute-start | bytes 466952 | tf_op jit(solution)/shard_map/ppermute | solution.py:22
  42.0 1.4 %collective-permute-start.14 = (bf16[304,256]{1,0:T(8,128)(2,1)S(1)}, bf16[304,256]{1,0:T(8,128)(2,1)S(1)}, u32[]{:S(2)}, u32[]{:S(2)}) collective-permute-start(bf16[304,256]{1,0:T(8,128)(2,1)S(1)} %collective-permute-done.12.far_part), channel_id=1, source_target_pairs={{0,1},{1,0},{2,3},{3,2},{4,5},{5,4},{6,7},{7,6},{8,9},{9,8},{10,11... | collective-permute-start | bytes 466952 | tf_op jit(solution)/shard_map/ppermute | solution.py:22

commit v11 on v10

--- a/solution.py
+++ b/solution.py
@@ -80,8 +80,8 @@
     return value if sums is None else sums + value
 
 
-def fetch_kernel(qs, qt, table, q_out, table_out, turned, totals, sems):
-    pairs = ((qs, q_out.at[0]), (qt, q_out.at[1]), (table, table_out))
+def fetch_kernel(qs, qt, table, live, q_out, table_out, turned, totals, live_held, sems):
+    pairs = ((qs, q_out.at[0]), (qt, q_out.at[1]), (table, table_out), (live, live_held))
     copies = [pltpu.make_async_copy(a, b, sems.at[i]) for i, (a, b) in enumerate(pairs)]
     for copy in copies:
         copy.start()
@@ -92,19 +92,22 @@
         totals[t] = jnp.sum(factor, axis=0, keepdims=True)
         turned[t] = factor.T.astype(bf16)
     copies[2].wait()
-
-
-def fetch(qs, qt, table):
+    copies[3].wait()
+    lane = lax.broadcasted_iota(jnp.int32, (1, rank), 1)
+    totals[2] = jnp.where(lane < rank // 2, live_held[0], live_held[1]).astype(f32)
+
+
+def fetch(qs, qt, table, live):
     rows, rank = qs.shape
     return call(
-        fetch_kernel, "fetch", [HBM] * 3, [VMEM] * 4,
+        fetch_kernel, "fetch", [HBM] * 4, [VMEM] * 4,
         [
             pltpu.VMEM((2, rows, rank), f32), pltpu.VMEM(table.shape, table.dtype),
-            pltpu.VMEM((2, rank, rows), bf16), array((2, 1, rank)),
+            pltpu.VMEM((2, rank, rows), bf16), array((3, 1, rank)),
         ],
-        [pltpu.SemaphoreType.DMA((3,))],
+        [pltpu.SMEM((2,), jnp.int32), pltpu.SemaphoreType.DMA((4,))],
         pl.CostEstimate(flops=0, bytes_accessed=8 * rows * rank, transcendentals=0),
-    )(*far(qs, qt, table))
+    )(*far(qs, qt, table, live))
 
 
 def stack_kernel(*refs):
@@ -223,7 +226,7 @@
     )(place, xs, xt, pieces)
 
 
-def cross_kernel(flip, at, place, live, part, q, turned, totals, *refs):
+def cross_kernel(flip, at, place, part, q, turned, totals, *refs):
     if at is not None:
         (x, even, odd), refs = refs[:3], refs[3:]
     emb, out, norms, *masks = refs
@@ -245,25 +248,25 @@
         norms[span, :] = squares
         norm_sum = add_to(norm_sum, fold(squares * q[t, span, :]))
     norm_sum = jnp.sum(norm_sum, axis=0, keepdims=True) * (1.0 / rank)
-    lane = lax.broadcasted_iota(jnp.int32, (1, rank), 1)
-    number = jnp.where(lane < rank // 2, live[0], live[1]).astype(f32)
+    number = totals[2]
     out[0:rank, :] = rest
     out[rank:, :] = jnp.concatenate([mean, totals[t], norm_sum, number, jnp.zeros((4, rank), f32)])
     for mask in masks:
         for i in range(2):
-            mask[i] = (lax.broadcasted_iota(jnp.int32, (rows, 1), 0) < live[i]).astype(f32)
-
-
-def cross(flip, at, place, live, part, q, turned, totals, *rest):
+            live = number[:, i * (rank // 2) : i * (rank // 2) + 1].astype(jnp.int32)
+            mask[i] = (lax.broadcasted_iota(jnp.int32, (rows, 1), 0) < live).astype(f32)
+
+
+def cross(flip, at, place, part, q, turned, totals, *rest):
     _, rows, rank = q.shape
     dim = part.shape[2]
     masks = [] if flip else [array((2, rows, 1))]
     return call(
-        functools.partial(cross_kernel, flip, at), "cross", [SMEM] * 2 + [VMEM] * (4 + len(rest)),
+        functools.partial(cross_kernel, flip, at), "cross", [SMEM] + [VMEM] * (4 + len(rest)),
         [VMEM] * (3 + len(masks)),
         [array((rows, dim)), array((rank + 8, dim)), array((rows, 1))] + masks,
         cost=pl.CostEstimate(flops=2 * rank * dim * q.shape[1], bytes_accessed=0, transcendentals=0),
-    )(place, live, part, *near(q, turned), totals, *rest)
+    )(place, part, *near(q, turned), totals, *rest)
 
 
 def split_row(row):
@@ -551,7 +554,7 @@
     opposite = bits[-1] | bits[-2]
     exchange = functools.partial(lax.all_to_all, axis_name="cell", split_axis=0, concat_axis=0)
 
-    q, own_table, turned, totals = fetch(source_prev, target_prev, loadings)
+    q, own_table, turned, totals = fetch(source_prev, target_prev, loadings, live)
     stack = stack_pieces([own_table, swap(loadings, count, opposite)], [totals])
     masks = [0, opposite]
     if count == 16 and loadings.shape[0] % 64 == 0:
@@ -571,8 +574,8 @@
             masks = masks + [m ^ bit for m in masks]
         emb = whole_product(place, source_expr, target_expr, masks, stack)
         at, rest = None, ()
-    emb_other, send, norms_other = cross(1, at, place, live, emb, q, turned, totals, *rest)
-    emb_own, own, norms_own, mask = cross(0, at, place, live, emb, q, turned, totals, *rest)
+    emb_other, send, norms_other = cross(1, at, place, emb, q, turned, totals, *rest)
+    emb_own, own, norms_own, mask = cross(0, at, place, emb, q, turned, totals, *rest)
 
     payload = pack_pair(own, swap(send, count, 1))
     cards = 2

time: 77.7 us -> 76.6 us (0.986)
  Pallas kernels: 15.6 us -> 14.5 us
    pallas_call x3, Pallas kernels: 5.13 us -> 4.08 us  [the longest x2 2.27 us: cross(): call(functools.partial(cross_kernel, flip, at), 'cross', [SMEM] + [VMEM]...]
  transfers between devices with their start and end apart: 15 -> 15, of which waited for: 8 -> 9; matrix products, arithmetic and copies ran while one was open for 0% -> 0% of each run, Pallas kernels for 13% -> 12%
where the time goes in v11:
time: 76.6 us; the launch traced here: 76.4 us
  blocking collectives  30 us (39%)
  starting transfers between devices  16.8 us (22%)
  Pallas kernels  14.5 us (19%)
  waiting for transfers between devices  14.2 us (19%)
  between operations  0.8 us (1%)
    all_to_all x2, blocking collectives, on_device(): exchange(copies)  20.8 us
    ppermute x15, starting transfers between devices, swap(): return lax.ppermute(value, 'cell', [(i, i ^ mask) for i in range(count)])  16.8 us
    ppermute x15, waiting for transfers between devices, swap(): return lax.ppermute(value, 'cell', [(i, i ^ mask) for i in range(count)])  14.2 us
    all_to_all x1, blocking collectives, on_device(): out_s, out_t, weights = finish(cells, *scaled, exchange(copies), consts)  9.2 us
    pallas_call x1, Pallas kernels, first_share(): call(functools.partial(first_kernel, masks, later_masks), 'embed_first',...  3.64 us
    pallas_call x2, Pallas kernels, cross(): call(functools.partial(cross_kernel, flip, at), 'cross', [SMEM] + [VMEM]...  2.27 us
    pallas_call x1, Pallas kernels, fetch(): call(fetch_kernel, 'fetch', [HBM] * 4, [VMEM] * 4, [pltpu.VMEM((2, rows,...  1.81 us
  transfers between devices with their start and end apart: 15, of which 9 were waited for; matrix products, arithmetic and copies ran while one was open for 0% of the time, Pallas kernels for 12%

profile of v11, /device:TPU:0, one launch (start us, length us, event | category | flops | bytes accessed | tf_op | source)
XLA Modules:
  0.0 76.4 jit_solution(3994501328334594141)
XLA Ops:
  0.6 5.1 %collective-permute-start = (bf16[128,256]{1,0:T(8,128)(2,1)}, bf16[128,256]{1,0:T(8,128)(2,1)S(1)}, u32[]{:S(2)}, u32[]{:S(2)}) collective-permute-start(bf16[128,256]{1,0:T(8,128)(2,1)} %table.1), channel_id=1, source_target_pairs={{0,12},{1,13},{2,14},{3,15},{4,8},{5,9},{6,10},{7,11},{8,4},{9,5},... | collective-permute-start | bytes 196616 | tf_op jit(solution)/shard_map/ppermute | solution.py:22
  5.7 1.8 %fetch.1 = (f32[2,1024,256]{2,1,0:T(8,128)S(1)}, bf16[128,256]{1,0:T(8,128)(2,1)S(1)}, bf16[2,256,1024]{2,1,0:T(8,128)(2,1)S(1)}, f32[3,1,256]{2,1,0:T(1,128)S(1)}) custom-call(f32[1024,256]{1,0:T(8,128)} %qs.1, f32[1024,256]{1,0:T(8,128)} %qt.1, bf16[128,256]{1,0:T(8,128)(2,1)} %table.1, s32[2]{0:T(128)} %bitcast.6), custom_call_target="tpu_custom_call" | custom-call | bytes 2097152 | tf_op jit(solution)/shard_map/fetch/pallas_call | solution.py:102
  7.6 0.7 collective-permute-done.refs_1_
  8.3 0.1 collective-permute-start.1
  8.3 2.1 %collective-permute-start.2 = (bf16[2,128,256]{2,1,0:T(8,128)(2,1)S(1)}, bf16[2,128,256]{2,1,0:T(8,128)(2,1)S(1)}, u32[]{:S(2)}, u32[]{:S(2)}) collective-permute-start(bf16[2,128,256]{2,1,0:T(8,128)(2,1)S(1)} %stack.1.even), channel_id=1, source_target_pairs={{0,6},{1,7},{2,4},{3,5},{4,2},{5,3},{6,0},{7,1},{8,14},{9,15},{10,... | collective-permute-start | bytes 393224 | tf_op jit(solution)/shard_map/ppermute | solution.py:22
  10.4 0.5 collective-permute-start.6
  10.9 1.0 %collective-permute-start.4 = (bf16[2,128,256]{2,1,0:T(8,128)(2,1)S(1)}, bf16[2,128,256]{2,1,0:T(8,128)(2,1)S(1)}, u32[]{:S(2)}, u32[]{:S(2)}) collective-permute-start(bf16[2,128,256]{2,1,0:T(8,128)(2,1)S(1)} %stack.1.even), channel_id=1, source_target_pairs={{0,4},{1,5},{2,6},{3,7},{4,0},{5,1},{6,2},{7,3},{8,12},{9,13},{10,... | collective-permute-start | bytes 393224 | tf_op jit(solution)/shard_map/ppermute | solution.py:22
  11.9 0.0 collective-permute-done.1.odd
  11.9 3.6 %embed_first.1 = (f32[2,1024,256]{2,1,0:T(8,128)S(1)}, bf16[2,6,1024,256]{3,2,1,0:T(8,128)(2,1)S(1)}) custom-call(s32[1]{0:T(128)} %bitcast.place, bf16[1024,2048]{1,0:T(8,128)(2,1)} %xs.1, bf16[1024,2048]{1,0:T(8,128)(2,1)} %xt.1, bf16[2,128,256]{2,1,0:T(8,128)(2,1)S(1)} %stack.1.even, bf16[2,128,256]{2,1,0:T(8,128)(2,1)S(1)} %collective-permute-done.1.odd), custom_call_target="tpu_custom_call" | custom-call | flops 1073741824 | bytes 8388608 | tf_op jit(solution)/shard_map/embed_first/pallas_call | solution.py:166
  15.6 0.1 collective-permute-done.2.value
  15.6 0.1 collective-permute-start.3
  15.7 2.6 %collective-permute-done.4.value = bf16[2,128,256]{2,1,0:T(8,128)(2,1)S(1)} collective-permute-done((bf16[2,128,256]{2,1,0:T(8,128)(2,1)S(1)}, bf16[2,128,256]{2,1,0:T(8,128)(2,1)S(1)}, u32[]{:S(2)}, u32[]{:S(2)}) %collective-permute-start.4) | collective-permute-done | bytes 131104 | tf_op jit(solution)/shard_map/ppermute | solution.py:22
  18.3 0.1 collective-permute-start.5
  18.4 0.0 collective-permute-done.6.value
  18.4 0.5 collective-permute-start.7
  19.0 0.0 collective-permute-done.3.odd
  19.0 0.7 embed_next.2.part
  19.7 0.0 collective-permute-done.5.odd
  19.7 0.7 embed_next.3.part
  20.4 0.0 collective-permute-done.7.refs_2_
  20.5 1.0 %cross.3 = (f32[1024,256]{1,0:T(8,128)S(1)}, f32[264,256]{1,0:T(8,128)S(1)}, f32[1024,1]{1,0:T(8,128)S(1)}) custom-call(s32[1]{0:T(128)} %bitcast.place, f32[2,1024,256]{2,1,0:T(8,128)S(1)} %embed_next.3.part, f32[2,1024,256]{2,1,0:T(8,128)S(1)} %get-tuple-element.31.q, bf16[2,256,1024]{2,1,0:T(8,128)(2,1)S(1)} %get-tuple-element.32.turned, ...), custom_call_target="tpu_custom_call" | custom-call | flops 134217728 | tf_op jit(solution)/shard_map/cross/pallas_call | solution.py:264
  21.5 0.0 copy-start
  21.5 0.2 collective-permute-start.8
  21.7 1.2 %cross.2 = (f32[1024,256]{1,0:T(8,128)S(1)}, f32[264,256]{1,0:T(8,128)S(1)}, f32[1024,1]{1,0:T(8,128)S(1)}, f32[2,1024,1]{2,1,0:T(8,128)S(1)}) custom-call(s32[1]{0:T(128)} %bitcast.place, f32[2,1024,256]{2,1,0:T(8,128)S(1)} %embed_next.3.part, f32[2,1024,256]{2,1,0:T(8,128)S(1)} %get-tuple-element.31.q, bf16[2,256,1024]{2,1,0:T(8,128)(2,1)S(1)} %get-tuple-element.32.turned, ...), custom_call_target="tpu_custom_call" | custom-call | flops 134217728 | tf_op jit(solution)/shard_map/cross/pallas_call | solution.py:264
  23.0 0.2 collective-permute-done.8.recv
  23.2 1.1 %collective-permute-start.11 = (bf16[272,256]{1,0:T(8,128)(2,1)S(1)}, bf16[272,256]{1,0:T(8,128)(2,1)S(1)}, u32[]{:S(2)}, u32[]{:S(2)}) collective-permute-start(bf16[272,256]{1,0:T(8,128)(2,1)S(1)} %pack_pair.1.refs_0_), channel_id=1, source_target_pairs={{0,6},{1,7},{2,4},{3,5},{4,2},{5,3},{6,0},{7,1},{8,14},{9,15},{10,... | collective-permute-start | bytes 417800 | tf_op jit(solution)/shard_map/ppermute | solution.py:22
  24.3 1.1 %collective-permute-start.10 = (bf16[272,256]{1,0:T(8,128)(2,1)S(1)}, bf16[272,256]{1,0:T(8,128)(2,1)S(1)}, u32[]{:S(2)}, u32[]{:S(2)}) collective-permute-start(bf16[272,256]{1,0:T(8,128)(2,1)S(1)} %pack_pair.1.refs_0_), channel_id=1, source_target_pairs={{0,4},{1,5},{2,6},{3,7},{4,0},{5,1},{6,2},{7,3},{8,12},{9,13},{10,... | collective-permute-start | bytes 417800 | tf_op jit(solution)/shard_map/ppermute | solution.py:22
  25.3 1.4 %collective-permute-start.9 = (bf16[272,256]{1,0:T(8,128)(2,1)S(1)}, bf16[272,256]{1,0:T(8,128)(2,1)S(1)}, u32[]{:S(2)}, u32[]{:S(2)}) collective-permute-start(bf16[272,256]{1,0:T(8,128)(2,1)S(1)} %pack_pair.1.refs_0_), channel_id=1, source_target_pairs={{0,2},{1,3},{2,0},{3,1},{4,6},{5,7},{6,4},{7,5},{8,10},{9,11},{10,... | collective-permute-start | bytes 417800 | tf_op jit(solution)/shard_map/ppermute | solution.py:22
  26.7 3.9 %collective-permute-done.11.refs_3_ = bf16[272,256]{1,0:T(8,128)(2,1)S(1)} collective-permute-done((bf16[272,256]{1,0:T(8,128)(2,1)S(1)}, bf16[272,256]{1,0:T(8,128)(2,1)S(1)}, u32[]{:S(2)}, u32[]{:S(2)}) %collective-permute-start.11) | collective-permute-done | bytes 139296 | tf_op jit(solution)/shard_map/ppermute | solution.py:22
  30.7 1.5 %collective-permute-done.10.refs_2_ = bf16[272,256]{1,0:T(8,128)(2,1)S(1)} collective-permute-done((bf16[272,256]{1,0:T(8,128)(2,1)S(1)}, bf16[272,256]{1,0:T(8,128)(2,1)S(1)}, u32[]{:S(2)}, u32[]{:S(2)}) %collective-permute-start.10) | collective-permute-done | bytes 139296 | tf_op jit(solution)/shard_map/ppermute | solution.py:22
  32.2 0.7 collective-permute-done.9.refs_1_
  32.9 0.1 merge.1.near_part
  33.0 3.6 %collective-permute-start.12 = (bf16[304,256]{1,0:T(8,128)(2,1)S(1)}, bf16[304,256]{1,0:T(8,128)(2,1)S(1)}, u32[]{:S(2)}, u32[]{:S(2)}) collective-permute-start(bf16[304,256]{1,0:T(8,128)(2,1)S(1)} %merge.1.near_part), channel_id=1, source_target_pairs={{0,12},{1,13},{2,14},{3,15},{4,8},{5,9},{6,10},{7,11},{8,4},{9,5},... | collective-permute-start | bytes 466952 | tf_op jit(solution)/shard_map/ppermute | solution.py:22
  36.6 0.0 collective-permute-start.13
  36.6 4.3 %collective-permute-done.12.far_part = bf16[304,256]{1,0:T(8,128)(2,1)S(1)} collective-permute-done((bf16[304,256]{1,0:T(8,128)(2,1)S(1)}, bf16[304,256]{1,0:T(8,128)(2,1)S(1)}, u32[]{:S(2)}, u32[]{:S(2)}) %collective-permute-start.12) | collective-permute-done | bytes 155680 | tf_op jit(solution)/shard_map/ppermute | solution.py:22
  40.9 0.0 collective-permute-start.14
  40.9 0.0 copy-done
  40.9 1.2 %kernel_other.1 = (f32[1024,256]{1,0:T(8,128)S(1)}, f32[8,256]{1,0:T(8,128)S(1)}, f32[264,256]{1,0:T(8,128)S(1)}) custom-call(s32[1]{0:T(128)} %bitcast.place, f32[2,1024,1]{2,1,0:T(8,128)S(1)} %get-tuple-element.33.mask, f32[1024,1]{1,0:T(8,128)S(1)} %get-tuple-element.36.norms, f32[1024,256]{1,0:T(8,128)S(1)} %get-tuple-element.37.emb, ...), custom_call_target="tpu_custom_call" | custom-call | flops 402653184 | tf_op jit(solution)/shard_map/kernel_other/pallas_call | solution.py:513
  42.1 0.0 collective-permute-done.13.near_part
  42.2 0.2 collective-permute-done.14.far_part
  42.3 1.2 %kernel_own.1 = (f32[1024,256]{1,0:T(8,128)S(1)}, f32[16,2,256]{2,1,0:T(2,128)S(1)}, f32[8,256]{1,0:T(8,128)S(1)}) custom-call(s32[1]{0:T(128)} %bitcast.place, f32[2,1024,1]{2,1,0:T(8,128)S(1)} %get-tuple-element.33.mask, f32[1024,1]{1,0:T(8,128)S(1)} %get-tuple-element.34.norms, f32[1024,256]{1,0:T(8,128)S(1)} %get-tuple-element.35.emb, ...), custom_call_target="tpu_custom_call" | custom-call | flops 402653184 | tf_op jit(solution)/shard_map/kernel_own/pallas_call | solution.py:517
  43.6 11.6 %all_to_all.15.parts = f32[16,2,256]{2,1,0:T(2,128)S(1)} all-to-all(f32[16,2,256]{2,1,0:T(2,128)S(1)} %get-tuple-element.44), channel_id=1, replica_groups=mesh['grp'=2,'cell'=16] {'cell'}, dimensions={0} | all-to-all | bytes 65536 | tf_op jit(solution)/shard_map/all_to_all | solution.py:600
  55.2 0.6 sweep.2
  55.8 9.2 %all_to_all.16.parts = f32[16,2,256]{2,1,0:T(2,128)S(1)} all-to-all(f32[16,2,256]{2,1,0:T(2,128)S(1)} %sweep.2), channel_id=1, replica_groups=mesh['grp'=2,'cell'=16] {'cell'}, dimensions={0} | all-to-all | bytes 65536 | tf_op jit(solution)/shard_map/all_to_all | solution.py:600
  65.0 0.7 sweep.3
  65.7 9.2 %all_to_all.17.parts = f32[16,2,256]{2,1,0:T(2,128)S(1)} all-to-all(f32[16,2,256]{2,1,0:T(2,128)S(1)} %get-tuple-element.47), channel_id=1, replica_groups=mesh['grp'=2,'cell'=16] {'cell'}, dimensions={0} | all-to-all | bytes 65536 | tf_op jit(solution)/shard_map/all_to_all | solution.py:601
  74.9 1.5 %finish.1 = (f32[1024,256]{1,0:T(8,128)}, f32[1024,256]{1,0:T(8,128)}, f32[1,256]{1,0:T(1,128)}) custom-call(f32[2,1024,256]{2,1,0:T(8,128)S(1)} %get-tuple-element.46.scaled, f32[16,2,256]{2,1,0:T(2,128)S(1)} %all_to_all.17.parts, f32[8,256]{1,0:T(8,128)S(1)} %get-tuple-element.45.consts), custom_call_target="tpu_custom_call" | custom-call | tf_op jit(solution)/shard_map/finish/pallas_call | solution.py:535
  (5 shorter events, 0.1 us)
Async XLA Ops:
  0.6 7.6 %collective-permute-start = (bf16[128,256]{1,0:T(8,128)(2,1)}, bf16[128,256]{1,0:T(8,128)(2,1)S(1)}, u32[]{:S(2)}, u32[]{:S(2)}) collective-permute-start(bf16[128,256]{1,0:T(8,128)(2,1)} %table.1), channel_id=1, source_target_pairs={{0,12},{1,13},{2,14},{3,15},{4,8},{5,9},{6,10},{7,11},{8,4},{9,5},... | collective-permute-start | bytes 196616 | tf_op jit(solution)/shard_map/ppermute | solution.py:22
  8.3 3.6 %collective-permute-start.1 = (bf16[2,128,256]{2,1,0:T(8,128)(2,1)S(1)}, bf16[2,128,256]{2,1,0:T(8,128)(2,1)S(1)}, u32[]{:S(2)}, u32[]{:S(2)}) collective-permute-start(bf16[2,128,256]{2,1,0:T(8,128)(2,1)S(1)} %stack.1.even), channel_id=1, source_target_pairs={{0,1},{1,0},{2,3},{3,2},{4,5},{5,4},{6,7},{7,6},{8,9},{9,8},{10,11... | collective-permute-start | bytes 393224 | tf_op jit(solution)/shard_map/ppermute | solution.py:22
  8.3 7.3 %collective-permute-start.2 = (bf16[2,128,256]{2,1,0:T(8,128)(2,1)S(1)}, bf16[2,128,256]{2,1,0:T(8,128)(2,1)S(1)}, u32[]{:S(2)}, u32[]{:S(2)}) collective-permute-start(bf16[2,128,256]{2,1,0:T(8,128)(2,1)S(1)} %stack.1.even), channel_id=1, source_target_pairs={{0,6},{1,7},{2,4},{3,5},{4,2},{5,3},{6,0},{7,1},{8,14},{9,15},{10,... | collective-permute-start | bytes 393224 | tf_op jit(solution)/shard_map/ppermute | solution.py:22
  10.4 8.0 %collective-permute-start.6 = (bf16[2,128,256]{2,1,0:T(8,128)(2,1)S(1)}, bf16[2,128,256]{2,1,0:T(8,128)(2,1)S(1)}, u32[]{:S(2)}, u32[]{:S(2)}) collective-permute-start(bf16[2,128,256]{2,1,0:T(8,128)(2,1)S(1)} %stack.1.even), channel_id=1, source_target_pairs={{0,2},{1,3},{2,0},{3,1},{4,6},{5,7},{6,4},{7,5},{8,10},{9,11},{10,... | collective-permute-start | bytes 393224 | tf_op jit(solution)/shard_map/ppermute | solution.py:22
  10.9 7.4 %collective-permute-start.4 = (bf16[2,128,256]{2,1,0:T(8,128)(2,1)S(1)}, bf16[2,128,256]{2,1,0:T(8,128)(2,1)S(1)}, u32[]{:S(2)}, u32[]{:S(2)}) collective-permute-start(bf16[2,128,256]{2,1,0:T(8,128)(2,1)S(1)} %stack.1.even), channel_id=1, source_target_pairs={{0,4},{1,5},{2,6},{3,7},{4,0},{5,1},{6,2},{7,3},{8,12},{9,13},{10,... | collective-permute-start | bytes 393224 | tf_op jit(solution)/shard_map/ppermute | solution.py:22
  15.6 3.3 %collective-permute-start.3 = (bf16[2,128,256]{2,1,0:T(8,128)(2,1)S(1)}, bf16[2,128,256]{2,1,0:T(8,128)(2,1)S(1)}, u32[]{:S(2)}, u32[]{:S(2)}) collective-permute-start(bf16[2,128,256]{2,1,0:T(8,128)(2,1)S(1)} %gate.3.even), channel_id=1, source_target_pairs={{0,1},{1,0},{2,3},{3,2},{4,5},{5,4},{6,7},{7,6},{8,9},{9,8},{10,11... | collective-permute-start | bytes 393224 | tf_op jit(solution)/shard_map/ppermute | solution.py:22
  18.3 1.4 %collective-permute-start.5 = (bf16[2,128,256]{2,1,0:T(8,128)(2,1)S(1)}, bf16[2,128,256]{2,1,0:T(8,128)(2,1)S(1)}, u32[]{:S(2)}, u32[]{:S(2)}) collective-permute-start(bf16[2,128,256]{2,1,0:T(8,128)(2,1)S(1)} %gate.4.even), channel_id=1, source_target_pairs={{0,1},{1,0},{2,3},{3,2},{4,5},{5,4},{6,7},{7,6},{8,9},{9,8},{10,11... | collective-permute-start | bytes 393224 | tf_op jit(solution)/shard_map/ppermute | solution.py:22
  18.4 2.0 %collective-permute-start.7 = (bf16[2,128,256]{2,1,0:T(8,128)(2,1)S(1)}, bf16[2,128,256]{2,1,0:T(8,128)(2,1)S(1)}, u32[]{:S(2)}, u32[]{:S(2)}) collective-permute-start(bf16[2,128,256]{2,1,0:T(8,128)(2,1)S(1)} %gate.5.refs_1_), channel_id=1, source_target_pairs={{0,1},{1,0},{2,3},{3,2},{4,5},{5,4},{6,7},{7,6},{8,9},{9,8},{10,11... | collective-permute-start | bytes 393224 | tf_op jit(solution)/shard_map/ppermute | solution.py:22
  21.5 19.4 %copy-start = (f32[256]{0:T(256)S(1)}, f32[256]{0:T(256)}, u32[]{:S(2)}) copy-start(f32[256]{0:T(256)} %param.12) | copy-start | bytes 3076
  21.5 1.6 %collective-permute-start.8 = (f32[264,256]{1,0:T(8,128)S(1)}, f32[264,256]{1,0:T(8,128)S(1)}, u32[]{:S(2)}, u32[]{:S(2)}) collective-permute-start(f32[264,256]{1,0:T(8,128)S(1)} %get-tuple-element.39), channel_id=1, source_target_pairs={{0,1},{1,0},{2,3},{3,2},{4,5},{5,4},{6,7},{7,6},{8,9},{9,8},{10,11... | collective-permute-start | bytes 811016 | tf_op jit(solution)/shard_map/ppermute | solution.py:22
  23.2 7.5 %collective-permute-start.11 = (bf16[272,256]{1,0:T(8,128)(2,1)S(1)}, bf16[272,256]{1,0:T(8,128)(2,1)S(1)}, u32[]{:S(2)}, u32[]{:S(2)}) collective-permute-start(bf16[272,256]{1,0:T(8,128)(2,1)S(1)} %pack_pair.1.refs_0_), channel_id=1, source_target_pairs={{0,6},{1,7},{2,4},{3,5},{4,2},{5,3},{6,0},{7,1},{8,14},{9,15},{10,... | collective-permute-start | bytes 417800 | tf_op jit(solution)/shard_map/ppermute | solution.py:22
  24.3 7.9 %collective-permute-start.10 = (bf16[272,256]{1,0:T(8,128)(2,1)S(1)}, bf16[272,256]{1,0:T(8,128)(2,1)S(1)}, u32[]{:S(2)}, u32[]{:S(2)}) collective-permute-start(bf16[272,256]{1,0:T(8,128)(2,1)S(1)} %pack_pair.1.refs_0_), channel_id=1, source_target_pairs={{0,4},{1,5},{2,6},{3,7},{4,0},{5,1},{6,2},{7,3},{8,12},{9,13},{10,... | collective-permute-start | bytes 417800 | tf_op jit(solution)/shard_map/ppermute | solution.py:22
  25.3 7.6 %collective-permute-start.9 = (bf16[272,256]{1,0:T(8,128)(2,1)S(1)}, bf16[272,256]{1,0:T(8,128)(2,1)S(1)}, u32[]{:S(2)}, u32[]{:S(2)}) collective-permute-start(bf16[272,256]{1,0:T(8,128)(2,1)S(1)} %pack_pair.1.refs_0_), channel_id=1, source_target_pairs={{0,2},{1,3},{2,0},{3,1},{4,6},{5,7},{6,4},{7,5},{8,10},{9,11},{10,... | collective-permute-start | bytes 417800 | tf_op jit(solution)/shard_map/ppermute | solution.py:22
  33.0 7.9 %collective-permute-start.12 = (bf16[304,256]{1,0:T(8,128)(2,1)S(1)}, bf16[304,256]{1,0:T(8,128)(2,1)S(1)}, u32[]{:S(2)}, u32[]{:S(2)}) collective-permute-start(bf16[304,256]{1,0:T(8,128)(2,1)S(1)} %merge.1.near_part), channel_id=1, source_target_pairs={{0,12},{1,13},{2,14},{3,15},{4,8},{5,9},{6,10},{7,11},{8,4},{9,5},... | collective-permute-start | bytes 466952 | tf_op jit(solution)/shard_map/ppermute | solution.py:22
  36.6 5.5 %collective-permute-start.13 = (bf16[304,256]{1,0:T(8,128)(2,1)S(1)}, bf16[304,256]{1,0:T(8,128)(2,1)S(1)}, u32[]{:S(2)}, u32[]{:S(2)}) collective-permute-start(bf16[304,256]{1,0:T(8,128)(2,1)S(1)} %merge.1.near_part), channel_id=1, source_target_pairs={{0,1},{1,0},{2,3},{3,2},{4,5},{5,4},{6,7},{7,6},{8,9},{9,8},{10,11... | collective-permute-start | bytes 466952 | tf_op jit(solution)/shard_map/ppermute | solution.py:22
  40.9 1.4 %collective-permute-start.14 = (bf16[304,256]{1,0:T(8,128)(2,1)S(1)}, bf16[304,256]{1,0:T(8,128)(2,1)S(1)}, u32[]{:S(2)}, u32[]{:S(2)}) collective-permute-start(bf16[304,256]{1,0:T(8,128)(2,1)S(1)} %collective-permute-done.12.far_part), channel_id=1, source_target_pairs={{0,1},{1,0},{2,3},{3,2},{4,5},{5,4},{6,7},{7,6},{8,9},{9,8},{10,11... | collective-permute-start | bytes 466952 | tf_op jit(solution)/shard_map/ppermute | solution.py:22

commit v12 on v11

--- a/solution.py
+++ b/solution.py
@@ -10,6 +10,7 @@
 D = 256
 ITERS = 3
 STEPS = 4
+SWEEP_STEPS = 1
 
 step_size = 1.0
 LOG2_E = 1.4426950408889634
@@ -470,11 +471,11 @@
     copies = refs[-1]
     core = place[0] & 1
     first = core == 0
-    block = k_own.shape[0] // STEPS
+    block = k_own.shape[0] // SWEEP_STEPS
 
     _, *duals = duals_of(parts, consts)
     sums = [None, None]
-    for step in range(STEPS):
+    for step in range(SWEEP_STEPS):
         at = slice(step * block, (step + 1) * block)
         for i, (k, t, dual) in enumerate(
             zip((k_own, k_other), (core, 1 - core), in_order(first, *duals))

time: 76.6 us -> 76.5 us (level)
  no operation moved by 1% of the time
where the time goes in v12:
time: 76.5 us; the launch traced here: 76.3 us
  blocking collectives  30 us (39%)
  starting transfers between devices  16.8 us (22%)
  Pallas kernels  14.5 us (19%)
  waiting for transfers between devices  14.2 us (19%)
  between operations  0.8 us (1%)
    all_to_all x2, blocking collectives, on_device(): exchange(copies)  20.8 us
    ppermute x15, starting transfers between devices, swap(): return lax.ppermute(value, 'cell', [(i, i ^ mask) for i in range(count)])  16.8 us
    ppermute x15, waiting for transfers between devices, swap(): return lax.ppermute(value, 'cell', [(i, i ^ mask) for i in range(count)])  14.2 us
    all_to_all x1, blocking collectives, on_device(): out_s, out_t, weights = finish(cells, *scaled, exchange(copies), consts)  9.2 us
    pallas_call x1, Pallas kernels, first_share(): call(functools.partial(first_kernel, masks, later_masks), 'embed_first',...  3.64 us
    pallas_call x2, Pallas kernels, cross(): call(functools.partial(cross_kernel, flip, at), 'cross', [SMEM] + [VMEM]...  2.27 us
    pallas_call x1, Pallas kernels, fetch(): call(fetch_kernel, 'fetch', [HBM] * 4, [VMEM] * 4, [pltpu.VMEM((2, rows,...  1.81 us
  transfers between devices with their start and end apart: 15, of which 9 were waited for; matrix products, arithmetic and copies ran while one was open for 0% of the time, Pallas kernels for 12%

profile of v12, /device:TPU:0, one launch (start us, length us, event | category | flops | bytes accessed | tf_op | source)
XLA Modules:
  0.0 76.3 jit_solution(11222328758939918786)
XLA Ops:
  0.6 5.1 %collective-permute-start = (bf16[128,256]{1,0:T(8,128)(2,1)}, bf16[128,256]{1,0:T(8,128)(2,1)S(1)}, u32[]{:S(2)}, u32[]{:S(2)}) collective-permute-start(bf16[128,256]{1,0:T(8,128)(2,1)} %table.1), channel_id=1, source_target_pairs={{0,12},{1,13},{2,14},{3,15},{4,8},{5,9},{6,10},{7,11},{8,4},{9,5},... | collective-permute-start | bytes 196616 | tf_op jit(solution)/shard_map/ppermute | solution.py:23
  5.7 1.8 %fetch.1 = (f32[2,1024,256]{2,1,0:T(8,128)S(1)}, bf16[128,256]{1,0:T(8,128)(2,1)S(1)}, bf16[2,256,1024]{2,1,0:T(8,128)(2,1)S(1)}, f32[3,1,256]{2,1,0:T(1,128)S(1)}) custom-call(f32[1024,256]{1,0:T(8,128)} %qs.1, f32[1024,256]{1,0:T(8,128)} %qt.1, bf16[128,256]{1,0:T(8,128)(2,1)} %table.1, s32[2]{0:T(128)} %bitcast.6), custom_call_target="tpu_custom_call" | custom-call | bytes 2097152 | tf_op jit(solution)/shard_map/fetch/pallas_call | solution.py:103
  7.6 0.7 collective-permute-done.refs_1_
  8.3 0.1 collective-permute-start.1
  8.3 2.1 %collective-permute-start.2 = (bf16[2,128,256]{2,1,0:T(8,128)(2,1)S(1)}, bf16[2,128,256]{2,1,0:T(8,128)(2,1)S(1)}, u32[]{:S(2)}, u32[]{:S(2)}) collective-permute-start(bf16[2,128,256]{2,1,0:T(8,128)(2,1)S(1)} %stack.1.even), channel_id=1, source_target_pairs={{0,6},{1,7},{2,4},{3,5},{4,2},{5,3},{6,0},{7,1},{8,14},{9,15},{10,... | collective-permute-start | bytes 393224 | tf_op jit(solution)/shard_map/ppermute | solution.py:23
  10.4 0.5 collective-permute-start.6
  10.9 1.0 %collective-permute-start.4 = (bf16[2,128,256]{2,1,0:T(8,128)(2,1)S(1)}, bf16[2,128,256]{2,1,0:T(8,128)(2,1)S(1)}, u32[]{:S(2)}, u32[]{:S(2)}) collective-permute-start(bf16[2,128,256]{2,1,0:T(8,128)(2,1)S(1)} %stack.1.even), channel_id=1, source_target_pairs={{0,4},{1,5},{2,6},{3,7},{4,0},{5,1},{6,2},{7,3},{8,12},{9,13},{10,... | collective-permute-start | bytes 393224 | tf_op jit(solution)/shard_map/ppermute | solution.py:23
  11.9 0.0 collective-permute-done.1.odd
  11.9 3.6 %embed_first.1 = (f32[2,1024,256]{2,1,0:T(8,128)S(1)}, bf16[2,6,1024,256]{3,2,1,0:T(8,128)(2,1)S(1)}) custom-call(s32[1]{0:T(128)} %bitcast.place, bf16[1024,2048]{1,0:T(8,128)(2,1)} %xs.1, bf16[1024,2048]{1,0:T(8,128)(2,1)} %xt.1, bf16[2,128,256]{2,1,0:T(8,128)(2,1)S(1)} %stack.1.even, bf16[2,128,256]{2,1,0:T(8,128)(2,1)S(1)} %collective-permute-done.1.odd), custom_call_target="tpu_custom_call" | custom-call | flops 1073741824 | bytes 8388608 | tf_op jit(solution)/shard_map/embed_first/pallas_call | solution.py:167
  15.6 0.1 collective-permute-done.2.value
  15.6 0.1 collective-permute-start.3
  15.7 2.6 %collective-permute-done.4.value = bf16[2,128,256]{2,1,0:T(8,128)(2,1)S(1)} collective-permute-done((bf16[2,128,256]{2,1,0:T(8,128)(2,1)S(1)}, bf16[2,128,256]{2,1,0:T(8,128)(2,1)S(1)}, u32[]{:S(2)}, u32[]{:S(2)}) %collective-permute-start.4) | collective-permute-done | bytes 131104 | tf_op jit(solution)/shard_map/ppermute | solution.py:23
  18.3 0.1 collective-permute-start.5
  18.4 0.0 collective-permute-done.6.value
  18.4 0.5 collective-permute-start.7
  19.0 0.0 collective-permute-done.3.odd
  19.0 0.7 embed_next.2.part
  19.7 0.0 collective-permute-done.5.odd
  19.7 0.7 embed_next.3.part
  20.4 0.0 collective-permute-done.7.refs_2_
  20.5 1.0 %cross.3 = (f32[1024,256]{1,0:T(8,128)S(1)}, f32[264,256]{1,0:T(8,128)S(1)}, f32[1024,1]{1,0:T(8,128)S(1)}) custom-call(s32[1]{0:T(128)} %bitcast.place, f32[2,1024,256]{2,1,0:T(8,128)S(1)} %embed_next.3.part, f32[2,1024,256]{2,1,0:T(8,128)S(1)} %get-tuple-element.31.q, bf16[2,256,1024]{2,1,0:T(8,128)(2,1)S(1)} %get-tuple-element.32.turned, ...), custom_call_target="tpu_custom_call" | custom-call | flops 134217728 | tf_op jit(solution)/shard_map/cross/pallas_call | solution.py:265
  21.5 0.0 copy-start
  21.5 0.2 collective-permute-start.8
  21.7 1.2 %cross.2 = (f32[1024,256]{1,0:T(8,128)S(1)}, f32[264,256]{1,0:T(8,128)S(1)}, f32[1024,1]{1,0:T(8,128)S(1)}, f32[2,1024,1]{2,1,0:T(8,128)S(1)}) custom-call(s32[1]{0:T(128)} %bitcast.place, f32[2,1024,256]{2,1,0:T(8,128)S(1)} %embed_next.3.part, f32[2,1024,256]{2,1,0:T(8,128)S(1)} %get-tuple-element.31.q, bf16[2,256,1024]{2,1,0:T(8,128)(2,1)S(1)} %get-tuple-element.32.turned, ...), custom_call_target="tpu_custom_call" | custom-call | flops 134217728 | tf_op jit(solution)/shard_map/cross/pallas_call | solution.py:265
  23.0 0.2 collective-permute-done.8.recv
  23.2 1.1 %collective-permute-start.11 = (bf16[272,256]{1,0:T(8,128)(2,1)S(1)}, bf16[272,256]{1,0:T(8,128)(2,1)S(1)}, u32[]{:S(2)}, u32[]{:S(2)}) collective-permute-start(bf16[272,256]{1,0:T(8,128)(2,1)S(1)} %pack_pair.1.refs_0_), channel_id=1, source_target_pairs={{0,6},{1,7},{2,4},{3,5},{4,2},{5,3},{6,0},{7,1},{8,14},{9,15},{10,... | collective-permute-start | bytes 417800 | tf_op jit(solution)/shard_map/ppermute | solution.py:23
  24.3 1.1 %collective-permute-start.10 = (bf16[272,256]{1,0:T(8,128)(2,1)S(1)}, bf16[272,256]{1,0:T(8,128)(2,1)S(1)}, u32[]{:S(2)}, u32[]{:S(2)}) collective-permute-start(bf16[272,256]{1,0:T(8,128)(2,1)S(1)} %pack_pair.1.refs_0_), channel_id=1, source_target_pairs={{0,4},{1,5},{2,6},{3,7},{4,0},{5,1},{6,2},{7,3},{8,12},{9,13},{10,... | collective-permute-start | bytes 417800 | tf_op jit(solution)/shard_map/ppermute | solution.py:23
  25.3 1.4 %collective-permute-start.9 = (bf16[272,256]{1,0:T(8,128)(2,1)S(1)}, bf16[272,256]{1,0:T(8,128)(2,1)S(1)}, u32[]{:S(2)}, u32[]{:S(2)}) collective-permute-start(bf16[272,256]{1,0:T(8,128)(2,1)S(1)} %pack_pair.1.refs_0_), channel_id=1, source_target_pairs={{0,2},{1,3},{2,0},{3,1},{4,6},{5,7},{6,4},{7,5},{8,10},{9,11},{10,... | collective-permute-start | bytes 417800 | tf_op jit(solution)/shard_map/ppermute | solution.py:23
  26.7 3.9 %collective-permute-done.11.refs_3_ = bf16[272,256]{1,0:T(8,128)(2,1)S(1)} collective-permute-done((bf16[272,256]{1,0:T(8,128)(2,1)S(1)}, bf16[272,256]{1,0:T(8,128)(2,1)S(1)}, u32[]{:S(2)}, u32[]{:S(2)}) %collective-permute-start.11) | collective-permute-done | bytes 139296 | tf_op jit(solution)/shard_map/ppermute | solution.py:23
  30.7 1.5 %collective-permute-done.10.refs_2_ = bf16[272,256]{1,0:T(8,128)(2,1)S(1)} collective-permute-done((bf16[272,256]{1,0:T(8,128)(2,1)S(1)}, bf16[272,256]{1,0:T(8,128)(2,1)S(1)}, u32[]{:S(2)}, u32[]{:S(2)}) %collective-permute-start.10) | collective-permute-done | bytes 139296 | tf_op jit(solution)/shard_map/ppermute | solution.py:23
  32.2 0.7 collective-permute-done.9.refs_1_
  32.9 0.1 merge.1.near_part
  33.0 3.6 %collective-permute-start.12 = (bf16[304,256]{1,0:T(8,128)(2,1)S(1)}, bf16[304,256]{1,0:T(8,128)(2,1)S(1)}, u32[]{:S(2)}, u32[]{:S(2)}) collective-permute-start(bf16[304,256]{1,0:T(8,128)(2,1)S(1)} %merge.1.near_part), channel_id=1, source_target_pairs={{0,12},{1,13},{2,14},{3,15},{4,8},{5,9},{6,10},{7,11},{8,4},{9,5},... | collective-permute-start | bytes 466952 | tf_op jit(solution)/shard_map/ppermute | solution.py:23
  36.6 0.0 collective-permute-start.13
  36.6 4.3 %collective-permute-done.12.far_part = bf16[304,256]{1,0:T(8,128)(2,1)S(1)} collective-permute-done((bf16[304,256]{1,0:T(8,128)(2,1)S(1)}, bf16[304,256]{1,0:T(8,128)(2,1)S(1)}, u32[]{:S(2)}, u32[]{:S(2)}) %collective-permute-start.12) | collective-permute-done | bytes 155680 | tf_op jit(solution)/shard_map/ppermute | solution.py:23
  40.9 0.0 collective-permute-start.14
  40.9 0.0 copy-done
  40.9 1.2 %kernel_other.1 = (f32[1024,256]{1,0:T(8,128)S(1)}, f32[8,256]{1,0:T(8,128)S(1)}, f32[264,256]{1,0:T(8,128)S(1)}) custom-call(s32[1]{0:T(128)} %bitcast.place, f32[2,1024,1]{2,1,0:T(8,128)S(1)} %get-tuple-element.33.mask, f32[1024,1]{1,0:T(8,128)S(1)} %get-tuple-element.36.norms, f32[1024,256]{1,0:T(8,128)S(1)} %get-tuple-element.37.emb, ...), custom_call_target="tpu_custom_call" | custom-call | flops 402653184 | tf_op jit(solution)/shard_map/kernel_other/pallas_call | solution.py:514
  42.1 0.0 collective-permute-done.13.near_part
  42.2 0.2 collective-permute-done.14.far_part
  42.3 1.2 %kernel_own.1 = (f32[1024,256]{1,0:T(8,128)S(1)}, f32[16,2,256]{2,1,0:T(2,128)S(1)}, f32[8,256]{1,0:T(8,128)S(1)}) custom-call(s32[1]{0:T(128)} %bitcast.place, f32[2,1024,1]{2,1,0:T(8,128)S(1)} %get-tuple-element.33.mask, f32[1024,1]{1,0:T(8,128)S(1)} %get-tuple-element.34.norms, f32[1024,256]{1,0:T(8,128)S(1)} %get-tuple-element.35.emb, ...), custom_call_target="tpu_custom_call" | custom-call | flops 402653184 | tf_op jit(solution)/shard_map/kernel_own/pallas_call | solution.py:518
  43.6 11.6 %all_to_all.15.parts = f32[16,2,256]{2,1,0:T(2,128)S(1)} all-to-all(f32[16,2,256]{2,1,0:T(2,128)S(1)} %get-tuple-element.44), channel_id=1, replica_groups=mesh['grp'=2,'cell'=16] {'cell'}, dimensions={0} | all-to-all | bytes 65536 | tf_op jit(solution)/shard_map/all_to_all | solution.py:601
  55.2 0.6 sweep.2
  55.8 9.2 %all_to_all.16.parts = f32[16,2,256]{2,1,0:T(2,128)S(1)} all-to-all(f32[16,2,256]{2,1,0:T(2,128)S(1)} %sweep.2), channel_id=1, replica_groups=mesh['grp'=2,'cell'=16] {'cell'}, dimensions={0} | all-to-all | bytes 65536 | tf_op jit(solution)/shard_map/all_to_all | solution.py:601
  65.0 0.6 sweep.3
  65.6 9.2 %all_to_all.17.parts = f32[16,2,256]{2,1,0:T(2,128)S(1)} all-to-all(f32[16,2,256]{2,1,0:T(2,128)S(1)} %get-tuple-element.47), channel_id=1, replica_groups=mesh['grp'=2,'cell'=16] {'cell'}, dimensions={0} | all-to-all | bytes 65536 | tf_op jit(solution)/shard_map/all_to_all | solution.py:602
  74.8 1.5 %finish.1 = (f32[1024,256]{1,0:T(8,128)}, f32[1024,256]{1,0:T(8,128)}, f32[1,256]{1,0:T(1,128)}) custom-call(f32[2,1024,256]{2,1,0:T(8,128)S(1)} %get-tuple-element.46.scaled, f32[16,2,256]{2,1,0:T(2,128)S(1)} %all_to_all.17.parts, f32[8,256]{1,0:T(8,128)S(1)} %get-tuple-element.45.consts), custom_call_target="tpu_custom_call" | custom-call | tf_op jit(solution)/shard_map/finish/pallas_call | solution.py:536
  (5 shorter events, 0.1 us)
Async XLA Ops:
  0.6 7.6 %collective-permute-start = (bf16[128,256]{1,0:T(8,128)(2,1)}, bf16[128,256]{1,0:T(8,128)(2,1)S(1)}, u32[]{:S(2)}, u32[]{:S(2)}) collective-permute-start(bf16[128,256]{1,0:T(8,128)(2,1)} %table.1), channel_id=1, source_target_pairs={{0,12},{1,13},{2,14},{3,15},{4,8},{5,9},{6,10},{7,11},{8,4},{9,5},... | collective-permute-start | bytes 196616 | tf_op jit(solution)/shard_map/ppermute | solution.py:23
  8.3 3.6 %collective-permute-start.1 = (bf16[2,128,256]{2,1,0:T(8,128)(2,1)S(1)}, bf16[2,128,256]{2,1,0:T(8,128)(2,1)S(1)}, u32[]{:S(2)}, u32[]{:S(2)}) collective-permute-start(bf16[2,128,256]{2,1,0:T(8,128)(2,1)S(1)} %stack.1.even), channel_id=1, source_target_pairs={{0,1},{1,0},{2,3},{3,2},{4,5},{5,4},{6,7},{7,6},{8,9},{9,8},{10,11... | collective-permute-start | bytes 393224 | tf_op jit(solution)/shard_map/ppermute | solution.py:23
  8.3 7.3 %collective-permute-start.2 = (bf16[2,128,256]{2,1,0:T(8,128)(2,1)S(1)}, bf16[2,128,256]{2,1,0:T(8,128)(2,1)S(1)}, u32[]{:S(2)}, u32[]{:S(2)}) collective-permute-start(bf16[2,128,256]{2,1,0:T(8,128)(2,1)S(1)} %stack.1.even), channel_id=1, source_target_pairs={{0,6},{1,7},{2,4},{3,5},{4,2},{5,3},{6,0},{7,1},{8,14},{9,15},{10,... | collective-permute-start | bytes 393224 | tf_op jit(solution)/shard_map/ppermute | solution.py:23
  10.4 8.0 %collective-permute-start.6 = (bf16[2,128,256]{2,1,0:T(8,128)(2,1)S(1)}, bf16[2,128,256]{2,1,0:T(8,128)(2,1)S(1)}, u32[]{:S(2)}, u32[]{:S(2)}) collective-permute-start(bf16[2,128,256]{2,1,0:T(8,128)(2,1)S(1)} %stack.1.even), channel_id=1, source_target_pairs={{0,2},{1,3},{2,0},{3,1},{4,6},{5,7},{6,4},{7,5},{8,10},{9,11},{10,... | collective-permute-start | bytes 393224 | tf_op jit(solution)/shard_map/ppermute | solution.py:23
  10.9 7.4 %collective-permute-start.4 = (bf16[2,128,256]{2,1,0:T(8,128)(2,1)S(1)}, bf16[2,128,256]{2,1,0:T(8,128)(2,1)S(1)}, u32[]{:S(2)}, u32[]{:S(2)}) collective-permute-start(bf16[2,128,256]{2,1,0:T(8,128)(2,1)S(1)} %stack.1.even), channel_id=1, source_target_pairs={{0,4},{1,5},{2,6},{3,7},{4,0},{5,1},{6,2},{7,3},{8,12},{9,13},{10,... | collective-permute-start | bytes 393224 | tf_op jit(solution)/shard_map/ppermute | solution.py:23
  15.6 3.3 %collective-permute-start.3 = (bf16[2,128,256]{2,1,0:T(8,128)(2,1)S(1)}, bf16[2,128,256]{2,1,0:T(8,128)(2,1)S(1)}, u32[]{:S(2)}, u32[]{:S(2)}) collective-permute-start(bf16[2,128,256]{2,1,0:T(8,128)(2,1)S(1)} %gate.3.even), channel_id=1, source_target_pairs={{0,1},{1,0},{2,3},{3,2},{4,5},{5,4},{6,7},{7,6},{8,9},{9,8},{10,11... | collective-permute-start | bytes 393224 | tf_op jit(solution)/shard_map/ppermute | solution.py:23
  18.3 1.4 %collective-permute-start.5 = (bf16[2,128,256]{2,1,0:T(8,128)(2,1)S(1)}, bf16[2,128,256]{2,1,0:T(8,128)(2,1)S(1)}, u32[]{:S(2)}, u32[]{:S(2)}) collective-permute-start(bf16[2,128,256]{2,1,0:T(8,128)(2,1)S(1)} %gate.4.even), channel_id=1, source_target_pairs={{0,1},{1,0},{2,3},{3,2},{4,5},{5,4},{6,7},{7,6},{8,9},{9,8},{10,11... | collective-permute-start | bytes 393224 | tf_op jit(solution)/shard_map/ppermute | solution.py:23
  18.4 2.0 %collective-permute-start.7 = (bf16[2,128,256]{2,1,0:T(8,128)(2,1)S(1)}, bf16[2,128,256]{2,1,0:T(8,128)(2,1)S(1)}, u32[]{:S(2)}, u32[]{:S(2)}) collective-permute-start(bf16[2,128,256]{2,1,0:T(8,128)(2,1)S(1)} %gate.5.refs_1_), channel_id=1, source_target_pairs={{0,1},{1,0},{2,3},{3,2},{4,5},{5,4},{6,7},{7,6},{8,9},{9,8},{10,11... | collective-permute-start | bytes 393224 | tf_op jit(solution)/shard_map/ppermute | solution.py:23
  21.5 19.4 %copy-start = (f32[256]{0:T(256)S(1)}, f32[256]{0:T(256)}, u32[]{:S(2)}) copy-start(f32[256]{0:T(256)} %param.12) | copy-start | bytes 3076
  21.5 1.6 %collective-permute-start.8 = (f32[264,256]{1,0:T(8,128)S(1)}, f32[264,256]{1,0:T(8,128)S(1)}, u32[]{:S(2)}, u32[]{:S(2)}) collective-permute-start(f32[264,256]{1,0:T(8,128)S(1)} %get-tuple-element.39), channel_id=1, source_target_pairs={{0,1},{1,0},{2,3},{3,2},{4,5},{5,4},{6,7},{7,6},{8,9},{9,8},{10,11... | collective-permute-start | bytes 811016 | tf_op jit(solution)/shard_map/ppermute | solution.py:23
  23.2 7.5 %collective-permute-start.11 = (bf16[272,256]{1,0:T(8,128)(2,1)S(1)}, bf16[272,256]{1,0:T(8,128)(2,1)S(1)}, u32[]{:S(2)}, u32[]{:S(2)}) collective-permute-start(bf16[272,256]{1,0:T(8,128)(2,1)S(1)} %pack_pair.1.refs_0_), channel_id=1, source_target_pairs={{0,6},{1,7},{2,4},{3,5},{4,2},{5,3},{6,0},{7,1},{8,14},{9,15},{10,... | collective-permute-start | bytes 417800 | tf_op jit(solution)/shard_map/ppermute | solution.py:23
  24.3 7.9 %collective-permute-start.10 = (bf16[272,256]{1,0:T(8,128)(2,1)S(1)}, bf16[272,256]{1,0:T(8,128)(2,1)S(1)}, u32[]{:S(2)}, u32[]{:S(2)}) collective-permute-start(bf16[272,256]{1,0:T(8,128)(2,1)S(1)} %pack_pair.1.refs_0_), channel_id=1, source_target_pairs={{0,4},{1,5},{2,6},{3,7},{4,0},{5,1},{6,2},{7,3},{8,12},{9,13},{10,... | collective-permute-start | bytes 417800 | tf_op jit(solution)/shard_map/ppermute | solution.py:23
  25.3 7.6 %collective-permute-start.9 = (bf16[272,256]{1,0:T(8,128)(2,1)S(1)}, bf16[272,256]{1,0:T(8,128)(2,1)S(1)}, u32[]{:S(2)}, u32[]{:S(2)}) collective-permute-start(bf16[272,256]{1,0:T(8,128)(2,1)S(1)} %pack_pair.1.refs_0_), channel_id=1, source_target_pairs={{0,2},{1,3},{2,0},{3,1},{4,6},{5,7},{6,4},{7,5},{8,10},{9,11},{10,... | collective-permute-start | bytes 417800 | tf_op jit(solution)/shard_map/ppermute | solution.py:23
  33.0 7.9 %collective-permute-start.12 = (bf16[304,256]{1,0:T(8,128)(2,1)S(1)}, bf16[304,256]{1,0:T(8,128)(2,1)S(1)}, u32[]{:S(2)}, u32[]{:S(2)}) collective-permute-start(bf16[304,256]{1,0:T(8,128)(2,1)S(1)} %merge.1.near_part), channel_id=1, source_target_pairs={{0,12},{1,13},{2,14},{3,15},{4,8},{5,9},{6,10},{7,11},{8,4},{9,5},... | collective-permute-start | bytes 466952 | tf_op jit(solution)/shard_map/ppermute | solution.py:23
  36.6 5.5 %collective-permute-start.13 = (bf16[304,256]{1,0:T(8,128)(2,1)S(1)}, bf16[304,256]{1,0:T(8,128)(2,1)S(1)}, u32[]{:S(2)}, u32[]{:S(2)}) collective-permute-start(bf16[304,256]{1,0:T(8,128)(2,1)S(1)} %merge.1.near_part), channel_id=1, source_target_pairs={{0,1},{1,0},{2,3},{3,2},{4,5},{5,4},{6,7},{7,6},{8,9},{9,8},{10,11... | collective-permute-start | bytes 466952 | tf_op jit(solution)/shard_map/ppermute | solution.py:23
  40.9 1.4 %collective-permute-start.14 = (bf16[304,256]{1,0:T(8,128)(2,1)S(1)}, bf16[304,256]{1,0:T(8,128)(2,1)S(1)}, u32[]{:S(2)}, u32[]{:S(2)}) collective-permute-start(bf16[304,256]{1,0:T(8,128)(2,1)S(1)} %collective-permute-done.12.far_part), channel_id=1, source_target_pairs={{0,1},{1,0},{2,3},{3,2},{4,5},{5,4},{6,7},{7,6},{8,9},{9,8},{10,11... | collective-permute-start | bytes 466952 | tf_op jit(solution)/shard_map/ppermute | solution.py:23

commit v13 on v12

--- a/solution.py
+++ b/solution.py
@@ -552,7 +552,7 @@
     rows, rank = source_prev.shape
     cells = rows * count
     bits = [1 << b for b in range(count.bit_length() - 1)]
-    opposite = bits[-1] | bits[-2]
+    opposite = bits[-1]
     exchange = functools.partial(lax.all_to_all, axis_name="cell", split_axis=0, concat_axis=0)
 
     q, own_table, turned, totals = fetch(source_prev, target_prev, loadings, live)
@@ -588,7 +588,7 @@
         others = [moved[m] for m in steps]
         payload = merge(rank, cards, used, place, payload, *others)
         cards = cards * (1 + len(others))
-    mine = [payload, swap(payload, count, opposite)]
+    mine = [payload, swap(payload, count, bits[-1] | bits[-2])]
     other = [swap(part, count, 1) for part in mine]
 
     k_own, k_other, copies, consts = kernels(

time: 76.5 us -> 76.5 us (level)
  waiting for transfers between devices: 14.2 us -> 15.9 us
  starting transfers between devices: 16.8 us -> 15.4 us
    ppermute x15, waiting for transfers between devices: 14.2 us -> 15.9 us  [swap(): return lax.ppermute(value, 'cell', [(i, i ^ mask) for i in range(count)])]
    ppermute x15, starting transfers between devices: 16.8 us -> 15.4 us  [swap(): return lax.ppermute(value, 'cell', [(i, i ^ mask) for i in range(count)])]
where the time goes in v13:
time: 76.5 us; the launch traced here: 76.2 us
  blocking collectives  29.7 us (39%)
  waiting for transfers between devices  15.9 us (21%)
  starting transfers between devices  15.4 us (20%)
  Pallas kernels  14.5 us (19%)
  between operations  0.8 us (1%)
    all_to_all x2, blocking collectives, on_device(): exchange(copies)  20.5 us
    ppermute x15, waiting for transfers between devices, swap(): return lax.ppermute(value, 'cell', [(i, i ^ mask) for i in range(count)])  15.9 us
    ppermute x15, starting transfers between devices, swap(): return lax.ppermute(value, 'cell', [(i, i ^ mask) for i in range(count)])  15.4 us
    all_to_all x1, blocking collectives, on_device(): out_s, out_t, weights = finish(cells, *scaled, exchange(copies), consts)  9.2 us
    pallas_call x1, Pallas kernels, first_share(): call(functools.partial(first_kernel, masks, later_masks), 'embed_first',...  3.64 us
    pallas_call x2, Pallas kernels, cross(): call(functools.partial(cross_kernel, flip, at), 'cross', [SMEM] + [VMEM]...  2.26 us
    pallas_call x1, Pallas kernels, fetch(): call(fetch_kernel, 'fetch', [HBM] * 4, [VMEM] * 4, [pltpu.VMEM((2, rows,...  1.81 us
  transfers between devices with their start and end apart: 15, of which 9 were waited for; matrix products, arithmetic and copies ran while one was open for 0% of the time, Pallas kernels for 12%

profile of v13, /device:TPU:0, one launch (start us, length us, event | category | flops | bytes accessed | tf_op | source)
XLA Modules:
  0.0 76.2 jit_solution(12098709551388362193)
XLA Ops:
  0.6 4.1 %collective-permute-start = (bf16[128,256]{1,0:T(8,128)(2,1)}, bf16[128,256]{1,0:T(8,128)(2,1)S(1)}, u32[]{:S(2)}, u32[]{:S(2)}) collective-permute-start(bf16[128,256]{1,0:T(8,128)(2,1)} %table.1), channel_id=1, source_target_pairs={{0,8},{1,9},{2,10},{3,11},{4,12},{5,13},{6,14},{7,15},{8,0},{9,1},... | collective-permute-start | bytes 196616 | tf_op jit(solution)/shard_map/ppermute | solution.py:23
  4.7 1.8 %fetch.1 = (f32[2,1024,256]{2,1,0:T(8,128)S(1)}, bf16[128,256]{1,0:T(8,128)(2,1)S(1)}, bf16[2,256,1024]{2,1,0:T(8,128)(2,1)S(1)}, f32[3,1,256]{2,1,0:T(1,128)S(1)}) custom-call(f32[1024,256]{1,0:T(8,128)} %qs.1, f32[1024,256]{1,0:T(8,128)} %qt.1, bf16[128,256]{1,0:T(8,128)(2,1)} %table.1, s32[2]{0:T(128)} %bitcast.6), custom_call_target="tpu_custom_call" | custom-call | bytes 2097152 | tf_op jit(solution)/shard_map/fetch/pallas_call | solution.py:103
  6.6 2.0 %collective-permute-done.refs_1_ = bf16[128,256]{1,0:T(8,128)(2,1)S(1)} collective-permute-done((bf16[128,256]{1,0:T(8,128)(2,1)}, bf16[128,256]{1,0:T(8,128)(2,1)S(1)}, u32[]{:S(2)}, u32[]{:S(2)}) %collective-permute-start) | collective-permute-done | bytes 65568 | tf_op jit(solution)/shard_map/ppermute | solution.py:23
  8.6 0.1 collective-permute-start.1
  8.7 1.7 %collective-permute-start.2 = (bf16[2,128,256]{2,1,0:T(8,128)(2,1)S(1)}, bf16[2,128,256]{2,1,0:T(8,128)(2,1)S(1)}, u32[]{:S(2)}, u32[]{:S(2)}) collective-permute-start(bf16[2,128,256]{2,1,0:T(8,128)(2,1)S(1)} %stack.1.even), channel_id=1, source_target_pairs={{0,6},{1,7},{2,4},{3,5},{4,2},{5,3},{6,0},{7,1},{8,14},{9,15},{10,... | collective-permute-start | bytes 393224 | tf_op jit(solution)/shard_map/ppermute | solution.py:23
  10.4 0.5 collective-permute-start.6
  10.9 1.4 %collective-permute-start.4 = (bf16[2,128,256]{2,1,0:T(8,128)(2,1)S(1)}, bf16[2,128,256]{2,1,0:T(8,128)(2,1)S(1)}, u32[]{:S(2)}, u32[]{:S(2)}) collective-permute-start(bf16[2,128,256]{2,1,0:T(8,128)(2,1)S(1)} %stack.1.even), channel_id=1, source_target_pairs={{0,4},{1,5},{2,6},{3,7},{4,0},{5,1},{6,2},{7,3},{8,12},{9,13},{10,... | collective-permute-start | bytes 393224 | tf_op jit(solution)/shard_map/ppermute | solution.py:23
  12.2 0.0 collective-permute-done.1.odd
  12.2 3.6 %embed_first.1 = (f32[2,1024,256]{2,1,0:T(8,128)S(1)}, bf16[2,6,1024,256]{3,2,1,0:T(8,128)(2,1)S(1)}) custom-call(s32[1]{0:T(128)} %bitcast.place, bf16[1024,2048]{1,0:T(8,128)(2,1)} %xs.1, bf16[1024,2048]{1,0:T(8,128)(2,1)} %xt.1, bf16[2,128,256]{2,1,0:T(8,128)(2,1)S(1)} %stack.1.even, bf16[2,128,256]{2,1,0:T(8,128)(2,1)S(1)} %collective-permute-done.1.odd), custom_call_target="tpu_custom_call" | custom-call | flops 1073741824 | bytes 8388608 | tf_op jit(solution)/shard_map/embed_first/pallas_call | solution.py:167
  15.9 0.1 collective-permute-done.2.value
  16.0 0.1 collective-permute-start.3
  16.1 2.5 %collective-permute-done.4.value = bf16[2,128,256]{2,1,0:T(8,128)(2,1)S(1)} collective-permute-done((bf16[2,128,256]{2,1,0:T(8,128)(2,1)S(1)}, bf16[2,128,256]{2,1,0:T(8,128)(2,1)S(1)}, u32[]{:S(2)}, u32[]{:S(2)}) %collective-permute-start.4) | collective-permute-done | bytes 131104 | tf_op jit(solution)/shard_map/ppermute | solution.py:23
  18.6 0.1 collective-permute-start.5
  18.7 0.0 collective-permute-done.6.value
  18.7 0.5 collective-permute-start.7
  19.3 0.0 collective-permute-done.3.odd
  19.3 0.7 embed_next.2.part
  20.0 0.0 collective-permute-done.5.odd
  20.0 0.7 embed_next.3.part
  20.8 0.0 collective-permute-done.7.refs_2_
  20.8 1.0 %cross.3 = (f32[1024,256]{1,0:T(8,128)S(1)}, f32[264,256]{1,0:T(8,128)S(1)}, f32[1024,1]{1,0:T(8,128)S(1)}) custom-call(s32[1]{0:T(128)} %bitcast.place, f32[2,1024,256]{2,1,0:T(8,128)S(1)} %embed_next.3.part, f32[2,1024,256]{2,1,0:T(8,128)S(1)} %get-tuple-element.31.q, bf16[2,256,1024]{2,1,0:T(8,128)(2,1)S(1)} %get-tuple-element.32.turned, ...), custom_call_target="tpu_custom_call" | custom-call | flops 134217728 | tf_op jit(solution)/shard_map/cross/pallas_call | solution.py:265
  21.8 0.0 copy-start
  21.9 0.2 collective-permute-start.8
  22.1 1.2 %cross.2 = (f32[1024,256]{1,0:T(8,128)S(1)}, f32[264,256]{1,0:T(8,128)S(1)}, f32[1024,1]{1,0:T(8,128)S(1)}, f32[2,1024,1]{2,1,0:T(8,128)S(1)}) custom-call(s32[1]{0:T(128)} %bitcast.place, f32[2,1024,256]{2,1,0:T(8,128)S(1)} %embed_next.3.part, f32[2,1024,256]{2,1,0:T(8,128)S(1)} %get-tuple-element.31.q, bf16[2,256,1024]{2,1,0:T(8,128)(2,1)S(1)} %get-tuple-element.32.turned, ...), custom_call_target="tpu_custom_call" | custom-call | flops 134217728 | tf_op jit(solution)/shard_map/cross/pallas_call | solution.py:265
  23.3 0.2 collective-permute-done.8.recv
  23.5 1.0 %collective-permute-start.11 = (bf16[272,256]{1,0:T(8,128)(2,1)S(1)}, bf16[272,256]{1,0:T(8,128)(2,1)S(1)}, u32[]{:S(2)}, u32[]{:S(2)}) collective-permute-start(bf16[272,256]{1,0:T(8,128)(2,1)S(1)} %pack_pair.1.refs_0_), channel_id=1, source_target_pairs={{0,6},{1,7},{2,4},{3,5},{4,2},{5,3},{6,0},{7,1},{8,14},{9,15},{10,... | collective-permute-start | bytes 417800 | tf_op jit(solution)/shard_map/ppermute | solution.py:23
  24.5 0.8 %collective-permute-start.10 = (bf16[272,256]{1,0:T(8,128)(2,1)S(1)}, bf16[272,256]{1,0:T(8,128)(2,1)S(1)}, u32[]{:S(2)}, u32[]{:S(2)}) collective-permute-start(bf16[272,256]{1,0:T(8,128)(2,1)S(1)} %pack_pair.1.refs_0_), channel_id=1, source_target_pairs={{0,4},{1,5},{2,6},{3,7},{4,0},{5,1},{6,2},{7,3},{8,12},{9,13},{10,... | collective-permute-start | bytes 417800 | tf_op jit(solution)/shard_map/ppermute | solution.py:23
  25.3 1.7 %collective-permute-start.9 = (bf16[272,256]{1,0:T(8,128)(2,1)S(1)}, bf16[272,256]{1,0:T(8,128)(2,1)S(1)}, u32[]{:S(2)}, u32[]{:S(2)}) collective-permute-start(bf16[272,256]{1,0:T(8,128)(2,1)S(1)} %pack_pair.1.refs_0_), channel_id=1, source_target_pairs={{0,2},{1,3},{2,0},{3,1},{4,6},{5,7},{6,4},{7,5},{8,10},{9,11},{10,... | collective-permute-start | bytes 417800 | tf_op jit(solution)/shard_map/ppermute | solution.py:23
  27.1 4.0 %collective-permute-done.11.refs_3_ = bf16[272,256]{1,0:T(8,128)(2,1)S(1)} collective-permute-done((bf16[272,256]{1,0:T(8,128)(2,1)S(1)}, bf16[272,256]{1,0:T(8,128)(2,1)S(1)}, u32[]{:S(2)}, u32[]{:S(2)}) %collective-permute-start.11) | collective-permute-done | bytes 139296 | tf_op jit(solution)/shard_map/ppermute | solution.py:23
  31.0 1.1 %collective-permute-done.10.refs_2_ = bf16[272,256]{1,0:T(8,128)(2,1)S(1)} collective-permute-done((bf16[272,256]{1,0:T(8,128)(2,1)S(1)}, bf16[272,256]{1,0:T(8,128)(2,1)S(1)}, u32[]{:S(2)}, u32[]{:S(2)}) %collective-permute-start.10) | collective-permute-done | bytes 139296 | tf_op jit(solution)/shard_map/ppermute | solution.py:23
  32.1 1.1 %collective-permute-done.9.refs_1_ = bf16[272,256]{1,0:T(8,128)(2,1)S(1)} collective-permute-done((bf16[272,256]{1,0:T(8,128)(2,1)S(1)}, bf16[272,256]{1,0:T(8,128)(2,1)S(1)}, u32[]{:S(2)}, u32[]{:S(2)}) %collective-permute-start.9) | collective-permute-done | bytes 139296 | tf_op jit(solution)/shard_map/ppermute | solution.py:23
  33.2 0.1 merge.1.near_part
  33.3 3.2 %collective-permute-start.12 = (bf16[304,256]{1,0:T(8,128)(2,1)S(1)}, bf16[304,256]{1,0:T(8,128)(2,1)S(1)}, u32[]{:S(2)}, u32[]{:S(2)}) collective-permute-start(bf16[304,256]{1,0:T(8,128)(2,1)S(1)} %merge.1.near_part), channel_id=1, source_target_pairs={{0,12},{1,13},{2,14},{3,15},{4,8},{5,9},{6,10},{7,11},{8,4},{9,5},... | collective-permute-start | bytes 466952 | tf_op jit(solution)/shard_map/ppermute | solution.py:23
  36.6 0.0 collective-permute-start.13
  36.6 4.7 %collective-permute-done.12.far_part = bf16[304,256]{1,0:T(8,128)(2,1)S(1)} collective-permute-done((bf16[304,256]{1,0:T(8,128)(2,1)S(1)}, bf16[304,256]{1,0:T(8,128)(2,1)S(1)}, u32[]{:S(2)}, u32[]{:S(2)}) %collective-permute-start.12) | collective-permute-done | bytes 155680 | tf_op jit(solution)/shard_map/ppermute | solution.py:23
  41.3 0.0 collective-permute-start.14
  41.3 0.0 copy-done
  41.3 1.2 %kernel_other.1 = (f32[1024,256]{1,0:T(8,128)S(1)}, f32[8,256]{1,0:T(8,128)S(1)}, f32[264,256]{1,0:T(8,128)S(1)}) custom-call(s32[1]{0:T(128)} %bitcast.place, f32[2,1024,1]{2,1,0:T(8,128)S(1)} %get-tuple-element.33.mask, f32[1024,1]{1,0:T(8,128)S(1)} %get-tuple-element.36.norms, f32[1024,256]{1,0:T(8,128)S(1)} %get-tuple-element.37.emb, ...), custom_call_target="tpu_custom_call" | custom-call | flops 402653184 | tf_op jit(solution)/shard_map/kernel_other/pallas_call | solution.py:514
  42.5 0.0 collective-permute-done.13.near_part
  42.5 0.2 collective-permute-done.14.far_part
  42.6 1.2 %kernel_own.1 = (f32[1024,256]{1,0:T(8,128)S(1)}, f32[16,2,256]{2,1,0:T(2,128)S(1)}, f32[8,256]{1,0:T(8,128)S(1)}) custom-call(s32[1]{0:T(128)} %bitcast.place, f32[2,1024,1]{2,1,0:T(8,128)S(1)} %get-tuple-element.33.mask, f32[1024,1]{1,0:T(8,128)S(1)} %get-tuple-element.34.norms, f32[1024,256]{1,0:T(8,128)S(1)} %get-tuple-element.35.emb, ...), custom_call_target="tpu_custom_call" | custom-call | flops 402653184 | tf_op jit(solution)/shard_map/kernel_own/pallas_call | solution.py:518
  43.9 11.2 %all_to_all.15.parts = f32[16,2,256]{2,1,0:T(2,128)S(1)} all-to-all(f32[16,2,256]{2,1,0:T(2,128)S(1)} %get-tuple-element.44), channel_id=1, replica_groups=mesh['grp'=2,'cell'=16] {'cell'}, dimensions={0} | all-to-all | bytes 65536 | tf_op jit(solution)/shard_map/all_to_all | solution.py:601
  55.1 0.6 sweep.2
  55.8 9.2 %all_to_all.16.parts = f32[16,2,256]{2,1,0:T(2,128)S(1)} all-to-all(f32[16,2,256]{2,1,0:T(2,128)S(1)} %sweep.2), channel_id=1, replica_groups=mesh['grp'=2,'cell'=16] {'cell'}, dimensions={0} | all-to-all | bytes 65536 | tf_op jit(solution)/shard_map/all_to_all | solution.py:601
  65.0 0.6 sweep.3
  65.6 9.2 %all_to_all.17.parts = f32[16,2,256]{2,1,0:T(2,128)S(1)} all-to-all(f32[16,2,256]{2,1,0:T(2,128)S(1)} %get-tuple-element.47), channel_id=1, replica_groups=mesh['grp'=2,'cell'=16] {'cell'}, dimensions={0} | all-to-all | bytes 65536 | tf_op jit(solution)/shard_map/all_to_all | solution.py:602
  74.8 1.5 %finish.1 = (f32[1024,256]{1,0:T(8,128)}, f32[1024,256]{1,0:T(8,128)}, f32[1,256]{1,0:T(1,128)}) custom-call(f32[2,1024,256]{2,1,0:T(8,128)S(1)} %get-tuple-element.46.scaled, f32[16,2,256]{2,1,0:T(2,128)S(1)} %all_to_all.17.parts, f32[8,256]{1,0:T(8,128)S(1)} %get-tuple-element.45.consts), custom_call_target="tpu_custom_call" | custom-call | tf_op jit(solution)/shard_map/finish/pallas_call | solution.py:536
  (5 shorter events, 0.1 us)
Async XLA Ops:
  0.6 8.0 %collective-permute-start = (bf16[128,256]{1,0:T(8,128)(2,1)}, bf16[128,256]{1,0:T(8,128)(2,1)S(1)}, u32[]{:S(2)}, u32[]{:S(2)}) collective-permute-start(bf16[128,256]{1,0:T(8,128)(2,1)} %table.1), channel_id=1, source_target_pairs={{0,8},{1,9},{2,10},{3,11},{4,12},{5,13},{6,14},{7,15},{8,0},{9,1},... | collective-permute-start | bytes 196616 | tf_op jit(solution)/shard_map/ppermute | solution.py:23
  8.6 3.6 %collective-permute-start.1 = (bf16[2,128,256]{2,1,0:T(8,128)(2,1)S(1)}, bf16[2,128,256]{2,1,0:T(8,128)(2,1)S(1)}, u32[]{:S(2)}, u32[]{:S(2)}) collective-permute-start(bf16[2,128,256]{2,1,0:T(8,128)(2,1)S(1)} %stack.1.even), channel_id=1, source_target_pairs={{0,1},{1,0},{2,3},{3,2},{4,5},{5,4},{6,7},{7,6},{8,9},{9,8},{10,11... | collective-permute-start | bytes 393224 | tf_op jit(solution)/shard_map/ppermute | solution.py:23
  8.7 7.3 %collective-permute-start.2 = (bf16[2,128,256]{2,1,0:T(8,128)(2,1)S(1)}, bf16[2,128,256]{2,1,0:T(8,128)(2,1)S(1)}, u32[]{:S(2)}, u32[]{:S(2)}) collective-permute-start(bf16[2,128,256]{2,1,0:T(8,128)(2,1)S(1)} %stack.1.even), channel_id=1, source_target_pairs={{0,6},{1,7},{2,4},{3,5},{4,2},{5,3},{6,0},{7,1},{8,14},{9,15},{10,... | collective-permute-start | bytes 393224 | tf_op jit(solution)/shard_map/ppermute | solution.py:23
  10.4 8.3 %collective-permute-start.6 = (bf16[2,128,256]{2,1,0:T(8,128)(2,1)S(1)}, bf16[2,128,256]{2,1,0:T(8,128)(2,1)S(1)}, u32[]{:S(2)}, u32[]{:S(2)}) collective-permute-start(bf16[2,128,256]{2,1,0:T(8,128)(2,1)S(1)} %stack.1.even), channel_id=1, source_target_pairs={{0,2},{1,3},{2,0},{3,1},{4,6},{5,7},{6,4},{7,5},{8,10},{9,11},{10,... | collective-permute-start | bytes 393224 | tf_op jit(solution)/shard_map/ppermute | solution.py:23
  10.9 7.7 %collective-permute-start.4 = (bf16[2,128,256]{2,1,0:T(8,128)(2,1)S(1)}, bf16[2,128,256]{2,1,0:T(8,128)(2,1)S(1)}, u32[]{:S(2)}, u32[]{:S(2)}) collective-permute-start(bf16[2,128,256]{2,1,0:T(8,128)(2,1)S(1)} %stack.1.even), channel_id=1, source_target_pairs={{0,4},{1,5},{2,6},{3,7},{4,0},{5,1},{6,2},{7,3},{8,12},{9,13},{10,... | collective-permute-start | bytes 393224 | tf_op jit(solution)/shard_map/ppermute | solution.py:23
  16.0 3.3 %collective-permute-start.3 = (bf16[2,128,256]{2,1,0:T(8,128)(2,1)S(1)}, bf16[2,128,256]{2,1,0:T(8,128)(2,1)S(1)}, u32[]{:S(2)}, u32[]{:S(2)}) collective-permute-start(bf16[2,128,256]{2,1,0:T(8,128)(2,1)S(1)} %gate.3.even), channel_id=1, source_target_pairs={{0,1},{1,0},{2,3},{3,2},{4,5},{5,4},{6,7},{7,6},{8,9},{9,8},{10,11... | collective-permute-start | bytes 393224 | tf_op jit(solution)/shard_map/ppermute | solution.py:23
  18.6 1.4 %collective-permute-start.5 = (bf16[2,128,256]{2,1,0:T(8,128)(2,1)S(1)}, bf16[2,128,256]{2,1,0:T(8,128)(2,1)S(1)}, u32[]{:S(2)}, u32[]{:S(2)}) collective-permute-start(bf16[2,128,256]{2,1,0:T(8,128)(2,1)S(1)} %gate.4.even), channel_id=1, source_target_pairs={{0,1},{1,0},{2,3},{3,2},{4,5},{5,4},{6,7},{7,6},{8,9},{9,8},{10,11... | collective-permute-start | bytes 393224 | tf_op jit(solution)/shard_map/ppermute | solution.py:23
  18.7 2.0 %collective-permute-start.7 = (bf16[2,128,256]{2,1,0:T(8,128)(2,1)S(1)}, bf16[2,128,256]{2,1,0:T(8,128)(2,1)S(1)}, u32[]{:S(2)}, u32[]{:S(2)}) collective-permute-start(bf16[2,128,256]{2,1,0:T(8,128)(2,1)S(1)} %gate.5.refs_1_), channel_id=1, source_target_pairs={{0,1},{1,0},{2,3},{3,2},{4,5},{5,4},{6,7},{7,6},{8,9},{9,8},{10,11... | collective-permute-start | bytes 393224 | tf_op jit(solution)/shard_map/ppermute | solution.py:23
  21.8 19.4 %copy-start = (f32[256]{0:T(256)S(1)}, f32[256]{0:T(256)}, u32[]{:S(2)}) copy-start(f32[256]{0:T(256)} %param.12) | copy-start | bytes 3076
  21.9 1.6 %collective-permute-start.8 = (f32[264,256]{1,0:T(8,128)S(1)}, f32[264,256]{1,0:T(8,128)S(1)}, u32[]{:S(2)}, u32[]{:S(2)}) collective-permute-start(f32[264,256]{1,0:T(8,128)S(1)} %get-tuple-element.39), channel_id=1, source_target_pairs={{0,1},{1,0},{2,3},{3,2},{4,5},{5,4},{6,7},{7,6},{8,9},{9,8},{10,11... | collective-permute-start | bytes 811016 | tf_op jit(solution)/shard_map/ppermute | solution.py:23
  23.5 7.5 %collective-permute-start.11 = (bf16[272,256]{1,0:T(8,128)(2,1)S(1)}, bf16[272,256]{1,0:T(8,128)(2,1)S(1)}, u32[]{:S(2)}, u32[]{:S(2)}) collective-permute-start(bf16[272,256]{1,0:T(8,128)(2,1)S(1)} %pack_pair.1.refs_0_), channel_id=1, source_target_pairs={{0,6},{1,7},{2,4},{3,5},{4,2},{5,3},{6,0},{7,1},{8,14},{9,15},{10,... | collective-permute-start | bytes 417800 | tf_op jit(solution)/shard_map/ppermute | solution.py:23
  24.5 7.6 %collective-permute-start.10 = (bf16[272,256]{1,0:T(8,128)(2,1)S(1)}, bf16[272,256]{1,0:T(8,128)(2,1)S(1)}, u32[]{:S(2)}, u32[]{:S(2)}) collective-permute-start(bf16[272,256]{1,0:T(8,128)(2,1)S(1)} %pack_pair.1.refs_0_), channel_id=1, source_target_pairs={{0,4},{1,5},{2,6},{3,7},{4,0},{5,1},{6,2},{7,3},{8,12},{9,13},{10,... | collective-permute-start | bytes 417800 | tf_op jit(solution)/shard_map/ppermute | solution.py:23
  25.3 7.9 %collective-permute-start.9 = (bf16[272,256]{1,0:T(8,128)(2,1)S(1)}, bf16[272,256]{1,0:T(8,128)(2,1)S(1)}, u32[]{:S(2)}, u32[]{:S(2)}) collective-permute-start(bf16[272,256]{1,0:T(8,128)(2,1)S(1)} %pack_pair.1.refs_0_), channel_id=1, source_target_pairs={{0,2},{1,3},{2,0},{3,1},{4,6},{5,7},{6,4},{7,5},{8,10},{9,11},{10,... | collective-permute-start | bytes 417800 | tf_op jit(solution)/shard_map/ppermute | solution.py:23
  33.3 7.9 %collective-permute-start.12 = (bf16[304,256]{1,0:T(8,128)(2,1)S(1)}, bf16[304,256]{1,0:T(8,128)(2,1)S(1)}, u32[]{:S(2)}, u32[]{:S(2)}) collective-permute-start(bf16[304,256]{1,0:T(8,128)(2,1)S(1)} %merge.1.near_part), channel_id=1, source_target_pairs={{0,12},{1,13},{2,14},{3,15},{4,8},{5,9},{6,10},{7,11},{8,4},{9,5},... | collective-permute-start | bytes 466952 | tf_op jit(solution)/shard_map/ppermute | solution.py:23
  36.6 5.9 %collective-permute-start.13 = (bf16[304,256]{1,0:T(8,128)(2,1)S(1)}, bf16[304,256]{1,0:T(8,128)(2,1)S(1)}, u32[]{:S(2)}, u32[]{:S(2)}) collective-permute-start(bf16[304,256]{1,0:T(8,128)(2,1)S(1)} %merge.1.near_part), channel_id=1, source_target_pairs={{0,1},{1,0},{2,3},{3,2},{4,5},{5,4},{6,7},{7,6},{8,9},{9,8},{10,11... | collective-permute-start | bytes 466952 | tf_op jit(solution)/shard_map/ppermute | solution.py:23
  41.3 1.4 %collective-permute-start.14 = (bf16[304,256]{1,0:T(8,128)(2,1)S(1)}, bf16[304,256]{1,0:T(8,128)(2,1)S(1)}, u32[]{:S(2)}, u32[]{:S(2)}) collective-permute-start(bf16[304,256]{1,0:T(8,128)(2,1)S(1)} %collective-permute-done.12.far_part), channel_id=1, source_target_pairs={{0,1},{1,0},{2,3},{3,2},{4,5},{5,4},{6,7},{7,6},{8,9},{9,8},{10,11... | collective-permute-start | bytes 466952 | tf_op jit(solution)/shard_map/ppermute | solution.py:23
